TPU v7x, 512 devices: a whole 4x8x8 slice. The times are simulated.
512 devices in a mesh: dp: 8 (over z_hi, x), ctx: 16 (over y, core), nbr: 4 (over z_lo).
Axes of the slice: x: 4, y: 8, z: 8 (z_hi: 2, z_lo: 4; z = z_hi * 4 + z_lo), core: 2. Of those that a mesh axis runs over, the one named last changes fastest.
Arguments:
- queries: bfloat16 [8, 4096, 2048], P('dp', 'ctx', 'nbr'), may hold values from -140 to 140
- cotangent: bfloat16 [8, 4096, 2048], P('dp', 'ctx', 'nbr'), may hold values from -6 to 6
- encoded: bfloat16 [8, 256, 64, 896], P('dp', 'ctx', 'nbr'), may hold values from -6 to 6
- kv_weight: bfloat16 [2, 896, 2048], P(None, None, 'nbr'), may hold values from -0.1875 to 0.1875
- neighbour_ids: int32 [8, 64, 4], P('dp', 'ctx'), may hold values from 0 to 255, as said below
Outputs:
- attended: bfloat16 [8, 4096, 2048], P('dp', 'ctx', 'nbr')
- query_grad: bfloat16 [8, 4096, 2048], P('dp', 'ctx', 'nbr')
- encoded_grad: bfloat16 [8, 256, 64, 896], P('dp', 'ctx', 'nbr')
- weight_grad: float32 [2, 896, 2048], P(None, 'dp', 'nbr')
Inputs may be any that keep to these rules, and one draw needn't show every extreme that they name: `neighbour_ids`: for every batch and every d < 16, the ids of the spans d * 4 to (d + 1) * 4 - 1 are exactly the blocks s * 16 + d + j for all s < 16 and j < 1, each named once.
All inputs are finite; a program needn't handle non-finite values.
Results may differ from a plain program's by a relative error of at most 0.029.
The roundings to bfloat16 on the way count: a program that leaves them out, or rounds other values in their place, can miss the bound.
Values may be sent and summed in bfloat16 or wider, within the bound.
No kernel may reach another device: no remote copies, remote signals or barrier semaphores. Data moves between devices by JAX's collectives and lax.ppermute only.
A program may use at most 128 MiB of HBM per device.

v0:
```python
import math

import jax
import jax.numpy as jnp
from jax import lax
from jax.sharding import PartitionSpec as P

HEAD_DIM = 128
SPAN = 64
PART = 64


def from_behind(block, axis, distance):
    devices = range(lax.axis_size(axis))
    route = [(i - distance, i) for i in devices if i - distance in devices]
    return lax.ppermute(block, axis, route)


def attend_forward(query_blocks, key_value):
    block_count, row_count, row_width = query_blocks.shape
    head_count = row_width // HEAD_DIM
    key_count = key_value.shape[1]
    scale_factor = 1.0 / math.sqrt(HEAD_DIM)
    query_heads = query_blocks.reshape(block_count, row_count, head_count, HEAD_DIM)
    key_heads = key_value[:, :, :row_width].reshape(block_count, key_count, head_count, HEAD_DIM)
    value_heads = key_value[:, :, row_width:].reshape(block_count, key_count, head_count, HEAD_DIM)
    scores = (
        jnp.einsum("cqhd,ckhd->chqk", query_heads, key_heads, preferred_element_type=jnp.float32)
        * scale_factor
    )
    score_top = jnp.max(scores, axis=-1, keepdims=True)
    raised = jnp.exp(scores - score_top)
    weights = raised / jnp.sum(raised, axis=-1, keepdims=True)
    weights_low = weights.astype(jnp.bfloat16)
    mixed = jnp.einsum(
        "chqk,ckhd->cqhd", weights_low, value_heads, preferred_element_type=jnp.float32
    )
    attended = mixed.astype(jnp.bfloat16).reshape(block_count, row_count, row_width)
    return (attended, (query_heads, key_heads, value_heads, weights, weights_low))


def attend_backward(saved, grad_blocks):
    query_heads, key_heads, value_heads, weights, weights_low = saved
    block_count, row_count, head_count, head_dim = query_heads.shape
    key_count = key_heads.shape[1]
    row_width = head_count * head_dim
    scale_factor = 1.0 / math.sqrt(HEAD_DIM)
    grad_heads = grad_blocks.reshape(block_count, row_count, head_count, head_dim)
    value_grads = jnp.einsum(
        "chqk,cqhd->ckhd", weights_low, grad_heads, preferred_element_type=jnp.float32
    )
    weight_grads = jnp.einsum(
        "cqhd,ckhd->chqk", grad_heads, value_heads, preferred_element_type=jnp.float32
    )
    inner = jnp.sum(weights * weight_grads, axis=-1, keepdims=True)
    score_grads = (weights * (weight_grads - inner) * scale_factor).astype(jnp.bfloat16)
    query_grads = jnp.einsum(
        "chqk,ckhd->cqhd", score_grads, key_heads, preferred_element_type=jnp.float32
    )
    key_grads = jnp.einsum(
        "chqk,cqhd->ckhd", score_grads, query_heads, preferred_element_type=jnp.float32
    )
    joined_grads = jnp.concatenate(
        (
            key_grads.reshape(block_count, key_count, row_width),
            value_grads.reshape(block_count, key_count, row_width),
        ),
        axis=-1,
    )
    return (
        query_grads.astype(jnp.bfloat16).reshape(block_count, row_count, row_width),
        joined_grads,
    )


def split_positions(values, groups):
    unit_count, position_count, width = values.shape
    return values.reshape(unit_count, groups, position_count // groups, width)


def shards(queries, cotangent, encoded, kv_weight, neighbour_ids):
    token_count = queries.shape[1]
    row_width = queries.shape[2]
    block_count = token_count // SPAN
    lead_rows = SPAN - 1
    unit_count = encoded.shape[1]
    owners = lax.axis_size("ctx")
    head_groups = lax.axis_size("nbr")
    group_size = unit_count // owners
    owner_index = lax.axis_index("ctx")
    joined = jnp.concatenate((kv_weight[0], kv_weight[1]), axis=1)
    gathered = lax.all_gather(encoded[0], "nbr", axis=1, tiled=True)
    relaid = lax.all_to_all(gathered, "ctx", split_axis=0, concat_axis=0, tiled=True)
    key_value = jnp.einsum(
        "upe,ef->upf", relaid, joined, preferred_element_type=jnp.float32
    ).astype(jnp.bfloat16)
    id_rows = neighbour_ids[0]
    local_rows = (
        id_rows // unit_count * group_size + id_rows % unit_count - owner_index * group_size
    ).reshape(-1)
    span_kv = jnp.take(key_value, local_rows, axis=0).reshape(block_count, 4 * PART, 2 * row_width)
    before = from_behind(span_kv[block_count - 1], "ctx", 1)
    all_kv = jnp.concatenate((before[None], span_kv), axis=0)
    zero_row = jnp.zeros((1, row_width), jnp.bfloat16)
    tail_pad = jnp.zeros((lead_rows, row_width), jnp.bfloat16)
    query_rows = jnp.concatenate((zero_row, queries[0], tail_pad), axis=0).reshape(
        block_count + 1, SPAN, row_width
    )
    grad_rows = jnp.concatenate((zero_row, cotangent[0], tail_pad), axis=0).reshape(
        block_count + 1, SPAN, row_width
    )
    attended_blocks, saved = attend_forward(query_rows, all_kv)
    query_grad_blocks, kv_grads = attend_backward(saved, grad_rows)
    attended = attended_blocks.reshape(-1, row_width)[1 : token_count + 1]
    query_grad = query_grad_blocks.reshape(-1, row_width)[1 : token_count + 1]
    returned = from_behind(kv_grads[0], "ctx", -1)
    span_grads = jnp.concatenate(
        (kv_grads[1:block_count], (kv_grads[block_count] + returned)[None]), axis=0
    )
    grads_low = span_grads.astype(jnp.bfloat16).reshape(block_count * 4, PART, 2 * row_width)
    inverse = (
        jnp.zeros((unit_count,), jnp.int32)
        .at[local_rows]
        .set(jnp.arange(unit_count, dtype=jnp.int32))
    )
    unit_grads = jnp.take(grads_low, inverse, axis=0)
    weight_term = jnp.einsum("upe,upf->ef", relaid, unit_grads, preferred_element_type=jnp.float32)
    dp_rows = lax.psum_scatter(weight_term, "dp", scatter_dimension=0, tiled=True)
    dp_piece = lax.psum(dp_rows, "ctx")
    weight_grad = jnp.stack((dp_piece[:, :row_width], dp_piece[:, row_width:]), axis=0)
    partial_grads = jnp.einsum(
        "upf,ef->upe", unit_grads, joined, preferred_element_type=jnp.float32
    ).astype(jnp.bfloat16)
    sent_back = lax.all_to_all(partial_grads, "ctx", split_axis=0, concat_axis=0, tiled=True)
    group_terms = lax.all_to_all(
        split_positions(sent_back, head_groups), "nbr", split_axis=1, concat_axis=1, tiled=True
    )
    encoded_grad = jnp.sum(group_terms.astype(jnp.float32), axis=1).astype(jnp.bfloat16)
    return (attended[None], query_grad[None], encoded_grad[None], weight_grad)


def solution(mesh):
    return jax.shard_map(
        shards,
        mesh=mesh,
        in_specs=(
            P("dp", "ctx", "nbr"),
            P("dp", "ctx", "nbr"),
            P("dp", "ctx", "nbr", None),
            P(None, None, "nbr"),
            P("dp", "ctx", None),
        ),
        out_specs=(
            P("dp", "ctx", "nbr"),
            P("dp", "ctx", "nbr"),
            P("dp", "ctx", "nbr", None),
            P(None, "dp", "nbr"),
        ),
        check_vma=False,
    )
```

profile of v0, /device:TPU:1, one launch (start us, length us, event | category | flops | bytes accessed | tf_op | source)
XLA Modules:
  0.0 447.0 jit_solution(783145999848141473)
XLA Ops:
  7.9 56.4 %all-gather.3.cloned.1.call-done = bf16[1,16,64,896]{3,2,1,0:T(8,128)(2,1)} async-done(((bf16[1,16,16,896]{3,2,1,0:T(8,128)(2,1)}), bf16[1,16,64,896]{3,2,1,0:T(8,128)(2,1)}) %all-gather.3.cloned.1.call-update) | async-done | bytes 1835024 | tf_op jit(solution)/shard_map/all_gather | solution.py:92
  64.3 7.8 %all-to-all-start = ((bf16[16,64,896]{2,1,0:T(8,128)(2,1)}), bf16[16,64,896]{2,1,0:T(8,128)(2,1)}, u32[]{:S(2)}, u32[]{:S(2)}) async-start(bf16[16,64,896]{2,1,0:T(8,128)(2,1)} %bitcast.89), calls=%async_computation | async-start | bytes 3670016 | tf_op jit(solution)/shard_map/all_to_all | solution.py:93
  73.4 42.4 %all-to-all-done = bf16[16,64,896]{2,1,0:T(8,128)(2,1)} async-done(((bf16[16,64,896]{2,1,0:T(8,128)(2,1)}), bf16[16,64,896]{2,1,0:T(8,128)(2,1)}, u32[]{:S(2)}, u32[]{:S(2)}) %all-to-all-start) | async-done | bytes 1835040 | tf_op jit(solution)/shard_map/all_to_all | solution.py:93
  115.8 4.1 convert_bitcast_fusion
  120.0 2.0 gather_fusion
  122.0 1.9 broadcast_select_fusion.1
  124.9 1.9 collective-permute-start
  127.4 2.6 copy.26
  130.0 3.3 collective-permute-done
  133.3 1.8 pad_maximum_fusion.1
  135.5 1.9 fusion.54
  137.8 4.1 fusion.33
  141.8 10.5 %fusion.13 = f32[5,4,128,256]{3,2,1,0:T(8,128)} fusion(f32[5,4,64,256]{3,2,1,0:T(8,128)S(1)} %fusion.37, bf16[5,64,4,128]{3,2,1,0:T(4,128)(2,1)S(1)} %reshape_reshape.12, f32[5,4,64,256]{3,2,1,0:T(8,128)} %get-tuple-element.28, f32[5,4,64]{2,1,0:T(4,128)S(1)} %get-tuple-element.27), kind=kOutput, calls=%fused_computation.31 | convolution fusion | flops 86181376 | bytes 5575680 | tf_op jit(solution)/shard_map/chqk,cqhd->ckhd/dot_general | solution.py:60
  152.4 2.1 copy.37
  154.5 3.2 copy.38
  157.7 2.1 fusion.29
  159.9 1.9 collective-permute-start.1
  162.7 1.8 fusion.3
  164.5 12.5 %collective-permute-done.1 = f32[256,1024]{1,0:T(8,128)} collective-permute-done((f32[256,1024]{1,0:T(8,128)}, f32[256,1024]{1,0:T(8,128)}, u32[]{:S(2)}, u32[]{:S(2)}) %collective-permute-start.1) | collective-permute-done | bytes 1048608 | tf_op jit(solution)/shard_map/ppermute | solution.py:16
  178.6 2.1 gather_fusion.1
  180.7 6.4 %convolution_bitcast_fusion = f32[896,1024]{0,1:T(8,128)} fusion(bf16[16,64,896]{2,1,0:T(8,128)(2,1)} %all-to-all-done, bf16[16,64,1024]{2,1,0:T(8,128)(2,1)} %gather_fusion.1, pred[16]{0:T(512)(128)(4,1)S(1)} %compare_and_fusion), kind=kOutput, calls=%fused_computation.17 | convolution fusion | flops 1880096768 | bytes 7602192 | tf_op jit(solution)/shard_map/upe,upf->ef/dot_general | solution.py:127
  187.1 5.0 %copy.45 = f32[896,1024]{1,0:T(8,128)} copy(f32[896,1024]{0,1:T(8,128)} %convolution_bitcast_fusion) | data formatting | bytes 7340032
  192.1 1.6 copy-done.5
  193.9 3.5 convolution_convert_fusion
  197.5 51.3 %all_to_all.15 = bf16[16,64,896]{2,1,0:T(8,128)(2,1)S(1)} all-to-all(bf16[16,64,896]{2,1,0:T(8,128)(2,1)S(1)} %convolution_convert_fusion), channel_id=1, replica_groups=mesh['dp'=8,'ctx'=16,'nbr'=4] {'ctx'}, dimensions={0} | all-to-all | bytes 3670016 | tf_op jit(solution)/shard_map/all_to_all | solution.py:134
  248.8 1.4 copy.39
  250.2 3.6 all-to-all-start.2
  253.9 9.9 %fusion.21 = bf16[5,64,4,128]{3,1,2,0:T(8,128)(2,1)S(1)} fusion(bf16[5,256,4,128]{1,3,2,0:T(8,128)(2,1)} %bitcast.85, f32[5,4,64,256]{3,2,1,0:T(8,128)} %copy-done.7, f32[5,4,64,256]{3,2,1,0:T(8,128)} %get-tuple-element.28, f32[5,4,64]{2,1,0:T(4,128)S(1)} %get-tuple-element.27), kind=kOutput, calls=%fused_computation.35 | convolution fusion | flops 86345216 | bytes 4264960 | tf_op jit(solution)/shard_map/chqk,ckhd->cqhd/dot_general | solution.py:57
  264.1 4.9 %fusion.24 = bf16[5,64,4,128]{3,1,2,0:T(8,128)(2,1)} fusion(bf16[5,256,4,128]{1,3,2,0:T(8,128)(2,1)S(1)} %bitcast.83, f32[5,4,64]{2,1,0:T(4,128)S(1)} %get-tuple-element.27, f32[5,4,64,256]{3,2,1,0:T(8,128)} %copy-done.4), kind=kOutput, calls=%fused_computation.36 | convolution fusion | flops 85034496 | bytes 2954240 | tf_op jit(solution)/shard_map/chqk,ckhd->cqhd/dot_general | solution.py:35
  270.2 46.9 %reduce-scatter.4.cloned.1.call-done = f32[112,1024]{1,0:T(8,128)} async-done(((f32[896,1024]{1,0:T(8,128)}), f32[112,1024]{1,0:T(8,128)}) %reduce-scatter.4.cloned.1.call-update) | async-done | bytes 458768
  317.1 2.0 copy.46
  321.2 117.2 %all-reduce.2.cloned.1.call-done = f32[112,1024]{0,1:T(8,128)} async-done(((f32[112,1024]{0,1:T(8,128)}), f32[112,1024]{0,1:T(8,128)}) %all-reduce.2.cloned.1.call-update) | async-done | bytes 458768 | tf_op jit(solution)/shard_map/psum | solution.py:129
  (64 shorter events, 12.7 us)
Async XLA Ops:
  7.2 57.1 %all-gather.3.cloned.1.call-start = ((), (), s32[]{:S(2)}) async-start(), calls=%async_computation.5 | async-start | bytes 2293760 | tf_op jit(solution)/shard_map/all_gather | solution.py:92
  64.3 7.9 %copy-start.12 = (s32[1,4,4]{2,1,0:T(4,128)S(1)}, s32[1,4,4]{2,1,0:T(4,128)}, u32[]{:S(2)}) copy-start(s32[1,4,4]{2,1,0:T(4,128)} %param.11) | copy-start | bytes 196
  64.3 8.0 %copy-start.6 = (bf16[2,896,512]{2,1,0:T(8,128)(2,1)S(1)}, bf16[2,896,512]{2,1,0:T(8,128)(2,1)}, u32[]{:S(2)}) copy-start(bf16[2,896,512]{2,1,0:T(8,128)(2,1)} %param.10) | copy-start | bytes 5505028
  64.3 51.6 %all-to-all-start = ((bf16[16,64,896]{2,1,0:T(8,128)(2,1)}), bf16[16,64,896]{2,1,0:T(8,128)(2,1)}, u32[]{:S(2)}, u32[]{:S(2)}) async-start(bf16[16,64,896]{2,1,0:T(8,128)(2,1)} %bitcast.89), calls=%async_computation | async-start | bytes 3670016 | tf_op jit(solution)/shard_map/all_to_all | solution.py:93
  72.1 245.0 %reduce-scatter.4.cloned.1.call-start = ((), (), s32[]{:S(2)}) async-start(), calls=%async_computation.6 | async-start | bytes 4128768
  73.4 46.6 %copy-start.8 = (bf16[896,512]{1,0:T(8,128)(2,1)}, bf16[896,512]{1,0:T(8,128)(2,1)S(1)}, u32[]{:S(2)}) copy-start(bf16[896,512]{1,0:T(8,128)(2,1)S(1)} %get-tuple-element.21) | copy-start | bytes 2752516
  123.9 3.1 copy-start.10
  123.9 3.1 copy-start.11
  124.9 8.3 %collective-permute-start = (bf16[256,1024]{0,1:T(8,128)(2,1)}, bf16[256,1024]{0,1:T(8,128)(2,1)}, u32[]{:S(2)}, u32[]{:S(2)}) collective-permute-start(bf16[256,1024]{0,1:T(8,128)(2,1)} %copy.25), channel_id=1, source_target_pairs={{0,4},{4,8},{8,12},{12,16},{16,20},{20,24},{24,28},{28,32},{32,36}... | collective-permute-start | bytes 1572872 | tf_op jit(solution)/shard_map/ppermute | solution.py:16
  135.1 2.3 copy-start.3
  135.1 2.3 copy-start.1
  135.5 2.3 copy-start.4
  137.7 4.1 copy-start.7
  159.9 17.2 %collective-permute-start.1 = (f32[256,1024]{1,0:T(8,128)}, f32[256,1024]{1,0:T(8,128)}, u32[]{:S(2)}, u32[]{:S(2)}) collective-permute-start(f32[256,1024]{1,0:T(8,128)} %fusion.29), channel_id=1, source_target_pairs={{4,0},{8,4},{12,8},{16,12},{20,16},{24,20},{28,24},{32,28},{36,32}... | collective-permute-start | bytes 3145736 | tf_op jit(solution)/shard_map/ppermute | solution.py:16
  162.7 14.3 %copy-start = (f32[5,256,512]{2,1,0:T(8,128)S(1)}, f32[5,256,512]{2,1,0:T(8,128)}, u32[]{:S(2)}) copy-start(f32[5,256,512]{2,1,0:T(8,128)} %copy.38) | copy-start | bytes 7864324
  192.1 1.6 copy-start.5
  192.1 1.8 copy-start.9
  250.2 69.9 %all-to-all-start.2 = ((bf16[16,4,16,896]{3,2,0,1:T(8,128)(2,1)}), bf16[16,4,16,896]{3,2,0,1:T(8,128)(2,1)S(1)}, u32[]{:S(2)}, u32[]{:S(2)}) async-start(bf16[16,4,16,896]{3,2,0,1:T(8,128)(2,1)} %copy.39), calls=%async_computation.2 | async-start | bytes 3670016 | tf_op jit(solution)/shard_map/all_to_all | solution.py:135
  253.8 10.3 %copy-start.2 = (bf16[5,256,512]{1,2,0:T(8,128)(2,1)S(1)}, bf16[5,256,512]{1,2,0:T(8,128)(2,1)}, u32[]{:S(2)}) copy-start(bf16[5,256,512]{1,2,0:T(8,128)(2,1)} %copy-done.1) | copy-start | bytes 3932164
  253.8 184.6 %all-reduce.2.cloned.1.call-start = ((), (), s32[]{:S(2)}) async-start(), calls=%async_computation.4 | async-start | bytes 1048576 | tf_op jit(solution)/shard_map/psum | solution.py:129
Sparse Core Ops, SparseCore 0:
  10.1 54.1 all-gather.2
  192.3 124.8 reduce-scatter.3
  319.6 118.8 all-reduce.1
where the time goes:
time: 448 us; the launch traced here: 447 us
  waiting for transfers between devices  279 us (62%)
  blocking collectives  51.3 us (11%)
  matrix products  44.1 us (10%)
  local copies, waits for them, and re-layouts  30.3 us (7%)
  starting transfers between devices  15.3 us (3%)
  between operations  14.1 us (3%)
  other arithmetic  12.5 us (3%)
    psum x1, waiting for transfers between devices, shards(): dp_piece = lax.psum(dp_rows, 'ctx')  117 us
    all_gather x1, waiting for transfers between devices, shards(): gathered = lax.all_gather(encoded[0], 'nbr', axis=1, tiled=True)  56.4 us
    all_to_all x1, blocking collectives, shards(): lax.all_to_all(partial_grads, 'ctx', split_axis=0, concat_axis=0, tiled=T...  51.3 us
    unnamed x4, waiting for transfers between devices  47.6 us
    all_to_all x1, waiting for transfers between devices, shards(): lax.all_to_all(gathered, 'ctx', split_axis=0, concat_axis=0, tiled=True)  42.4 us
    ppermute x2, waiting for transfers between devices, from_behind(): return lax.ppermute(block, axis, route)  15.8 us
    dot_general x1, matrix products, attend_backward(): jnp.einsum('chqk,cqhd->ckhd', score_grads, query_heads, preferred_element...  10.5 us
    unnamed x31, local copies, waits for them, and re-layouts  9.95 us
  transfers between devices with their start and end apart: 7, of which 6 were waited for; matrix products, arithmetic and copies ran while one was open for 7% of the time, Pallas kernels for 0%

commit v1 on v0

v1 whole, which is shorter than its diff:
```python
import math

import jax
import jax.numpy as jnp
from jax import lax
from jax.experimental import pallas as pl
from jax.experimental.pallas import tpu as pltpu
from jax.sharding import PartitionSpec as P

HEAD_DIM = 128
SPAN = 64
PART = 64
LEAD = SPAN - 1
SCALE = 1.0 / math.sqrt(HEAD_DIM)
NT = (((1,), (1,)), ((), ()))
TN = (((0,), (0,)), ((), ()))
NN = (((1,), (0,)), ((), ()))


def dot(a, b, dims):
    return lax.dot_general(a, b, dims, preferred_element_type=jnp.float32)


def attention_kernel(slots, heads, piece, units_ref, q_ref, g_ref, *refs):
    kv_refs = refs[:slots]
    att_ref, dq_ref = refs[slots : slots + 2]
    dkv_refs = refs[slots + 2 :]
    width = heads * HEAD_DIM
    spans = q_ref.shape[0] // SPAN
    for j in range(spans):
        starts = [pl.multiple_of(units_ref[j * 4 + r] * piece, piece) for r in range(4)]
        rows = pl.ds(j * SPAN, SPAN)
        for h in range(heads):
            cols = pl.ds(h * HEAD_DIM, HEAD_DIM)
            vcols = pl.ds(width + h * HEAD_DIM, HEAD_DIM)
            q = q_ref[rows, cols]
            g = g_ref[rows, cols]
            k = jnp.concatenate([ref[pl.ds(s, piece), cols] for s in starts for ref in kv_refs], axis=0)
            v = jnp.concatenate([ref[pl.ds(s, piece), vcols] for s in starts for ref in kv_refs], axis=0)
            scores = dot(q, k, NT) * SCALE
            top = jnp.max(scores, axis=-1, keepdims=True)
            raised = jnp.exp(scores - top)
            weights = raised / jnp.sum(raised, axis=-1, keepdims=True)
            low = weights.astype(jnp.bfloat16)
            d_weights = dot(g, v, NT)
            inner = jnp.sum(weights * d_weights, axis=-1, keepdims=True)
            d_scores = (weights * (d_weights - inner) * SCALE).astype(jnp.bfloat16)
            att_ref[rows, cols] = dot(low, v, NN).astype(jnp.bfloat16)
            dq_ref[rows, cols] = dot(d_scores, k, NN).astype(jnp.bfloat16)
            dk = dot(d_scores, q, TN).astype(jnp.bfloat16)
            dv = dot(low, g, TN).astype(jnp.bfloat16)
            for r, s in enumerate(starts):
                for n, ref in enumerate(dkv_refs):
                    at = (r * slots + n) * piece
                    ref[pl.ds(s, piece), cols] = dk[at : at + piece]
                    ref[pl.ds(s, piece), vcols] = dv[at : at + piece]


def attention(units, q, g, kvs, piece):
    slots = len(kvs)
    rows, width = q.shape
    heads = width // HEAD_DIM

    def body(*refs):
        attention_kernel(slots, heads, piece, *refs)

    vmem = pl.BlockSpec(memory_space=pltpu.VMEM)
    return pl.pallas_call(
        body,
        out_shape=[jax.ShapeDtypeStruct((rows, width), jnp.bfloat16)] * 2
        + [jax.ShapeDtypeStruct(kv.shape, jnp.bfloat16) for kv in kvs],
        in_specs=[pl.BlockSpec(memory_space=pltpu.SMEM)] + [vmem] * (2 + slots),
        out_specs=[vmem] * (2 + slots),
        compiler_params=pltpu.CompilerParams(vmem_limit_bytes=48 * 1024 * 1024),
        name="attention",
    )(units, q, g, *kvs)


def permute(x, axis, to):
    n = lax.axis_size(axis)
    return lax.ppermute(x, axis, [(i, to(i)) for i in range(n) if 0 <= to(i) < n])


def shards(queries, cotangent, encoded, kv_weight, neighbour_ids):
    q, g, enc = queries[0], cotangent[0], encoded[0]
    tokens, width = q.shape
    units, piece, enc_width = enc.shape
    groups = lax.axis_size("nbr")
    ctx = lax.axis_index("ctx")
    dp = lax.axis_index("dp")
    joined = jnp.concatenate((kv_weight[0], kv_weight[1]), axis=1)

    head = jnp.concatenate((q[:LEAD], g[:LEAD]), axis=1)
    ahead = permute(head, "ctx", lambda i: i - 1)
    q_rows = jnp.concatenate((q[LEAD:], ahead[:, :width]), axis=0)
    g_rows = jnp.concatenate((g[LEAD:], ahead[:, width:]), axis=0)

    own = lax.all_to_all(enc, "ctx", split_axis=0, concat_axis=0, tiled=True).reshape(units * piece, enc_width)
    slots = [own] + [permute(own, "nbr", lambda i, k=k: (i + k) % groups) for k in range(1, groups)]
    kvs = [dot(x, joined, NN).astype(jnp.bfloat16) for x in slots]

    unit_of = (neighbour_ids[0] // units).reshape(-1)
    att, dq, *dkvs = attention(unit_of, q_rows, g_rows, kvs, piece)

    partials = [dot(d, joined, NT).astype(jnp.bfloat16) for d in dkvs]
    terms = [permute(partials[k], "nbr", lambda i, k=k: (i - k) % groups) for k in range(1, groups)]
    total = partials[0].astype(jnp.float32)
    for t in terms:
        total = total + t.astype(jnp.float32)
    total = total.astype(jnp.bfloat16).reshape(units, piece, enc_width)
    encoded_grad = lax.all_to_all(total, "ctx", split_axis=0, concat_axis=0, tiled=True)

    tail = jnp.concatenate((att[tokens - LEAD :], dq[tokens - LEAD :]), axis=1)
    behind = permute(tail, "ctx", lambda i: i + 1)
    attended = jnp.concatenate((behind[:, :width], att[: tokens - LEAD]), axis=0)
    query_grad = jnp.concatenate((behind[:, width:], dq[: tokens - LEAD]), axis=0)

    x_all = jnp.concatenate(slots, axis=0)
    d_all = jnp.concatenate(dkvs, axis=0).reshape(-1, 2, width)
    core = ctx % 2
    d_mine = lax.dynamic_index_in_dim(d_all, core, 1, keepdims=False)
    d_other = lax.dynamic_index_in_dim(d_all, 1 - core, 1, keepdims=False)
    away = permute(dot(x_all, d_other, TN).astype(jnp.bfloat16), "ctx", lambda i: i ^ 1)
    part = dot(x_all, d_mine, TN) + away.astype(jnp.float32)
    rows = enc_width // 8
    part = part.reshape(2, 4, rows, width)
    low = part.astype(jnp.bfloat16)
    x = dp % 4
    held = lax.dynamic_index_in_dim(part, x, 1, keepdims=False)
    for k in (1, 3, 2):
        piece_k = lax.dynamic_index_in_dim(low, (x + k) % 4, 1, keepdims=False)
        held = held + permute(piece_k, "dp", lambda i, k=k: i // 4 * 4 + (i + k) % 4).astype(jnp.float32)
    high = dp // 4
    other = lax.dynamic_index_in_dim(held, 1 - high, 0, keepdims=False).astype(jnp.bfloat16)
    mine = lax.dynamic_index_in_dim(held, high, 0, keepdims=False)
    mine = mine + permute(other, "dp", lambda i: (i + 4) % 8).astype(jnp.float32)
    for bit in (2, 4, 8):
        mine = mine.astype(jnp.bfloat16)
        mine = mine.astype(jnp.float32) + permute(mine, "ctx", lambda i, b=bit: i ^ b).astype(jnp.float32)
    theirs = permute(mine, "ctx", lambda i: i ^ 1)
    keys_here = core == 0
    weight_grad = jnp.stack((jnp.where(keys_here, mine, theirs), jnp.where(keys_here, theirs, mine)), axis=0)
    return (attended[None], query_grad[None], encoded_grad[None], weight_grad)


def solution(mesh):
    return jax.shard_map(
        shards,
        mesh=mesh,
        in_specs=(
            P("dp", "ctx", "nbr"),
            P("dp", "ctx", "nbr"),
            P("dp", "ctx", "nbr", None),
            P(None, None, "nbr"),
            P("dp", "ctx", None),
        ),
        out_specs=(
            P("dp", "ctx", "nbr"),
            P("dp", "ctx", "nbr"),
            P("dp", "ctx", "nbr", None),
            P(None, "dp", "nbr"),
        ),
        check_vma=False,
    )
```

time: 448 us -> 212 us (0.47)
  the two profiles are of different devices: /device:TPU:1 before, /device:TPU:65 now
where the time goes in v1:
time: 212 us; the launch traced here: 211 us
  waiting for transfers between devices  86.5 us (41%)
  starting transfers between devices  77.9 us (37%)
  local copies, waits for them, and re-layouts  17.9 us (8%)
  matrix products  14.9 us (7%)
  Pallas kernels  8.21 us (4%)
  other arithmetic  4.37 us (2%)
    ppermute x17, waiting for transfers between devices, permute(): lax.ppermute(x, axis, [(i, to(i)) for i in range(n) if 0 <= to(i) < n])  73.7 us
    ppermute x17, starting transfers between devices, permute(): lax.ppermute(x, axis, [(i, to(i)) for i in range(n) if 0 <= to(i) < n])  66.8 us
    dot_general x10, matrix products, dot(): return lax.dot_general(a, b, dims, preferred_element_type=jnp.float32)  14.9 us
    all_to_all x1, waiting for transfers between devices, shards(): lax.all_to_all(enc, 'ctx', split_axis=0, concat_axis=0, tiled=True)  12.8 us
    pallas_call x1, Pallas kernels, attention(): pl.pallas_call(body, out_shape=[jax.ShapeDtypeStruct((rows, width), jnp.b...  8.21 us
    dynamic_slice x1, local copies, waits for them, and re-layouts, shards(): d_mine = lax.dynamic_index_in_dim(d_all, core, 1, keepdims=False)  8.01 us
    all_to_all x1, starting transfers between devices, shards(): lax.all_to_all(enc, 'ctx', split_axis=0, concat_axis=0, tiled=True)  7.24 us
    reshape x1, local copies, waits for them, and re-layouts, shards(): d_all = jnp.concatenate(dkvs, axis=0).reshape(-1, 2, width)  4.49 us
  transfers between devices with their start and end apart: 19, of which 9 were waited for; matrix products, arithmetic and copies ran while one was open for 6% of the time, Pallas kernels for 0%

profile of v1, /device:TPU:65, one launch (start us, length us, event | category | flops | bytes accessed | tf_op | source)
XLA Modules:
  0.0 211.0 jit_solution(16564338295595363228)
XLA Ops:
  1.7 2.6 %collective-permute-start = (bf16[63,1024]{1,0:T(8,128)(2,1)S(1)}, bf16[63,1024]{1,0:T(8,128)(2,1)S(1)}, u32[]{:S(2)}, u32[]{:S(2)}) collective-permute-start(bf16[63,1024]{1,0:T(8,128)(2,1)S(1)} %pad_maximum_fusion.8), channel_id=1, source_target_pairs={{4,0},{8,4},{12,8},{16,12},{20,16},{24,20},{28,24},{32,28},{36,32}... | collective-permute-start | bytes 387080 | tf_op jit(solution)/shard_map/ppermute | solution.py:81
  4.3 7.2 %all-to-all-start = ((bf16[16,16,896]{2,1,0:T(8,128)(2,1)}), bf16[16,16,896]{2,1,0:T(8,128)(2,1)}, u32[]{:S(2)}, u32[]{:S(2)}) async-start(bf16[16,16,896]{2,1,0:T(8,128)(2,1)} %bitcast.68), calls=%async_computation | async-start | bytes 917504 | tf_op jit(solution)/shard_map/all_to_all | solution.py:98
  14.7 12.8 %all-to-all-done = bf16[16,16,896]{2,1,0:T(8,128)(2,1)} async-done(((bf16[16,16,896]{2,1,0:T(8,128)(2,1)}), bf16[16,16,896]{2,1,0:T(8,128)(2,1)}, u32[]{:S(2)}, u32[]{:S(2)}) %all-to-all-start) | async-done | bytes 458784 | tf_op jit(solution)/shard_map/all_to_all | solution.py:98
  27.6 4.0 %collective-permute-start.1 = (bf16[256,896]{1,0:T(8,128)(2,1)}, bf16[256,896]{1,0:T(8,128)(2,1)S(1)}, u32[]{:S(2)}, u32[]{:S(2)}) collective-permute-start(bf16[256,896]{1,0:T(8,128)(2,1)} %bitcast.7), channel_id=1, source_target_pairs={{0,1},{1,2},{2,3},{3,0},{4,5},{5,6},{6,7},{7,4},{8,9},{9,10},{10,1... | collective-permute-start | bytes 1376264 | tf_op jit(solution)/shard_map/ppermute | solution.py:81
  31.7 3.7 %collective-permute-start.2 = (bf16[256,896]{1,0:T(8,128)(2,1)}, bf16[256,896]{1,0:T(8,128)(2,1)S(1)}, u32[]{:S(2)}, u32[]{:S(2)}) collective-permute-start(bf16[256,896]{1,0:T(8,128)(2,1)} %bitcast.7), channel_id=1, source_target_pairs={{0,2},{1,3},{2,0},{3,1},{4,6},{5,7},{6,4},{7,5},{8,10},{9,11},{10,... | collective-permute-start | bytes 1376264 | tf_op jit(solution)/shard_map/ppermute | solution.py:81
  35.4 3.4 %collective-permute-start.3 = (bf16[256,896]{1,0:T(8,128)(2,1)}, bf16[256,896]{1,0:T(8,128)(2,1)S(1)}, u32[]{:S(2)}, u32[]{:S(2)}) collective-permute-start(bf16[256,896]{1,0:T(8,128)(2,1)} %bitcast.7), channel_id=1, source_target_pairs={{0,3},{1,0},{2,1},{3,2},{4,7},{5,4},{6,5},{7,6},{8,11},{9,8},{10,9... | collective-permute-start | bytes 1376264 | tf_op jit(solution)/shard_map/ppermute | solution.py:81
  38.8 2.1 fusion.1.refs_3_
  40.9 20.9 %collective-permute-done.1 = bf16[256,896]{1,0:T(8,128)(2,1)S(1)} collective-permute-done((bf16[256,896]{1,0:T(8,128)(2,1)}, bf16[256,896]{1,0:T(8,128)(2,1)S(1)}, u32[]{:S(2)}, u32[]{:S(2)}) %collective-permute-start.1) | collective-permute-done | bytes 458784 | tf_op jit(solution)/shard_map/ppermute | solution.py:81
  62.6 8.5 %collective-permute-done.2 = bf16[256,896]{1,0:T(8,128)(2,1)S(1)} collective-permute-done((bf16[256,896]{1,0:T(8,128)(2,1)}, bf16[256,896]{1,0:T(8,128)(2,1)S(1)}, u32[]{:S(2)}, u32[]{:S(2)}) %collective-permute-start.2) | collective-permute-done | bytes 458784 | tf_op jit(solution)/shard_map/ppermute | solution.py:81
  74.0 8.2 %attention.1 = (bf16[256,512]{1,0:T(8,128)(2,1)S(1)}, bf16[256,512]{1,0:T(8,128)(2,1)S(1)}, bf16[256,1024]{1,0:T(8,128)(2,1)S(1)}, bf16[256,1024]{1,0:T(8,128)(2...) custom-call(s32[16]{0:T(128)S(1)} %and_select_fusion.refs_0_, ...), custom_call_target="tpu_custom_call" | custom-call | tf_op jit(solution)/shard_map/attention/pallas_call | solution.py:68
  83.8 4.5 %reshape.29 = bf16[1024,2,512]{2,1,0:T(2,128)(2,1)} reshape(bf16[1024,1024]{1,0:T(8,128)(2,1)} %pad_maximum_fusion) | data formatting | bytes 4194304 | tf_op jit(solution)/shard_map/reshape | solution.py:119
  88.3 8.0 %constant_dynamic-slice_fusion.1 = (bf16[1024,1,512]{2,1,0:T(2,128)(2,1)}, bf16[1024,1,512]{2,1,0:T(2,128)(2,1)S(1)}) fusion(bf16[1024,2,512]{2,1,0:T(2,128)(2,1)} %reshape.29, s32[]{:T(128)S(6)} %select_n.76, s32[]{:T(128)S(6)} %select_n.77), kind=kLoop, calls=%fused_computation.50 | loop fusion | bytes 4194312 | tf_op jit(solution)/shard_map/jit(dynamic_index_in_dim)/dynamic_slice | solution.py:121
  96.3 3.1 %convolution_convert_fusion = bf16[896,512]{1,0:T(8,128)(2,1)} fusion(bf16[1024,1,512]{2,1,0:T(2,128)(2,1)S(1)} %get-tuple-element.17, bf16[256,896]{1,0:T(8,128)(2,1)S(1)} %copy-done.12, bf16[256,896]{1,0:T(8,128)(2,1)S(1)} %copy-done.9, bf16[256,896]{1,0:T(8,128)(2,1)S(1)} %copy-done.6, bf16[256,896]{1,0:T(8,128)(2,1)} %bitcast.7), kind=kOutput, calls=%fused_computation.4 | convolution fusion | flops 947322880 | bytes 3801088 | tf_op jit(solution)/shard_map/dot_general | solution.py:21
  99.4 2.5 %collective-permute-start.8 = (bf16[896,512]{1,0:T(8,128)(2,1)}, bf16[896,512]{1,0:T(8,128)(2,1)}, u32[]{:S(2)}, u32[]{:S(2)}) collective-permute-start(bf16[896,512]{1,0:T(8,128)(2,1)} %convolution_convert_fusion), channel_id=1, source_target_pairs={{0,4},{4,0},{8,12},{12,8},{16,20},{20,16},{24,28},{28,24},{32,36},... | collective-permute-start | bytes 2752520 | tf_op jit(solution)/shard_map/ppermute | solution.py:81
  102.0 2.1 convolution_convert_fusion.5
  104.2 2.5 %convert_add_fusion = f32[896,512]{1,0:T(8,128)S(1)} fusion(bf16[896,512]{1,0:T(8,128)(2,1)} %collective-permute-done.8, bf16[1024,1,512]{2,1,0:T(2,128)(2,1)S(1)} %copy-done, bf16[256,896]{1,0:T(8,128)(2,1)S(1)} %copy-done.13, bf16[256,896]{1,0:T(8,128)(2,1)S(1)} %copy-done.10, bf16[256,896]{1,0:T(8,128)(2,1)S(1)} %copy-done.7, bf16[256,896]{1,0:T(8,128)(2,1)} %bitcast.7), kind=kOutput, calls=%fused_computation.3 | convolution fusion | flops 947781632 | bytes 5636096 | tf_op jit(solution)/shard_map/dot_general | solution.py:21
  106.9 4.8 %collective-permute-start.11 = (bf16[2,112,512]{2,1,0:T(8,128)(2,1)S(1)}, bf16[2,112,512]{2,1,0:T(8,128)(2,1)S(1)}, u32[]{:S(2)}, u32[]{:S(2)}) collective-permute-start(bf16[2,112,512]{2,1,0:T(8,128)(2,1)S(1)} %get-tuple-element.21), channel_id=1, source_target_pairs={{0,128},{64,192},{128,0},{192,64},{256,384},{320,448},{384,256},{4... | collective-permute-start | bytes 688136 | tf_op jit(solution)/shard_map/ppermute | solution.py:81
  111.6 2.8 %collective-permute-start.10 = (bf16[2,112,512]{2,1,0:T(8,128)(2,1)S(1)}, bf16[2,112,512]{2,1,0:T(8,128)(2,1)S(1)}, u32[]{:S(2)}, u32[]{:S(2)}) collective-permute-start(bf16[2,112,512]{2,1,0:T(8,128)(2,1)S(1)} %get-tuple-element.22), channel_id=1, source_target_pairs={{0,192},{64,0},{128,64},{192,128},{256,448},{320,256},{384,320},{4... | collective-permute-start | bytes 688136 | tf_op jit(solution)/shard_map/ppermute | solution.py:81
  114.4 2.5 %collective-permute-start.9 = (bf16[2,112,512]{2,1,0:T(8,128)(2,1)S(1)}, bf16[2,112,512]{2,1,0:T(8,128)(2,1)S(1)}, u32[]{:S(2)}, u32[]{:S(2)}) collective-permute-start(bf16[2,112,512]{2,1,0:T(8,128)(2,1)S(1)} %get-tuple-element.20), channel_id=1, source_target_pairs={{0,64},{64,128},{128,192},{192,0},{256,320},{320,384},{384,448},{4... | collective-permute-start | bytes 688136 | tf_op jit(solution)/shard_map/ppermute | solution.py:81
  117.7 4.5 %collective-permute-done.10 = bf16[2,112,512]{2,1,0:T(8,128)(2,1)S(1)} collective-permute-done((bf16[2,112,512]{2,1,0:T(8,128)(2,1)S(1)}, bf16[2,112,512]{2,1,0:T(8,128)(2,1)S(1)}, u32[]{:S(2)}, u32[]{:S(2)}) %collective-permute-start.10) | collective-permute-done | bytes 229408 | tf_op jit(solution)/shard_map/ppermute | solution.py:81
  123.9 8.5 %collective-permute-start.12 = (bf16[112,512]{1,0:T(8,128)(2,1)S(1)}, bf16[112,512]{1,0:T(8,128)(2,1)S(1)}, u32[]{:S(2)}, u32[]{:S(2)}) collective-permute-start(bf16[112,512]{1,0:T(8,128)(2,1)S(1)} %fusion.8), channel_id=1, source_target_pairs={{0,256},{64,320},{128,384},{192,448},{256,0},{320,64},{384,128},{4... | collective-permute-start | bytes 344072 | tf_op jit(solution)/shard_map/ppermute | solution.py:81
  135.2 3.7 %collective-permute-start.6 = (bf16[256,896]{1,0:T(8,128)(2,1)S(1)}, bf16[256,896]{1,0:T(8,128)(2,1)S(1)}, u32[]{:S(2)}, u32[]{:S(2)}) collective-permute-start(bf16[256,896]{1,0:T(8,128)(2,1)S(1)} %convolution_convert_fusion.6), channel_id=1, source_target_pairs={{0,2},{1,3},{2,0},{3,1},{4,6},{5,7},{6,4},{7,5},{8,10},{9,11},{10,... | collective-permute-start | bytes 1376264 | tf_op jit(solution)/shard_map/ppermute | solution.py:81
  138.9 3.4 %collective-permute-start.5 = (bf16[256,896]{1,0:T(8,128)(2,1)S(1)}, bf16[256,896]{1,0:T(8,128)(2,1)S(1)}, u32[]{:S(2)}, u32[]{:S(2)}) collective-permute-start(bf16[256,896]{1,0:T(8,128)(2,1)S(1)} %convolution_convert_fusion.7), channel_id=1, source_target_pairs={{0,3},{1,0},{2,1},{3,2},{4,7},{5,4},{6,5},{7,6},{8,11},{9,8},{10,9... | collective-permute-start | bytes 1376264 | tf_op jit(solution)/shard_map/ppermute | solution.py:81
  142.3 1.9 collective-permute-start.13
  144.3 6.2 %collective-permute-start.4 = (bf16[63,1024]{1,0:T(8,128)(2,1)S(1)}, bf16[63,1024]{1,0:T(8,128)(2,1)S(1)}, u32[]{:S(2)}, u32[]{:S(2)}) collective-permute-start(bf16[63,1024]{1,0:T(8,128)(2,1)S(1)} %pad_maximum_fusion.9), channel_id=1, source_target_pairs={{0,4},{4,8},{8,12},{12,16},{16,20},{20,24},{24,28},{28,32},{32,36}... | collective-permute-start | bytes 387080 | tf_op jit(solution)/shard_map/ppermute | solution.py:81
  150.6 2.8 %collective-permute-start.14 = (bf16[112,512]{1,0:T(8,128)(2,1)S(1)}, bf16[112,512]{1,0:T(8,128)(2,1)S(1)}, u32[]{:S(2)}, u32[]{:S(2)}) collective-permute-start(bf16[112,512]{1,0:T(8,128)(2,1)S(1)} %add_convert_fusion.2), channel_id=1, source_target_pairs={{0,16},{4,20},{8,24},{12,28},{16,0},{20,4},{24,8},{28,12},{32,48},... | collective-permute-start | bytes 344072 | tf_op jit(solution)/shard_map/ppermute | solution.py:81
  153.4 19.2 %collective-permute-done.6 = bf16[256,896]{1,0:T(8,128)(2,1)S(1)} collective-permute-done((bf16[256,896]{1,0:T(8,128)(2,1)S(1)}, bf16[256,896]{1,0:T(8,128)(2,1)S(1)}, u32[]{:S(2)}, u32[]{:S(2)}) %collective-permute-start.6) | collective-permute-done | bytes 458784 | tf_op jit(solution)/shard_map/ppermute | solution.py:81
  172.6 5.9 %collective-permute-done.5 = bf16[256,896]{1,0:T(8,128)(2,1)S(1)} collective-permute-done((bf16[256,896]{1,0:T(8,128)(2,1)S(1)}, bf16[256,896]{1,0:T(8,128)(2,1)S(1)}, u32[]{:S(2)}, u32[]{:S(2)}) %collective-permute-start.5) | collective-permute-done | bytes 458784 | tf_op jit(solution)/shard_map/ppermute | solution.py:81
  180.2 3.8 %all-to-all-start.1 = ((bf16[16,16,896]{2,1,0:T(8,128)(2,1)}), bf16[16,16,896]{2,1,0:T(8,128)(2,1)S(1)}, u32[]{:S(2)}, u32[]{:S(2)}) async-start(bf16[16,16,896]{2,1,0:T(8,128)(2,1)} %bitcast.14), calls=%async_computation.1 | async-start | bytes 917504 | tf_op jit(solution)/shard_map/all_to_all | solution.py:111
  184.1 7.2 %collective-permute-start.15 = (bf16[112,512]{1,0:T(8,128)(2,1)S(1)}, bf16[112,512]{1,0:T(8,128)(2,1)S(1)}, u32[]{:S(2)}, u32[]{:S(2)}) collective-permute-start(bf16[112,512]{1,0:T(8,128)(2,1)S(1)} %add_convert_fusion.1), channel_id=1, source_target_pairs={{0,32},{4,36},{8,40},{12,44},{16,48},{20,52},{24,56},{28,60},{32,0... | collective-permute-start | bytes 344072 | tf_op jit(solution)/shard_map/ppermute | solution.py:81
  191.3 11.6 %collective-permute-done.15 = bf16[112,512]{1,0:T(8,128)(2,1)S(1)} collective-permute-done((bf16[112,512]{1,0:T(8,128)(2,1)S(1)}, bf16[112,512]{1,0:T(8,128)(2,1)S(1)}, u32[]{:S(2)}, u32[]{:S(2)}) %collective-permute-start.15) | collective-permute-done | bytes 114720 | tf_op jit(solution)/shard_map/ppermute | solution.py:81
  203.0 4.9 %collective-permute-start.16 = (f32[112,512]{1,0:T(8,128)S(1)}, f32[112,512]{1,0:T(8,128)S(1)}, u32[]{:S(2)}, u32[]{:S(2)}) collective-permute-start(f32[112,512]{1,0:T(8,128)S(1)} %convert_add_fusion.1), channel_id=1, source_target_pairs={{0,4},{4,0},{8,12},{12,8},{16,20},{20,16},{24,28},{28,24},{32,36},... | collective-permute-start | bytes 688136 | tf_op jit(solution)/shard_map/ppermute | solution.py:81
  (77 shorter events, 19.8 us)
Async XLA Ops:
  0.6 12.9 %copy-start.4 = (s32[1,4,4]{2,1,0:T(4,128)S(1)}, s32[1,4,4]{2,1,0:T(4,128)}, u32[]{:S(2)}) copy-start(s32[1,4,4]{2,1,0:T(4,128)} %param.9) | copy-start | bytes 196
  0.6 13.0 %copy-start.1 = (bf16[2,896,512]{2,1,0:T(8,128)(2,1)S(1)}, bf16[2,896,512]{2,1,0:T(8,128)(2,1)}, u32[]{:S(2)}) copy-start(bf16[2,896,512]{2,1,0:T(8,128)(2,1)} %param.8) | copy-start | bytes 5505028
  1.7 13.0 %collective-permute-start = (bf16[63,1024]{1,0:T(8,128)(2,1)S(1)}, bf16[63,1024]{1,0:T(8,128)(2,1)S(1)}, u32[]{:S(2)}, u32[]{:S(2)}) collective-permute-start(bf16[63,1024]{1,0:T(8,128)(2,1)S(1)} %pad_maximum_fusion.8), channel_id=1, source_target_pairs={{4,0},{8,4},{12,8},{16,12},{20,16},{24,20},{28,24},{32,28},{36,32}... | collective-permute-start | bytes 387080 | tf_op jit(solution)/shard_map/ppermute | solution.py:81
  4.3 23.3 %all-to-all-start = ((bf16[16,16,896]{2,1,0:T(8,128)(2,1)}), bf16[16,16,896]{2,1,0:T(8,128)(2,1)}, u32[]{:S(2)}, u32[]{:S(2)}) async-start(bf16[16,16,896]{2,1,0:T(8,128)(2,1)} %bitcast.68), calls=%async_computation | async-start | bytes 917504 | tf_op jit(solution)/shard_map/all_to_all | solution.py:98
  27.6 34.2 %collective-permute-start.1 = (bf16[256,896]{1,0:T(8,128)(2,1)}, bf16[256,896]{1,0:T(8,128)(2,1)S(1)}, u32[]{:S(2)}, u32[]{:S(2)}) collective-permute-start(bf16[256,896]{1,0:T(8,128)(2,1)} %bitcast.7), channel_id=1, source_target_pairs={{0,1},{1,2},{2,3},{3,0},{4,5},{5,6},{6,7},{7,4},{8,9},{9,10},{10,1... | collective-permute-start | bytes 1376264 | tf_op jit(solution)/shard_map/ppermute | solution.py:81
  31.7 39.5 %collective-permute-start.2 = (bf16[256,896]{1,0:T(8,128)(2,1)}, bf16[256,896]{1,0:T(8,128)(2,1)S(1)}, u32[]{:S(2)}, u32[]{:S(2)}) collective-permute-start(bf16[256,896]{1,0:T(8,128)(2,1)} %bitcast.7), channel_id=1, source_target_pairs={{0,2},{1,3},{2,0},{3,1},{4,6},{5,7},{6,4},{7,5},{8,10},{9,11},{10,... | collective-permute-start | bytes 1376264 | tf_op jit(solution)/shard_map/ppermute | solution.py:81
  35.4 37.9 %collective-permute-start.3 = (bf16[256,896]{1,0:T(8,128)(2,1)}, bf16[256,896]{1,0:T(8,128)(2,1)S(1)}, u32[]{:S(2)}, u32[]{:S(2)}) collective-permute-start(bf16[256,896]{1,0:T(8,128)(2,1)} %bitcast.7), channel_id=1, source_target_pairs={{0,3},{1,0},{2,1},{3,2},{4,7},{5,4},{6,5},{7,6},{8,11},{9,8},{10,9... | collective-permute-start | bytes 1376264 | tf_op jit(solution)/shard_map/ppermute | solution.py:81
  38.8 23.1 %copy-start.2 = (bf16[896,512]{1,0:T(8,128)(2,1)S(1)}, bf16[896,512]{1,0:T(8,128)(2,1)}, u32[]{:S(2)}) copy-start(bf16[896,512]{1,0:T(8,128)(2,1)} %get-tuple-element.19) | copy-start | bytes 2752516
  61.8 0.8 copy-start.5
  73.3 0.8 copy-start.11
  88.3 8.0 %copy-start.6 = (bf16[256,896]{1,0:T(8,128)(2,1)S(1)}, bf16[256,896]{1,0:T(8,128)(2,1)}, u32[]{:S(2)}) copy-start(bf16[256,896]{1,0:T(8,128)(2,1)} %copy-done.5) | copy-start | bytes 1376260
  88.3 8.0 %copy-start.9 = (bf16[256,896]{1,0:T(8,128)(2,1)S(1)}, bf16[256,896]{1,0:T(8,128)(2,1)}, u32[]{:S(2)}) copy-start(bf16[256,896]{1,0:T(8,128)(2,1)} %copy-done.8) | copy-start | bytes 1376260
  88.3 8.0 %copy-start.12 = (bf16[256,896]{1,0:T(8,128)(2,1)S(1)}, bf16[256,896]{1,0:T(8,128)(2,1)}, u32[]{:S(2)}) copy-start(bf16[256,896]{1,0:T(8,128)(2,1)} %copy-done.11) | copy-start | bytes 1376260
  99.4 4.7 %collective-permute-start.8 = (bf16[896,512]{1,0:T(8,128)(2,1)}, bf16[896,512]{1,0:T(8,128)(2,1)}, u32[]{:S(2)}, u32[]{:S(2)}) collective-permute-start(bf16[896,512]{1,0:T(8,128)(2,1)} %convolution_convert_fusion), channel_id=1, source_target_pairs={{0,4},{4,0},{8,12},{12,8},{16,20},{20,16},{24,28},{28,24},{32,36},... | collective-permute-start | bytes 2752520 | tf_op jit(solution)/shard_map/ppermute | solution.py:81
  102.0 2.1 %copy-start = (bf16[1024,1,512]{2,1,0:T(2,128)(2,1)S(1)}, bf16[1024,1,512]{2,1,0:T(2,128)(2,1)}, u32[]{:S(2)}) copy-start(bf16[1024,1,512]{2,1,0:T(2,128)(2,1)} %get-tuple-element.16) | copy-start | bytes 3145732
  102.0 2.1 %copy-start.7 = (bf16[256,896]{1,0:T(8,128)(2,1)S(1)}, bf16[256,896]{1,0:T(8,128)(2,1)}, u32[]{:S(2)}) copy-start(bf16[256,896]{1,0:T(8,128)(2,1)} %copy-done.5) | copy-start | bytes 1376260
  102.0 2.1 %copy-start.10 = (bf16[256,896]{1,0:T(8,128)(2,1)S(1)}, bf16[256,896]{1,0:T(8,128)(2,1)}, u32[]{:S(2)}) copy-start(bf16[256,896]{1,0:T(8,128)(2,1)} %copy-done.8) | copy-start | bytes 1376260
  102.0 2.2 %copy-start.13 = (bf16[256,896]{1,0:T(8,128)(2,1)S(1)}, bf16[256,896]{1,0:T(8,128)(2,1)}, u32[]{:S(2)}) copy-start(bf16[256,896]{1,0:T(8,128)(2,1)} %copy-done.11) | copy-start | bytes 1376260
  106.6 10.3 %copy-start.3 = (bf16[896,512]{1,0:T(8,128)(2,1)S(1)}, bf16[896,512]{1,0:T(8,128)(2,1)}, u32[]{:S(2)}) copy-start(bf16[896,512]{1,0:T(8,128)(2,1)} %get-tuple-element.19) | copy-start | bytes 2752516
  106.9 10.8 %collective-permute-start.11 = (bf16[2,112,512]{2,1,0:T(8,128)(2,1)S(1)}, bf16[2,112,512]{2,1,0:T(8,128)(2,1)S(1)}, u32[]{:S(2)}, u32[]{:S(2)}) collective-permute-start(bf16[2,112,512]{2,1,0:T(8,128)(2,1)S(1)} %get-tuple-element.21), channel_id=1, source_target_pairs={{0,128},{64,192},{128,0},{192,64},{256,384},{320,448},{384,256},{4... | collective-permute-start | bytes 688136 | tf_op jit(solution)/shard_map/ppermute | solution.py:81
  111.6 10.6 %collective-permute-start.10 = (bf16[2,112,512]{2,1,0:T(8,128)(2,1)S(1)}, bf16[2,112,512]{2,1,0:T(8,128)(2,1)S(1)}, u32[]{:S(2)}, u32[]{:S(2)}) collective-permute-start(bf16[2,112,512]{2,1,0:T(8,128)(2,1)S(1)} %get-tuple-element.22), channel_id=1, source_target_pairs={{0,192},{64,0},{128,64},{192,128},{256,448},{320,256},{384,320},{4... | collective-permute-start | bytes 688136 | tf_op jit(solution)/shard_map/ppermute | solution.py:81
  114.4 9.3 %collective-permute-start.9 = (bf16[2,112,512]{2,1,0:T(8,128)(2,1)S(1)}, bf16[2,112,512]{2,1,0:T(8,128)(2,1)S(1)}, u32[]{:S(2)}, u32[]{:S(2)}) collective-permute-start(bf16[2,112,512]{2,1,0:T(8,128)(2,1)S(1)} %get-tuple-element.20), channel_id=1, source_target_pairs={{0,64},{64,128},{128,192},{192,0},{256,320},{320,384},{384,448},{4... | collective-permute-start | bytes 688136 | tf_op jit(solution)/shard_map/ppermute | solution.py:81
  123.9 18.4 %collective-permute-start.12 = (bf16[112,512]{1,0:T(8,128)(2,1)S(1)}, bf16[112,512]{1,0:T(8,128)(2,1)S(1)}, u32[]{:S(2)}, u32[]{:S(2)}) collective-permute-start(bf16[112,512]{1,0:T(8,128)(2,1)S(1)} %fusion.8), channel_id=1, source_target_pairs={{0,256},{64,320},{128,384},{192,448},{256,0},{320,64},{384,128},{4... | collective-permute-start | bytes 344072 | tf_op jit(solution)/shard_map/ppermute | solution.py:81
  133.2 20.2 %collective-permute-start.7 = (bf16[256,896]{1,0:T(8,128)(2,1)S(1)}, bf16[256,896]{1,0:T(8,128)(2,1)S(1)}, u32[]{:S(2)}, u32[]{:S(2)}) collective-permute-start(bf16[256,896]{1,0:T(8,128)(2,1)S(1)} %convolution_convert_fusion.5), channel_id=1, source_target_pairs={{0,1},{1,2},{2,3},{3,0},{4,5},{5,6},{6,7},{7,4},{8,9},{9,10},{10,1... | collective-permute-start | bytes 1376264 | tf_op jit(solution)/shard_map/ppermute | solution.py:81
  135.2 37.5 %collective-permute-start.6 = (bf16[256,896]{1,0:T(8,128)(2,1)S(1)}, bf16[256,896]{1,0:T(8,128)(2,1)S(1)}, u32[]{:S(2)}, u32[]{:S(2)}) collective-permute-start(bf16[256,896]{1,0:T(8,128)(2,1)S(1)} %convolution_convert_fusion.6), channel_id=1, source_target_pairs={{0,2},{1,3},{2,0},{3,1},{4,6},{5,7},{6,4},{7,5},{8,10},{9,11},{10,... | collective-permute-start | bytes 1376264 | tf_op jit(solution)/shard_map/ppermute | solution.py:81
  138.9 39.7 %collective-permute-start.5 = (bf16[256,896]{1,0:T(8,128)(2,1)S(1)}, bf16[256,896]{1,0:T(8,128)(2,1)S(1)}, u32[]{:S(2)}, u32[]{:S(2)}) collective-permute-start(bf16[256,896]{1,0:T(8,128)(2,1)S(1)} %convolution_convert_fusion.7), channel_id=1, source_target_pairs={{0,3},{1,0},{2,1},{3,2},{4,7},{5,4},{6,5},{7,6},{8,11},{9,8},{10,9... | collective-permute-start | bytes 1376264 | tf_op jit(solution)/shard_map/ppermute | solution.py:81
  142.3 8.2 %collective-permute-start.13 = (bf16[112,512]{1,0:T(8,128)(2,1)S(1)}, bf16[112,512]{1,0:T(8,128)(2,1)S(1)}, u32[]{:S(2)}, u32[]{:S(2)}) collective-permute-start(bf16[112,512]{1,0:T(8,128)(2,1)S(1)} %fusion.7), channel_id=1, source_target_pairs={{0,8},{4,12},{8,0},{12,4},{16,24},{20,28},{24,16},{28,20},{32,40},... | collective-permute-start | bytes 344072 | tf_op jit(solution)/shard_map/ppermute | solution.py:81
  144.3 47.0 %collective-permute-start.4 = (bf16[63,1024]{1,0:T(8,128)(2,1)S(1)}, bf16[63,1024]{1,0:T(8,128)(2,1)S(1)}, u32[]{:S(2)}, u32[]{:S(2)}) collective-permute-start(bf16[63,1024]{1,0:T(8,128)(2,1)S(1)} %pad_maximum_fusion.9), channel_id=1, source_target_pairs={{0,4},{4,8},{8,12},{12,16},{16,20},{20,24},{24,28},{28,32},{32,36}... | collective-permute-start | bytes 387080 | tf_op jit(solution)/shard_map/ppermute | solution.py:81
  150.6 33.4 %collective-permute-start.14 = (bf16[112,512]{1,0:T(8,128)(2,1)S(1)}, bf16[112,512]{1,0:T(8,128)(2,1)S(1)}, u32[]{:S(2)}, u32[]{:S(2)}) collective-permute-start(bf16[112,512]{1,0:T(8,128)(2,1)S(1)} %add_convert_fusion.2), channel_id=1, source_target_pairs={{0,16},{4,20},{8,24},{12,28},{16,0},{20,4},{24,8},{28,12},{32,48},... | collective-permute-start | bytes 344072 | tf_op jit(solution)/shard_map/ppermute | solution.py:81
  180.2 29.2 %all-to-all-start.1 = ((bf16[16,16,896]{2,1,0:T(8,128)(2,1)}), bf16[16,16,896]{2,1,0:T(8,128)(2,1)S(1)}, u32[]{:S(2)}, u32[]{:S(2)}) async-start(bf16[16,16,896]{2,1,0:T(8,128)(2,1)} %bitcast.14), calls=%async_computation.1 | async-start | bytes 917504 | tf_op jit(solution)/shard_map/all_to_all | solution.py:111
  184.1 18.9 %collective-permute-start.15 = (bf16[112,512]{1,0:T(8,128)(2,1)S(1)}, bf16[112,512]{1,0:T(8,128)(2,1)S(1)}, u32[]{:S(2)}, u32[]{:S(2)}) collective-permute-start(bf16[112,512]{1,0:T(8,128)(2,1)S(1)} %add_convert_fusion.1), channel_id=1, source_target_pairs={{0,32},{4,36},{8,40},{12,44},{16,48},{20,52},{24,56},{28,60},{32,0... | collective-permute-start | bytes 344072 | tf_op jit(solution)/shard_map/ppermute | solution.py:81
  203.0 6.4 %collective-permute-start.16 = (f32[112,512]{1,0:T(8,128)S(1)}, f32[112,512]{1,0:T(8,128)S(1)}, u32[]{:S(2)}, u32[]{:S(2)}) collective-permute-start(f32[112,512]{1,0:T(8,128)S(1)} %convert_add_fusion.1), channel_id=1, source_target_pairs={{0,4},{4,0},{8,12},{12,8},{16,20},{20,16},{24,28},{28,24},{32,36},... | collective-permute-start | bytes 688136 | tf_op jit(solution)/shard_map/ppermute | solution.py:81
  (1 other events, 0.8 us)

commit v2 on v1

--- a/solution.py
+++ b/solution.py
@@ -76,60 +76,126 @@
     )(units, q, g, *kvs)
 
 
+def weight_kernel(slots, blocks, half, core_ref, *refs):
+    x_refs, d_refs = refs[:slots], refs[slots : 2 * slots]
+    width = d_refs[0].shape[1] // 2
+    core = core_ref[0]
+    start = pl.multiple_of((core if half else 1 - core) * width, width)
+    for b in range(blocks):
+        cols = pl.ds(b * 128, 128)
+        yield cols, sum(dot(x[:, cols], d[:, pl.ds(start, width)], TN) for x, d in zip(x_refs, d_refs))
+
+
+def weight_sent(core, xs, ds):
+    slots, enc_width, width = len(xs), xs[0].shape[1], ds[0].shape[1] // 2
+
+    def body(core_ref, *refs):
+        for rows, term in weight_kernel(slots, enc_width // 128, False, core_ref, *refs):
+            refs[-1][rows, :] = term.astype(jnp.bfloat16)
+
+    vmem = pl.BlockSpec(memory_space=pltpu.VMEM)
+    return pl.pallas_call(
+        body,
+        out_shape=jax.ShapeDtypeStruct((enc_width, width), jnp.bfloat16),
+        in_specs=[pl.BlockSpec(memory_space=pltpu.SMEM)] + [vmem] * (2 * slots),
+        out_specs=vmem,
+        compiler_params=pltpu.CompilerParams(vmem_limit_bytes=48 * 1024 * 1024),
+        name="weight_sent",
+    )(core, *xs, *ds)
+
+
+def weight_kept(core, xs, ds, away):
+    slots, enc_width, width = len(xs), xs[0].shape[1], ds[0].shape[1] // 2
+    rows = enc_width // 8
+
+    def body(core_ref, *refs):
+        away_ref, own_ref, *send_refs, total = refs[2 * slots :]
+        for at, term in weight_kernel(slots, enc_width // 128, True, core_ref, *refs[: 2 * slots]):
+            total[at, :] = term + away_ref[at, :].astype(jnp.float32)
+        x = core_ref[1]
+        for high in range(2):
+            at = pl.multiple_of((high * 4 + x) * rows, 16)
+            own_ref[high] = total[pl.ds(at, rows), :]
+            for k in (1, 2, 3):
+                at = pl.multiple_of((high * 4 + lax.rem(x + k, 4)) * rows, 16)
+                send_refs[k - 1][high] = total[pl.ds(at, rows), :].astype(jnp.bfloat16)
+
+    vmem = pl.BlockSpec(memory_space=pltpu.VMEM)
+    return pl.pallas_call(
+        body,
+        out_shape=[jax.ShapeDtypeStruct((2, rows, width), jnp.float32)]
+        + [jax.ShapeDtypeStruct((2, rows, width), jnp.bfloat16)] * 3,
+        in_specs=[pl.BlockSpec(memory_space=pltpu.SMEM)] + [vmem] * (2 * slots + 1),
+        out_specs=[vmem] * 4,
+        scratch_shapes=[pltpu.VMEM((enc_width, width), jnp.float32)],
+        compiler_params=pltpu.CompilerParams(vmem_limit_bytes=48 * 1024 * 1024),
+        name="weight_kept",
+    )(core, *xs, *ds, away)
+
+
 def permute(x, axis, to):
     n = lax.axis_size(axis)
     return lax.ppermute(x, axis, [(i, to(i)) for i in range(n) if 0 <= to(i) < n])
+
+
+def exchange(x):
+    return lax.all_to_all(x, "ctx", split_axis=0, concat_axis=0, tiled=True)
+
+
+def pair(x, bit):
+    return permute(x, "nbr", lambda i: i ^ bit)
+
+
+def add(a, b):
+    return (a.astype(jnp.float32) + b.astype(jnp.float32)).astype(jnp.bfloat16)
 
 
 def shards(queries, cotangent, encoded, kv_weight, neighbour_ids):
     q, g, enc = queries[0], cotangent[0], encoded[0]
     tokens, width = q.shape
     units, piece, enc_width = enc.shape
-    groups = lax.axis_size("nbr")
+    half = piece // 2
+    flat = (units * piece, enc_width)
     ctx = lax.axis_index("ctx")
     dp = lax.axis_index("dp")
     joined = jnp.concatenate((kv_weight[0], kv_weight[1]), axis=1)
+
+    enc_a, enc_b = enc[:, :half], enc[:, half:]
+    own_a = exchange(enc_a)
+    b_02 = exchange(jnp.concatenate((enc_b, pair(enc_b, 2)), axis=1)).reshape(flat)
+    a_02 = jnp.concatenate((own_a, pair(own_a, 2)), axis=1).reshape(flat)
+    a_13 = pair(a_02, 1)
+    b_13 = pair(b_02, 1)
+    xs = [a_02, b_02, a_13, b_13]
+    kvs = [dot(x, joined, NN).astype(jnp.bfloat16) for x in xs]
 
     head = jnp.concatenate((q[:LEAD], g[:LEAD]), axis=1)
     ahead = permute(head, "ctx", lambda i: i - 1)
     q_rows = jnp.concatenate((q[LEAD:], ahead[:, :width]), axis=0)
     g_rows = jnp.concatenate((g[LEAD:], ahead[:, width:]), axis=0)
 
-    own = lax.all_to_all(enc, "ctx", split_axis=0, concat_axis=0, tiled=True).reshape(units * piece, enc_width)
-    slots = [own] + [permute(own, "nbr", lambda i, k=k: (i + k) % groups) for k in range(1, groups)]
-    kvs = [dot(x, joined, NN).astype(jnp.bfloat16) for x in slots]
-
     unit_of = (neighbour_ids[0] // units).reshape(-1)
-    att, dq, *dkvs = attention(unit_of, q_rows, g_rows, kvs, piece)
-
-    partials = [dot(d, joined, NT).astype(jnp.bfloat16) for d in dkvs]
-    terms = [permute(partials[k], "nbr", lambda i, k=k: (i - k) % groups) for k in range(1, groups)]
-    total = partials[0].astype(jnp.float32)
-    for t in terms:
-        total = total + t.astype(jnp.float32)
-    total = total.astype(jnp.bfloat16).reshape(units, piece, enc_width)
-    encoded_grad = lax.all_to_all(total, "ctx", split_axis=0, concat_axis=0, tiled=True)
+    att, dq, *ds = attention(unit_of, q_rows, g_rows, kvs, piece)
+
+    p_a02, p_b02, p_a13, p_b13 = [dot(d, joined, NT).astype(jnp.bfloat16) for d in ds]
+    s_b = add(p_b02, pair(p_b13, 1)).reshape(units, piece, enc_width)
+    s_a = add(p_a02, pair(p_a13, 1)).reshape(units, piece, enc_width)
+    back_b = exchange(s_b)
+    grad_b = add(back_b[:, :half], pair(back_b[:, half:], 2))
+    grad_a = exchange(add(s_a[:, :half], pair(s_a[:, half:], 2)))
+    encoded_grad = jnp.concatenate((grad_a, grad_b), axis=1)
 
     tail = jnp.concatenate((att[tokens - LEAD :], dq[tokens - LEAD :]), axis=1)
     behind = permute(tail, "ctx", lambda i: i + 1)
     attended = jnp.concatenate((behind[:, :width], att[: tokens - LEAD]), axis=0)
     query_grad = jnp.concatenate((behind[:, width:], dq[: tokens - LEAD]), axis=0)
 
-    x_all = jnp.concatenate(slots, axis=0)
-    d_all = jnp.concatenate(dkvs, axis=0).reshape(-1, 2, width)
     core = ctx % 2
-    d_mine = lax.dynamic_index_in_dim(d_all, core, 1, keepdims=False)
-    d_other = lax.dynamic_index_in_dim(d_all, 1 - core, 1, keepdims=False)
-    away = permute(dot(x_all, d_other, TN).astype(jnp.bfloat16), "ctx", lambda i: i ^ 1)
-    part = dot(x_all, d_mine, TN) + away.astype(jnp.float32)
-    rows = enc_width // 8
-    part = part.reshape(2, 4, rows, width)
-    low = part.astype(jnp.bfloat16)
-    x = dp % 4
-    held = lax.dynamic_index_in_dim(part, x, 1, keepdims=False)
+    place = jnp.stack((core, dp % 4)).astype(jnp.int32)
+    away = permute(weight_sent(place, xs, ds), "ctx", lambda i: i ^ 1)
+    held, *sends = weight_kept(place, xs, ds, away)
     for k in (1, 3, 2):
-        piece_k = lax.dynamic_index_in_dim(low, (x + k) % 4, 1, keepdims=False)
-        held = held + permute(piece_k, "dp", lambda i, k=k: i // 4 * 4 + (i + k) % 4).astype(jnp.float32)
+        held = held + permute(sends[k - 1], "dp", lambda i, k=k: i // 4 * 4 + (i + k) % 4).astype(jnp.float32)
     high = dp // 4
     other = lax.dynamic_index_in_dim(held, 1 - high, 0, keepdims=False).astype(jnp.bfloat16)
     mine = lax.dynamic_index_in_dim(held, high, 0, keepdims=False)

time: 212 us -> 203 us (0.958)
  the two profiles are of different devices: /device:TPU:65 before, /device:TPU:1 now
where the time goes in v2:
time: 203 us; the launch traced here: 201 us
  starting transfers between devices  98.7 us (49%)
  waiting for transfers between devices  55.7 us (27%)
  Pallas kernels  13.5 us (7%)
  matrix products  13 us (6%)
  local copies, waits for them, and re-layouts  9.89 us (5%)
  other arithmetic  9.11 us (4%)
    ppermute x19, starting transfers between devices, permute(): lax.ppermute(x, axis, [(i, to(i)) for i in range(n) if 0 <= to(i) < n])  74.7 us
    ppermute x19, waiting for transfers between devices, permute(): lax.ppermute(x, axis, [(i, to(i)) for i in range(n) if 0 <= to(i) < n])  55.7 us
    all_to_all x4, starting transfers between devices, exchange(): return lax.all_to_all(x, 'ctx', split_axis=0, concat_axis=0, tiled=True)  24.1 us
    dot_general x8, matrix products, dot(): return lax.dot_general(a, b, dims, preferred_element_type=jnp.float32)  13 us
    pallas_call x1, Pallas kernels, attention(): pl.pallas_call(body, out_shape=[jax.ShapeDtypeStruct((rows, width), jnp.b...  8.22 us
  transfers between devices with their start and end apart: 23, of which 9 were waited for; matrix products, arithmetic and copies ran while one was open for 14% of the time, Pallas kernels for 1%

profile of v2, /device:TPU:1, one launch (start us, length us, event | category | flops | bytes accessed | tf_op | source)
XLA Modules:
  0.0 201.2 jit_solution(18189663877022172026)
XLA Ops:
  2.4 8.8 %collective-permute-start = (bf16[63,1024]{1,0:T(8,128)(2,1)}, bf16[63,1024]{1,0:T(8,128)(2,1)}, u32[]{:S(2)}, u32[]{:S(2)}) collective-permute-start(bf16[63,1024]{1,0:T(8,128)(2,1)} %pad_maximum_fusion.6), channel_id=1, source_target_pairs={{4,0},{8,4},{12,8},{16,12},{20,16},{24,20},{28,24},{32,28},{36,32}... | collective-permute-start | bytes 387080 | tf_op jit(solution)/shard_map/ppermute | solution.py:138
  12.9 3.4 %all-to-all-start = ((bf16[16,8,896]{2,1,0:T(8,128)(2,1)}), bf16[16,8,896]{2,1,0:T(8,128)(2,1)S(1)}, u32[]{:S(2)}, u32[]{:S(2)}) async-start(bf16[16,8,896]{2,1,0:T(8,128)(2,1)} %get-tuple-element.29), calls=%async_computation | async-start | bytes 458752 | tf_op jit(solution)/shard_map/all_to_all | solution.py:142
  16.4 4.2 %collective-permute-start.2 = (bf16[16,8,896]{2,1,0:T(8,128)(2,1)S(1)}, bf16[16,8,896]{2,1,0:T(8,128)(2,1)}, u32[]{:S(2)}, u32[]{:S(2)}) collective-permute-start(bf16[16,8,896]{2,1,0:T(8,128)(2,1)S(1)} %get-tuple-element.28), channel_id=1, source_target_pairs={{0,2},{1,3},{2,0},{3,1},{4,6},{5,7},{6,4},{7,5},{8,10},{9,11},{10,... | collective-permute-start | bytes 688136 | tf_op jit(solution)/shard_map/ppermute | solution.py:138
  23.1 8.4 %collective-permute-done.2 = bf16[16,8,896]{2,1,0:T(8,128)(2,1)} collective-permute-done((bf16[16,8,896]{2,1,0:T(8,128)(2,1)S(1)}, bf16[16,8,896]{2,1,0:T(8,128)(2,1)}, u32[]{:S(2)}, u32[]{:S(2)}) %collective-permute-start.2) | collective-permute-done | bytes 229408 | tf_op jit(solution)/shard_map/ppermute | solution.py:138
  33.3 7.5 %all-to-all-start.1 = ((bf16[16,16,896]{2,1,0:T(8,128)(2,1)}), bf16[16,16,896]{2,1,0:T(8,128)(2,1)S(1)}, u32[]{:S(2)}, u32[]{:S(2)}) async-start(bf16[16,16,896]{2,1,0:T(8,128)(2,1)} %pad_maximum_fusion.2), calls=%async_computation.1 | async-start | bytes 917504 | tf_op jit(solution)/shard_map/all_to_all | solution.py:142
  45.1 11.5 %collective-permute-done.1 = bf16[16,8,896]{2,1,0:T(8,128)(2,1)S(1)} collective-permute-done((bf16[16,8,896]{2,1,0:T(8,128)(2,1)S(1)}, bf16[16,8,896]{2,1,0:T(8,128)(2,1)S(1)}, u32[]{:S(2)}, u32[]{:S(2)}) %collective-permute-start.1) | collective-permute-done | bytes 229408 | tf_op jit(solution)/shard_map/ppermute | solution.py:138
  58.6 2.7 %convolution_convert_fusion.3.refs_3_ = bf16[256,1024]{1,0:T(8,128)(2,1)} fusion(bf16[256,896]{1,0:T(8,128)(2,1)S(1)} %bitcast.48, bf16[896,512]{1,0:T(8,128)(2,1)} %get-tuple-element.25, bf16[896,512]{1,0:T(8,128)(2,1)S(1)} %get-tuple-element.24), kind=kOutput, calls=%fused_computation.4 | convolution fusion | flops 473694208 | bytes 2818048 | tf_op jit(solution)/shard_map/dot_general | solution.py:21
  61.3 3.5 %collective-permute-start.4 = (bf16[256,896]{1,0:T(8,128)(2,1)S(1)}, bf16[256,896]{1,0:T(8,128)(2,1)S(1)}, u32[]{:S(2)}, u32[]{:S(2)}) collective-permute-start(bf16[256,896]{1,0:T(8,128)(2,1)S(1)} %bitcast.43), channel_id=1, source_target_pairs={{0,1},{1,0},{2,3},{3,2},{4,5},{5,4},{6,7},{7,6},{8,9},{9,8},{10,11... | collective-permute-start | bytes 1376264 | tf_op jit(solution)/shard_map/ppermute | solution.py:138
  66.6 3.0 %collective-permute-done.3.refs_2_ = bf16[256,896]{1,0:T(8,128)(2,1)S(1)} collective-permute-done((bf16[256,896]{1,0:T(8,128)(2,1)S(1)}, bf16[256,896]{1,0:T(8,128)(2,1)S(1)}, u32[]{:S(2)}, u32[]{:S(2)}) %collective-permute-start.3) | collective-permute-done | bytes 458784 | tf_op jit(solution)/shard_map/ppermute | solution.py:138
  70.4 9.1 %collective-permute-done.4.refs_3_ = bf16[256,896]{1,0:T(8,128)(2,1)S(1)} collective-permute-done((bf16[256,896]{1,0:T(8,128)(2,1)S(1)}, bf16[256,896]{1,0:T(8,128)(2,1)S(1)}, u32[]{:S(2)}, u32[]{:S(2)}) %collective-permute-start.4) | collective-permute-done | bytes 458784 | tf_op jit(solution)/shard_map/ppermute | solution.py:138
  80.3 8.2 %attention.1 = (bf16[256,512]{1,0:T(8,128)(2,1)S(1)}, bf16[256,512]{1,0:T(8,128)(2,1)S(1)}, bf16[256,1024]{1,0:T(8,128)(2,1)S(1)}, bf16[256,1024]{1,0:T(8,128)(2...) custom-call(s32[16]{0:T(128)S(1)} %and_select_fusion.refs_0_, bf16[256,512]{1,0:T(8,128)(2,1)S(1)} %copy-done.2, ...), custom_call_target="tpu_custom_call" | custom-call | tf_op jit(solution)/shard_map/attention/pallas_call | solution.py:68
  88.5 2.7 %weight_sent.1 = bf16[896,512]{1,0:T(8,128)(2,1)} custom-call(s32[2]{0:T(128)S(1)} %pad_add_fusion.core_ref, bf16[256,896]{1,0:T(8,128)(2,1)S(1)} %bitcast.49, bf16[256,896]{1,0:T(8,128)(2,1)S(1)} %bitcast.45, bf16[256,896]{1,0:T(8,128)(2,1)S(1)} %collective-permute-done.3.refs_2_, bf16[256,896]{1,0:T(8,128)(2,1)S(1)} %collective-permute-done.4.refs_3_, ...), custom_call_target="tpu_custom_call" | custom-call | tf_op jit(solution)/shard_map/weight_sent/pallas_call | solution.py:97
  91.2 3.7 %collective-permute-start.10 = (bf16[896,512]{1,0:T(8,128)(2,1)}, bf16[896,512]{1,0:T(8,128)(2,1)}, u32[]{:S(2)}, u32[]{:S(2)}) collective-permute-start(bf16[896,512]{1,0:T(8,128)(2,1)} %weight_sent.1), channel_id=1, source_target_pairs={{0,4},{4,0},{8,12},{12,8},{16,20},{20,16},{24,28},{28,24},{32,36},... | collective-permute-start | bytes 2752520 | tf_op jit(solution)/shard_map/ppermute | solution.py:138
  98.6 3.0 %collective-permute-start.5 = (bf16[63,1024]{1,0:T(8,128)(2,1)S(1)}, bf16[63,1024]{1,0:T(8,128)(2,1)S(1)}, u32[]{:S(2)}, u32[]{:S(2)}) collective-permute-start(bf16[63,1024]{1,0:T(8,128)(2,1)S(1)} %pad_maximum_fusion.7), channel_id=1, source_target_pairs={{0,4},{4,8},{8,12},{12,16},{16,20},{20,24},{24,28},{28,32},{32,36}... | collective-permute-start | bytes 387080 | tf_op jit(solution)/shard_map/ppermute | solution.py:138
  101.6 2.2 %convolution_convert_fusion.4 = bf16[256,896]{1,0:T(8,128)(2,1)S(1)} fusion(bf16[256,1024]{1,0:T(8,128)(2,1)S(1)} %get-tuple-element.19.refs_7_, bf16[896,512]{1,0:T(8,128)(2,1)} %get-tuple-element.25, bf16[896,512]{1,0:T(8,128)(2,1)} %copy-done.8), kind=kOutput, calls=%fused_computation.5 | convolution fusion | flops 473661440 | bytes 2818048 | tf_op jit(solution)/shard_map/dot_general | solution.py:21
  107.4 3.3 %collective-permute-start.6 = (bf16[256,896]{1,0:T(8,128)(2,1)}, bf16[256,896]{1,0:T(8,128)(2,1)}, u32[]{:S(2)}, u32[]{:S(2)}) collective-permute-start(bf16[256,896]{1,0:T(8,128)(2,1)} %convolution_convert_fusion.6), channel_id=1, source_target_pairs={{0,1},{1,0},{2,3},{3,2},{4,5},{5,4},{6,7},{7,6},{8,9},{9,8},{10,11... | collective-permute-start | bytes 1376264 | tf_op jit(solution)/shard_map/ppermute | solution.py:138
  110.8 2.6 %weight_kept.1 = (f32[2,112,512]{2,1,0:T(8,128)S(1)}, bf16[2,112,512]{2,1,0:T(8,128)(2,1)S(1)}, bf16[2,112,512]{2,1,0:T(8,128)(2,1)S(1)}, bf16[2,112,512]{2,1,0:T(8,128)(2,1)S(1)}) custom-call(s32[2]{0:T(128)S(1)} %pad_add_fusion.core_ref, bf16[256,896]{1,0:T(8,128)(2,1)S(1)} %bitcast.50, bf16[256,896]{1,0:T(8,128)(2,1)S(1)} %bitcast.46, ...), custom_call_target="tpu_custom_call" | custom-call | tf_op jit(solution)/shard_map/weight_kept/pallas_call | solution.py:124
  113.4 4.7 %collective-permute-start.13 = (bf16[2,112,512]{2,1,0:T(8,128)(2,1)S(1)}, bf16[2,112,512]{2,1,0:T(8,128)(2,1)S(1)}, u32[]{:S(2)}, u32[]{:S(2)}) collective-permute-start(bf16[2,112,512]{2,1,0:T(8,128)(2,1)S(1)} %get-tuple-element.23), channel_id=1, source_target_pairs={{0,128},{64,192},{128,0},{192,64},{256,384},{320,448},{384,256},{4... | collective-permute-start | bytes 688136 | tf_op jit(solution)/shard_map/ppermute | solution.py:138
  118.1 2.8 %collective-permute-start.12 = (bf16[2,112,512]{2,1,0:T(8,128)(2,1)S(1)}, bf16[2,112,512]{2,1,0:T(8,128)(2,1)S(1)}, u32[]{:S(2)}, u32[]{:S(2)}) collective-permute-start(bf16[2,112,512]{2,1,0:T(8,128)(2,1)S(1)} %get-tuple-element.22), channel_id=1, source_target_pairs={{0,192},{64,0},{128,64},{192,128},{256,448},{320,256},{384,320},{4... | collective-permute-start | bytes 688136 | tf_op jit(solution)/shard_map/ppermute | solution.py:138
  120.9 2.5 %collective-permute-start.11 = (bf16[2,112,512]{2,1,0:T(8,128)(2,1)S(1)}, bf16[2,112,512]{2,1,0:T(8,128)(2,1)S(1)}, u32[]{:S(2)}, u32[]{:S(2)}) collective-permute-start(bf16[2,112,512]{2,1,0:T(8,128)(2,1)S(1)} %get-tuple-element.21), channel_id=1, source_target_pairs={{0,64},{64,128},{128,192},{192,0},{256,320},{320,384},{384,448},{4... | collective-permute-start | bytes 688136 | tf_op jit(solution)/shard_map/ppermute | solution.py:138
  124.2 4.8 %collective-permute-done.12 = bf16[2,112,512]{2,1,0:T(8,128)(2,1)S(1)} collective-permute-done((bf16[2,112,512]{2,1,0:T(8,128)(2,1)S(1)}, bf16[2,112,512]{2,1,0:T(8,128)(2,1)S(1)}, u32[]{:S(2)}, u32[]{:S(2)}) %collective-permute-start.12) | collective-permute-done | bytes 229408 | tf_op jit(solution)/shard_map/ppermute | solution.py:138
  130.6 9.2 %collective-permute-start.14 = (bf16[112,512]{1,0:T(8,128)(2,1)S(1)}, bf16[112,512]{1,0:T(8,128)(2,1)S(1)}, u32[]{:S(2)}, u32[]{:S(2)}) collective-permute-start(bf16[112,512]{1,0:T(8,128)(2,1)S(1)} %fusion.3), channel_id=1, source_target_pairs={{0,256},{64,320},{128,384},{192,448},{256,0},{320,64},{384,128},{4... | collective-permute-start | bytes 344072 | tf_op jit(solution)/shard_map/ppermute | solution.py:138
  142.1 3.5 %collective-permute-start.15 = (bf16[112,512]{1,0:T(8,128)(2,1)S(1)}, bf16[112,512]{1,0:T(8,128)(2,1)}, u32[]{:S(2)}, u32[]{:S(2)}) collective-permute-start(bf16[112,512]{1,0:T(8,128)(2,1)S(1)} %fusion.2), channel_id=1, source_target_pairs={{0,8},{4,12},{8,0},{12,4},{16,24},{20,28},{24,16},{28,20},{32,40},... | collective-permute-start | bytes 344072 | tf_op jit(solution)/shard_map/ppermute | solution.py:138
  147.2 8.5 %all-to-all-start.3 = ((bf16[16,16,896]{2,1,0:T(8,128)(2,1)}), bf16[16,16,896]{2,1,0:T(8,128)(2,1)S(1)}, u32[]{:S(2)}, u32[]{:S(2)}) async-start(bf16[16,16,896]{2,1,0:T(8,128)(2,1)} %bitcast.52), calls=%async_computation.3 | async-start | bytes 917504 | tf_op jit(solution)/shard_map/all_to_all | solution.py:142
  156.6 4.2 %collective-permute-start.16 = (bf16[112,512]{1,0:T(8,128)(2,1)S(1)}, bf16[112,512]{1,0:T(8,128)(2,1)S(1)}, u32[]{:S(2)}, u32[]{:S(2)}) collective-permute-start(bf16[112,512]{1,0:T(8,128)(2,1)S(1)} %add_convert_fusion.5), channel_id=1, source_target_pairs={{0,16},{4,20},{8,24},{12,28},{16,0},{20,4},{24,8},{28,12},{32,48},... | collective-permute-start | bytes 344072 | tf_op jit(solution)/shard_map/ppermute | solution.py:138
  162.7 3.9 %collective-permute-start.7 = (bf16[16,8,896]{2,1,0:T(8,128)(2,1)S(1)}, bf16[16,8,896]{2,1,0:T(8,128)(2,1)S(1)}, u32[]{:S(2)}, u32[]{:S(2)}) collective-permute-start(bf16[16,8,896]{2,1,0:T(8,128)(2,1)S(1)} %slice.103), channel_id=1, source_target_pairs={{0,2},{1,3},{2,0},{3,1},{4,6},{5,7},{6,4},{7,5},{8,10},{9,11},{10,... | collective-permute-start | bytes 688136 | tf_op jit(solution)/shard_map/ppermute | solution.py:138
  166.6 7.1 %collective-permute-done.16 = bf16[112,512]{1,0:T(8,128)(2,1)S(1)} collective-permute-done((bf16[112,512]{1,0:T(8,128)(2,1)S(1)}, bf16[112,512]{1,0:T(8,128)(2,1)S(1)}, u32[]{:S(2)}, u32[]{:S(2)}) %collective-permute-start.16) | collective-permute-done | bytes 114720 | tf_op jit(solution)/shard_map/ppermute | solution.py:138
  173.7 5.3 %collective-permute-start.17 = (bf16[112,512]{1,0:T(8,128)(2,1)S(1)}, bf16[112,512]{1,0:T(8,128)(2,1)S(1)}, u32[]{:S(2)}, u32[]{:S(2)}) collective-permute-start(bf16[112,512]{1,0:T(8,128)(2,1)S(1)} %add_convert_fusion.4), channel_id=1, source_target_pairs={{0,32},{4,36},{8,40},{12,44},{16,48},{20,52},{24,56},{28,60},{32,0... | collective-permute-start | bytes 344072 | tf_op jit(solution)/shard_map/ppermute | solution.py:138
  179.8 4.7 %all-to-all-start.2 = ((bf16[16,8,896]{2,1,0:T(8,128)(2,1)}), bf16[16,8,896]{2,1,0:T(8,128)(2,1)S(1)}, u32[]{:S(2)}, u32[]{:S(2)}) async-start(bf16[16,8,896]{2,1,0:T(8,128)(2,1)} %add_convert_fusion.3), calls=%async_computation.2 | async-start | bytes 458752 | tf_op jit(solution)/shard_map/all_to_all | solution.py:142
  184.5 3.9 %collective-permute-start.9 = (bf16[16,8,896]{2,1,0:T(8,128)(2,1)S(1)}, bf16[16,8,896]{2,1,0:T(8,128)(2,1)S(1)}, u32[]{:S(2)}, u32[]{:S(2)}) collective-permute-start(bf16[16,8,896]{2,1,0:T(8,128)(2,1)S(1)} %slice.105), channel_id=1, source_target_pairs={{0,2},{1,3},{2,0},{3,1},{4,6},{5,7},{6,4},{7,5},{8,10},{9,11},{10,... | collective-permute-start | bytes 688136 | tf_op jit(solution)/shard_map/ppermute | solution.py:138
  188.5 2.3 %collective-permute-start.18 = (f32[112,512]{1,0:T(8,128)S(1)}, f32[112,512]{1,0:T(8,128)S(1)}, u32[]{:S(2)}, u32[]{:S(2)}) collective-permute-start(f32[112,512]{1,0:T(8,128)S(1)} %convert_add_fusion.1), channel_id=1, source_target_pairs={{0,4},{4,0},{8,12},{12,8},{16,20},{20,16},{24,28},{28,24},{32,36},... | collective-permute-start | bytes 688136 | tf_op jit(solution)/shard_map/ppermute | solution.py:138
  190.8 8.6 %collective-permute-done.9 = bf16[16,8,896]{2,1,0:T(8,128)(2,1)S(1)} collective-permute-done((bf16[16,8,896]{2,1,0:T(8,128)(2,1)S(1)}, bf16[16,8,896]{2,1,0:T(8,128)(2,1)S(1)}, u32[]{:S(2)}, u32[]{:S(2)}) %collective-permute-start.9) | collective-permute-done | bytes 229408 | tf_op jit(solution)/shard_map/ppermute | solution.py:138
  (92 shorter events, 36.0 us)
Async XLA Ops:
  0.6 20.0 %copy-start.14 = (bf16[1,256,512]{2,1,0:T(8,128)(2,1)S(1)}, bf16[1,256,512]{2,1,0:T(8,128)(2,1)}, u32[]{:S(2)}) copy-start(bf16[1,256,512]{2,1,0:T(8,128)(2,1)} %param.5) | copy-start | bytes 786436
  0.6 20.0 %copy-start.15 = (s32[1,4,4]{2,1,0:T(4,128)S(1)}, s32[1,4,4]{2,1,0:T(4,128)}, u32[]{:S(2)}) copy-start(s32[1,4,4]{2,1,0:T(4,128)} %param.9) | copy-start | bytes 196
  0.7 20.1 %copy-start.7 = (bf16[2,896,512]{2,1,0:T(8,128)(2,1)S(1)}, bf16[2,896,512]{2,1,0:T(8,128)(2,1)}, u32[]{:S(2)}) copy-start(bf16[2,896,512]{2,1,0:T(8,128)(2,1)} %param.8) | copy-start | bytes 5505028
  2.4 38.5 %collective-permute-start = (bf16[63,1024]{1,0:T(8,128)(2,1)}, bf16[63,1024]{1,0:T(8,128)(2,1)}, u32[]{:S(2)}, u32[]{:S(2)}) collective-permute-start(bf16[63,1024]{1,0:T(8,128)(2,1)} %pad_maximum_fusion.6), channel_id=1, source_target_pairs={{4,0},{8,4},{12,8},{16,12},{20,16},{24,20},{28,24},{32,28},{36,32}... | collective-permute-start | bytes 387080 | tf_op jit(solution)/shard_map/ppermute | solution.py:138
  12.9 20.4 %all-to-all-start = ((bf16[16,8,896]{2,1,0:T(8,128)(2,1)}), bf16[16,8,896]{2,1,0:T(8,128)(2,1)S(1)}, u32[]{:S(2)}, u32[]{:S(2)}) async-start(bf16[16,8,896]{2,1,0:T(8,128)(2,1)} %get-tuple-element.29), calls=%async_computation | async-start | bytes 458752 | tf_op jit(solution)/shard_map/all_to_all | solution.py:142
  16.4 15.2 %collective-permute-start.2 = (bf16[16,8,896]{2,1,0:T(8,128)(2,1)S(1)}, bf16[16,8,896]{2,1,0:T(8,128)(2,1)}, u32[]{:S(2)}, u32[]{:S(2)}) collective-permute-start(bf16[16,8,896]{2,1,0:T(8,128)(2,1)S(1)} %get-tuple-element.28), channel_id=1, source_target_pairs={{0,2},{1,3},{2,0},{3,1},{4,6},{5,7},{6,4},{7,5},{8,10},{9,11},{10,... | collective-permute-start | bytes 688136 | tf_op jit(solution)/shard_map/ppermute | solution.py:138
  21.9 57.7 %copy-start.8 = (bf16[896,512]{1,0:T(8,128)(2,1)}, bf16[896,512]{1,0:T(8,128)(2,1)S(1)}, u32[]{:S(2)}) copy-start(bf16[896,512]{1,0:T(8,128)(2,1)S(1)} %get-tuple-element.24) | copy-start | bytes 2752516
  33.3 28.0 %all-to-all-start.1 = ((bf16[16,16,896]{2,1,0:T(8,128)(2,1)}), bf16[16,16,896]{2,1,0:T(8,128)(2,1)S(1)}, u32[]{:S(2)}, u32[]{:S(2)}) async-start(bf16[16,16,896]{2,1,0:T(8,128)(2,1)} %pad_maximum_fusion.2), calls=%async_computation.1 | async-start | bytes 917504 | tf_op jit(solution)/shard_map/all_to_all | solution.py:142
  41.7 14.9 %collective-permute-start.1 = (bf16[16,8,896]{2,1,0:T(8,128)(2,1)S(1)}, bf16[16,8,896]{2,1,0:T(8,128)(2,1)S(1)}, u32[]{:S(2)}, u32[]{:S(2)}) collective-permute-start(bf16[16,8,896]{2,1,0:T(8,128)(2,1)S(1)} %all-to-all-done), channel_id=1, source_target_pairs={{0,2},{1,3},{2,0},{3,1},{4,6},{5,7},{6,4},{7,5},{8,10},{9,11},{10,... | collective-permute-start | bytes 688136 | tf_op jit(solution)/shard_map/ppermute | solution.py:138
  56.6 13.1 %collective-permute-start.3 = (bf16[256,896]{1,0:T(8,128)(2,1)S(1)}, bf16[256,896]{1,0:T(8,128)(2,1)S(1)}, u32[]{:S(2)}, u32[]{:S(2)}) collective-permute-start(bf16[256,896]{1,0:T(8,128)(2,1)S(1)} %bitcast.47), channel_id=1, source_target_pairs={{0,1},{1,0},{2,3},{3,2},{4,5},{5,4},{6,7},{7,6},{8,9},{9,8},{10,11... | collective-permute-start | bytes 1376264 | tf_op jit(solution)/shard_map/ppermute | solution.py:138
  61.3 18.3 %collective-permute-start.4 = (bf16[256,896]{1,0:T(8,128)(2,1)S(1)}, bf16[256,896]{1,0:T(8,128)(2,1)S(1)}, u32[]{:S(2)}, u32[]{:S(2)}) collective-permute-start(bf16[256,896]{1,0:T(8,128)(2,1)S(1)} %bitcast.43), channel_id=1, source_target_pairs={{0,1},{1,0},{2,3},{3,2},{4,5},{5,4},{6,7},{7,6},{8,9},{9,8},{10,11... | collective-permute-start | bytes 1376264 | tf_op jit(solution)/shard_map/ppermute | solution.py:138
  70.4 9.8 %copy-start.2 = (bf16[256,512]{1,0:T(8,128)(2,1)S(1)}, bf16[256,512]{1,0:T(8,128)(2,1)}, u32[]{:S(2)}) copy-start(bf16[256,512]{1,0:T(8,128)(2,1)} %pad_maximum_fusion.4.refs_1_) | copy-start | bytes 786436
  70.4 9.8 %copy-start.3 = (bf16[256,512]{1,0:T(8,128)(2,1)S(1)}, bf16[256,512]{1,0:T(8,128)(2,1)}, u32[]{:S(2)}) copy-start(bf16[256,512]{1,0:T(8,128)(2,1)} %pad_maximum_fusion.5.refs_2_) | copy-start | bytes 786436
  70.4 9.8 %copy-start.4 = (bf16[256,1024]{1,0:T(8,128)(2,1)S(1)}, bf16[256,1024]{1,0:T(8,128)(2,1)}, u32[]{:S(2)}) copy-start(bf16[256,1024]{1,0:T(8,128)(2,1)} %convolution_convert_fusion.3.refs_3_) | copy-start | bytes 1572868
  91.2 19.5 %collective-permute-start.10 = (bf16[896,512]{1,0:T(8,128)(2,1)}, bf16[896,512]{1,0:T(8,128)(2,1)}, u32[]{:S(2)}, u32[]{:S(2)}) collective-permute-start(bf16[896,512]{1,0:T(8,128)(2,1)} %weight_sent.1), channel_id=1, source_target_pairs={{0,4},{4,0},{8,12},{12,8},{16,20},{20,16},{24,28},{28,24},{32,36},... | collective-permute-start | bytes 2752520 | tf_op jit(solution)/shard_map/ppermute | solution.py:138
  98.6 22.3 %collective-permute-start.5 = (bf16[63,1024]{1,0:T(8,128)(2,1)S(1)}, bf16[63,1024]{1,0:T(8,128)(2,1)S(1)}, u32[]{:S(2)}, u32[]{:S(2)}) collective-permute-start(bf16[63,1024]{1,0:T(8,128)(2,1)S(1)} %pad_maximum_fusion.7), channel_id=1, source_target_pairs={{0,4},{4,8},{8,12},{12,16},{16,20},{20,24},{24,28},{28,32},{32,36}... | collective-permute-start | bytes 387080 | tf_op jit(solution)/shard_map/ppermute | solution.py:138
  103.8 41.9 %collective-permute-start.8 = (bf16[256,896]{1,0:T(8,128)(2,1)S(1)}, bf16[256,896]{1,0:T(8,128)(2,1)S(1)}, u32[]{:S(2)}, u32[]{:S(2)}) collective-permute-start(bf16[256,896]{1,0:T(8,128)(2,1)S(1)} %convolution_convert_fusion.4), channel_id=1, source_target_pairs={{0,1},{1,0},{2,3},{3,2},{4,5},{5,4},{6,7},{7,6},{8,9},{9,8},{10,11... | collective-permute-start | bytes 1376264 | tf_op jit(solution)/shard_map/ppermute | solution.py:138
  107.4 53.4 %collective-permute-start.6 = (bf16[256,896]{1,0:T(8,128)(2,1)}, bf16[256,896]{1,0:T(8,128)(2,1)}, u32[]{:S(2)}, u32[]{:S(2)}) collective-permute-start(bf16[256,896]{1,0:T(8,128)(2,1)} %convolution_convert_fusion.6), channel_id=1, source_target_pairs={{0,1},{1,0},{2,3},{3,2},{4,5},{5,4},{6,7},{7,6},{8,9},{9,8},{10,11... | collective-permute-start | bytes 1376264 | tf_op jit(solution)/shard_map/ppermute | solution.py:138
  113.4 10.8 %collective-permute-start.13 = (bf16[2,112,512]{2,1,0:T(8,128)(2,1)S(1)}, bf16[2,112,512]{2,1,0:T(8,128)(2,1)S(1)}, u32[]{:S(2)}, u32[]{:S(2)}) collective-permute-start(bf16[2,112,512]{2,1,0:T(8,128)(2,1)S(1)} %get-tuple-element.23), channel_id=1, source_target_pairs={{0,128},{64,192},{128,0},{192,64},{256,384},{320,448},{384,256},{4... | collective-permute-start | bytes 688136 | tf_op jit(solution)/shard_map/ppermute | solution.py:138
  118.1 10.9 %collective-permute-start.12 = (bf16[2,112,512]{2,1,0:T(8,128)(2,1)S(1)}, bf16[2,112,512]{2,1,0:T(8,128)(2,1)S(1)}, u32[]{:S(2)}, u32[]{:S(2)}) collective-permute-start(bf16[2,112,512]{2,1,0:T(8,128)(2,1)S(1)} %get-tuple-element.22), channel_id=1, source_target_pairs={{0,192},{64,0},{128,64},{192,128},{256,448},{320,256},{384,320},{4... | collective-permute-start | bytes 688136 | tf_op jit(solution)/shard_map/ppermute | solution.py:138
  120.9 9.6 %collective-permute-start.11 = (bf16[2,112,512]{2,1,0:T(8,128)(2,1)S(1)}, bf16[2,112,512]{2,1,0:T(8,128)(2,1)S(1)}, u32[]{:S(2)}, u32[]{:S(2)}) collective-permute-start(bf16[2,112,512]{2,1,0:T(8,128)(2,1)S(1)} %get-tuple-element.21), channel_id=1, source_target_pairs={{0,64},{64,128},{128,192},{192,0},{256,320},{320,384},{384,448},{4... | collective-permute-start | bytes 688136 | tf_op jit(solution)/shard_map/ppermute | solution.py:138
  130.6 11.4 %collective-permute-start.14 = (bf16[112,512]{1,0:T(8,128)(2,1)S(1)}, bf16[112,512]{1,0:T(8,128)(2,1)S(1)}, u32[]{:S(2)}, u32[]{:S(2)}) collective-permute-start(bf16[112,512]{1,0:T(8,128)(2,1)S(1)} %fusion.3), channel_id=1, source_target_pairs={{0,256},{64,320},{128,384},{192,448},{256,0},{320,64},{384,128},{4... | collective-permute-start | bytes 344072 | tf_op jit(solution)/shard_map/ppermute | solution.py:138
  142.1 18.7 %copy-start.10 = (bf16[896,512]{1,0:T(8,128)(2,1)S(1)}, bf16[896,512]{1,0:T(8,128)(2,1)}, u32[]{:S(2)}) copy-start(bf16[896,512]{1,0:T(8,128)(2,1)} %copy-done.8) | copy-start | bytes 2752516
  142.1 18.7 %copy-start.13 = (bf16[896,512]{1,0:T(8,128)(2,1)S(1)}, bf16[896,512]{1,0:T(8,128)(2,1)}, u32[]{:S(2)}) copy-start(bf16[896,512]{1,0:T(8,128)(2,1)} %get-tuple-element.25) | copy-start | bytes 2752516
  142.1 13.5 %collective-permute-start.15 = (bf16[112,512]{1,0:T(8,128)(2,1)S(1)}, bf16[112,512]{1,0:T(8,128)(2,1)}, u32[]{:S(2)}, u32[]{:S(2)}) collective-permute-start(bf16[112,512]{1,0:T(8,128)(2,1)S(1)} %fusion.2), channel_id=1, source_target_pairs={{0,8},{4,12},{8,0},{12,4},{16,24},{20,28},{24,16},{28,20},{32,40},... | collective-permute-start | bytes 344072 | tf_op jit(solution)/shard_map/ppermute | solution.py:138
  147.2 32.7 %all-to-all-start.3 = ((bf16[16,16,896]{2,1,0:T(8,128)(2,1)}), bf16[16,16,896]{2,1,0:T(8,128)(2,1)S(1)}, u32[]{:S(2)}, u32[]{:S(2)}) async-start(bf16[16,16,896]{2,1,0:T(8,128)(2,1)} %bitcast.52), calls=%async_computation.3 | async-start | bytes 917504 | tf_op jit(solution)/shard_map/all_to_all | solution.py:142
  156.6 17.1 %collective-permute-start.16 = (bf16[112,512]{1,0:T(8,128)(2,1)S(1)}, bf16[112,512]{1,0:T(8,128)(2,1)S(1)}, u32[]{:S(2)}, u32[]{:S(2)}) collective-permute-start(bf16[112,512]{1,0:T(8,128)(2,1)S(1)} %add_convert_fusion.5), channel_id=1, source_target_pairs={{0,16},{4,20},{8,24},{12,28},{16,0},{20,4},{24,8},{28,12},{32,48},... | collective-permute-start | bytes 344072 | tf_op jit(solution)/shard_map/ppermute | solution.py:138
  162.7 16.4 %collective-permute-start.7 = (bf16[16,8,896]{2,1,0:T(8,128)(2,1)S(1)}, bf16[16,8,896]{2,1,0:T(8,128)(2,1)S(1)}, u32[]{:S(2)}, u32[]{:S(2)}) collective-permute-start(bf16[16,8,896]{2,1,0:T(8,128)(2,1)S(1)} %slice.103), channel_id=1, source_target_pairs={{0,2},{1,3},{2,0},{3,1},{4,6},{5,7},{6,4},{7,5},{8,10},{9,11},{10,... | collective-permute-start | bytes 688136 | tf_op jit(solution)/shard_map/ppermute | solution.py:138
  173.7 14.7 %collective-permute-start.17 = (bf16[112,512]{1,0:T(8,128)(2,1)S(1)}, bf16[112,512]{1,0:T(8,128)(2,1)S(1)}, u32[]{:S(2)}, u32[]{:S(2)}) collective-permute-start(bf16[112,512]{1,0:T(8,128)(2,1)S(1)} %add_convert_fusion.4), channel_id=1, source_target_pairs={{0,32},{4,36},{8,40},{12,44},{16,48},{20,52},{24,56},{28,60},{32,0... | collective-permute-start | bytes 344072 | tf_op jit(solution)/shard_map/ppermute | solution.py:138
  179.8 19.6 %all-to-all-start.2 = ((bf16[16,8,896]{2,1,0:T(8,128)(2,1)}), bf16[16,8,896]{2,1,0:T(8,128)(2,1)S(1)}, u32[]{:S(2)}, u32[]{:S(2)}) async-start(bf16[16,8,896]{2,1,0:T(8,128)(2,1)} %add_convert_fusion.3), calls=%async_computation.2 | async-start | bytes 458752 | tf_op jit(solution)/shard_map/all_to_all | solution.py:142
  184.5 14.9 %collective-permute-start.9 = (bf16[16,8,896]{2,1,0:T(8,128)(2,1)S(1)}, bf16[16,8,896]{2,1,0:T(8,128)(2,1)S(1)}, u32[]{:S(2)}, u32[]{:S(2)}) collective-permute-start(bf16[16,8,896]{2,1,0:T(8,128)(2,1)S(1)} %slice.105), channel_id=1, source_target_pairs={{0,2},{1,3},{2,0},{3,1},{4,6},{5,7},{6,4},{7,5},{8,10},{9,11},{10,... | collective-permute-start | bytes 688136 | tf_op jit(solution)/shard_map/ppermute | solution.py:138
  188.5 11.8 %collective-permute-start.18 = (f32[112,512]{1,0:T(8,128)S(1)}, f32[112,512]{1,0:T(8,128)S(1)}, u32[]{:S(2)}, u32[]{:S(2)}) collective-permute-start(f32[112,512]{1,0:T(8,128)S(1)} %convert_add_fusion.1), channel_id=1, source_target_pairs={{0,4},{4,0},{8,12},{12,8},{16,20},{20,16},{24,28},{28,24},{32,36},... | collective-permute-start | bytes 688136 | tf_op jit(solution)/shard_map/ppermute | solution.py:138
  (7 other events, 44.4 us)

commit v3 on v1

v3 whole, which is shorter than its diff:
```python
import math

import jax
import jax.numpy as jnp
from jax import lax
from jax.experimental import pallas as pl
from jax.experimental.pallas import tpu as pltpu
from jax.sharding import PartitionSpec as P

HEAD_DIM = 128
SPAN = 64
PART = 64
LEAD = SPAN - 1
SCALE = 1.0 / math.sqrt(HEAD_DIM)
NT = (((1,), (1,)), ((), ()))
TN = (((0,), (0,)), ((), ()))
NN = (((1,), (0,)), ((), ()))
VMEM = pl.BlockSpec(memory_space=pltpu.VMEM)
SMEM = pl.BlockSpec(memory_space=pltpu.SMEM)
PARAMS = pltpu.CompilerParams(vmem_limit_bytes=50 * 1024 * 1024)


def dot(a, b, dims):
    return lax.dot_general(a, b, dims, preferred_element_type=jnp.float32)


def span_rows(own, ahead):
    own, ahead = own.astype(jnp.float32), ahead.astype(jnp.float32)
    row = lax.broadcasted_iota(jnp.int32, ahead.shape, 0)
    mixed = jnp.concatenate((jnp.where(row < LEAD, ahead, own[:SPAN]), own[SPAN:]), axis=0)
    return pltpu.roll(mixed, own.shape[0] - LEAD, 0).astype(jnp.bfloat16)


def block_body(slots, units, piece, units_ref, place_ref, q_ref, g_ref, ahead_ref, w_ref, *refs):
    xa_refs, xb_ref = refs[:slots], refs[slots]
    att_ref, dq_ref, *p_refs = refs[slots + 1 : 2 * slots + 3]
    sent_ref, kept_ref, xa, key, value, grad, q_rows, g_rows, att, dq = refs[2 * slots + 3 :]
    tokens, width = q_ref.shape
    first = xa.shape[1]
    enc_width = w_ref.shape[1]
    heads = width // HEAD_DIM
    for n, ref in enumerate(xa_refs):
        for u in range(units):
            xa[u * PART + n * piece : u * PART + (n + 1) * piece, :] = ref[u * piece : (u + 1) * piece, :]
    chunk = 4 * PART
    for c in range(units // 4):
        rows = pl.ds(c * chunk, chunk)
        for kind, out in enumerate((key, value)):
            term = dot(xa[rows, :], w_ref[kind, :first, :], NN) + dot(xb_ref[rows, :], w_ref[kind, first:, :], NN)
            out[rows, :] = term.astype(jnp.bfloat16)
    for h in range(heads):
        cols = pl.ds(h * HEAD_DIM, HEAD_DIM)
        q_rows[:, cols] = span_rows(q_ref[:, cols], ahead_ref[:, cols])
        g_rows[:, cols] = span_rows(g_ref[:, cols], ahead_ref[:, pl.ds(width + h * HEAD_DIM, HEAD_DIM)])
    for j in range(tokens // SPAN):
        starts = [pl.multiple_of(units_ref[j * 4 + r] * PART, PART) for r in range(4)]
        rows = pl.ds(j * SPAN, SPAN)
        for h in range(heads):
            cols = pl.ds(h * HEAD_DIM, HEAD_DIM)
            q = q_rows[rows, cols]
            g = g_rows[rows, cols]
            k = jnp.concatenate([key[pl.ds(s, PART), cols] for s in starts], axis=0)
            v = jnp.concatenate([value[pl.ds(s, PART), cols] for s in starts], axis=0)
            scores = dot(q, k, NT) * SCALE
            raised = jnp.exp(scores - jnp.max(scores, axis=-1, keepdims=True))
            weights = raised / jnp.sum(raised, axis=-1, keepdims=True)
            low = weights.astype(jnp.bfloat16)
            d_weights = dot(g, v, NT)
            inner = jnp.sum(weights * d_weights, axis=-1, keepdims=True)
            d_scores = (weights * (d_weights - inner) * SCALE).astype(jnp.bfloat16)
            att[rows, cols] = dot(low, v, NN)
            dq[rows, cols] = dot(d_scores, k, NN)
            dk = dot(d_scores, q, TN).astype(jnp.bfloat16)
            dv = dot(low, g, TN).astype(jnp.bfloat16)
            for r, s in enumerate(starts):
                grad[0, pl.ds(s, PART), cols] = dk[r * PART : (r + 1) * PART]
                grad[1, pl.ds(s, PART), cols] = dv[r * PART : (r + 1) * PART]
    for h in range(heads):
        cols = pl.ds(h * HEAD_DIM, HEAD_DIM)
        att_ref[:, cols] = pltpu.roll(att[:, cols], LEAD, 0).astype(jnp.bfloat16)
        dq_ref[:, cols] = pltpu.roll(dq[:, cols], LEAD, 0).astype(jnp.bfloat16)
    for c in range(units // 4):
        rows = pl.ds(c * chunk, chunk)
        term = dot(grad[0, rows, :], w_ref[0], NT) + dot(grad[1, rows, :], w_ref[1], NT)
        term = term.astype(jnp.bfloat16)
        for u in range(4):
            for n, ref in enumerate(p_refs):
                at = u * PART + n * piece
                ref[(c * 4 + u) * piece : (c * 4 + u + 1) * piece, :] = term[at : at + piece]
    core = place_ref[0]
    for e in range(0, enc_width, 128):
        x = xa[:, e : e + 128] if e < first else xb_ref[:, e - first : e - first + 128]
        x = x.T
        sent_ref[e : e + 128, :] = dot(x, grad[1 - core], NN).astype(jnp.bfloat16)
        kept_ref[e : e + 128, :] = dot(x, grad[core], NN)


def block(units_of, place, q, g, ahead, w, xa, xb):
    slots = len(xa)
    tokens, width = q.shape
    first = xa[0].shape[1]
    enc_width = w.shape[1]
    all_rows = xb.shape[0]
    units, piece = all_rows // PART, PART // slots

    def body(*refs):
        block_body(slots, units, piece, *refs)

    def low(*shape):
        return jax.ShapeDtypeStruct(shape, jnp.bfloat16)

    return pl.pallas_call(
        body,
        out_shape=[low(tokens, width)] * 2
        + [low(units * piece, enc_width)] * slots
        + [low(enc_width, width), jax.ShapeDtypeStruct((enc_width, width), jnp.float32)],
        in_specs=[SMEM] * 2 + [VMEM] * (5 + slots),
        out_specs=[VMEM] * (4 + slots),
        scratch_shapes=[
            pltpu.VMEM((all_rows, first), jnp.bfloat16),
            pltpu.VMEM((all_rows, width), jnp.bfloat16),
            pltpu.VMEM((all_rows, width), jnp.bfloat16),
            pltpu.VMEM((2, all_rows, width), jnp.bfloat16),
            pltpu.VMEM((tokens, width), jnp.bfloat16),
            pltpu.VMEM((tokens, width), jnp.bfloat16),
            pltpu.VMEM((tokens, width), jnp.float32),
            pltpu.VMEM((tokens, width), jnp.float32),
        ],
        compiler_params=PARAMS,
        name="block",
    )(units_of, place, q, g, ahead, w, *xa, xb)


def cut(place, kept, away):
    enc_width, width = kept.shape
    rows = enc_width // 8

    def body(place_ref, kept_ref, away_ref, own_ref, *send_refs):
        x = place_ref[1]
        for high in range(2):
            for k in range(4):
                at = pl.multiple_of((high * 4 + lax.rem(x + k, 4)) * rows, 16)
                term = kept_ref[pl.ds(at, rows), :] + away_ref[pl.ds(at, rows), :].astype(jnp.float32)
                if k:
                    send_refs[k - 1][high] = term.astype(jnp.bfloat16)
                else:
                    own_ref[high] = term

    return pl.pallas_call(
        body,
        out_shape=[jax.ShapeDtypeStruct((2, rows, width), jnp.float32)]
        + [jax.ShapeDtypeStruct((2, rows, width), jnp.bfloat16)] * 3,
        in_specs=[SMEM] + [VMEM] * 2,
        out_specs=[VMEM] * 4,
        compiler_params=PARAMS,
        name="cut",
    )(place, kept, away)


def fold(place, own, parts, partial, terms):
    _, rows, width = own.shape

    def body(place_ref, own_ref, *refs):
        part_refs, partial_ref, term_refs = refs[:3], refs[3], refs[4:7]
        mine_ref, other_ref, total_ref = refs[7:]
        high = place_ref[2]
        for ref, at in ((mine_ref, high), (other_ref, 1 - high)):
            total = own_ref[at]
            for part in part_refs:
                total = total + part[at].astype(jnp.float32)
            ref[...] = total.astype(ref.dtype)
        total = partial_ref[...].astype(jnp.float32)
        for term in term_refs:
            total = total + term[...].astype(jnp.float32)
        total_ref[...] = total.astype(jnp.bfloat16)

    return pl.pallas_call(
        body,
        out_shape=[
            jax.ShapeDtypeStruct((rows, width), jnp.float32),
            jax.ShapeDtypeStruct((rows, width), jnp.bfloat16),
            jax.ShapeDtypeStruct(partial.shape, jnp.bfloat16),
        ],
        in_specs=[SMEM] + [VMEM] * 8,
        out_specs=[VMEM] * 3,
        compiler_params=PARAMS,
        name="fold",
    )(place, own, *parts, partial, *terms)


def permute(x, axis, to):
    n = lax.axis_size(axis)
    return lax.ppermute(x, axis, [(i, to(i)) for i in range(n) if 0 <= to(i) < n])


def exchange(x):
    return lax.all_to_all(x, "ctx", split_axis=0, concat_axis=0, tiled=True)


def shards(queries, cotangent, encoded, kv_weight, neighbour_ids):
    q, g, enc = queries[0], cotangent[0], encoded[0]
    width = q.shape[1]
    units, piece, enc_width = enc.shape
    groups = lax.axis_size("nbr")
    ctx = lax.axis_index("ctx")
    dp = lax.axis_index("dp")
    place = jnp.stack((ctx % 2, dp % 4, dp // 4)).astype(jnp.int32)

    def gathered(x):
        return [x] + [permute(x, "nbr", lambda i, k=k: (i + k) % groups) for k in range(1, groups)]

    first = enc_width // 7 * 5
    xa = gathered(exchange(enc[:, :, :first]).reshape(units * piece, first))
    xb = exchange(jnp.concatenate(gathered(enc[:, :, first:]), axis=1)).reshape(-1, enc_width - first)

    head = jnp.concatenate((q[:SPAN], g[:SPAN]), axis=1)
    ahead = permute(head, "ctx", lambda i: i - 1)

    unit_of = (neighbour_ids[0] // units).reshape(-1)
    att, dq, *partials, sent, kept = block(unit_of, place, q, g, ahead, kv_weight, xa, xb)

    away = permute(sent, "ctx", lambda i: i ^ 1)
    own, *sends = cut(place, kept, away)
    parts = [
        permute(sends[k - 1], "dp", lambda i, k=k: i // 4 * 4 + (i + k) % 4) for k in (1, 2, 3)
    ]
    terms = [permute(partials[k], "nbr", lambda i, k=k: (i - k) % groups) for k in range(1, groups)]
    mine, other, total = fold(place, own, parts, partials[0], terms)
    encoded_grad = exchange(total.reshape(units, piece, enc_width))
    mine = mine + permute(other, "dp", lambda i: (i + 4) % 8).astype(jnp.float32)
    low = mine.astype(jnp.bfloat16)
    low = add(low, permute(low, "ctx", lambda i: i ^ 2)).astype(jnp.bfloat16)
    by = [permute(low, "ctx", lambda i, b=b: i ^ b) for b in (4, 8, 12)]
    mine = add(low, by[0]) + add(by[1], by[2])
    theirs = permute(mine, "ctx", lambda i: i ^ 1)
    keys_here = ctx % 2 == 0
    weight_grad = jnp.stack((jnp.where(keys_here, mine, theirs), jnp.where(keys_here, theirs, mine)), axis=0)

    tail = jnp.concatenate((att[:SPAN], dq[:SPAN]), axis=1)
    behind = permute(tail, "ctx", lambda i: i + 1)
    lead = lax.broadcasted_iota(jnp.int32, (SPAN, width), 0) < LEAD
    attended = jnp.concatenate((jnp.where(lead, behind[:, :width], att[:SPAN]), att[SPAN:]), axis=0)
    query_grad = jnp.concatenate((jnp.where(lead, behind[:, width:], dq[:SPAN]), dq[SPAN:]), axis=0)
    return (attended[None], query_grad[None], encoded_grad[None], weight_grad)


def add(a, b):
    return a.astype(jnp.float32) + b.astype(jnp.float32)


def solution(mesh):
    return jax.shard_map(
        shards,
        mesh=mesh,
        in_specs=(
            P("dp", "ctx", "nbr"),
            P("dp", "ctx", "nbr"),
            P("dp", "ctx", "nbr", None),
            P(None, None, "nbr"),
            P("dp", "ctx", None),
        ),
        out_specs=(
            P("dp", "ctx", "nbr"),
            P("dp", "ctx", "nbr"),
            P("dp", "ctx", "nbr", None),
            P(None, "dp", "nbr"),
        ),
        check_vma=False,
    )
```

time: 212 us -> 205 us (0.967)
  the two profiles are of different devices: /device:TPU:65 before, /device:TPU:1 now
where the time goes in v3:
time: 205 us; the launch traced here: 204 us
  starting transfers between devices  109 us (53%)
  waiting for transfers between devices  65.1 us (32%)
  Pallas kernels  19.4 us (9%)
  local copies, waits for them, and re-layouts  5.92 us (3%)
  other arithmetic  3.43 us (2%)
    ppermute x21, starting transfers between devices, permute(): lax.ppermute(x, axis, [(i, to(i)) for i in range(n) if 0 <= to(i) < n])  83.5 us
    ppermute x21, waiting for transfers between devices, permute(): lax.ppermute(x, axis, [(i, to(i)) for i in range(n) if 0 <= to(i) < n])  65.1 us
    all_to_all x3, starting transfers between devices, exchange(): return lax.all_to_all(x, 'ctx', split_axis=0, concat_axis=0, tiled=True)  25.2 us
    pallas_call x1, Pallas kernels, block(): pl.pallas_call(body, out_shape=[low(tokens, width)] * 2 + [low(units * pi...  17.1 us
  transfers between devices with their start and end apart: 24, of which 9 were waited for; matrix products, arithmetic and copies ran while one was open for 2% of the time, Pallas kernels for 0%

profile of v3, /device:TPU:1, one launch (start us, length us, event | category | flops | bytes accessed | tf_op | source)
XLA Modules:
  0.0 203.5 jit_solution(11547377768674680792)
XLA Ops:
  2.4 10.3 %all-to-all-start = ((bf16[16,16,640]{2,1,0:T(8,128)(2,1)}), bf16[16,16,640]{2,1,0:T(8,128)(2,1)S(1)}, u32[]{:S(2)}, u32[]{:S(2)}) async-start(bf16[16,16,640]{2,1,0:T(8,128)(2,1)} %slice.50), calls=%async_computation | async-start | bytes 655360 | tf_op jit(solution)/shard_map/all_to_all | solution.py:197
  13.7 2.4 %collective-permute-start.4 = (bf16[16,16,256]{2,1,0:T(8,128)(2,1)S(1)}, bf16[16,16,256]{2,1,0:T(8,128)(2,1)S(1)}, u32[]{:S(2)}, u32[]{:S(2)}) collective-permute-start(bf16[16,16,256]{2,1,0:T(8,128)(2,1)S(1)} %slice.51), channel_id=1, source_target_pairs={{0,1},{1,2},{2,3},{3,0},{4,5},{5,6},{6,7},{7,4},{8,9},{9,10},{10,1... | collective-permute-start | bytes 393224 | tf_op jit(solution)/shard_map/ppermute | solution.py:193
  16.1 5.8 %collective-permute-start.5 = (bf16[16,16,256]{2,1,0:T(8,128)(2,1)S(1)}, bf16[16,16,256]{2,1,0:T(8,128)(2,1)S(1)}, u32[]{:S(2)}, u32[]{:S(2)}) collective-permute-start(bf16[16,16,256]{2,1,0:T(8,128)(2,1)S(1)} %slice.51), channel_id=1, source_target_pairs={{0,2},{1,3},{2,0},{3,1},{4,6},{5,7},{6,4},{7,5},{8,10},{9,11},{10,... | collective-permute-start | bytes 393224 | tf_op jit(solution)/shard_map/ppermute | solution.py:193
  21.9 2.2 %collective-permute-start.6 = (bf16[16,16,256]{2,1,0:T(8,128)(2,1)S(1)}, bf16[16,16,256]{2,1,0:T(8,128)(2,1)S(1)}, u32[]{:S(2)}, u32[]{:S(2)}) collective-permute-start(bf16[16,16,256]{2,1,0:T(8,128)(2,1)S(1)} %slice.51), channel_id=1, source_target_pairs={{0,3},{1,0},{2,1},{3,2},{4,7},{5,4},{6,5},{7,6},{8,11},{9,8},{10,9... | collective-permute-start | bytes 393224 | tf_op jit(solution)/shard_map/ppermute | solution.py:193
  24.1 5.2 %collective-permute-done.5 = bf16[16,16,256]{2,1,0:T(8,128)(2,1)S(1)} collective-permute-done((bf16[16,16,256]{2,1,0:T(8,128)(2,1)S(1)}, bf16[16,16,256]{2,1,0:T(8,128)(2,1)S(1)}, u32[]{:S(2)}, u32[]{:S(2)}) %collective-permute-start.5) | collective-permute-done | bytes 131104 | tf_op jit(solution)/shard_map/ppermute | solution.py:193
  29.4 2.4 %collective-permute-done.6 = bf16[16,16,256]{2,1,0:T(8,128)(2,1)S(1)} collective-permute-done((bf16[16,16,256]{2,1,0:T(8,128)(2,1)S(1)}, bf16[16,16,256]{2,1,0:T(8,128)(2,1)S(1)}, u32[]{:S(2)}, u32[]{:S(2)}) %collective-permute-start.6) | collective-permute-done | bytes 131104 | tf_op jit(solution)/shard_map/ppermute | solution.py:193
  32.6 7.5 %all-to-all-start.1 = ((bf16[16,64,256]{2,1,0:T(8,128)(2,1)}), bf16[16,64,256]{2,1,0:T(8,128)(2,1)S(1)}, u32[]{:S(2)}, u32[]{:S(2)}) async-start(bf16[16,64,256]{2,1,0:T(8,128)(2,1)} %pad_maximum_fusion), calls=%async_computation.1 | async-start | bytes 1048576 | tf_op jit(solution)/shard_map/all_to_all | solution.py:197
  40.2 2.0 collective-permute-start
  42.3 2.4 %collective-permute-start.1 = (bf16[256,640]{1,0:T(8,128)(2,1)S(1)}, bf16[256,640]{1,0:T(8,128)(2,1)S(1)}, u32[]{:S(2)}, u32[]{:S(2)}) collective-permute-start(bf16[256,640]{1,0:T(8,128)(2,1)S(1)} %bitcast.22), channel_id=1, source_target_pairs={{0,1},{1,2},{2,3},{3,0},{4,5},{5,6},{6,7},{7,4},{8,9},{9,10},{10,1... | collective-permute-start | bytes 983048 | tf_op jit(solution)/shard_map/ppermute | solution.py:193
  44.7 3.3 %collective-permute-start.2 = (bf16[256,640]{1,0:T(8,128)(2,1)S(1)}, bf16[256,640]{1,0:T(8,128)(2,1)S(1)}, u32[]{:S(2)}, u32[]{:S(2)}) collective-permute-start(bf16[256,640]{1,0:T(8,128)(2,1)S(1)} %bitcast.23), channel_id=1, source_target_pairs={{0,2},{1,3},{2,0},{3,1},{4,6},{5,7},{6,4},{7,5},{8,10},{9,11},{10,... | collective-permute-start | bytes 983048 | tf_op jit(solution)/shard_map/ppermute | solution.py:193
  48.1 3.2 %collective-permute-start.3 = (bf16[256,640]{1,0:T(8,128)(2,1)S(1)}, bf16[256,640]{1,0:T(8,128)(2,1)S(1)}, u32[]{:S(2)}, u32[]{:S(2)}) collective-permute-start(bf16[256,640]{1,0:T(8,128)(2,1)S(1)} %bitcast.24), channel_id=1, source_target_pairs={{0,3},{1,0},{2,1},{3,2},{4,7},{5,4},{6,5},{7,6},{8,11},{9,8},{10,9... | collective-permute-start | bytes 983048 | tf_op jit(solution)/shard_map/ppermute | solution.py:193
  51.4 4.2 %collective-permute-done.refs_4_ = bf16[64,1024]{1,0:T(8,128)(2,1)S(1)} collective-permute-done((bf16[64,1024]{1,0:T(8,128)(2,1)S(1)}, bf16[64,1024]{1,0:T(8,128)(2,1)S(1)}, u32[]{:S(2)}, u32[]{:S(2)}) %collective-permute-start) | collective-permute-done | bytes 131104 | tf_op jit(solution)/shard_map/ppermute | solution.py:193
  55.8 13.8 %collective-permute-done.2.refs_8_ = bf16[256,640]{1,0:T(8,128)(2,1)S(1)} collective-permute-done((bf16[256,640]{1,0:T(8,128)(2,1)S(1)}, bf16[256,640]{1,0:T(8,128)(2,1)S(1)}, u32[]{:S(2)}, u32[]{:S(2)}) %collective-permute-start.2) | collective-permute-done | bytes 327712 | tf_op jit(solution)/shard_map/ppermute | solution.py:193
  70.4 17.1 %block.1 = (bf16[256,512]{1,0:T(8,128)(2,1)S(1)}, bf16[256,512]{1,0:T(8,128)(2,1)S(1)}, bf16[256,896]{1,0:T(8,128)(2,1)S(1)}, bf16[256,896]{1,0:T(8,128)(2,1)S(1...) custom-call(s32[16]{0:T(128)S(1)} %and_select_fusion.refs_0_, ...), custom_call_target="tpu_custom_call" | custom-call | tf_op jit(solution)/shard_map/block/pallas_call | solution.py:112
  87.5 2.3 %collective-permute-start.8 = (bf16[896,512]{1,0:T(8,128)(2,1)}, bf16[896,512]{1,0:T(8,128)(2,1)S(1)}, u32[]{:S(2)}, u32[]{:S(2)}) collective-permute-start(bf16[896,512]{1,0:T(8,128)(2,1)} %get-tuple-element.22), channel_id=1, source_target_pairs={{0,4},{4,0},{8,12},{12,8},{16,20},{20,16},{24,28},{28,24},{32,36},... | collective-permute-start | bytes 2752520 | tf_op jit(solution)/shard_map/ppermute | solution.py:193
  89.9 7.6 %collective-permute-start.12 = (bf16[256,896]{1,0:T(8,128)(2,1)S(1)}, bf16[256,896]{1,0:T(8,128)(2,1)S(1)}, u32[]{:S(2)}, u32[]{:S(2)}) collective-permute-start(bf16[256,896]{1,0:T(8,128)(2,1)S(1)} %get-tuple-element.28), channel_id=1, source_target_pairs={{0,3},{1,0},{2,1},{3,2},{4,7},{5,4},{6,5},{7,6},{8,11},{9,8},{10,9... | collective-permute-start | bytes 1376264 | tf_op jit(solution)/shard_map/ppermute | solution.py:193
  97.5 4.7 %collective-permute-start.13 = (bf16[256,896]{1,0:T(8,128)(2,1)S(1)}, bf16[256,896]{1,0:T(8,128)(2,1)S(1)}, u32[]{:S(2)}, u32[]{:S(2)}) collective-permute-start(bf16[256,896]{1,0:T(8,128)(2,1)S(1)} %get-tuple-element.29), channel_id=1, source_target_pairs={{0,2},{1,3},{2,0},{3,1},{4,6},{5,7},{6,4},{7,5},{8,10},{9,11},{10,... | collective-permute-start | bytes 1376264 | tf_op jit(solution)/shard_map/ppermute | solution.py:193
  102.2 1.9 collective-permute-start.14
  106.3 4.7 %collective-permute-start.10 = (bf16[2,112,512]{2,1,0:T(8,128)(2,1)S(1)}, bf16[2,112,512]{2,1,0:T(8,128)(2,1)S(1)}, u32[]{:S(2)}, u32[]{:S(2)}) collective-permute-start(bf16[2,112,512]{2,1,0:T(8,128)(2,1)S(1)} %get-tuple-element.25), channel_id=1, source_target_pairs={{0,128},{64,192},{128,0},{192,64},{256,384},{320,448},{384,256},{4... | collective-permute-start | bytes 688136 | tf_op jit(solution)/shard_map/ppermute | solution.py:193
  111.0 2.8 %collective-permute-start.11 = (bf16[2,112,512]{2,1,0:T(8,128)(2,1)S(1)}, bf16[2,112,512]{2,1,0:T(8,128)(2,1)S(1)}, u32[]{:S(2)}, u32[]{:S(2)}) collective-permute-start(bf16[2,112,512]{2,1,0:T(8,128)(2,1)S(1)} %get-tuple-element.26), channel_id=1, source_target_pairs={{0,192},{64,0},{128,64},{192,128},{256,448},{320,256},{384,320},{4... | collective-permute-start | bytes 688136 | tf_op jit(solution)/shard_map/ppermute | solution.py:193
  113.8 2.5 %collective-permute-start.9 = (bf16[2,112,512]{2,1,0:T(8,128)(2,1)S(1)}, bf16[2,112,512]{2,1,0:T(8,128)(2,1)S(1)}, u32[]{:S(2)}, u32[]{:S(2)}) collective-permute-start(bf16[2,112,512]{2,1,0:T(8,128)(2,1)S(1)} %get-tuple-element.24), channel_id=1, source_target_pairs={{0,64},{64,128},{128,192},{192,0},{256,320},{320,384},{384,448},{4... | collective-permute-start | bytes 688136 | tf_op jit(solution)/shard_map/ppermute | solution.py:193
  116.3 24.0 %collective-permute-done.13.refs_5_ = bf16[256,896]{1,0:T(8,128)(2,1)S(1)} collective-permute-done((bf16[256,896]{1,0:T(8,128)(2,1)S(1)}, bf16[256,896]{1,0:T(8,128)(2,1)S(1)}, u32[]{:S(2)}, u32[]{:S(2)}) %collective-permute-start.13) | collective-permute-done | bytes 458784 | tf_op jit(solution)/shard_map/ppermute | solution.py:193
  141.9 10.2 %collective-permute-start.15 = (bf16[112,512]{1,0:T(8,128)(2,1)S(1)}, bf16[112,512]{1,0:T(8,128)(2,1)S(1)}, u32[]{:S(2)}, u32[]{:S(2)}) collective-permute-start(bf16[112,512]{1,0:T(8,128)(2,1)S(1)} %get-tuple-element.33), channel_id=1, source_target_pairs={{0,256},{64,320},{128,384},{192,448},{256,0},{320,64},{384,128},{4... | collective-permute-start | bytes 344072 | tf_op jit(solution)/shard_map/ppermute | solution.py:193
  152.2 2.5 %collective-permute-done.15 = bf16[112,512]{1,0:T(8,128)(2,1)S(1)} collective-permute-done((bf16[112,512]{1,0:T(8,128)(2,1)S(1)}, bf16[112,512]{1,0:T(8,128)(2,1)S(1)}, u32[]{:S(2)}, u32[]{:S(2)}) %collective-permute-start.15) | collective-permute-done | bytes 114720 | tf_op jit(solution)/shard_map/ppermute | solution.py:193
  154.8 3.8 %collective-permute-start.16 = (bf16[112,512]{1,0:T(8,128)(2,1)S(1)}, bf16[112,512]{1,0:T(8,128)(2,1)S(1)}, u32[]{:S(2)}, u32[]{:S(2)}) collective-permute-start(bf16[112,512]{1,0:T(8,128)(2,1)S(1)} %add_convert_fusion.1), channel_id=1, source_target_pairs={{0,8},{4,12},{8,0},{12,4},{16,24},{20,28},{24,16},{28,20},{32,40},... | collective-permute-start | bytes 344072 | tf_op jit(solution)/shard_map/ppermute | solution.py:193
  158.7 5.7 %collective-permute-start.7 = (bf16[64,1024]{1,0:T(8,128)(2,1)S(1)}, bf16[64,1024]{1,0:T(8,128)(2,1)S(1)}, u32[]{:S(2)}, u32[]{:S(2)}) collective-permute-start(bf16[64,1024]{1,0:T(8,128)(2,1)S(1)} %pad_maximum_fusion.3), channel_id=1, source_target_pairs={{0,4},{4,8},{8,12},{12,16},{16,20},{20,24},{24,28},{28,32},{32,36}... | collective-permute-start | bytes 393224 | tf_op jit(solution)/shard_map/ppermute | solution.py:193
  164.3 7.3 %all-to-all-start.2 = ((bf16[16,16,896]{2,1,0:T(8,128)(2,1)}), bf16[16,16,896]{2,1,0:T(8,128)(2,1)S(1)}, u32[]{:S(2)}, u32[]{:S(2)}) async-start(bf16[16,16,896]{2,1,0:T(8,128)(2,1)} %bitcast.12), calls=%async_computation.2 | async-start | bytes 917504 | tf_op jit(solution)/shard_map/all_to_all | solution.py:197
  171.7 4.2 %collective-permute-start.17 = (bf16[112,512]{1,0:T(8,128)(2,1)S(1)}, bf16[112,512]{1,0:T(8,128)(2,1)S(1)}, u32[]{:S(2)}, u32[]{:S(2)}) collective-permute-start(bf16[112,512]{1,0:T(8,128)(2,1)S(1)} %add_convert_fusion), channel_id=1, source_target_pairs={{0,16},{4,20},{8,24},{12,28},{16,0},{20,4},{24,8},{28,12},{32,48},... | collective-permute-start | bytes 344072 | tf_op jit(solution)/shard_map/ppermute | solution.py:193
  175.9 5.2 %collective-permute-start.18 = (bf16[112,512]{1,0:T(8,128)(2,1)S(1)}, bf16[112,512]{1,0:T(8,128)(2,1)S(1)}, u32[]{:S(2)}, u32[]{:S(2)}) collective-permute-start(bf16[112,512]{1,0:T(8,128)(2,1)S(1)} %add_convert_fusion), channel_id=1, source_target_pairs={{0,32},{4,36},{8,40},{12,44},{16,48},{20,52},{24,56},{28,60},{32,0... | collective-permute-start | bytes 344072 | tf_op jit(solution)/shard_map/ppermute | solution.py:193
  181.1 2.0 collective-permute-start.19
  183.2 11.3 %collective-permute-done.17 = bf16[112,512]{1,0:T(8,128)(2,1)S(1)} collective-permute-done((bf16[112,512]{1,0:T(8,128)(2,1)S(1)}, bf16[112,512]{1,0:T(8,128)(2,1)S(1)}, u32[]{:S(2)}, u32[]{:S(2)}) %collective-permute-start.17) | collective-permute-done | bytes 114720 | tf_op jit(solution)/shard_map/ppermute | solution.py:193
  195.9 4.5 %collective-permute-start.20 = (f32[112,512]{1,0:T(8,128)S(1)}, f32[112,512]{1,0:T(8,128)S(1)}, u32[]{:S(2)}, u32[]{:S(2)}) collective-permute-start(f32[112,512]{1,0:T(8,128)S(1)} %add_add_fusion), channel_id=1, source_target_pairs={{0,4},{4,0},{8,12},{12,8},{16,20},{20,16},{24,28},{28,24},{32,36},... | collective-permute-start | bytes 688136 | tf_op jit(solution)/shard_map/ppermute | solution.py:193
  (52 shorter events, 13.1 us)
Async XLA Ops:
  0.6 39.5 %copy-start.1 = (bf16[1,256,512]{2,1,0:T(8,128)(2,1)S(1)}, bf16[1,256,512]{2,1,0:T(8,128)(2,1)}, u32[]{:S(2)}) copy-start(bf16[1,256,512]{2,1,0:T(8,128)(2,1)} %param.5) | copy-start | bytes 786436
  0.6 39.5 %copy-start.2 = (bf16[1,256,512]{2,1,0:T(8,128)(2,1)S(1)}, bf16[1,256,512]{2,1,0:T(8,128)(2,1)}, u32[]{:S(2)}) copy-start(bf16[1,256,512]{2,1,0:T(8,128)(2,1)} %param.6) | copy-start | bytes 786436
  2.4 39.8 %copy-start.4 = (s32[1,4,4]{2,1,0:T(4,128)S(1)}, s32[1,4,4]{2,1,0:T(4,128)}, u32[]{:S(2)}) copy-start(s32[1,4,4]{2,1,0:T(4,128)} %param.9) | copy-start | bytes 196
  2.4 30.2 %all-to-all-start = ((bf16[16,16,640]{2,1,0:T(8,128)(2,1)}), bf16[16,16,640]{2,1,0:T(8,128)(2,1)S(1)}, u32[]{:S(2)}, u32[]{:S(2)}) async-start(bf16[16,16,640]{2,1,0:T(8,128)(2,1)} %slice.50), calls=%async_computation | async-start | bytes 655360 | tf_op jit(solution)/shard_map/all_to_all | solution.py:197
  13.7 10.4 %collective-permute-start.4 = (bf16[16,16,256]{2,1,0:T(8,128)(2,1)S(1)}, bf16[16,16,256]{2,1,0:T(8,128)(2,1)S(1)}, u32[]{:S(2)}, u32[]{:S(2)}) collective-permute-start(bf16[16,16,256]{2,1,0:T(8,128)(2,1)S(1)} %slice.51), channel_id=1, source_target_pairs={{0,1},{1,2},{2,3},{3,0},{4,5},{5,6},{6,7},{7,4},{8,9},{9,10},{10,1... | collective-permute-start | bytes 393224 | tf_op jit(solution)/shard_map/ppermute | solution.py:193
  16.1 13.2 %collective-permute-start.5 = (bf16[16,16,256]{2,1,0:T(8,128)(2,1)S(1)}, bf16[16,16,256]{2,1,0:T(8,128)(2,1)S(1)}, u32[]{:S(2)}, u32[]{:S(2)}) collective-permute-start(bf16[16,16,256]{2,1,0:T(8,128)(2,1)S(1)} %slice.51), channel_id=1, source_target_pairs={{0,2},{1,3},{2,0},{3,1},{4,6},{5,7},{6,4},{7,5},{8,10},{9,11},{10,... | collective-permute-start | bytes 393224 | tf_op jit(solution)/shard_map/ppermute | solution.py:193
  21.9 9.8 %collective-permute-start.6 = (bf16[16,16,256]{2,1,0:T(8,128)(2,1)S(1)}, bf16[16,16,256]{2,1,0:T(8,128)(2,1)S(1)}, u32[]{:S(2)}, u32[]{:S(2)}) collective-permute-start(bf16[16,16,256]{2,1,0:T(8,128)(2,1)S(1)} %slice.51), channel_id=1, source_target_pairs={{0,3},{1,0},{2,1},{3,2},{4,7},{5,4},{6,5},{7,6},{8,11},{9,8},{10,9... | collective-permute-start | bytes 393224 | tf_op jit(solution)/shard_map/ppermute | solution.py:193
  32.6 37.0 %all-to-all-start.1 = ((bf16[16,64,256]{2,1,0:T(8,128)(2,1)}), bf16[16,64,256]{2,1,0:T(8,128)(2,1)S(1)}, u32[]{:S(2)}, u32[]{:S(2)}) async-start(bf16[16,64,256]{2,1,0:T(8,128)(2,1)} %pad_maximum_fusion), calls=%async_computation.1 | async-start | bytes 1048576 | tf_op jit(solution)/shard_map/all_to_all | solution.py:197
  40.2 15.5 %collective-permute-start = (bf16[64,1024]{1,0:T(8,128)(2,1)S(1)}, bf16[64,1024]{1,0:T(8,128)(2,1)S(1)}, u32[]{:S(2)}, u32[]{:S(2)}) collective-permute-start(bf16[64,1024]{1,0:T(8,128)(2,1)S(1)} %pad_maximum_fusion.2), channel_id=1, source_target_pairs={{4,0},{8,4},{12,8},{16,12},{20,16},{24,20},{28,24},{32,28},{36,32}... | collective-permute-start | bytes 393224 | tf_op jit(solution)/shard_map/ppermute | solution.py:193
  42.3 13.5 %collective-permute-start.1 = (bf16[256,640]{1,0:T(8,128)(2,1)S(1)}, bf16[256,640]{1,0:T(8,128)(2,1)S(1)}, u32[]{:S(2)}, u32[]{:S(2)}) collective-permute-start(bf16[256,640]{1,0:T(8,128)(2,1)S(1)} %bitcast.22), channel_id=1, source_target_pairs={{0,1},{1,2},{2,3},{3,0},{4,5},{5,6},{6,7},{7,4},{8,9},{9,10},{10,1... | collective-permute-start | bytes 983048 | tf_op jit(solution)/shard_map/ppermute | solution.py:193
  44.7 24.9 %collective-permute-start.2 = (bf16[256,640]{1,0:T(8,128)(2,1)S(1)}, bf16[256,640]{1,0:T(8,128)(2,1)S(1)}, u32[]{:S(2)}, u32[]{:S(2)}) collective-permute-start(bf16[256,640]{1,0:T(8,128)(2,1)S(1)} %bitcast.23), channel_id=1, source_target_pairs={{0,2},{1,3},{2,0},{3,1},{4,6},{5,7},{6,4},{7,5},{8,10},{9,11},{10,... | collective-permute-start | bytes 983048 | tf_op jit(solution)/shard_map/ppermute | solution.py:193
  48.1 21.6 %collective-permute-start.3 = (bf16[256,640]{1,0:T(8,128)(2,1)S(1)}, bf16[256,640]{1,0:T(8,128)(2,1)S(1)}, u32[]{:S(2)}, u32[]{:S(2)}) collective-permute-start(bf16[256,640]{1,0:T(8,128)(2,1)S(1)} %bitcast.24), channel_id=1, source_target_pairs={{0,3},{1,0},{2,1},{3,2},{4,7},{5,4},{6,5},{7,6},{8,11},{9,8},{10,9... | collective-permute-start | bytes 983048 | tf_op jit(solution)/shard_map/ppermute | solution.py:193
  69.6 0.8 copy-start.3
  87.5 16.6 %collective-permute-start.8 = (bf16[896,512]{1,0:T(8,128)(2,1)}, bf16[896,512]{1,0:T(8,128)(2,1)S(1)}, u32[]{:S(2)}, u32[]{:S(2)}) collective-permute-start(bf16[896,512]{1,0:T(8,128)(2,1)} %get-tuple-element.22), channel_id=1, source_target_pairs={{0,4},{4,0},{8,12},{12,8},{16,20},{20,16},{24,28},{28,24},{32,36},... | collective-permute-start | bytes 2752520 | tf_op jit(solution)/shard_map/ppermute | solution.py:193
  89.9 23.9 %collective-permute-start.12 = (bf16[256,896]{1,0:T(8,128)(2,1)S(1)}, bf16[256,896]{1,0:T(8,128)(2,1)S(1)}, u32[]{:S(2)}, u32[]{:S(2)}) collective-permute-start(bf16[256,896]{1,0:T(8,128)(2,1)S(1)} %get-tuple-element.28), channel_id=1, source_target_pairs={{0,3},{1,0},{2,1},{3,2},{4,7},{5,4},{6,5},{7,6},{8,11},{9,8},{10,9... | collective-permute-start | bytes 1376264 | tf_op jit(solution)/shard_map/ppermute | solution.py:193
  97.5 42.9 %collective-permute-start.13 = (bf16[256,896]{1,0:T(8,128)(2,1)S(1)}, bf16[256,896]{1,0:T(8,128)(2,1)S(1)}, u32[]{:S(2)}, u32[]{:S(2)}) collective-permute-start(bf16[256,896]{1,0:T(8,128)(2,1)S(1)} %get-tuple-element.29), channel_id=1, source_target_pairs={{0,2},{1,3},{2,0},{3,1},{4,6},{5,7},{6,4},{7,5},{8,10},{9,11},{10,... | collective-permute-start | bytes 1376264 | tf_op jit(solution)/shard_map/ppermute | solution.py:193
  102.2 38.2 %collective-permute-start.14 = (bf16[256,896]{1,0:T(8,128)(2,1)}, bf16[256,896]{1,0:T(8,128)(2,1)S(1)}, u32[]{:S(2)}, u32[]{:S(2)}) collective-permute-start(bf16[256,896]{1,0:T(8,128)(2,1)} %get-tuple-element.30), channel_id=1, source_target_pairs={{0,1},{1,2},{2,3},{3,0},{4,5},{5,6},{6,7},{7,4},{8,9},{9,10},{10,1... | collective-permute-start | bytes 1376264 | tf_op jit(solution)/shard_map/ppermute | solution.py:193
  104.1 1.5 copy-start
  106.3 34.0 %collective-permute-start.10 = (bf16[2,112,512]{2,1,0:T(8,128)(2,1)S(1)}, bf16[2,112,512]{2,1,0:T(8,128)(2,1)S(1)}, u32[]{:S(2)}, u32[]{:S(2)}) collective-permute-start(bf16[2,112,512]{2,1,0:T(8,128)(2,1)S(1)} %get-tuple-element.25), channel_id=1, source_target_pairs={{0,128},{64,192},{128,0},{192,64},{256,384},{320,448},{384,256},{4... | collective-permute-start | bytes 688136 | tf_op jit(solution)/shard_map/ppermute | solution.py:193
  111.0 29.4 %collective-permute-start.11 = (bf16[2,112,512]{2,1,0:T(8,128)(2,1)S(1)}, bf16[2,112,512]{2,1,0:T(8,128)(2,1)S(1)}, u32[]{:S(2)}, u32[]{:S(2)}) collective-permute-start(bf16[2,112,512]{2,1,0:T(8,128)(2,1)S(1)} %get-tuple-element.26), channel_id=1, source_target_pairs={{0,192},{64,0},{128,64},{192,128},{256,448},{320,256},{384,320},{4... | collective-permute-start | bytes 688136 | tf_op jit(solution)/shard_map/ppermute | solution.py:193
  113.8 26.6 %collective-permute-start.9 = (bf16[2,112,512]{2,1,0:T(8,128)(2,1)S(1)}, bf16[2,112,512]{2,1,0:T(8,128)(2,1)S(1)}, u32[]{:S(2)}, u32[]{:S(2)}) collective-permute-start(bf16[2,112,512]{2,1,0:T(8,128)(2,1)S(1)} %get-tuple-element.24), channel_id=1, source_target_pairs={{0,64},{64,128},{128,192},{192,0},{256,320},{320,384},{384,448},{4... | collective-permute-start | bytes 688136 | tf_op jit(solution)/shard_map/ppermute | solution.py:193
  141.9 12.9 %collective-permute-start.15 = (bf16[112,512]{1,0:T(8,128)(2,1)S(1)}, bf16[112,512]{1,0:T(8,128)(2,1)S(1)}, u32[]{:S(2)}, u32[]{:S(2)}) collective-permute-start(bf16[112,512]{1,0:T(8,128)(2,1)S(1)} %get-tuple-element.33), channel_id=1, source_target_pairs={{0,256},{64,320},{128,384},{192,448},{256,0},{320,64},{384,128},{4... | collective-permute-start | bytes 344072 | tf_op jit(solution)/shard_map/ppermute | solution.py:193
  154.8 16.9 %collective-permute-start.16 = (bf16[112,512]{1,0:T(8,128)(2,1)S(1)}, bf16[112,512]{1,0:T(8,128)(2,1)S(1)}, u32[]{:S(2)}, u32[]{:S(2)}) collective-permute-start(bf16[112,512]{1,0:T(8,128)(2,1)S(1)} %add_convert_fusion.1), channel_id=1, source_target_pairs={{0,8},{4,12},{8,0},{12,4},{16,24},{20,28},{24,16},{28,20},{32,40},... | collective-permute-start | bytes 344072 | tf_op jit(solution)/shard_map/ppermute | solution.py:193
  158.7 24.5 %collective-permute-start.7 = (bf16[64,1024]{1,0:T(8,128)(2,1)S(1)}, bf16[64,1024]{1,0:T(8,128)(2,1)S(1)}, u32[]{:S(2)}, u32[]{:S(2)}) collective-permute-start(bf16[64,1024]{1,0:T(8,128)(2,1)S(1)} %pad_maximum_fusion.3), channel_id=1, source_target_pairs={{0,4},{4,8},{8,12},{12,16},{16,20},{20,24},{24,28},{28,32},{32,36}... | collective-permute-start | bytes 393224 | tf_op jit(solution)/shard_map/ppermute | solution.py:193
  164.3 38.4 %all-to-all-start.2 = ((bf16[16,16,896]{2,1,0:T(8,128)(2,1)}), bf16[16,16,896]{2,1,0:T(8,128)(2,1)S(1)}, u32[]{:S(2)}, u32[]{:S(2)}) async-start(bf16[16,16,896]{2,1,0:T(8,128)(2,1)} %bitcast.12), calls=%async_computation.2 | async-start | bytes 917504 | tf_op jit(solution)/shard_map/all_to_all | solution.py:197
  171.7 22.9 %collective-permute-start.17 = (bf16[112,512]{1,0:T(8,128)(2,1)S(1)}, bf16[112,512]{1,0:T(8,128)(2,1)S(1)}, u32[]{:S(2)}, u32[]{:S(2)}) collective-permute-start(bf16[112,512]{1,0:T(8,128)(2,1)S(1)} %add_convert_fusion), channel_id=1, source_target_pairs={{0,16},{4,20},{8,24},{12,28},{16,0},{20,4},{24,8},{28,12},{32,48},... | collective-permute-start | bytes 344072 | tf_op jit(solution)/shard_map/ppermute | solution.py:193
  175.9 20.0 %collective-permute-start.18 = (bf16[112,512]{1,0:T(8,128)(2,1)S(1)}, bf16[112,512]{1,0:T(8,128)(2,1)S(1)}, u32[]{:S(2)}, u32[]{:S(2)}) collective-permute-start(bf16[112,512]{1,0:T(8,128)(2,1)S(1)} %add_convert_fusion), channel_id=1, source_target_pairs={{0,32},{4,36},{8,40},{12,44},{16,48},{20,52},{24,56},{28,60},{32,0... | collective-permute-start | bytes 344072 | tf_op jit(solution)/shard_map/ppermute | solution.py:193
  181.1 14.8 %collective-permute-start.19 = (bf16[112,512]{1,0:T(8,128)(2,1)S(1)}, bf16[112,512]{1,0:T(8,128)(2,1)S(1)}, u32[]{:S(2)}, u32[]{:S(2)}) collective-permute-start(bf16[112,512]{1,0:T(8,128)(2,1)S(1)} %add_convert_fusion), channel_id=1, source_target_pairs={{0,48},{4,52},{8,56},{12,60},{16,32},{20,36},{24,40},{28,44},{32,1... | collective-permute-start | bytes 344072 | tf_op jit(solution)/shard_map/ppermute | solution.py:193
  195.9 5.9 %collective-permute-start.20 = (f32[112,512]{1,0:T(8,128)S(1)}, f32[112,512]{1,0:T(8,128)S(1)}, u32[]{:S(2)}, u32[]{:S(2)}) collective-permute-start(f32[112,512]{1,0:T(8,128)S(1)} %add_add_fusion), channel_id=1, source_target_pairs={{0,4},{4,0},{8,12},{12,8},{16,20},{20,16},{24,28},{28,24},{32,36},... | collective-permute-start | bytes 688136 | tf_op jit(solution)/shard_map/ppermute | solution.py:193

commit v4 on v3

v4 whole, which is shorter than its diff:
```python
import math

import jax
import jax.numpy as jnp
from jax import lax
from jax.experimental import pallas as pl
from jax.experimental.pallas import tpu as pltpu
from jax.sharding import PartitionSpec as P

HEAD_DIM = 128
SPAN = 64
PART = 64
LEAD = SPAN - 1
SCALE = 1.0 / math.sqrt(HEAD_DIM)
NT = (((1,), (1,)), ((), ()))
TN = (((0,), (0,)), ((), ()))
NN = (((1,), (0,)), ((), ()))
VMEM = pl.BlockSpec(memory_space=pltpu.VMEM)
SMEM = pl.BlockSpec(memory_space=pltpu.SMEM)
PARAMS = pltpu.CompilerParams(vmem_limit_bytes=50 * 1024 * 1024)


def dot(a, b, dims):
    return lax.dot_general(a, b, dims, preferred_element_type=jnp.float32)


def span_rows(own, ahead):
    own, ahead = own.astype(jnp.float32), ahead.astype(jnp.float32)
    row = lax.broadcasted_iota(jnp.int32, ahead.shape, 0)
    mixed = jnp.concatenate((jnp.where(row < LEAD, ahead, own[:SPAN]), own[SPAN:]), axis=0)
    return pltpu.roll(mixed, own.shape[0] - LEAD, 0).astype(jnp.bfloat16)


def block_body(
    units_ref, place_ref, q_ref, g_ref, ahead_ref, w_ref, x_ref, att_ref, dq_ref, partial_ref, sent_ref, kept_ref,
    key, value, grad, q_rows, g_rows, att, dq,
):
    tokens, width = q_ref.shape
    all_rows, enc_width = x_ref.shape
    heads = width // HEAD_DIM
    chunk = 4 * PART
    for c in range(all_rows // chunk):
        rows = pl.ds(c * chunk, chunk)
        for kind, out in enumerate((key, value)):
            out[rows, :] = dot(x_ref[rows, :], w_ref[kind], NN).astype(jnp.bfloat16)
    for h in range(heads):
        cols = pl.ds(h * HEAD_DIM, HEAD_DIM)
        q_rows[:, cols] = span_rows(q_ref[:, cols], ahead_ref[:, cols])
        g_rows[:, cols] = span_rows(g_ref[:, cols], ahead_ref[:, pl.ds(width + h * HEAD_DIM, HEAD_DIM)])
    for j in range(tokens // SPAN):
        starts = [pl.multiple_of(units_ref[j * 4 + r] * PART, PART) for r in range(4)]
        rows = pl.ds(j * SPAN, SPAN)
        for h in range(heads):
            cols = pl.ds(h * HEAD_DIM, HEAD_DIM)
            q = q_rows[rows, cols]
            g = g_rows[rows, cols]
            k = jnp.concatenate([key[pl.ds(s, PART), cols] for s in starts], axis=0)
            v = jnp.concatenate([value[pl.ds(s, PART), cols] for s in starts], axis=0)
            scores = dot(q, k, NT) * SCALE
            raised = jnp.exp(scores - jnp.max(scores, axis=-1, keepdims=True))
            weights = raised / jnp.sum(raised, axis=-1, keepdims=True)
            low = weights.astype(jnp.bfloat16)
            d_weights = dot(g, v, NT)
            inner = jnp.sum(weights * d_weights, axis=-1, keepdims=True)
            d_scores = (weights * (d_weights - inner) * SCALE).astype(jnp.bfloat16)
            att[rows, cols] = dot(low, v, NN)
            dq[rows, cols] = dot(d_scores, k, NN)
            dk = dot(d_scores, q, TN).astype(jnp.bfloat16)
            dv = dot(low, g, TN).astype(jnp.bfloat16)
            for r, s in enumerate(starts):
                grad[0, pl.ds(s, PART), cols] = dk[r * PART : (r + 1) * PART]
                grad[1, pl.ds(s, PART), cols] = dv[r * PART : (r + 1) * PART]
    for h in range(heads):
        cols = pl.ds(h * HEAD_DIM, HEAD_DIM)
        att_ref[:, cols] = pltpu.roll(att[:, cols], LEAD, 0).astype(jnp.bfloat16)
        dq_ref[:, cols] = pltpu.roll(dq[:, cols], LEAD, 0).astype(jnp.bfloat16)
    for c in range(all_rows // chunk):
        rows = pl.ds(c * chunk, chunk)
        term = dot(grad[0, rows, :], w_ref[0], NT) + dot(grad[1, rows, :], w_ref[1], NT)
        partial_ref[rows, :] = term.astype(jnp.bfloat16)
    core = place_ref[0]
    for e in range(0, enc_width, 128):
        x = x_ref[:, e : e + 128].T
        sent_ref[e : e + 128, :] = dot(x, grad[1 - core], NN).astype(jnp.bfloat16)
        kept_ref[e : e + 128, :] = dot(x, grad[core], NN)


def block(units_of, place, q, g, ahead, w, x):
    tokens, width = q.shape
    all_rows, enc_width = x.shape

    def low(*shape):
        return jax.ShapeDtypeStruct(shape, jnp.bfloat16)

    return pl.pallas_call(
        block_body,
        out_shape=[
            low(tokens, width),
            low(tokens, width),
            low(all_rows, enc_width),
            low(enc_width, width),
            jax.ShapeDtypeStruct((enc_width, width), jnp.float32),
        ],
        in_specs=[SMEM] * 2 + [VMEM] * 5,
        out_specs=[VMEM] * 5,
        scratch_shapes=[
            pltpu.VMEM((all_rows, width), jnp.bfloat16),
            pltpu.VMEM((all_rows, width), jnp.bfloat16),
            pltpu.VMEM((2, all_rows, width), jnp.bfloat16),
            pltpu.VMEM((tokens, width), jnp.bfloat16),
            pltpu.VMEM((tokens, width), jnp.bfloat16),
            pltpu.VMEM((tokens, width), jnp.float32),
            pltpu.VMEM((tokens, width), jnp.float32),
        ],
        compiler_params=PARAMS,
        name="block",
    )(units_of, place, q, g, ahead, w, x)


def cut(place, kept, away, att, dq, behind):
    enc_width, width = kept.shape
    rows = enc_width // 8

    def body(place_ref, kept_ref, away_ref, att_ref, dq_ref, behind_ref, own_ref, *refs):
        send_refs, full_refs = refs[:3], refs[3:]
        x = place_ref[1]
        for high in range(2):
            for k in range(4):
                at = pl.multiple_of((high * 4 + lax.rem(x + k, 4)) * rows, 16)
                term = kept_ref[pl.ds(at, rows), :] + away_ref[pl.ds(at, rows), :].astype(jnp.float32)
                if k:
                    send_refs[k - 1][high] = term.astype(jnp.bfloat16)
                else:
                    own_ref[high] = term
        lead = lax.broadcasted_iota(jnp.int32, (SPAN, width), 0) < LEAD
        for n, (ref, full) in enumerate(zip((att_ref, dq_ref), full_refs)):
            came = behind_ref[:, n * width : (n + 1) * width].astype(jnp.float32)
            full[:SPAN, :] = jnp.where(lead, came, ref[:SPAN, :].astype(jnp.float32)).astype(jnp.bfloat16)
            full[SPAN:, :] = ref[SPAN:, :]

    return pl.pallas_call(
        body,
        out_shape=[jax.ShapeDtypeStruct((2, rows, width), jnp.float32)]
        + [jax.ShapeDtypeStruct((2, rows, width), jnp.bfloat16)] * 3
        + [jax.ShapeDtypeStruct(att.shape, jnp.bfloat16)] * 2,
        in_specs=[SMEM] + [VMEM] * 5,
        out_specs=[VMEM] * 6,
        compiler_params=PARAMS,
        name="cut",
    )(place, kept, away, att, dq, behind)


def permute(x, axis, to):
    n = lax.axis_size(axis)
    return lax.ppermute(x, axis, [(i, to(i)) for i in range(n) if 0 <= to(i) < n])


def exchange(x):
    outer, inner, *rest = x.shape
    x = lax.all_to_all(x.reshape(outer * inner, *rest), ("ctx", "nbr"), split_axis=0, concat_axis=0, tiled=True)
    return x.reshape(outer, inner, *rest)


def shards(queries, cotangent, encoded, kv_weight, neighbour_ids):
    q, g, enc = queries[0], cotangent[0], encoded[0]
    units, piece, enc_width = enc.shape
    groups = lax.axis_size("nbr")
    ctx = lax.axis_index("ctx")
    dp = lax.axis_index("dp")
    place = jnp.stack((ctx % 2, dp % 4, dp // 4)).astype(jnp.int32)

    copies = jnp.broadcast_to(enc[:, None], (units, groups, piece, enc_width))
    x = exchange(copies).reshape(units * PART, enc_width)

    head = jnp.concatenate((q[:SPAN], g[:SPAN]), axis=1)
    ahead = permute(head, "ctx", lambda i: i - 1)

    unit_of = (neighbour_ids[0] // units).reshape(-1)
    att, dq, partial, sent, kept = block(unit_of, place, q, g, ahead, kv_weight, x)

    terms = exchange(partial.reshape(units, groups, piece, enc_width))
    encoded_grad = jnp.sum(terms.astype(jnp.float32), axis=1).astype(jnp.bfloat16)

    away = permute(sent, "ctx", lambda i: i ^ 1)
    tail = jnp.concatenate((att[:SPAN], dq[:SPAN]), axis=1)
    behind = permute(tail, "ctx", lambda i: i + 1)
    held, *sends, attended, query_grad = cut(place, kept, away, att, dq, behind)
    for k in (1, 3, 2):
        held = add(held, permute(sends[k - 1], "dp", lambda i, k=k: i // 4 * 4 + (i + k) % 4))
    high = dp // 4
    other = lax.dynamic_index_in_dim(held, 1 - high, 0, keepdims=False).astype(jnp.bfloat16)
    mine = lax.dynamic_index_in_dim(held, high, 0, keepdims=False)
    low = add(mine, permute(other, "dp", lambda i: (i + 4) % 8)).astype(jnp.bfloat16)
    low = add(low, permute(low, "ctx", lambda i: i ^ 2)).astype(jnp.bfloat16)
    by = [permute(low, "ctx", lambda i, b=b: i ^ b) for b in (4, 8, 12)]
    mine = add(low, by[0]) + add(by[1], by[2])
    theirs = permute(mine, "ctx", lambda i: i ^ 1)
    keys_here = ctx % 2 == 0
    weight_grad = jnp.stack((jnp.where(keys_here, mine, theirs), jnp.where(keys_here, theirs, mine)), axis=0)
    return (attended[None], query_grad[None], encoded_grad[None], weight_grad)


def add(a, b):
    return a.astype(jnp.float32) + b.astype(jnp.float32)


def solution(mesh):
    return jax.shard_map(
        shards,
        mesh=mesh,
        in_specs=(
            P("dp", "ctx", "nbr"),
            P("dp", "ctx", "nbr"),
            P("dp", "ctx", "nbr", None),
            P(None, None, "nbr"),
            P("dp", "ctx", None),
        ),
        out_specs=(
            P("dp", "ctx", "nbr"),
            P("dp", "ctx", "nbr"),
            P("dp", "ctx", "nbr", None),
            P(None, "dp", "nbr"),
        ),
        check_vma=False,
    )
```

time: 205 us -> 199 us (0.971)
  starting transfers between devices: 109 us -> 72.7 us
  waiting for transfers between devices: 65.1 us -> 95.9 us
  local copies, waits for them, and re-layouts: 5.92 us -> 3.82 us
    ppermute x21 -> x12, starting transfers between devices: 83.5 us -> 51 us  [permute(): lax.ppermute(x, axis, [(i, to(i)) for i in range(n) if 0 <= to(i) < n])]
    ppermute x21 -> x12, waiting for transfers between devices: 65.1 us -> 93.7 us  [permute(): lax.ppermute(x, axis, [(i, to(i)) for i in range(n) if 0 <= to(i) < n])]
    all_to_all x3 -> x2, starting transfers between devices: 25.2 us -> 21.7 us  [exchange(): lax.all_to_all(x.reshape(outer * inner, *rest), ('ctx', 'nbr'), split_axi...]
    slice x4 -> x0, local copies, waits for them, and re-layouts: 2.72 us -> none  [the longest x1 1.78 us: shards(): xa = gathered(exchange(enc[:, :, :first]).reshape(units * piece, first))]
    reduce_sum x0 -> x1, other arithmetic: none -> 2.66 us  [shards(): jnp.sum(terms.astype(jnp.float32), axis=1).astype(jnp.bfloat16)]
    broadcast_in_dim x0 -> x1, local copies, waits for them, and re-layouts: none -> 2.42 us  [shards(): copies = jnp.broadcast_to(enc[:, None], (units, groups, piece, enc_width))]
    all_to_all x3 -> x2, waiting for transfers between devices: 0.01 us -> 2.22 us  [exchange(): lax.all_to_all(x.reshape(outer * inner, *rest), ('ctx', 'nbr'), split_axi...]
    pallas_call x2 -> x1, Pallas kernels: 18.7 us -> 17.8 us  [block(): pl.pallas_call(block_body, out_shape=[low(tokens, width), low(tokens, wid...]
  transfers between devices with their start and end apart: 24 -> 14, of which waited for: 9 -> 8; matrix products, arithmetic and copies ran while one was open for 2% -> 1% of each run, Pallas kernels for 0% -> 1%
where the time goes in v4:
time: 199 us; the launch traced here: 197 us
  waiting for transfers between devices  95.9 us (48%)
  starting transfers between devices  72.7 us (37%)
  Pallas kernels  20.3 us (10%)
  other arithmetic  3.83 us (2%)
  local copies, waits for them, and re-layouts  3.82 us (2%)
    ppermute x12, waiting for transfers between devices, permute(): lax.ppermute(x, axis, [(i, to(i)) for i in range(n) if 0 <= to(i) < n])  93.7 us
    ppermute x12, starting transfers between devices, permute(): lax.ppermute(x, axis, [(i, to(i)) for i in range(n) if 0 <= to(i) < n])  51 us
    all_to_all x2, starting transfers between devices, exchange(): lax.all_to_all(x.reshape(outer * inner, *rest), ('ctx', 'nbr'), split_axi...  21.7 us
    pallas_call x1, Pallas kernels, block(): pl.pallas_call(block_body, out_shape=[low(tokens, width), low(tokens, wid...  17.8 us
  transfers between devices with their start and end apart: 14, of which 8 were waited for; matrix products, arithmetic and copies ran while one was open for 1% of the time, Pallas kernels for 1%

profile of v4, /device:TPU:1, one launch (start us, length us, event | category | flops | bytes accessed | tf_op | source)
XLA Modules:
  0.0 197.4 jit_solution(7837395004139613290)
XLA Ops:
  0.6 2.4 %broadcast_in_dim.17 = bf16[16,4,16,896]{3,2,1,0:T(8,128)(2,1)} broadcast(bf16[16,16,896]{2,1,0:T(8,128)(2,1)} %bitcast.32), dimensions={0,2,3} | broadcast | bytes 2293760 | tf_op jit(solution)/shard_map/broadcast_in_dim | solution.py:172
  3.1 14.7 %all-to-all-start = ((bf16[64,16,896]{2,1,0:T(8,128)(2,1)}), bf16[64,16,896]{2,1,0:T(8,128)(2,1)S(1)}, u32[]{:S(2)}, u32[]{:S(2)}) async-start(bf16[64,16,896]{2,1,0:T(8,128)(2,1)} %bitcast.31), calls=%async_computation | async-start | bytes 3670016 | tf_op jit(solution)/shard_map/all_to_all | solution.py:160
  17.8 2.4 %collective-permute-start = (bf16[64,1024]{1,0:T(8,128)(2,1)S(1)}, bf16[64,1024]{1,0:T(8,128)(2,1)S(1)}, u32[]{:S(2)}, u32[]{:S(2)}) collective-permute-start(bf16[64,1024]{1,0:T(8,128)(2,1)S(1)} %pad_maximum_fusion.1), channel_id=1, source_target_pairs={{4,0},{8,4},{12,8},{16,12},{20,16},{24,20},{28,24},{32,28},{36,32}... | collective-permute-start | bytes 393224 | tf_op jit(solution)/shard_map/ppermute | solution.py:155
  20.2 0.1 squeeze.14
  20.3 0.1 pad_add_fusion.place_ref
  20.4 40.6 %collective-permute-done.ahead_ref = bf16[64,1024]{1,0:T(8,128)(2,1)S(1)} collective-permute-done((bf16[64,1024]{1,0:T(8,128)(2,1)S(1)}, bf16[64,1024]{1,0:T(8,128)(2,1)S(1)}, u32[]{:S(2)}, u32[]{:S(2)}) %collective-permute-start) | collective-permute-done | bytes 131104 | tf_op jit(solution)/shard_map/ppermute | solution.py:155
  61.0 2.2 %all-to-all-done = bf16[64,16,896]{2,1,0:T(8,128)(2,1)S(1)} async-done(((bf16[64,16,896]{2,1,0:T(8,128)(2,1)}), bf16[64,16,896]{2,1,0:T(8,128)(2,1)S(1)}, u32[]{:S(2)}, u32[]{:S(2)}) %all-to-all-start) | async-done | bytes 1835040 | tf_op jit(solution)/shard_map/all_to_all | solution.py:160
  63.2 1.3 copy-done.2
  64.5 17.8 %block.1 = (bf16[256,512]{1,0:T(8,128)(2,1)S(1)}, bf16[256,512]{1,0:T(8,128)(2,1)S(1)}, bf16[1024,896]{1,0:T(8,128)(2,1)}, bf16[896,512]{1,0:T(8,128)(2,1)S(1)}, f32[896,512]{1,0:T(8,128)}) custom-call(s32[16]{0:T(128)S(1)} %and_select_fusion.units_ref, s32[3]{0:T(128)S(1)} %pad_add_fusion.place_ref, bf16[256,512]{1,0:T(8,128)(2,1)S(1)} %bitcast.28, ...), custom_call_target="tpu_custom_call" | custom-call | tf_op jit(solution)/shard_map/block/pallas_call | solution.py:95
  82.3 7.0 %all-to-all-start.1 = ((bf16[64,16,896]{2,1,0:T(8,128)(2,1)}), bf16[64,16,896]{2,1,0:T(8,128)(2,1)}, u32[]{:S(2)}, u32[]{:S(2)}) async-start(bf16[64,16,896]{2,1,0:T(8,128)(2,1)} %bitcast.12), calls=%async_computation.1 | async-start | bytes 3670016 | tf_op jit(solution)/shard_map/all_to_all | solution.py:160
  89.3 2.4 %collective-permute-start.1 = (bf16[896,512]{1,0:T(8,128)(2,1)S(1)}, bf16[896,512]{1,0:T(8,128)(2,1)S(1)}, u32[]{:S(2)}, u32[]{:S(2)}) collective-permute-start(bf16[896,512]{1,0:T(8,128)(2,1)S(1)} %get-tuple-element.16), channel_id=1, source_target_pairs={{0,4},{4,0},{8,12},{12,8},{16,20},{20,16},{24,28},{28,24},{32,36},... | collective-permute-start | bytes 2752520 | tf_op jit(solution)/shard_map/ppermute | solution.py:155
  91.7 3.2 %collective-permute-start.2 = (bf16[64,1024]{1,0:T(8,128)(2,1)S(1)}, bf16[64,1024]{1,0:T(8,128)(2,1)S(1)}, u32[]{:S(2)}, u32[]{:S(2)}) collective-permute-start(bf16[64,1024]{1,0:T(8,128)(2,1)S(1)} %pad_maximum_fusion.2), channel_id=1, source_target_pairs={{0,4},{4,8},{8,12},{12,16},{16,20},{20,24},{24,28},{28,32},{32,36}... | collective-permute-start | bytes 393224 | tf_op jit(solution)/shard_map/ppermute | solution.py:155
  94.9 34.6 %collective-permute-done.2.behind_ref = bf16[64,1024]{1,0:T(8,128)(2,1)S(1)} collective-permute-done((bf16[64,1024]{1,0:T(8,128)(2,1)S(1)}, bf16[64,1024]{1,0:T(8,128)(2,1)S(1)}, u32[]{:S(2)}, u32[]{:S(2)}) %collective-permute-start.2) | collective-permute-done | bytes 131104 | tf_op jit(solution)/shard_map/ppermute | solution.py:155
  129.5 2.5 %cut.1 = (f32[2,112,512]{2,1,0:T(8,128)S(1)}, bf16[2,112,512]{2,1,0:T(8,128)(2,1)S(1)}, bf16[2,112,512]{2,1,0:T(8,128)(2,1)S(1)}, bf16[2,112,512]{2,1,0:T(8,128)...) custom-call(s32[3]{0:T(128)S(1)} %pad_add_fusion.place_ref, f32[896,512]{1,0:T(8,128)} %get-tuple-element.15.kept_ref, ...), custom_call_target="tpu_custom_call" | custom-call | tf_op jit(solution)/shard_map/cut/pallas_call | solution.py:141
  132.0 3.1 %collective-permute-start.3 = (bf16[2,112,512]{2,1,0:T(8,128)(2,1)S(1)}, bf16[2,112,512]{2,1,0:T(8,128)(2,1)S(1)}, u32[]{:S(2)}, u32[]{:S(2)}) collective-permute-start(bf16[2,112,512]{2,1,0:T(8,128)(2,1)S(1)} %get-tuple-element.23), channel_id=1, source_target_pairs={{0,64},{64,128},{128,192},{192,0},{256,320},{320,384},{384,448},{4... | collective-permute-start | bytes 688136 | tf_op jit(solution)/shard_map/ppermute | solution.py:155
  135.1 3.4 %collective-permute-start.4 = (bf16[2,112,512]{2,1,0:T(8,128)(2,1)S(1)}, bf16[2,112,512]{2,1,0:T(8,128)(2,1)S(1)}, u32[]{:S(2)}, u32[]{:S(2)}) collective-permute-start(bf16[2,112,512]{2,1,0:T(8,128)(2,1)S(1)} %get-tuple-element.24), channel_id=1, source_target_pairs={{0,192},{64,0},{128,64},{192,128},{256,448},{320,256},{384,320},{4... | collective-permute-start | bytes 688136 | tf_op jit(solution)/shard_map/ppermute | solution.py:155
  138.5 3.4 %collective-permute-start.5 = (bf16[2,112,512]{2,1,0:T(8,128)(2,1)S(1)}, bf16[2,112,512]{2,1,0:T(8,128)(2,1)S(1)}, u32[]{:S(2)}, u32[]{:S(2)}) collective-permute-start(bf16[2,112,512]{2,1,0:T(8,128)(2,1)S(1)} %get-tuple-element.25), channel_id=1, source_target_pairs={{0,128},{64,192},{128,0},{192,64},{256,384},{320,448},{384,256},{4... | collective-permute-start | bytes 688136 | tf_op jit(solution)/shard_map/ppermute | solution.py:155
  142.0 4.8 %collective-permute-done.5 = bf16[2,112,512]{2,1,0:T(8,128)(2,1)S(1)} collective-permute-done((bf16[2,112,512]{2,1,0:T(8,128)(2,1)S(1)}, bf16[2,112,512]{2,1,0:T(8,128)(2,1)S(1)}, u32[]{:S(2)}, u32[]{:S(2)}) %collective-permute-start.5) | collective-permute-done | bytes 229408 | tf_op jit(solution)/shard_map/ppermute | solution.py:155
  146.8 0.1 convert_add_fusion
  146.9 7.9 %collective-permute-start.6 = (bf16[112,512]{1,0:T(8,128)(2,1)S(1)}, bf16[112,512]{1,0:T(8,128)(2,1)S(1)}, u32[]{:S(2)}, u32[]{:S(2)}) collective-permute-start(bf16[112,512]{1,0:T(8,128)(2,1)S(1)} %fusion.1), channel_id=1, source_target_pairs={{0,256},{64,320},{128,384},{192,448},{256,0},{320,64},{384,128},{4... | collective-permute-start | bytes 344072 | tf_op jit(solution)/shard_map/ppermute | solution.py:155
  154.9 2.3 %collective-permute-done.6 = bf16[112,512]{1,0:T(8,128)(2,1)S(1)} collective-permute-done((bf16[112,512]{1,0:T(8,128)(2,1)S(1)}, bf16[112,512]{1,0:T(8,128)(2,1)S(1)}, u32[]{:S(2)}, u32[]{:S(2)}) %collective-permute-start.6) | collective-permute-done | bytes 114720 | tf_op jit(solution)/shard_map/ppermute | solution.py:155
  157.1 6.9 %collective-permute-start.7 = (bf16[112,512]{1,0:T(8,128)(2,1)S(1)}, bf16[112,512]{1,0:T(8,128)(2,1)S(1)}, u32[]{:S(2)}, u32[]{:S(2)}) collective-permute-start(bf16[112,512]{1,0:T(8,128)(2,1)S(1)} %fusion), channel_id=1, source_target_pairs={{0,8},{4,12},{8,0},{12,4},{16,24},{20,28},{24,16},{28,20},{32,40},... | collective-permute-start | bytes 344072 | tf_op jit(solution)/shard_map/ppermute | solution.py:155
  164.1 2.2 %collective-permute-done.7 = bf16[112,512]{1,0:T(8,128)(2,1)S(1)} collective-permute-done((bf16[112,512]{1,0:T(8,128)(2,1)S(1)}, bf16[112,512]{1,0:T(8,128)(2,1)S(1)}, u32[]{:S(2)}, u32[]{:S(2)}) %collective-permute-start.7) | collective-permute-done | bytes 114720 | tf_op jit(solution)/shard_map/ppermute | solution.py:155
  166.3 2.5 %collective-permute-start.10 = (bf16[112,512]{1,0:T(8,128)(2,1)S(1)}, bf16[112,512]{1,0:T(8,128)(2,1)S(1)}, u32[]{:S(2)}, u32[]{:S(2)}) collective-permute-start(bf16[112,512]{1,0:T(8,128)(2,1)S(1)} %add_convert_fusion), channel_id=1, source_target_pairs={{0,48},{4,52},{8,56},{12,60},{16,32},{20,36},{24,40},{28,44},{32,1... | collective-permute-start | bytes 344072 | tf_op jit(solution)/shard_map/ppermute | solution.py:155
  168.8 4.4 %collective-permute-start.8 = (bf16[112,512]{1,0:T(8,128)(2,1)S(1)}, bf16[112,512]{1,0:T(8,128)(2,1)S(1)}, u32[]{:S(2)}, u32[]{:S(2)}) collective-permute-start(bf16[112,512]{1,0:T(8,128)(2,1)S(1)} %add_convert_fusion), channel_id=1, source_target_pairs={{0,16},{4,20},{8,24},{12,28},{16,0},{20,4},{24,8},{28,12},{32,48},... | collective-permute-start | bytes 344072 | tf_op jit(solution)/shard_map/ppermute | solution.py:155
  173.2 4.5 %collective-permute-start.9 = (bf16[112,512]{1,0:T(8,128)(2,1)S(1)}, bf16[112,512]{1,0:T(8,128)(2,1)S(1)}, u32[]{:S(2)}, u32[]{:S(2)}) collective-permute-start(bf16[112,512]{1,0:T(8,128)(2,1)S(1)} %add_convert_fusion), channel_id=1, source_target_pairs={{0,32},{4,36},{8,40},{12,44},{16,48},{20,52},{24,56},{28,60},{32,0... | collective-permute-start | bytes 344072 | tf_op jit(solution)/shard_map/ppermute | solution.py:155
  177.7 8.2 %collective-permute-done.9 = bf16[112,512]{1,0:T(8,128)(2,1)S(1)} collective-permute-done((bf16[112,512]{1,0:T(8,128)(2,1)S(1)}, bf16[112,512]{1,0:T(8,128)(2,1)S(1)}, u32[]{:S(2)}, u32[]{:S(2)}) %collective-permute-start.9) | collective-permute-done | bytes 114720 | tf_op jit(solution)/shard_map/ppermute | solution.py:155
  185.9 0.1 add_add_fusion
  185.9 6.9 %collective-permute-start.11 = (f32[112,512]{1,0:T(8,128)S(1)}, f32[112,512]{1,0:T(8,128)S(1)}, u32[]{:S(2)}, u32[]{:S(2)}) collective-permute-start(f32[112,512]{1,0:T(8,128)S(1)} %add_add_fusion), channel_id=1, source_target_pairs={{0,4},{4,0},{8,12},{12,8},{16,20},{20,16},{24,28},{28,24},{32,36},... | collective-permute-start | bytes 688136 | tf_op jit(solution)/shard_map/ppermute | solution.py:155
  192.8 1.1 collective-permute-done.11
  194.0 0.8 pad_maximum_fusion
  194.8 2.7 %bitcast_reduce_fusion = bf16[16,16,896]{2,1,0:T(8,128)(2,1)} fusion(bf16[64,16,896]{2,1,0:T(8,128)(2,1)} %all-to-all-done.1), kind=kLoop, calls=%fused_computation | loop fusion | flops 688128 | bytes 2293760 | tf_op jit(solution)/shard_map/reduce_sum | solution.py:182
  (23 shorter events, 0.2 us)
Async XLA Ops:
  3.0 14.7 %copy-start = (bf16[1,256,512]{2,1,0:T(8,128)(2,1)S(1)}, bf16[1,256,512]{2,1,0:T(8,128)(2,1)}, u32[]{:S(2)}) copy-start(bf16[1,256,512]{2,1,0:T(8,128)(2,1)} %param.5) | copy-start | bytes 786436
  3.0 14.7 %copy-start.1 = (bf16[1,256,512]{2,1,0:T(8,128)(2,1)S(1)}, bf16[1,256,512]{2,1,0:T(8,128)(2,1)}, u32[]{:S(2)}) copy-start(bf16[1,256,512]{2,1,0:T(8,128)(2,1)} %param.6) | copy-start | bytes 786436
  3.1 17.2 %copy-start.3 = (s32[1,4,4]{2,1,0:T(4,128)S(1)}, s32[1,4,4]{2,1,0:T(4,128)}, u32[]{:S(2)}) copy-start(s32[1,4,4]{2,1,0:T(4,128)} %param.9) | copy-start | bytes 196
  3.1 60.1 %all-to-all-start = ((bf16[64,16,896]{2,1,0:T(8,128)(2,1)}), bf16[64,16,896]{2,1,0:T(8,128)(2,1)S(1)}, u32[]{:S(2)}, u32[]{:S(2)}) async-start(bf16[64,16,896]{2,1,0:T(8,128)(2,1)} %bitcast.31), calls=%async_computation | async-start | bytes 3670016 | tf_op jit(solution)/shard_map/all_to_all | solution.py:160
  17.8 43.1 %collective-permute-start = (bf16[64,1024]{1,0:T(8,128)(2,1)S(1)}, bf16[64,1024]{1,0:T(8,128)(2,1)S(1)}, u32[]{:S(2)}, u32[]{:S(2)}) collective-permute-start(bf16[64,1024]{1,0:T(8,128)(2,1)S(1)} %pad_maximum_fusion.1), channel_id=1, source_target_pairs={{4,0},{8,4},{12,8},{16,12},{20,16},{24,20},{28,24},{32,28},{36,32}... | collective-permute-start | bytes 393224 | tf_op jit(solution)/shard_map/ppermute | solution.py:155
  63.2 1.3 copy-start.2
  82.3 112.5 %all-to-all-start.1 = ((bf16[64,16,896]{2,1,0:T(8,128)(2,1)}), bf16[64,16,896]{2,1,0:T(8,128)(2,1)}, u32[]{:S(2)}, u32[]{:S(2)}) async-start(bf16[64,16,896]{2,1,0:T(8,128)(2,1)} %bitcast.12), calls=%async_computation.1 | async-start | bytes 3670016 | tf_op jit(solution)/shard_map/all_to_all | solution.py:160
  89.3 40.3 %collective-permute-start.1 = (bf16[896,512]{1,0:T(8,128)(2,1)S(1)}, bf16[896,512]{1,0:T(8,128)(2,1)S(1)}, u32[]{:S(2)}, u32[]{:S(2)}) collective-permute-start(bf16[896,512]{1,0:T(8,128)(2,1)S(1)} %get-tuple-element.16), channel_id=1, source_target_pairs={{0,4},{4,0},{8,12},{12,8},{16,20},{20,16},{24,28},{28,24},{32,36},... | collective-permute-start | bytes 2752520 | tf_op jit(solution)/shard_map/ppermute | solution.py:155
  91.7 37.8 %collective-permute-start.2 = (bf16[64,1024]{1,0:T(8,128)(2,1)S(1)}, bf16[64,1024]{1,0:T(8,128)(2,1)S(1)}, u32[]{:S(2)}, u32[]{:S(2)}) collective-permute-start(bf16[64,1024]{1,0:T(8,128)(2,1)S(1)} %pad_maximum_fusion.2), channel_id=1, source_target_pairs={{0,4},{4,8},{8,12},{12,16},{16,20},{20,24},{24,28},{28,32},{32,36}... | collective-permute-start | bytes 393224 | tf_op jit(solution)/shard_map/ppermute | solution.py:155
  132.0 10.0 %collective-permute-start.3 = (bf16[2,112,512]{2,1,0:T(8,128)(2,1)S(1)}, bf16[2,112,512]{2,1,0:T(8,128)(2,1)S(1)}, u32[]{:S(2)}, u32[]{:S(2)}) collective-permute-start(bf16[2,112,512]{2,1,0:T(8,128)(2,1)S(1)} %get-tuple-element.23), channel_id=1, source_target_pairs={{0,64},{64,128},{128,192},{192,0},{256,320},{320,384},{384,448},{4... | collective-permute-start | bytes 688136 | tf_op jit(solution)/shard_map/ppermute | solution.py:155
  135.1 6.9 %collective-permute-start.4 = (bf16[2,112,512]{2,1,0:T(8,128)(2,1)S(1)}, bf16[2,112,512]{2,1,0:T(8,128)(2,1)S(1)}, u32[]{:S(2)}, u32[]{:S(2)}) collective-permute-start(bf16[2,112,512]{2,1,0:T(8,128)(2,1)S(1)} %get-tuple-element.24), channel_id=1, source_target_pairs={{0,192},{64,0},{128,64},{192,128},{256,448},{320,256},{384,320},{4... | collective-permute-start | bytes 688136 | tf_op jit(solution)/shard_map/ppermute | solution.py:155
  138.5 8.3 %collective-permute-start.5 = (bf16[2,112,512]{2,1,0:T(8,128)(2,1)S(1)}, bf16[2,112,512]{2,1,0:T(8,128)(2,1)S(1)}, u32[]{:S(2)}, u32[]{:S(2)}) collective-permute-start(bf16[2,112,512]{2,1,0:T(8,128)(2,1)S(1)} %get-tuple-element.25), channel_id=1, source_target_pairs={{0,128},{64,192},{128,0},{192,64},{256,384},{320,448},{384,256},{4... | collective-permute-start | bytes 688136 | tf_op jit(solution)/shard_map/ppermute | solution.py:155
  146.9 10.2 %collective-permute-start.6 = (bf16[112,512]{1,0:T(8,128)(2,1)S(1)}, bf16[112,512]{1,0:T(8,128)(2,1)S(1)}, u32[]{:S(2)}, u32[]{:S(2)}) collective-permute-start(bf16[112,512]{1,0:T(8,128)(2,1)S(1)} %fusion.1), channel_id=1, source_target_pairs={{0,256},{64,320},{128,384},{192,448},{256,0},{320,64},{384,128},{4... | collective-permute-start | bytes 344072 | tf_op jit(solution)/shard_map/ppermute | solution.py:155
  157.1 9.1 %collective-permute-start.7 = (bf16[112,512]{1,0:T(8,128)(2,1)S(1)}, bf16[112,512]{1,0:T(8,128)(2,1)S(1)}, u32[]{:S(2)}, u32[]{:S(2)}) collective-permute-start(bf16[112,512]{1,0:T(8,128)(2,1)S(1)} %fusion), channel_id=1, source_target_pairs={{0,8},{4,12},{8,0},{12,4},{16,24},{20,28},{24,16},{28,20},{32,40},... | collective-permute-start | bytes 344072 | tf_op jit(solution)/shard_map/ppermute | solution.py:155
  166.3 11.4 %collective-permute-start.10 = (bf16[112,512]{1,0:T(8,128)(2,1)S(1)}, bf16[112,512]{1,0:T(8,128)(2,1)S(1)}, u32[]{:S(2)}, u32[]{:S(2)}) collective-permute-start(bf16[112,512]{1,0:T(8,128)(2,1)S(1)} %add_convert_fusion), channel_id=1, source_target_pairs={{0,48},{4,52},{8,56},{12,60},{16,32},{20,36},{24,40},{28,44},{32,1... | collective-permute-start | bytes 344072 | tf_op jit(solution)/shard_map/ppermute | solution.py:155
  168.8 8.9 %collective-permute-start.8 = (bf16[112,512]{1,0:T(8,128)(2,1)S(1)}, bf16[112,512]{1,0:T(8,128)(2,1)S(1)}, u32[]{:S(2)}, u32[]{:S(2)}) collective-permute-start(bf16[112,512]{1,0:T(8,128)(2,1)S(1)} %add_convert_fusion), channel_id=1, source_target_pairs={{0,16},{4,20},{8,24},{12,28},{16,0},{20,4},{24,8},{28,12},{32,48},... | collective-permute-start | bytes 344072 | tf_op jit(solution)/shard_map/ppermute | solution.py:155
  173.2 12.7 %collective-permute-start.9 = (bf16[112,512]{1,0:T(8,128)(2,1)S(1)}, bf16[112,512]{1,0:T(8,128)(2,1)S(1)}, u32[]{:S(2)}, u32[]{:S(2)}) collective-permute-start(bf16[112,512]{1,0:T(8,128)(2,1)S(1)} %add_convert_fusion), channel_id=1, source_target_pairs={{0,32},{4,36},{8,40},{12,44},{16,48},{20,52},{24,56},{28,60},{32,0... | collective-permute-start | bytes 344072 | tf_op jit(solution)/shard_map/ppermute | solution.py:155
  185.9 8.0 %collective-permute-start.11 = (f32[112,512]{1,0:T(8,128)S(1)}, f32[112,512]{1,0:T(8,128)S(1)}, u32[]{:S(2)}, u32[]{:S(2)}) collective-permute-start(f32[112,512]{1,0:T(8,128)S(1)} %add_add_fusion), channel_id=1, source_target_pairs={{0,4},{4,0},{8,12},{12,8},{16,20},{20,16},{24,28},{28,24},{32,36},... | collective-permute-start | bytes 688136 | tf_op jit(solution)/shard_map/ppermute | solution.py:155

commit v5 on v4

--- a/solution.py
+++ b/solution.py
@@ -32,11 +32,14 @@
 
 
 def block_body(
-    units_ref, place_ref, q_ref, g_ref, ahead_ref, w_ref, x_ref, att_ref, dq_ref, partial_ref, sent_ref, kept_ref,
-    key, value, grad, q_rows, g_rows, att, dq,
+    units_ref, q_ref, g_ref, ahead_ref, w_ref, x_ref, att_ref, dq_ref, grad, *refs
 ):
+    p_refs = refs[:-7]
+    key, value, q_rows, g_rows, att, dq, spare = refs[-7:]
+    nbr = units_ref[units_ref.shape[0] - 1]
     tokens, width = q_ref.shape
-    all_rows, enc_width = x_ref.shape
+    all_rows = x_ref.shape[0]
+    piece = PART // len(p_refs)
     heads = width // HEAD_DIM
     chunk = 4 * PART
     for c in range(all_rows // chunk):
@@ -77,44 +80,56 @@
     for c in range(all_rows // chunk):
         rows = pl.ds(c * chunk, chunk)
         term = dot(grad[0, rows, :], w_ref[0], NT) + dot(grad[1, rows, :], w_ref[1], NT)
-        partial_ref[rows, :] = term.astype(jnp.bfloat16)
-    core = place_ref[0]
-    for e in range(0, enc_width, 128):
-        x = x_ref[:, e : e + 128].T
-        sent_ref[e : e + 128, :] = dot(x, grad[1 - core], NN).astype(jnp.bfloat16)
-        kept_ref[e : e + 128, :] = dot(x, grad[core], NN)
-
-
-def block(units_of, place, q, g, ahead, w, x):
+        spare[...] = term.astype(jnp.bfloat16)
+        for n, ref in enumerate(p_refs):
+            slot = lax.rem(nbr + n, len(p_refs))
+            for u in range(4):
+                at = pl.multiple_of(u * PART + slot * piece, piece)
+                ref[(c * 4 + u) * piece : (c * 4 + u + 1) * piece, :] = spare[pl.ds(at, piece), :]
+
+
+def low(*shape):
+    return jax.ShapeDtypeStruct(shape, jnp.bfloat16)
+
+
+def wide(*shape):
+    return jax.ShapeDtypeStruct(shape, jnp.float32)
+
+
+def call(body, name, out_shape, scratch, place, *args):
+    return pl.pallas_call(
+        body,
+        out_shape=out_shape,
+        in_specs=[SMEM] + [VMEM] * len(args),
+        out_specs=jax.tree.map(lambda _: VMEM, out_shape),
+        scratch_shapes=scratch,
+        compiler_params=PARAMS,
+        name=name,
+    )(place, *args)
+
+
+def block(slots, units_of, q, g, ahead, w, x):
     tokens, width = q.shape
     all_rows, enc_width = x.shape
-
-    def low(*shape):
-        return jax.ShapeDtypeStruct(shape, jnp.bfloat16)
-
-    return pl.pallas_call(
-        block_body,
-        out_shape=[
-            low(tokens, width),
-            low(tokens, width),
-            low(all_rows, enc_width),
-            low(enc_width, width),
-            jax.ShapeDtypeStruct((enc_width, width), jnp.float32),
-        ],
-        in_specs=[SMEM] * 2 + [VMEM] * 5,
-        out_specs=[VMEM] * 5,
-        scratch_shapes=[
-            pltpu.VMEM((all_rows, width), jnp.bfloat16),
-            pltpu.VMEM((all_rows, width), jnp.bfloat16),
-            pltpu.VMEM((2, all_rows, width), jnp.bfloat16),
-            pltpu.VMEM((tokens, width), jnp.bfloat16),
-            pltpu.VMEM((tokens, width), jnp.bfloat16),
-            pltpu.VMEM((tokens, width), jnp.float32),
-            pltpu.VMEM((tokens, width), jnp.float32),
-        ],
-        compiler_params=PARAMS,
-        name="block",
-    )(units_of, place, q, g, ahead, w, x)
+    out_shape = [low(tokens, width), low(tokens, width), low(2, all_rows, width)]
+    out_shape += [low(all_rows // slots, enc_width)] * slots
+    scratch = [pltpu.VMEM((all_rows, width), jnp.bfloat16)] * 2
+    scratch += [pltpu.VMEM((tokens, width), jnp.bfloat16)] * 2
+    scratch += [pltpu.VMEM((tokens, width), jnp.float32)] * 2 + [pltpu.VMEM((4 * PART, enc_width), jnp.bfloat16)]
+    return call(block_body, "block", out_shape, scratch, units_of, q, g, ahead, w, x)
+
+
+def products(place, x, grad):
+    enc_width, width = x.shape[1], grad.shape[2]
+
+    def body(place_ref, x_ref, grad_ref, sent_ref, kept_ref):
+        core = place_ref[0]
+        for e in range(0, enc_width, 128):
+            part = x_ref[:, e : e + 128].T
+            sent_ref[e : e + 128, :] = dot(part, grad_ref[1 - core], NN).astype(jnp.bfloat16)
+            kept_ref[e : e + 128, :] = dot(part, grad_ref[core], NN)
+
+    return call(body, "products", [low(enc_width, width), wide(enc_width, width)], [], place, x, grad)
 
 
 def cut(place, kept, away, att, dq, behind):
@@ -138,16 +153,49 @@
             full[:SPAN, :] = jnp.where(lead, came, ref[:SPAN, :].astype(jnp.float32)).astype(jnp.bfloat16)
             full[SPAN:, :] = ref[SPAN:, :]
 
-    return pl.pallas_call(
-        body,
-        out_shape=[jax.ShapeDtypeStruct((2, rows, width), jnp.float32)]
-        + [jax.ShapeDtypeStruct((2, rows, width), jnp.bfloat16)] * 3
-        + [jax.ShapeDtypeStruct(att.shape, jnp.bfloat16)] * 2,
-        in_specs=[SMEM] + [VMEM] * 5,
-        out_specs=[VMEM] * 6,
-        compiler_params=PARAMS,
-        name="cut",
-    )(place, kept, away, att, dq, behind)
+    out_shape = [wide(2, rows, width)] + [low(2, rows, width)] * 3 + [low(*att.shape)] * 2
+    return call(body, "cut", out_shape, [], place, kept, away, att, dq, behind)
+
+
+def x_sum(place, own, parts, partial, term):
+    def body(_, own_ref, *refs):
+        part_refs, partial_ref, term_ref, held_ref, acc_ref = refs[:3], *refs[3:]
+        total = own_ref[...]
+        for ref in part_refs:
+            total = total + ref[...].astype(jnp.float32)
+        held_ref[...] = total.astype(jnp.bfloat16)
+        acc_ref[...] = add(partial_ref[...], term_ref[...])
+
+    return call(body, "x_sum", [low(*own.shape), wide(*partial.shape)], [], place, own, *parts, partial, term)
+
+
+def y_pair(place, held, came, acc, term):
+    def body(_, held_ref, came_ref, acc_ref, term_ref, both_ref, out_ref):
+        both_ref[...] = add(held_ref[...], came_ref[...]).astype(jnp.bfloat16)
+        out_ref[...] = add(acc_ref[...], term_ref[...])
+
+    return call(body, "y_pair", [low(*held.shape), wide(*acc.shape)], [], place, held, came, acc, term)
+
+
+def fold(place, held, by, acc, term):
+    _, rows, width = held.shape
+
+    def body(place_ref, held_ref, a_ref, b_ref, c_ref, acc_ref, term_ref, mine_ref, other_ref, total_ref):
+        high = place_ref[2]
+        for ref, at in ((mine_ref, high), (other_ref, 1 - high)):
+            ref[...] = (add(held_ref[at], a_ref[at]) + add(b_ref[at], c_ref[at])).astype(ref.dtype)
+        total_ref[...] = add(acc_ref[...], term_ref[...]).astype(jnp.bfloat16)
+
+    out_shape = [wide(rows, width), low(rows, width), low(*acc.shape)]
+    return call(body, "fold", out_shape, [], place, held, *by, acc, term)
+
+
+def join(place, mine, theirs):
+    def body(place_ref, mine_ref, theirs_ref, out_ref):
+        out_ref[place_ref[0]] = mine_ref[...]
+        out_ref[1 - place_ref[0]] = theirs_ref[...]
+
+    return call(body, "join", wide(2, *mine.shape), [], place, mine, theirs)
 
 
 def permute(x, axis, to):
@@ -155,10 +203,8 @@
     return lax.ppermute(x, axis, [(i, to(i)) for i in range(n) if 0 <= to(i) < n])
 
 
-def exchange(x):
-    outer, inner, *rest = x.shape
-    x = lax.all_to_all(x.reshape(outer * inner, *rest), ("ctx", "nbr"), split_axis=0, concat_axis=0, tiled=True)
-    return x.reshape(outer, inner, *rest)
+def exchange(x, axes):
+    return lax.all_to_all(x, axes, split_axis=0, concat_axis=0, tiled=True)
 
 
 def shards(queries, cotangent, encoded, kv_weight, neighbour_ids):
@@ -167,36 +213,34 @@
     groups = lax.axis_size("nbr")
     ctx = lax.axis_index("ctx")
     dp = lax.axis_index("dp")
+    nbr = lax.axis_index("nbr")
     place = jnp.stack((ctx % 2, dp % 4, dp // 4)).astype(jnp.int32)
 
     copies = jnp.broadcast_to(enc[:, None], (units, groups, piece, enc_width))
-    x = exchange(copies).reshape(units * PART, enc_width)
+    x = exchange(copies.reshape(units * groups, piece, enc_width), ("ctx", "nbr")).reshape(units * PART, enc_width)
 
     head = jnp.concatenate((q[:SPAN], g[:SPAN]), axis=1)
     ahead = permute(head, "ctx", lambda i: i - 1)
 
     unit_of = (neighbour_ids[0] // units).reshape(-1)
-    att, dq, partial, sent, kept = block(unit_of, place, q, g, ahead, kv_weight, x)
-
-    terms = exchange(partial.reshape(units, groups, piece, enc_width))
-    encoded_grad = jnp.sum(terms.astype(jnp.float32), axis=1).astype(jnp.bfloat16)
-
+    scalars = jnp.concatenate((unit_of, nbr[None])).astype(jnp.int32)
+    att, dq, grad, *partials = block(groups, scalars, q, g, ahead, kv_weight, x)
+
+    terms = [permute(partials[k], "nbr", lambda i, k=k: (i + k) % groups) for k in range(1, groups)]
+
+    sent, kept = products(place, x, grad)
     away = permute(sent, "ctx", lambda i: i ^ 1)
     tail = jnp.concatenate((att[:SPAN], dq[:SPAN]), axis=1)
     behind = permute(tail, "ctx", lambda i: i + 1)
-    held, *sends, attended, query_grad = cut(place, kept, away, att, dq, behind)
-    for k in (1, 3, 2):
-        held = add(held, permute(sends[k - 1], "dp", lambda i, k=k: i // 4 * 4 + (i + k) % 4))
-    high = dp // 4
-    other = lax.dynamic_index_in_dim(held, 1 - high, 0, keepdims=False).astype(jnp.bfloat16)
-    mine = lax.dynamic_index_in_dim(held, high, 0, keepdims=False)
-    low = add(mine, permute(other, "dp", lambda i: (i + 4) % 8)).astype(jnp.bfloat16)
-    low = add(low, permute(low, "ctx", lambda i: i ^ 2)).astype(jnp.bfloat16)
-    by = [permute(low, "ctx", lambda i, b=b: i ^ b) for b in (4, 8, 12)]
-    mine = add(low, by[0]) + add(by[1], by[2])
-    theirs = permute(mine, "ctx", lambda i: i ^ 1)
-    keys_here = ctx % 2 == 0
-    weight_grad = jnp.stack((jnp.where(keys_here, mine, theirs), jnp.where(keys_here, theirs, mine)), axis=0)
+    own, *sends, attended, query_grad = cut(place, kept, away, att, dq, behind)
+    parts = [permute(sends[k - 1], "dp", lambda i, k=k: i // 4 * 4 + (i + k) % 4) for k in (1, 2, 3)]
+    held, acc = x_sum(place, own, parts, partials[0], terms[1])
+    held, acc = y_pair(place, held, permute(held, "ctx", lambda i: i ^ 2), acc, terms[0])
+    by = [permute(held, "ctx", lambda i, b=b: i ^ b) for b in (4, 8, 12)]
+    mine, other, total = fold(place, held, by, acc, terms[2])
+    encoded_grad = exchange(total.reshape(units, piece, enc_width), "ctx")
+    mine = add(mine, permute(other, "dp", lambda i: (i + 4) % 8))
+    weight_grad = join(place, mine, permute(mine, "ctx", lambda i: i ^ 1))
     return (attended[None], query_grad[None], encoded_grad[None], weight_grad)
 
 

time: 199 us -> 186 us (0.935)
  the two profiles are of different devices: /device:TPU:1 before, /device:TPU:15 now
where the time goes in v5:
time: 186 us; the launch traced here: 185 us
  starting transfers between devices  81.2 us (44%)
  waiting for transfers between devices  71.6 us (38%)
  Pallas kernels  25.2 us (14%)
  local copies, waits for them, and re-layouts  5.8 us (3%)
    ppermute x15, waiting for transfers between devices, permute(): lax.ppermute(x, axis, [(i, to(i)) for i in range(n) if 0 <= to(i) < n])  70.1 us
    ppermute x15, starting transfers between devices, permute(): lax.ppermute(x, axis, [(i, to(i)) for i in range(n) if 0 <= to(i) < n])  60.9 us
    pallas_call x7, Pallas kernels, call(): pl.pallas_call(body, out_shape=out_shape, in_specs=[SMEM] + [VMEM] * len(...  25.2 us
    all_to_all x2, starting transfers between devices, exchange(): return lax.all_to_all(x, axes, split_axis=0, concat_axis=0, tiled=True)  20.2 us
  transfers between devices with their start and end apart: 17, of which 10 were waited for; matrix products, arithmetic and copies ran while one was open for 0% of the time, Pallas kernels for 3%

profile of v5, /device:TPU:15, one launch (start us, length us, event | category | flops | bytes accessed | tf_op | source)
XLA Modules:
  0.0 185.0 jit_solution(18420421159391543038)
XLA Ops:
  0.6 2.4 %broadcast_in_dim.20 = bf16[16,4,16,896]{3,2,1,0:T(8,128)(2,1)} broadcast(bf16[16,16,896]{2,1,0:T(8,128)(2,1)} %bitcast.23), dimensions={0,2,3} | broadcast | bytes 2293760 | tf_op jit(solution)/shard_map/broadcast_in_dim | solution.py:219
  3.1 14.0 %all-to-all-start = ((bf16[64,16,896]{2,1,0:T(8,128)(2,1)}), bf16[64,16,896]{2,1,0:T(8,128)(2,1)S(1)}, u32[]{:S(2)}, u32[]{:S(2)}) async-start(bf16[64,16,896]{2,1,0:T(8,128)(2,1)} %bitcast.21), calls=%async_computation | async-start | bytes 3670016 | tf_op jit(solution)/shard_map/all_to_all | solution.py:207
  17.1 2.3 %collective-permute-start = (bf16[64,1024]{1,0:T(8,128)(2,1)S(1)}, bf16[64,1024]{1,0:T(8,128)(2,1)S(1)}, u32[]{:S(2)}, u32[]{:S(2)}) collective-permute-start(bf16[64,1024]{1,0:T(8,128)(2,1)S(1)} %pad_maximum_fusion), channel_id=1, source_target_pairs={{4,0},{8,4},{12,8},{16,12},{20,16},{24,20},{28,24},{32,28},{36,32}... | collective-permute-start | bytes 393224 | tf_op jit(solution)/shard_map/ppermute | solution.py:203
  19.6 39.6 %collective-permute-done.ahead_ref = bf16[64,1024]{1,0:T(8,128)(2,1)S(1)} collective-permute-done((bf16[64,1024]{1,0:T(8,128)(2,1)S(1)}, bf16[64,1024]{1,0:T(8,128)(2,1)S(1)}, u32[]{:S(2)}, u32[]{:S(2)}) %collective-permute-start) | collective-permute-done | bytes 131104 | tf_op jit(solution)/shard_map/ppermute | solution.py:203
  59.2 1.6 all-to-all-done
  62.0 14.4 %block.1 = (bf16[256,512]{1,0:T(8,128)(2,1)S(1)}, bf16[256,512]{1,0:T(8,128)(2,1)S(1)}, bf16[2,1024,512]{2,1,0:T(8,128)(2,1)}, bf16[256,896]{1,0:T(8,128)(2,1)S(...) custom-call(s32[17]{0:T(128)S(1)} %pad_add_fusion.1.units_ref, ...), custom_call_target="tpu_custom_call" | custom-call | tf_op jit(solution)/shard_map/block/pallas_call | solution.py:100
  76.4 4.2 %products.1 = (bf16[896,512]{1,0:T(8,128)(2,1)S(1)}, f32[896,512]{1,0:T(8,128)S(1)}) custom-call(s32[3]{0:T(128)S(1)} %pad_add_fusion.place_ref._, bf16[1024,896]{1,0:T(8,128)(2,1)} %bitcast.20, bf16[2,1024,512]{2,1,0:T(8,128)(2,1)} %get-tuple-element.26.grad_ref), custom_call_target="tpu_custom_call" | custom-call | tf_op jit(solution)/shard_map/products/pallas_call | solution.py:100
  81.9 3.1 %collective-permute-start.1 = (bf16[896,512]{1,0:T(8,128)(2,1)S(1)}, bf16[896,512]{1,0:T(8,128)(2,1)S(1)}, u32[]{:S(2)}, u32[]{:S(2)}) collective-permute-start(bf16[896,512]{1,0:T(8,128)(2,1)S(1)} %get-tuple-element.28), channel_id=1, source_target_pairs={{0,4},{4,0},{8,12},{12,8},{16,20},{20,16},{24,28},{28,24},{32,36},... | collective-permute-start | bytes 2752520 | tf_op jit(solution)/shard_map/ppermute | solution.py:203
  85.1 4.3 %collective-permute-start.6 = (bf16[256,896]{1,0:T(8,128)(2,1)S(1)}, bf16[256,896]{1,0:T(8,128)(2,1)S(1)}, u32[]{:S(2)}, u32[]{:S(2)}) collective-permute-start(bf16[256,896]{1,0:T(8,128)(2,1)S(1)} %get-tuple-element.38), channel_id=1, source_target_pairs={{0,2},{1,3},{2,0},{3,1},{4,6},{5,7},{6,4},{7,5},{8,10},{9,11},{10,... | collective-permute-start | bytes 1376264 | tf_op jit(solution)/shard_map/ppermute | solution.py:203
  89.4 1.9 %collective-permute-start.2 = (bf16[64,1024]{1,0:T(8,128)(2,1)S(1)}, bf16[64,1024]{1,0:T(8,128)(2,1)S(1)}, u32[]{:S(2)}, u32[]{:S(2)}) collective-permute-start(bf16[64,1024]{1,0:T(8,128)(2,1)S(1)} %pad_maximum_fusion.1), channel_id=1, source_target_pairs={{0,4},{4,8},{8,12},{12,16},{16,20},{20,24},{24,28},{28,32},{32,36}... | collective-permute-start | bytes 393224 | tf_op jit(solution)/shard_map/ppermute | solution.py:203
  91.3 1.9 %collective-permute-done.2.behind_ref = bf16[64,1024]{1,0:T(8,128)(2,1)S(1)} collective-permute-done((bf16[64,1024]{1,0:T(8,128)(2,1)S(1)}, bf16[64,1024]{1,0:T(8,128)(2,1)S(1)}, u32[]{:S(2)}, u32[]{:S(2)}) %collective-permute-start.2) | collective-permute-done | bytes 131104 | tf_op jit(solution)/shard_map/ppermute | solution.py:203
  93.2 2.5 %cut.1 = (f32[2,112,512]{2,1,0:T(8,128)S(1)}, bf16[2,112,512]{2,1,0:T(8,128)(2,1)S(1)}, bf16[2,112,512]{2,1,0:T(8,128)(2,1)S(1)}, bf16[2,112,512]{2,1,0:T(8,128)...) custom-call(s32[3]{0:T(128)S(1)} %pad_add_fusion.place_ref._, f32[896,512]{1,0:T(8,128)} %copy-done, ...), custom_call_target="tpu_custom_call" | custom-call | tf_op jit(solution)/shard_map/cut/pallas_call | solution.py:100
  95.7 2.1 %collective-permute-start.3 = (bf16[2,112,512]{2,1,0:T(8,128)(2,1)S(1)}, bf16[2,112,512]{2,1,0:T(8,128)(2,1)S(1)}, u32[]{:S(2)}, u32[]{:S(2)}) collective-permute-start(bf16[2,112,512]{2,1,0:T(8,128)(2,1)S(1)} %get-tuple-element.34), channel_id=1, source_target_pairs={{0,64},{64,128},{128,192},{192,0},{256,320},{320,384},{384,448},{4... | collective-permute-start | bytes 688136 | tf_op jit(solution)/shard_map/ppermute | solution.py:203
  97.8 4.0 %collective-permute-start.4 = (bf16[2,112,512]{2,1,0:T(8,128)(2,1)S(1)}, bf16[2,112,512]{2,1,0:T(8,128)(2,1)S(1)}, u32[]{:S(2)}, u32[]{:S(2)}) collective-permute-start(bf16[2,112,512]{2,1,0:T(8,128)(2,1)S(1)} %get-tuple-element.35), channel_id=1, source_target_pairs={{0,128},{64,192},{128,0},{192,64},{256,384},{320,448},{384,256},{4... | collective-permute-start | bytes 688136 | tf_op jit(solution)/shard_map/ppermute | solution.py:203
  101.9 1.9 %collective-permute-start.5 = (bf16[2,112,512]{2,1,0:T(8,128)(2,1)S(1)}, bf16[2,112,512]{2,1,0:T(8,128)(2,1)S(1)}, u32[]{:S(2)}, u32[]{:S(2)}) collective-permute-start(bf16[2,112,512]{2,1,0:T(8,128)(2,1)S(1)} %get-tuple-element.36), channel_id=1, source_target_pairs={{0,192},{64,0},{128,64},{192,128},{256,448},{320,256},{384,320},{4... | collective-permute-start | bytes 688136 | tf_op jit(solution)/shard_map/ppermute | solution.py:203
  103.8 3.1 %collective-permute-start.8 = (bf16[256,896]{1,0:T(8,128)(2,1)S(1)}, bf16[256,896]{1,0:T(8,128)(2,1)S(1)}, u32[]{:S(2)}, u32[]{:S(2)}) collective-permute-start(bf16[256,896]{1,0:T(8,128)(2,1)S(1)} %get-tuple-element.41), channel_id=1, source_target_pairs={{0,1},{1,2},{2,3},{3,0},{4,5},{5,6},{6,7},{7,4},{8,9},{9,10},{10,1... | collective-permute-start | bytes 1376264 | tf_op jit(solution)/shard_map/ppermute | solution.py:203
  106.9 3.0 %collective-permute-done.6.refs_4_ = bf16[256,896]{1,0:T(8,128)(2,1)S(1)} collective-permute-done((bf16[256,896]{1,0:T(8,128)(2,1)S(1)}, bf16[256,896]{1,0:T(8,128)(2,1)S(1)}, u32[]{:S(2)}, u32[]{:S(2)}) %collective-permute-start.6) | collective-permute-done | bytes 458784 | tf_op jit(solution)/shard_map/ppermute | solution.py:203
  109.9 2.9 %collective-permute-done.5.refs_2_ = bf16[2,112,512]{2,1,0:T(8,128)(2,1)S(1)} collective-permute-done((bf16[2,112,512]{2,1,0:T(8,128)(2,1)S(1)}, bf16[2,112,512]{2,1,0:T(8,128)(2,1)S(1)}, u32[]{:S(2)}, u32[]{:S(2)}) %collective-permute-start.5) | collective-permute-done | bytes 229408 | tf_op jit(solution)/shard_map/ppermute | solution.py:203
  113.6 3.5 %collective-permute-start.7 = (bf16[2,112,512]{2,1,0:T(8,128)(2,1)S(1)}, bf16[2,112,512]{2,1,0:T(8,128)(2,1)S(1)}, u32[]{:S(2)}, u32[]{:S(2)}) collective-permute-start(bf16[2,112,512]{2,1,0:T(8,128)(2,1)S(1)} %get-tuple-element.39.held_ref), channel_id=1, source_target_pairs={{0,8},{4,12},{8,0},{12,4},{16,24},{20,28},{24,16},{28,20},{32,40},... | collective-permute-start | bytes 688136 | tf_op jit(solution)/shard_map/ppermute | solution.py:203
  117.0 3.8 %collective-permute-start.12 = (bf16[256,896]{1,0:T(8,128)(2,1)S(1)}, bf16[256,896]{1,0:T(8,128)(2,1)S(1)}, u32[]{:S(2)}, u32[]{:S(2)}) collective-permute-start(bf16[256,896]{1,0:T(8,128)(2,1)S(1)} %get-tuple-element.44), channel_id=1, source_target_pairs={{0,3},{1,0},{2,1},{3,2},{4,7},{5,4},{6,5},{7,6},{8,11},{9,8},{10,9... | collective-permute-start | bytes 1376264 | tf_op jit(solution)/shard_map/ppermute | solution.py:203
  121.5 9.9 %collective-permute-start.11 = (bf16[2,112,512]{2,1,0:T(8,128)(2,1)S(1)}, bf16[2,112,512]{2,1,0:T(8,128)(2,1)S(1)}, u32[]{:S(2)}, u32[]{:S(2)}) collective-permute-start(bf16[2,112,512]{2,1,0:T(8,128)(2,1)S(1)} %get-tuple-element.42.held_ref), channel_id=1, source_target_pairs={{0,48},{4,52},{8,56},{12,60},{16,32},{20,36},{24,40},{28,44},{32,1... | collective-permute-start | bytes 688136 | tf_op jit(solution)/shard_map/ppermute | solution.py:203
  131.5 7.7 %collective-permute-start.10 = (bf16[2,112,512]{2,1,0:T(8,128)(2,1)S(1)}, bf16[2,112,512]{2,1,0:T(8,128)(2,1)S(1)}, u32[]{:S(2)}, u32[]{:S(2)}) collective-permute-start(bf16[2,112,512]{2,1,0:T(8,128)(2,1)S(1)} %get-tuple-element.42.held_ref), channel_id=1, source_target_pairs={{0,32},{4,36},{8,40},{12,44},{16,48},{20,52},{24,56},{28,60},{32,0... | collective-permute-start | bytes 688136 | tf_op jit(solution)/shard_map/ppermute | solution.py:203
  139.2 1.9 %collective-permute-start.9 = (bf16[2,112,512]{2,1,0:T(8,128)(2,1)S(1)}, bf16[2,112,512]{2,1,0:T(8,128)(2,1)S(1)}, u32[]{:S(2)}, u32[]{:S(2)}) collective-permute-start(bf16[2,112,512]{2,1,0:T(8,128)(2,1)S(1)} %get-tuple-element.42.held_ref), channel_id=1, source_target_pairs={{0,16},{4,20},{8,24},{12,28},{16,0},{20,4},{24,8},{28,12},{32,48},... | collective-permute-start | bytes 688136 | tf_op jit(solution)/shard_map/ppermute | solution.py:203
  141.1 9.2 %collective-permute-done.11.c_ref = bf16[2,112,512]{2,1,0:T(8,128)(2,1)S(1)} collective-permute-done((bf16[2,112,512]{2,1,0:T(8,128)(2,1)S(1)}, bf16[2,112,512]{2,1,0:T(8,128)(2,1)S(1)}, u32[]{:S(2)}, u32[]{:S(2)}) %collective-permute-start.11) | collective-permute-done | bytes 229408 | tf_op jit(solution)/shard_map/ppermute | solution.py:203
  150.3 1.8 collective-permute-done.10.b_ref
  152.1 7.2 %collective-permute-done.9.a_ref = bf16[2,112,512]{2,1,0:T(8,128)(2,1)S(1)} collective-permute-done((bf16[2,112,512]{2,1,0:T(8,128)(2,1)S(1)}, bf16[2,112,512]{2,1,0:T(8,128)(2,1)S(1)}, u32[]{:S(2)}, u32[]{:S(2)}) %collective-permute-start.9) | collective-permute-done | bytes 229408 | tf_op jit(solution)/shard_map/ppermute | solution.py:203
  159.3 1.4 fold.1
  160.7 6.3 %all-to-all-start.1 = ((bf16[16,16,896]{2,1,0:T(8,128)(2,1)}), bf16[16,16,896]{2,1,0:T(8,128)(2,1)S(1)}, u32[]{:S(2)}, u32[]{:S(2)}) async-start(bf16[16,16,896]{2,1,0:T(8,128)(2,1)} %bitcast.13), calls=%async_computation.1 | async-start | bytes 917504 | tf_op jit(solution)/shard_map/all_to_all | solution.py:207
  167.0 8.7 %collective-permute-start.13 = (bf16[112,512]{1,0:T(8,128)(2,1)S(1)}, bf16[112,512]{1,0:T(8,128)(2,1)S(1)}, u32[]{:S(2)}, u32[]{:S(2)}) collective-permute-start(bf16[112,512]{1,0:T(8,128)(2,1)S(1)} %get-tuple-element.47), channel_id=1, source_target_pairs={{0,256},{64,320},{128,384},{192,448},{256,0},{320,64},{384,128},{4... | collective-permute-start | bytes 344072 | tf_op jit(solution)/shard_map/ppermute | solution.py:203
  175.6 3.3 %collective-permute-done.13 = bf16[112,512]{1,0:T(8,128)(2,1)S(1)} collective-permute-done((bf16[112,512]{1,0:T(8,128)(2,1)S(1)}, bf16[112,512]{1,0:T(8,128)(2,1)S(1)}, u32[]{:S(2)}, u32[]{:S(2)}) %collective-permute-start.13) | collective-permute-done | bytes 114720 | tf_op jit(solution)/shard_map/ppermute | solution.py:203
  179.0 2.7 %collective-permute-start.14 = (f32[112,512]{1,0:T(8,128)S(1)}, f32[112,512]{1,0:T(8,128)S(1)}, u32[]{:S(2)}, u32[]{:S(2)}) collective-permute-start(f32[112,512]{1,0:T(8,128)S(1)} %convert_add_fusion.mine_ref), channel_id=1, source_target_pairs={{0,4},{4,0},{8,12},{12,8},{16,20},{20,16},{24,28},{28,24},{32,36},... | collective-permute-start | bytes 688136 | tf_op jit(solution)/shard_map/ppermute | solution.py:203
  182.8 1.3 join.1
  (31 shorter events, 6.1 us)
Async XLA Ops:
  3.0 14.0 %copy-start.1 = (bf16[1,256,512]{2,1,0:T(8,128)(2,1)S(1)}, bf16[1,256,512]{2,1,0:T(8,128)(2,1)}, u32[]{:S(2)}) copy-start(bf16[1,256,512]{2,1,0:T(8,128)(2,1)} %param.5) | copy-start | bytes 786436
  3.0 14.0 %copy-start.2 = (bf16[1,256,512]{2,1,0:T(8,128)(2,1)S(1)}, bf16[1,256,512]{2,1,0:T(8,128)(2,1)}, u32[]{:S(2)}) copy-start(bf16[1,256,512]{2,1,0:T(8,128)(2,1)} %param.6) | copy-start | bytes 786436
  3.0 16.3 %copy-start.4 = (s32[1,4,4]{2,1,0:T(4,128)S(1)}, s32[1,4,4]{2,1,0:T(4,128)}, u32[]{:S(2)}) copy-start(s32[1,4,4]{2,1,0:T(4,128)} %param.9) | copy-start | bytes 196
  3.1 57.7 %all-to-all-start = ((bf16[64,16,896]{2,1,0:T(8,128)(2,1)}), bf16[64,16,896]{2,1,0:T(8,128)(2,1)S(1)}, u32[]{:S(2)}, u32[]{:S(2)}) async-start(bf16[64,16,896]{2,1,0:T(8,128)(2,1)} %bitcast.21), calls=%async_computation | async-start | bytes 3670016 | tf_op jit(solution)/shard_map/all_to_all | solution.py:207
  17.1 42.1 %collective-permute-start = (bf16[64,1024]{1,0:T(8,128)(2,1)S(1)}, bf16[64,1024]{1,0:T(8,128)(2,1)S(1)}, u32[]{:S(2)}, u32[]{:S(2)}) collective-permute-start(bf16[64,1024]{1,0:T(8,128)(2,1)S(1)} %pad_maximum_fusion), channel_id=1, source_target_pairs={{4,0},{8,4},{12,8},{16,12},{20,16},{24,20},{28,24},{32,28},{36,32}... | collective-permute-start | bytes 393224 | tf_op jit(solution)/shard_map/ppermute | solution.py:203
  60.8 1.2 copy-start.3
  80.7 1.3 copy-start
  81.9 11.3 %collective-permute-start.1 = (bf16[896,512]{1,0:T(8,128)(2,1)S(1)}, bf16[896,512]{1,0:T(8,128)(2,1)S(1)}, u32[]{:S(2)}, u32[]{:S(2)}) collective-permute-start(bf16[896,512]{1,0:T(8,128)(2,1)S(1)} %get-tuple-element.28), channel_id=1, source_target_pairs={{0,4},{4,0},{8,12},{12,8},{16,20},{20,16},{24,28},{28,24},{32,36},... | collective-permute-start | bytes 2752520 | tf_op jit(solution)/shard_map/ppermute | solution.py:203
  85.1 24.8 %collective-permute-start.6 = (bf16[256,896]{1,0:T(8,128)(2,1)S(1)}, bf16[256,896]{1,0:T(8,128)(2,1)S(1)}, u32[]{:S(2)}, u32[]{:S(2)}) collective-permute-start(bf16[256,896]{1,0:T(8,128)(2,1)S(1)} %get-tuple-element.38), channel_id=1, source_target_pairs={{0,2},{1,3},{2,0},{3,1},{4,6},{5,7},{6,4},{7,5},{8,10},{9,11},{10,... | collective-permute-start | bytes 1376264 | tf_op jit(solution)/shard_map/ppermute | solution.py:203
  89.4 3.9 %collective-permute-start.2 = (bf16[64,1024]{1,0:T(8,128)(2,1)S(1)}, bf16[64,1024]{1,0:T(8,128)(2,1)S(1)}, u32[]{:S(2)}, u32[]{:S(2)}) collective-permute-start(bf16[64,1024]{1,0:T(8,128)(2,1)S(1)} %pad_maximum_fusion.1), channel_id=1, source_target_pairs={{0,4},{4,8},{8,12},{12,16},{16,20},{20,24},{24,28},{28,32},{32,36}... | collective-permute-start | bytes 393224 | tf_op jit(solution)/shard_map/ppermute | solution.py:203
  95.7 14.2 %collective-permute-start.3 = (bf16[2,112,512]{2,1,0:T(8,128)(2,1)S(1)}, bf16[2,112,512]{2,1,0:T(8,128)(2,1)S(1)}, u32[]{:S(2)}, u32[]{:S(2)}) collective-permute-start(bf16[2,112,512]{2,1,0:T(8,128)(2,1)S(1)} %get-tuple-element.34), channel_id=1, source_target_pairs={{0,64},{64,128},{128,192},{192,0},{256,320},{320,384},{384,448},{4... | collective-permute-start | bytes 688136 | tf_op jit(solution)/shard_map/ppermute | solution.py:203
  97.8 12.1 %collective-permute-start.4 = (bf16[2,112,512]{2,1,0:T(8,128)(2,1)S(1)}, bf16[2,112,512]{2,1,0:T(8,128)(2,1)S(1)}, u32[]{:S(2)}, u32[]{:S(2)}) collective-permute-start(bf16[2,112,512]{2,1,0:T(8,128)(2,1)S(1)} %get-tuple-element.35), channel_id=1, source_target_pairs={{0,128},{64,192},{128,0},{192,64},{256,384},{320,448},{384,256},{4... | collective-permute-start | bytes 688136 | tf_op jit(solution)/shard_map/ppermute | solution.py:203
  101.9 11.0 %collective-permute-start.5 = (bf16[2,112,512]{2,1,0:T(8,128)(2,1)S(1)}, bf16[2,112,512]{2,1,0:T(8,128)(2,1)S(1)}, u32[]{:S(2)}, u32[]{:S(2)}) collective-permute-start(bf16[2,112,512]{2,1,0:T(8,128)(2,1)S(1)} %get-tuple-element.36), channel_id=1, source_target_pairs={{0,192},{64,0},{128,64},{192,128},{256,448},{320,256},{384,320},{4... | collective-permute-start | bytes 688136 | tf_op jit(solution)/shard_map/ppermute | solution.py:203
  103.8 17.0 %collective-permute-start.8 = (bf16[256,896]{1,0:T(8,128)(2,1)S(1)}, bf16[256,896]{1,0:T(8,128)(2,1)S(1)}, u32[]{:S(2)}, u32[]{:S(2)}) collective-permute-start(bf16[256,896]{1,0:T(8,128)(2,1)S(1)} %get-tuple-element.41), channel_id=1, source_target_pairs={{0,1},{1,2},{2,3},{3,0},{4,5},{5,6},{6,7},{7,4},{8,9},{9,10},{10,1... | collective-permute-start | bytes 1376264 | tf_op jit(solution)/shard_map/ppermute | solution.py:203
  113.6 7.3 %collective-permute-start.7 = (bf16[2,112,512]{2,1,0:T(8,128)(2,1)S(1)}, bf16[2,112,512]{2,1,0:T(8,128)(2,1)S(1)}, u32[]{:S(2)}, u32[]{:S(2)}) collective-permute-start(bf16[2,112,512]{2,1,0:T(8,128)(2,1)S(1)} %get-tuple-element.39.held_ref), channel_id=1, source_target_pairs={{0,8},{4,12},{8,0},{12,4},{16,24},{20,28},{24,16},{28,20},{32,40},... | collective-permute-start | bytes 688136 | tf_op jit(solution)/shard_map/ppermute | solution.py:203
  117.0 24.1 %collective-permute-start.12 = (bf16[256,896]{1,0:T(8,128)(2,1)S(1)}, bf16[256,896]{1,0:T(8,128)(2,1)S(1)}, u32[]{:S(2)}, u32[]{:S(2)}) collective-permute-start(bf16[256,896]{1,0:T(8,128)(2,1)S(1)} %get-tuple-element.44), channel_id=1, source_target_pairs={{0,3},{1,0},{2,1},{3,2},{4,7},{5,4},{6,5},{7,6},{8,11},{9,8},{10,9... | collective-permute-start | bytes 1376264 | tf_op jit(solution)/shard_map/ppermute | solution.py:203
  121.5 28.8 %collective-permute-start.11 = (bf16[2,112,512]{2,1,0:T(8,128)(2,1)S(1)}, bf16[2,112,512]{2,1,0:T(8,128)(2,1)S(1)}, u32[]{:S(2)}, u32[]{:S(2)}) collective-permute-start(bf16[2,112,512]{2,1,0:T(8,128)(2,1)S(1)} %get-tuple-element.42.held_ref), channel_id=1, source_target_pairs={{0,48},{4,52},{8,56},{12,60},{16,32},{20,36},{24,40},{28,44},{32,1... | collective-permute-start | bytes 688136 | tf_op jit(solution)/shard_map/ppermute | solution.py:203
  131.5 20.6 %collective-permute-start.10 = (bf16[2,112,512]{2,1,0:T(8,128)(2,1)S(1)}, bf16[2,112,512]{2,1,0:T(8,128)(2,1)S(1)}, u32[]{:S(2)}, u32[]{:S(2)}) collective-permute-start(bf16[2,112,512]{2,1,0:T(8,128)(2,1)S(1)} %get-tuple-element.42.held_ref), channel_id=1, source_target_pairs={{0,32},{4,36},{8,40},{12,44},{16,48},{20,52},{24,56},{28,60},{32,0... | collective-permute-start | bytes 688136 | tf_op jit(solution)/shard_map/ppermute | solution.py:203
  139.2 20.1 %collective-permute-start.9 = (bf16[2,112,512]{2,1,0:T(8,128)(2,1)S(1)}, bf16[2,112,512]{2,1,0:T(8,128)(2,1)S(1)}, u32[]{:S(2)}, u32[]{:S(2)}) collective-permute-start(bf16[2,112,512]{2,1,0:T(8,128)(2,1)S(1)} %get-tuple-element.42.held_ref), channel_id=1, source_target_pairs={{0,16},{4,20},{8,24},{12,28},{16,0},{20,4},{24,8},{28,12},{32,48},... | collective-permute-start | bytes 688136 | tf_op jit(solution)/shard_map/ppermute | solution.py:203
  160.7 23.5 %all-to-all-start.1 = ((bf16[16,16,896]{2,1,0:T(8,128)(2,1)}), bf16[16,16,896]{2,1,0:T(8,128)(2,1)S(1)}, u32[]{:S(2)}, u32[]{:S(2)}) async-start(bf16[16,16,896]{2,1,0:T(8,128)(2,1)} %bitcast.13), calls=%async_computation.1 | async-start | bytes 917504 | tf_op jit(solution)/shard_map/all_to_all | solution.py:207
  167.0 12.0 %collective-permute-start.13 = (bf16[112,512]{1,0:T(8,128)(2,1)S(1)}, bf16[112,512]{1,0:T(8,128)(2,1)S(1)}, u32[]{:S(2)}, u32[]{:S(2)}) collective-permute-start(bf16[112,512]{1,0:T(8,128)(2,1)S(1)} %get-tuple-element.47), channel_id=1, source_target_pairs={{0,256},{64,320},{128,384},{192,448},{256,0},{320,64},{384,128},{4... | collective-permute-start | bytes 344072 | tf_op jit(solution)/shard_map/ppermute | solution.py:203
  179.0 3.8 %collective-permute-start.14 = (f32[112,512]{1,0:T(8,128)S(1)}, f32[112,512]{1,0:T(8,128)S(1)}, u32[]{:S(2)}, u32[]{:S(2)}) collective-permute-start(f32[112,512]{1,0:T(8,128)S(1)} %convert_add_fusion.mine_ref), channel_id=1, source_target_pairs={{0,4},{4,0},{8,12},{12,8},{16,20},{20,16},{24,28},{28,24},{32,36},... | collective-permute-start | bytes 688136 | tf_op jit(solution)/shard_map/ppermute | solution.py:203

commit v6 on v5

--- a/solution.py
+++ b/solution.py
@@ -32,14 +32,10 @@
 
 
 def block_body(
-    units_ref, q_ref, g_ref, ahead_ref, w_ref, x_ref, att_ref, dq_ref, grad, *refs
+    units_ref, q_ref, g_ref, ahead_ref, w_ref, x_ref, att_ref, dq_ref, grad, partial_ref, key, value, q_rows, g_rows, att, dq
 ):
-    p_refs = refs[:-7]
-    key, value, q_rows, g_rows, att, dq, spare = refs[-7:]
-    nbr = units_ref[units_ref.shape[0] - 1]
     tokens, width = q_ref.shape
     all_rows = x_ref.shape[0]
-    piece = PART // len(p_refs)
     heads = width // HEAD_DIM
     chunk = 4 * PART
     for c in range(all_rows // chunk):
@@ -80,12 +76,7 @@
     for c in range(all_rows // chunk):
         rows = pl.ds(c * chunk, chunk)
         term = dot(grad[0, rows, :], w_ref[0], NT) + dot(grad[1, rows, :], w_ref[1], NT)
-        spare[...] = term.astype(jnp.bfloat16)
-        for n, ref in enumerate(p_refs):
-            slot = lax.rem(nbr + n, len(p_refs))
-            for u in range(4):
-                at = pl.multiple_of(u * PART + slot * piece, piece)
-                ref[(c * 4 + u) * piece : (c * 4 + u + 1) * piece, :] = spare[pl.ds(at, piece), :]
+        partial_ref[rows, :] = term.astype(jnp.bfloat16)
 
 
 def low(*shape):
@@ -108,14 +99,13 @@
     )(place, *args)
 
 
-def block(slots, units_of, q, g, ahead, w, x):
+def block(units_of, q, g, ahead, w, x):
     tokens, width = q.shape
     all_rows, enc_width = x.shape
-    out_shape = [low(tokens, width), low(tokens, width), low(2, all_rows, width)]
-    out_shape += [low(all_rows // slots, enc_width)] * slots
+    out_shape = [low(tokens, width), low(tokens, width), low(2, all_rows, width), low(all_rows, enc_width)]
     scratch = [pltpu.VMEM((all_rows, width), jnp.bfloat16)] * 2
     scratch += [pltpu.VMEM((tokens, width), jnp.bfloat16)] * 2
-    scratch += [pltpu.VMEM((tokens, width), jnp.float32)] * 2 + [pltpu.VMEM((4 * PART, enc_width), jnp.bfloat16)]
+    scratch += [pltpu.VMEM((tokens, width), jnp.float32)] * 2
     return call(block_body, "block", out_shape, scratch, units_of, q, g, ahead, w, x)
 
 
@@ -132,62 +122,43 @@
     return call(body, "products", [low(enc_width, width), wide(enc_width, width)], [], place, x, grad)
 
 
-def cut(place, kept, away, att, dq, behind):
+def cut(place, kept, away):
     enc_width, width = kept.shape
     rows = enc_width // 8
 
-    def body(place_ref, kept_ref, away_ref, att_ref, dq_ref, behind_ref, own_ref, *refs):
-        send_refs, full_refs = refs[:3], refs[3:]
+    def body(place_ref, kept_ref, away_ref, own_ref, *send_refs):
         x = place_ref[1]
         for high in range(2):
             for k in range(4):
                 at = pl.multiple_of((high * 4 + lax.rem(x + k, 4)) * rows, 16)
-                term = kept_ref[pl.ds(at, rows), :] + away_ref[pl.ds(at, rows), :].astype(jnp.float32)
+                term = add(kept_ref[pl.ds(at, rows), :], away_ref[pl.ds(at, rows), :])
                 if k:
                     send_refs[k - 1][high] = term.astype(jnp.bfloat16)
                 else:
                     own_ref[high] = term
+
+    return call(body, "cut", [wide(2, rows, width)] + [low(2, rows, width)] * 3, [], place, kept, away)
+
+
+def y_pair(place, held, came, terms, att, dq, behind):
+    units, groups, piece, enc_width = terms.shape
+    width = att.shape[1]
+
+    def body(_, held_ref, came_ref, terms_ref, att_ref, dq_ref, behind_ref, both_ref, total_ref, *full_refs):
+        both_ref[...] = add(held_ref[...], came_ref[...]).astype(jnp.bfloat16)
+        for u in range(units):
+            total = add(terms_ref[u, 0], terms_ref[u, 1])
+            for n in range(2, groups):
+                total = add(total, terms_ref[u, n])
+            total_ref[u] = total.astype(jnp.bfloat16)
         lead = lax.broadcasted_iota(jnp.int32, (SPAN, width), 0) < LEAD
         for n, (ref, full) in enumerate(zip((att_ref, dq_ref), full_refs)):
             came = behind_ref[:, n * width : (n + 1) * width].astype(jnp.float32)
             full[:SPAN, :] = jnp.where(lead, came, ref[:SPAN, :].astype(jnp.float32)).astype(jnp.bfloat16)
             full[SPAN:, :] = ref[SPAN:, :]
 
-    out_shape = [wide(2, rows, width)] + [low(2, rows, width)] * 3 + [low(*att.shape)] * 2
-    return call(body, "cut", out_shape, [], place, kept, away, att, dq, behind)
-
-
-def x_sum(place, own, parts, partial, term):
-    def body(_, own_ref, *refs):
-        part_refs, partial_ref, term_ref, held_ref, acc_ref = refs[:3], *refs[3:]
-        total = own_ref[...]
-        for ref in part_refs:
-            total = total + ref[...].astype(jnp.float32)
-        held_ref[...] = total.astype(jnp.bfloat16)
-        acc_ref[...] = add(partial_ref[...], term_ref[...])
-
-    return call(body, "x_sum", [low(*own.shape), wide(*partial.shape)], [], place, own, *parts, partial, term)
-
-
-def y_pair(place, held, came, acc, term):
-    def body(_, held_ref, came_ref, acc_ref, term_ref, both_ref, out_ref):
-        both_ref[...] = add(held_ref[...], came_ref[...]).astype(jnp.bfloat16)
-        out_ref[...] = add(acc_ref[...], term_ref[...])
-
-    return call(body, "y_pair", [low(*held.shape), wide(*acc.shape)], [], place, held, came, acc, term)
-
-
-def fold(place, held, by, acc, term):
-    _, rows, width = held.shape
-
-    def body(place_ref, held_ref, a_ref, b_ref, c_ref, acc_ref, term_ref, mine_ref, other_ref, total_ref):
-        high = place_ref[2]
-        for ref, at in ((mine_ref, high), (other_ref, 1 - high)):
-            ref[...] = (add(held_ref[at], a_ref[at]) + add(b_ref[at], c_ref[at])).astype(ref.dtype)
-        total_ref[...] = add(acc_ref[...], term_ref[...]).astype(jnp.bfloat16)
-
-    out_shape = [wide(rows, width), low(rows, width), low(*acc.shape)]
-    return call(body, "fold", out_shape, [], place, held, *by, acc, term)
+    out_shape = [low(*held.shape), low(units, piece, enc_width), low(*att.shape), low(*dq.shape)]
+    return call(body, "y_pair", out_shape, [], place, held, came, terms, att, dq, behind)
 
 
 def join(place, mine, theirs):
@@ -203,8 +174,10 @@
     return lax.ppermute(x, axis, [(i, to(i)) for i in range(n) if 0 <= to(i) < n])
 
 
-def exchange(x, axes):
-    return lax.all_to_all(x, axes, split_axis=0, concat_axis=0, tiled=True)
+def exchange(x):
+    outer, inner, *rest = x.shape
+    x = lax.all_to_all(x.reshape(outer * inner, *rest), ("ctx", "nbr"), split_axis=0, concat_axis=0, tiled=True)
+    return x.reshape(outer, inner, *rest)
 
 
 def shards(queries, cotangent, encoded, kv_weight, neighbour_ids):
@@ -213,33 +186,33 @@
     groups = lax.axis_size("nbr")
     ctx = lax.axis_index("ctx")
     dp = lax.axis_index("dp")
-    nbr = lax.axis_index("nbr")
     place = jnp.stack((ctx % 2, dp % 4, dp // 4)).astype(jnp.int32)
 
     copies = jnp.broadcast_to(enc[:, None], (units, groups, piece, enc_width))
-    x = exchange(copies.reshape(units * groups, piece, enc_width), ("ctx", "nbr")).reshape(units * PART, enc_width)
+    x = exchange(copies).reshape(units * PART, enc_width)
 
     head = jnp.concatenate((q[:SPAN], g[:SPAN]), axis=1)
     ahead = permute(head, "ctx", lambda i: i - 1)
 
     unit_of = (neighbour_ids[0] // units).reshape(-1)
-    scalars = jnp.concatenate((unit_of, nbr[None])).astype(jnp.int32)
-    att, dq, grad, *partials = block(groups, scalars, q, g, ahead, kv_weight, x)
-
-    terms = [permute(partials[k], "nbr", lambda i, k=k: (i + k) % groups) for k in range(1, groups)]
-
-    sent, kept = products(place, x, grad)
-    away = permute(sent, "ctx", lambda i: i ^ 1)
+    att, dq, grad, partial = block(unit_of, q, g, ahead, kv_weight, x)
+
+    terms = exchange(partial.reshape(units, groups, piece, enc_width))
     tail = jnp.concatenate((att[:SPAN], dq[:SPAN]), axis=1)
     behind = permute(tail, "ctx", lambda i: i + 1)
-    own, *sends, attended, query_grad = cut(place, kept, away, att, dq, behind)
-    parts = [permute(sends[k - 1], "dp", lambda i, k=k: i // 4 * 4 + (i + k) % 4) for k in (1, 2, 3)]
-    held, acc = x_sum(place, own, parts, partials[0], terms[1])
-    held, acc = y_pair(place, held, permute(held, "ctx", lambda i: i ^ 2), acc, terms[0])
-    by = [permute(held, "ctx", lambda i, b=b: i ^ b) for b in (4, 8, 12)]
-    mine, other, total = fold(place, held, by, acc, terms[2])
-    encoded_grad = exchange(total.reshape(units, piece, enc_width), "ctx")
-    mine = add(mine, permute(other, "dp", lambda i: (i + 4) % 8))
+
+    sent, kept = products(place, x, grad)
+    held, *sends = cut(place, kept, permute(sent, "ctx", lambda i: i ^ 1))
+    for k in (1, 3, 2):
+        held = add(held, permute(sends[k - 1], "dp", lambda i, k=k: i // 4 * 4 + (i + k) % 4))
+    high = dp // 4
+    other = lax.dynamic_index_in_dim(held, 1 - high, 0, keepdims=False).astype(jnp.bfloat16)
+    mine = lax.dynamic_index_in_dim(held, high, 0, keepdims=False)
+    rows = add(mine, permute(other, "dp", lambda i: (i + 4) % 8)).astype(jnp.bfloat16)
+    came = permute(rows, "ctx", lambda i: i ^ 2)
+    rows, encoded_grad, attended, query_grad = y_pair(place, rows, came, terms, att, dq, behind)
+    by = [permute(rows, "ctx", lambda i, b=b: i ^ b) for b in (4, 8, 12)]
+    mine = add(rows, by[0]) + add(by[1], by[2])
     weight_grad = join(place, mine, permute(mine, "ctx", lambda i: i ^ 1))
     return (attended[None], query_grad[None], encoded_grad[None], weight_grad)
 

time: 186 us -> 172 us (0.925)
  the two profiles are of different devices: /device:TPU:15 before, /device:TPU:1 now
where the time goes in v6:
time: 172 us; the launch traced here: 171 us
  starting transfers between devices  77.7 us (45%)
  waiting for transfers between devices  63.9 us (37%)
  Pallas kernels  22.3 us (13%)
  local copies, waits for them, and re-layouts  5.03 us (3%)
    ppermute x12, waiting for transfers between devices, permute(): lax.ppermute(x, axis, [(i, to(i)) for i in range(n) if 0 <= to(i) < n])  61.7 us
    ppermute x12, starting transfers between devices, permute(): lax.ppermute(x, axis, [(i, to(i)) for i in range(n) if 0 <= to(i) < n])  56.2 us
    pallas_call x5, Pallas kernels, call(): pl.pallas_call(body, out_shape=out_shape, in_specs=[SMEM] + [VMEM] * len(...  22.3 us
    all_to_all x2, starting transfers between devices, exchange(): lax.all_to_all(x.reshape(outer * inner, *rest), ('ctx', 'nbr'), split_axi...  21.5 us
  transfers between devices with their start and end apart: 14, of which 9 were waited for; matrix products, arithmetic and copies ran while one was open for 1% of the time, Pallas kernels for 3%

profile of v6, /device:TPU:1, one launch (start us, length us, event | category | flops | bytes accessed | tf_op | source)
XLA Modules:
  0.0 171.3 jit_solution(3044965478061541178)
XLA Ops:
  0.6 2.4 %broadcast_in_dim.17 = bf16[16,4,16,896]{3,2,1,0:T(8,128)(2,1)} broadcast(bf16[16,16,896]{2,1,0:T(8,128)(2,1)} %bitcast.30), dimensions={0,2,3} | broadcast | bytes 2293760 | tf_op jit(solution)/shard_map/broadcast_in_dim | solution.py:191
  3.1 14.7 %all-to-all-start = ((bf16[64,16,896]{2,1,0:T(8,128)(2,1)}), bf16[64,16,896]{2,1,0:T(8,128)(2,1)S(1)}, u32[]{:S(2)}, u32[]{:S(2)}) async-start(bf16[64,16,896]{2,1,0:T(8,128)(2,1)} %bitcast.29), calls=%async_computation | async-start | bytes 3670016 | tf_op jit(solution)/shard_map/all_to_all | solution.py:179
  17.8 2.4 %collective-permute-start = (bf16[64,1024]{1,0:T(8,128)(2,1)S(1)}, bf16[64,1024]{1,0:T(8,128)(2,1)S(1)}, u32[]{:S(2)}, u32[]{:S(2)}) collective-permute-start(bf16[64,1024]{1,0:T(8,128)(2,1)S(1)} %pad_maximum_fusion), channel_id=1, source_target_pairs={{4,0},{8,4},{12,8},{16,12},{20,16},{24,20},{28,24},{32,28},{36,32}... | collective-permute-start | bytes 393224 | tf_op jit(solution)/shard_map/ppermute | solution.py:174
  20.3 40.7 %collective-permute-done.ahead_ref = bf16[64,1024]{1,0:T(8,128)(2,1)S(1)} collective-permute-done((bf16[64,1024]{1,0:T(8,128)(2,1)S(1)}, bf16[64,1024]{1,0:T(8,128)(2,1)S(1)}, u32[]{:S(2)}, u32[]{:S(2)}) %collective-permute-start) | collective-permute-done | bytes 131104 | tf_op jit(solution)/shard_map/ppermute | solution.py:174
  61.0 2.2 %all-to-all-done = bf16[64,16,896]{2,1,0:T(8,128)(2,1)S(1)} async-done(((bf16[64,16,896]{2,1,0:T(8,128)(2,1)}), bf16[64,16,896]{2,1,0:T(8,128)(2,1)S(1)}, u32[]{:S(2)}, u32[]{:S(2)}) %all-to-all-start) | async-done | bytes 1835040 | tf_op jit(solution)/shard_map/all_to_all | solution.py:179
  63.2 1.3 copy-done.3
  64.5 14.3 %block.1 = (bf16[256,512]{1,0:T(8,128)(2,1)S(1)}, bf16[256,512]{1,0:T(8,128)(2,1)S(1)}, bf16[2,1024,512]{2,1,0:T(8,128)(2,1)}, bf16[1024,896]{1,0:T(8,128)(2,1)S(1)}) custom-call(s32[16]{0:T(128)S(1)} %and_select_fusion.units_ref, bf16[256,512]{1,0:T(8,128)(2,1)S(1)} %bitcast.25, bf16[256,512]{1,0:T(8,128)(2,1)S(1)} %bitcast.26, ...), custom_call_target="tpu_custom_call" | custom-call | tf_op jit(solution)/shard_map/block/pallas_call | solution.py:91
  78.8 1.2 copy-done
  80.0 6.8 %all-to-all-start.1 = ((bf16[64,16,896]{2,1,0:T(8,128)(2,1)}), bf16[64,16,896]{2,1,0:T(8,128)(2,1)S(1)}, u32[]{:S(2)}, u32[]{:S(2)}) async-start(bf16[64,16,896]{2,1,0:T(8,128)(2,1)} %bitcast.24), calls=%async_computation.1 | async-start | bytes 3670016 | tf_op jit(solution)/shard_map/all_to_all | solution.py:179
  86.9 4.2 %products.1 = (bf16[896,512]{1,0:T(8,128)(2,1)S(1)}, f32[896,512]{1,0:T(8,128)S(1)}) custom-call(s32[3]{0:T(128)S(1)} %pad_add_fusion.place_ref._, bf16[1024,896]{1,0:T(8,128)(2,1)} %bitcast.28, bf16[2,1024,512]{2,1,0:T(8,128)(2,1)} %get-tuple-element.18.grad_ref), custom_call_target="tpu_custom_call" | custom-call | tf_op jit(solution)/shard_map/products/pallas_call | solution.py:91
  91.1 2.4 %collective-permute-start.1 = (bf16[896,512]{1,0:T(8,128)(2,1)S(1)}, bf16[896,512]{1,0:T(8,128)(2,1)S(1)}, u32[]{:S(2)}, u32[]{:S(2)}) collective-permute-start(bf16[896,512]{1,0:T(8,128)(2,1)S(1)} %get-tuple-element.20), channel_id=1, source_target_pairs={{0,4},{4,0},{8,12},{12,8},{16,20},{20,16},{24,28},{28,24},{32,36},... | collective-permute-start | bytes 2752520 | tf_op jit(solution)/shard_map/ppermute | solution.py:174
  93.5 2.1 %collective-permute-done.1.away_ref = bf16[896,512]{1,0:T(8,128)(2,1)S(1)} collective-permute-done((bf16[896,512]{1,0:T(8,128)(2,1)S(1)}, bf16[896,512]{1,0:T(8,128)(2,1)S(1)}, u32[]{:S(2)}, u32[]{:S(2)}) %collective-permute-start.1) | collective-permute-done | bytes 917536 | tf_op jit(solution)/shard_map/ppermute | solution.py:174
  95.6 0.7 cut.1
  96.3 3.1 %collective-permute-start.2 = (bf16[2,112,512]{2,1,0:T(8,128)(2,1)S(1)}, bf16[2,112,512]{2,1,0:T(8,128)(2,1)}, u32[]{:S(2)}, u32[]{:S(2)}) collective-permute-start(bf16[2,112,512]{2,1,0:T(8,128)(2,1)S(1)} %get-tuple-element.22), channel_id=1, source_target_pairs={{0,64},{64,128},{128,192},{192,0},{256,320},{320,384},{384,448},{4... | collective-permute-start | bytes 688136 | tf_op jit(solution)/shard_map/ppermute | solution.py:174
  99.5 3.4 %collective-permute-start.3 = (bf16[2,112,512]{2,1,0:T(8,128)(2,1)S(1)}, bf16[2,112,512]{2,1,0:T(8,128)(2,1)}, u32[]{:S(2)}, u32[]{:S(2)}) collective-permute-start(bf16[2,112,512]{2,1,0:T(8,128)(2,1)S(1)} %get-tuple-element.23), channel_id=1, source_target_pairs={{0,192},{64,0},{128,64},{192,128},{256,448},{320,256},{384,320},{4... | collective-permute-start | bytes 688136 | tf_op jit(solution)/shard_map/ppermute | solution.py:174
  102.8 3.4 %collective-permute-start.4 = (bf16[2,112,512]{2,1,0:T(8,128)(2,1)S(1)}, bf16[2,112,512]{2,1,0:T(8,128)(2,1)}, u32[]{:S(2)}, u32[]{:S(2)}) collective-permute-start(bf16[2,112,512]{2,1,0:T(8,128)(2,1)S(1)} %get-tuple-element.24), channel_id=1, source_target_pairs={{0,128},{64,192},{128,0},{192,64},{256,384},{320,448},{384,256},{4... | collective-permute-start | bytes 688136 | tf_op jit(solution)/shard_map/ppermute | solution.py:174
  106.4 1.6 collective-permute-done.3
  108.0 4.6 %collective-permute-done.4 = bf16[2,112,512]{2,1,0:T(8,128)(2,1)} collective-permute-done((bf16[2,112,512]{2,1,0:T(8,128)(2,1)S(1)}, bf16[2,112,512]{2,1,0:T(8,128)(2,1)}, u32[]{:S(2)}, u32[]{:S(2)}) %collective-permute-start.4) | collective-permute-done | bytes 229408 | tf_op jit(solution)/shard_map/ppermute | solution.py:174
  112.5 1.3 convert_add_fusion
  113.8 7.9 %collective-permute-start.5 = (bf16[112,512]{1,0:T(8,128)(2,1)S(1)}, bf16[112,512]{1,0:T(8,128)(2,1)S(1)}, u32[]{:S(2)}, u32[]{:S(2)}) collective-permute-start(bf16[112,512]{1,0:T(8,128)(2,1)S(1)} %fusion.1), channel_id=1, source_target_pairs={{0,256},{64,320},{128,384},{192,448},{256,0},{320,64},{384,128},{4... | collective-permute-start | bytes 344072 | tf_op jit(solution)/shard_map/ppermute | solution.py:174
  121.8 5.2 %collective-permute-start.7 = (bf16[64,1024]{1,0:T(8,128)(2,1)S(1)}, bf16[64,1024]{1,0:T(8,128)(2,1)S(1)}, u32[]{:S(2)}, u32[]{:S(2)}) collective-permute-start(bf16[64,1024]{1,0:T(8,128)(2,1)S(1)} %pad_maximum_fusion.1), channel_id=1, source_target_pairs={{0,4},{4,8},{8,12},{12,16},{16,20},{20,24},{24,28},{28,32},{32,36}... | collective-permute-start | bytes 393224 | tf_op jit(solution)/shard_map/ppermute | solution.py:174
  127.0 5.2 %collective-permute-done.5 = bf16[112,512]{1,0:T(8,128)(2,1)S(1)} collective-permute-done((bf16[112,512]{1,0:T(8,128)(2,1)S(1)}, bf16[112,512]{1,0:T(8,128)(2,1)S(1)}, u32[]{:S(2)}, u32[]{:S(2)}) %collective-permute-start.5) | collective-permute-done | bytes 114720 | tf_op jit(solution)/shard_map/ppermute | solution.py:174
  132.2 8.5 %collective-permute-start.6 = (bf16[112,512]{1,0:T(8,128)(2,1)S(1)}, bf16[112,512]{1,0:T(8,128)(2,1)S(1)}, u32[]{:S(2)}, u32[]{:S(2)}) collective-permute-start(bf16[112,512]{1,0:T(8,128)(2,1)S(1)} %fusion.held_ref), channel_id=1, source_target_pairs={{0,8},{4,12},{8,0},{12,4},{16,24},{20,28},{24,16},{28,20},{32,40},... | collective-permute-start | bytes 344072 | tf_op jit(solution)/shard_map/ppermute | solution.py:174
  140.8 2.2 %collective-permute-done.6.came_ref = bf16[112,512]{1,0:T(8,128)(2,1)S(1)} collective-permute-done((bf16[112,512]{1,0:T(8,128)(2,1)S(1)}, bf16[112,512]{1,0:T(8,128)(2,1)S(1)}, u32[]{:S(2)}, u32[]{:S(2)}) %collective-permute-start.6) | collective-permute-done | bytes 114720 | tf_op jit(solution)/shard_map/ppermute | solution.py:174
  142.9 1.6 y_pair.1
  144.6 3.5 %collective-permute-start.10 = (bf16[112,512]{1,0:T(8,128)(2,1)S(1)}, bf16[112,512]{1,0:T(8,128)(2,1)S(1)}, u32[]{:S(2)}, u32[]{:S(2)}) collective-permute-start(bf16[112,512]{1,0:T(8,128)(2,1)S(1)} %get-tuple-element.31), channel_id=1, source_target_pairs={{0,48},{4,52},{8,56},{12,60},{16,32},{20,36},{24,40},{28,44},{32,1... | collective-permute-start | bytes 344072 | tf_op jit(solution)/shard_map/ppermute | solution.py:174
  148.1 4.2 %collective-permute-start.8 = (bf16[112,512]{1,0:T(8,128)(2,1)S(1)}, bf16[112,512]{1,0:T(8,128)(2,1)S(1)}, u32[]{:S(2)}, u32[]{:S(2)}) collective-permute-start(bf16[112,512]{1,0:T(8,128)(2,1)S(1)} %get-tuple-element.31), channel_id=1, source_target_pairs={{0,16},{4,20},{8,24},{12,28},{16,0},{20,4},{24,8},{28,12},{32,48},... | collective-permute-start | bytes 344072 | tf_op jit(solution)/shard_map/ppermute | solution.py:174
  152.3 5.2 %collective-permute-start.9 = (bf16[112,512]{1,0:T(8,128)(2,1)S(1)}, bf16[112,512]{1,0:T(8,128)(2,1)S(1)}, u32[]{:S(2)}, u32[]{:S(2)}) collective-permute-start(bf16[112,512]{1,0:T(8,128)(2,1)S(1)} %get-tuple-element.31), channel_id=1, source_target_pairs={{0,32},{4,36},{8,40},{12,44},{16,48},{20,52},{24,56},{28,60},{32,0... | collective-permute-start | bytes 344072 | tf_op jit(solution)/shard_map/ppermute | solution.py:174
  157.5 4.3 %collective-permute-done.9 = bf16[112,512]{1,0:T(8,128)(2,1)S(1)} collective-permute-done((bf16[112,512]{1,0:T(8,128)(2,1)S(1)}, bf16[112,512]{1,0:T(8,128)(2,1)S(1)}, u32[]{:S(2)}, u32[]{:S(2)}) %collective-permute-start.9) | collective-permute-done | bytes 114720 | tf_op jit(solution)/shard_map/ppermute | solution.py:174
  161.9 6.9 %collective-permute-start.11 = (f32[112,512]{1,0:T(8,128)S(1)}, f32[112,512]{1,0:T(8,128)S(1)}, u32[]{:S(2)}, u32[]{:S(2)}) collective-permute-start(f32[112,512]{1,0:T(8,128)S(1)} %add_add_fusion.mine_ref), channel_id=1, source_target_pairs={{0,4},{4,0},{8,12},{12,8},{16,20},{20,16},{24,28},{28,24},{32,36},... | collective-permute-start | bytes 688136 | tf_op jit(solution)/shard_map/ppermute | solution.py:174
  168.8 1.1 collective-permute-done.11.theirs_ref
  169.9 1.3 join.1
  (24 shorter events, 0.4 us)
Async XLA Ops:
  3.0 14.7 %copy-start.1 = (bf16[1,256,512]{2,1,0:T(8,128)(2,1)S(1)}, bf16[1,256,512]{2,1,0:T(8,128)(2,1)}, u32[]{:S(2)}) copy-start(bf16[1,256,512]{2,1,0:T(8,128)(2,1)} %param.5) | copy-start | bytes 786436
  3.0 14.7 %copy-start.2 = (bf16[1,256,512]{2,1,0:T(8,128)(2,1)S(1)}, bf16[1,256,512]{2,1,0:T(8,128)(2,1)}, u32[]{:S(2)}) copy-start(bf16[1,256,512]{2,1,0:T(8,128)(2,1)} %param.6) | copy-start | bytes 786436
  3.0 17.2 %copy-start.4 = (s32[1,4,4]{2,1,0:T(4,128)S(1)}, s32[1,4,4]{2,1,0:T(4,128)}, u32[]{:S(2)}) copy-start(s32[1,4,4]{2,1,0:T(4,128)} %param.9) | copy-start | bytes 196
  3.1 60.1 %all-to-all-start = ((bf16[64,16,896]{2,1,0:T(8,128)(2,1)}), bf16[64,16,896]{2,1,0:T(8,128)(2,1)S(1)}, u32[]{:S(2)}, u32[]{:S(2)}) async-start(bf16[64,16,896]{2,1,0:T(8,128)(2,1)} %bitcast.29), calls=%async_computation | async-start | bytes 3670016 | tf_op jit(solution)/shard_map/all_to_all | solution.py:179
  17.8 43.1 %collective-permute-start = (bf16[64,1024]{1,0:T(8,128)(2,1)S(1)}, bf16[64,1024]{1,0:T(8,128)(2,1)S(1)}, u32[]{:S(2)}, u32[]{:S(2)}) collective-permute-start(bf16[64,1024]{1,0:T(8,128)(2,1)S(1)} %pad_maximum_fusion), channel_id=1, source_target_pairs={{4,0},{8,4},{12,8},{16,12},{20,16},{24,20},{28,24},{32,28},{36,32}... | collective-permute-start | bytes 393224 | tf_op jit(solution)/shard_map/ppermute | solution.py:174
  63.2 1.3 copy-start.3
  78.7 1.2 copy-start
  80.0 63.0 %all-to-all-start.1 = ((bf16[64,16,896]{2,1,0:T(8,128)(2,1)}), bf16[64,16,896]{2,1,0:T(8,128)(2,1)S(1)}, u32[]{:S(2)}, u32[]{:S(2)}) async-start(bf16[64,16,896]{2,1,0:T(8,128)(2,1)} %bitcast.24), calls=%async_computation.1 | async-start | bytes 3670016 | tf_op jit(solution)/shard_map/all_to_all | solution.py:179
  91.1 4.4 %collective-permute-start.1 = (bf16[896,512]{1,0:T(8,128)(2,1)S(1)}, bf16[896,512]{1,0:T(8,128)(2,1)S(1)}, u32[]{:S(2)}, u32[]{:S(2)}) collective-permute-start(bf16[896,512]{1,0:T(8,128)(2,1)S(1)} %get-tuple-element.20), channel_id=1, source_target_pairs={{0,4},{4,0},{8,12},{12,8},{16,20},{20,16},{24,28},{28,24},{32,36},... | collective-permute-start | bytes 2752520 | tf_op jit(solution)/shard_map/ppermute | solution.py:174
  96.3 10.0 %collective-permute-start.2 = (bf16[2,112,512]{2,1,0:T(8,128)(2,1)S(1)}, bf16[2,112,512]{2,1,0:T(8,128)(2,1)}, u32[]{:S(2)}, u32[]{:S(2)}) collective-permute-start(bf16[2,112,512]{2,1,0:T(8,128)(2,1)S(1)} %get-tuple-element.22), channel_id=1, source_target_pairs={{0,64},{64,128},{128,192},{192,0},{256,320},{320,384},{384,448},{4... | collective-permute-start | bytes 688136 | tf_op jit(solution)/shard_map/ppermute | solution.py:174
  99.5 8.5 %collective-permute-start.3 = (bf16[2,112,512]{2,1,0:T(8,128)(2,1)S(1)}, bf16[2,112,512]{2,1,0:T(8,128)(2,1)}, u32[]{:S(2)}, u32[]{:S(2)}) collective-permute-start(bf16[2,112,512]{2,1,0:T(8,128)(2,1)S(1)} %get-tuple-element.23), channel_id=1, source_target_pairs={{0,192},{64,0},{128,64},{192,128},{256,448},{320,256},{384,320},{4... | collective-permute-start | bytes 688136 | tf_op jit(solution)/shard_map/ppermute | solution.py:174
  102.8 9.7 %collective-permute-start.4 = (bf16[2,112,512]{2,1,0:T(8,128)(2,1)S(1)}, bf16[2,112,512]{2,1,0:T(8,128)(2,1)}, u32[]{:S(2)}, u32[]{:S(2)}) collective-permute-start(bf16[2,112,512]{2,1,0:T(8,128)(2,1)S(1)} %get-tuple-element.24), channel_id=1, source_target_pairs={{0,128},{64,192},{128,0},{192,64},{256,384},{320,448},{384,256},{4... | collective-permute-start | bytes 688136 | tf_op jit(solution)/shard_map/ppermute | solution.py:174
  113.8 18.4 %collective-permute-start.5 = (bf16[112,512]{1,0:T(8,128)(2,1)S(1)}, bf16[112,512]{1,0:T(8,128)(2,1)S(1)}, u32[]{:S(2)}, u32[]{:S(2)}) collective-permute-start(bf16[112,512]{1,0:T(8,128)(2,1)S(1)} %fusion.1), channel_id=1, source_target_pairs={{0,256},{64,320},{128,384},{192,448},{256,0},{320,64},{384,128},{4... | collective-permute-start | bytes 344072 | tf_op jit(solution)/shard_map/ppermute | solution.py:174
  121.8 19.0 %collective-permute-start.7 = (bf16[64,1024]{1,0:T(8,128)(2,1)S(1)}, bf16[64,1024]{1,0:T(8,128)(2,1)S(1)}, u32[]{:S(2)}, u32[]{:S(2)}) collective-permute-start(bf16[64,1024]{1,0:T(8,128)(2,1)S(1)} %pad_maximum_fusion.1), channel_id=1, source_target_pairs={{0,4},{4,8},{8,12},{12,16},{16,20},{20,24},{24,28},{28,32},{32,36}... | collective-permute-start | bytes 393224 | tf_op jit(solution)/shard_map/ppermute | solution.py:174
  132.2 10.7 %collective-permute-start.6 = (bf16[112,512]{1,0:T(8,128)(2,1)S(1)}, bf16[112,512]{1,0:T(8,128)(2,1)S(1)}, u32[]{:S(2)}, u32[]{:S(2)}) collective-permute-start(bf16[112,512]{1,0:T(8,128)(2,1)S(1)} %fusion.held_ref), channel_id=1, source_target_pairs={{0,8},{4,12},{8,0},{12,4},{16,24},{20,28},{24,16},{28,20},{32,40},... | collective-permute-start | bytes 344072 | tf_op jit(solution)/shard_map/ppermute | solution.py:174
  144.6 12.9 %collective-permute-start.10 = (bf16[112,512]{1,0:T(8,128)(2,1)S(1)}, bf16[112,512]{1,0:T(8,128)(2,1)S(1)}, u32[]{:S(2)}, u32[]{:S(2)}) collective-permute-start(bf16[112,512]{1,0:T(8,128)(2,1)S(1)} %get-tuple-element.31), channel_id=1, source_target_pairs={{0,48},{4,52},{8,56},{12,60},{16,32},{20,36},{24,40},{28,44},{32,1... | collective-permute-start | bytes 344072 | tf_op jit(solution)/shard_map/ppermute | solution.py:174
  148.1 9.4 %collective-permute-start.8 = (bf16[112,512]{1,0:T(8,128)(2,1)S(1)}, bf16[112,512]{1,0:T(8,128)(2,1)S(1)}, u32[]{:S(2)}, u32[]{:S(2)}) collective-permute-start(bf16[112,512]{1,0:T(8,128)(2,1)S(1)} %get-tuple-element.31), channel_id=1, source_target_pairs={{0,16},{4,20},{8,24},{12,28},{16,0},{20,4},{24,8},{28,12},{32,48},... | collective-permute-start | bytes 344072 | tf_op jit(solution)/shard_map/ppermute | solution.py:174
  152.3 9.5 %collective-permute-start.9 = (bf16[112,512]{1,0:T(8,128)(2,1)S(1)}, bf16[112,512]{1,0:T(8,128)(2,1)S(1)}, u32[]{:S(2)}, u32[]{:S(2)}) collective-permute-start(bf16[112,512]{1,0:T(8,128)(2,1)S(1)} %get-tuple-element.31), channel_id=1, source_target_pairs={{0,32},{4,36},{8,40},{12,44},{16,48},{20,52},{24,56},{28,60},{32,0... | collective-permute-start | bytes 344072 | tf_op jit(solution)/shard_map/ppermute | solution.py:174
  161.9 8.0 %collective-permute-start.11 = (f32[112,512]{1,0:T(8,128)S(1)}, f32[112,512]{1,0:T(8,128)S(1)}, u32[]{:S(2)}, u32[]{:S(2)}) collective-permute-start(f32[112,512]{1,0:T(8,128)S(1)} %add_add_fusion.mine_ref), channel_id=1, source_target_pairs={{0,4},{4,0},{8,12},{12,8},{16,20},{20,16},{24,28},{28,24},{32,36},... | collective-permute-start | bytes 688136 | tf_op jit(solution)/shard_map/ppermute | solution.py:174

commit v7 on v6

--- a/solution.py
+++ b/solution.py
@@ -17,6 +17,7 @@
 NN = (((1,), (0,)), ((), ()))
 VMEM = pl.BlockSpec(memory_space=pltpu.VMEM)
 SMEM = pl.BlockSpec(memory_space=pltpu.SMEM)
+HBM = pl.BlockSpec(memory_space=pl.ANY)
 PARAMS = pltpu.CompilerParams(vmem_limit_bytes=50 * 1024 * 1024)
 
 
@@ -32,51 +33,65 @@
 
 
 def block_body(
-    units_ref, q_ref, g_ref, ahead_ref, w_ref, x_ref, att_ref, dq_ref, grad, partial_ref, key, value, q_rows, g_rows, att, dq
+    units_ref, q_ref, g_ref, ahead_ref, w_ref, x_hbm, att_ref, dq_ref, tail_ref, grad_hbm, partial_hbm,
+    x, key, value, grad, partial, q_rows, g_rows, att, dq, x_sems, grad_sems, partial_sems,
 ):
     tokens, width = q_ref.shape
-    all_rows = x_ref.shape[0]
     heads = width // HEAD_DIM
     chunk = 4 * PART
-    for c in range(all_rows // chunk):
-        rows = pl.ds(c * chunk, chunk)
-        for kind, out in enumerate((key, value)):
-            out[rows, :] = dot(x_ref[rows, :], w_ref[kind], NN).astype(jnp.bfloat16)
-    for h in range(heads):
-        cols = pl.ds(h * HEAD_DIM, HEAD_DIM)
+    chunks = [pl.ds(c * chunk, chunk) for c in range(x.shape[0] // chunk)]
+    head_cols = [pl.ds(h * HEAD_DIM, HEAD_DIM) for h in range(heads)]
+    x_copies = [pltpu.make_async_copy(x_hbm.at[rows], x.at[rows], x_sems.at[c]) for c, rows in enumerate(chunks)]
+    for copy in x_copies:
+        copy.start()
+    for h, cols in enumerate(head_cols):
         q_rows[:, cols] = span_rows(q_ref[:, cols], ahead_ref[:, cols])
         g_rows[:, cols] = span_rows(g_ref[:, cols], ahead_ref[:, pl.ds(width + h * HEAD_DIM, HEAD_DIM)])
+    for copy, rows in zip(x_copies, chunks):
+        copy.wait()
+        for kind, out in enumerate((key, value)):
+            out[rows, :] = dot(x[rows, :], w_ref[kind], NN).astype(jnp.bfloat16)
     for j in range(tokens // SPAN):
         starts = [pl.multiple_of(units_ref[j * 4 + r] * PART, PART) for r in range(4)]
         rows = pl.ds(j * SPAN, SPAN)
-        for h in range(heads):
-            cols = pl.ds(h * HEAD_DIM, HEAD_DIM)
-            q = q_rows[rows, cols]
-            g = g_rows[rows, cols]
-            k = jnp.concatenate([key[pl.ds(s, PART), cols] for s in starts], axis=0)
-            v = jnp.concatenate([value[pl.ds(s, PART), cols] for s in starts], axis=0)
-            scores = dot(q, k, NT) * SCALE
-            raised = jnp.exp(scores - jnp.max(scores, axis=-1, keepdims=True))
-            weights = raised / jnp.sum(raised, axis=-1, keepdims=True)
-            low = weights.astype(jnp.bfloat16)
-            d_weights = dot(g, v, NT)
-            inner = jnp.sum(weights * d_weights, axis=-1, keepdims=True)
-            d_scores = (weights * (d_weights - inner) * SCALE).astype(jnp.bfloat16)
-            att[rows, cols] = dot(low, v, NN)
-            dq[rows, cols] = dot(d_scores, k, NN)
-            dk = dot(d_scores, q, TN).astype(jnp.bfloat16)
-            dv = dot(low, g, TN).astype(jnp.bfloat16)
+        qs = [q_rows[rows, cols] for cols in head_cols]
+        gs = [g_rows[rows, cols] for cols in head_cols]
+        ks = [jnp.concatenate([key[pl.ds(s, PART), cols] for s in starts], axis=0) for cols in head_cols]
+        vs = [jnp.concatenate([value[pl.ds(s, PART), cols] for s in starts], axis=0) for cols in head_cols]
+        scores = [dot(q, k, NT) * SCALE for q, k in zip(qs, ks)]
+        d_weights = [dot(g, v, NT) for g, v in zip(gs, vs)]
+        lows, d_scores = [], []
+        for s, dw in zip(scores, d_weights):
+            raised = jnp.exp(s - jnp.max(s, axis=-1, keepdims=True))
+            weights = raised * (1.0 / jnp.sum(raised, axis=-1, keepdims=True))
+            inner = jnp.sum(weights * dw, axis=-1, keepdims=True)
+            lows.append(weights.astype(jnp.bfloat16))
+            d_scores.append((weights * (dw - inner) * SCALE).astype(jnp.bfloat16))
+        for h, cols in enumerate(head_cols):
+            att[rows, cols] = dot(lows[h], vs[h], NN)
+            dq[rows, cols] = dot(d_scores[h], ks[h], NN)
+            dk = dot(d_scores[h], qs[h], TN).astype(jnp.bfloat16)
+            dv = dot(lows[h], gs[h], TN).astype(jnp.bfloat16)
             for r, s in enumerate(starts):
                 grad[0, pl.ds(s, PART), cols] = dk[r * PART : (r + 1) * PART]
                 grad[1, pl.ds(s, PART), cols] = dv[r * PART : (r + 1) * PART]
-    for h in range(heads):
-        cols = pl.ds(h * HEAD_DIM, HEAD_DIM)
+    grad_copies = [pltpu.make_async_copy(grad.at[n], grad_hbm.at[n], grad_sems.at[n]) for n in range(2)]
+    partial_copies = [
+        pltpu.make_async_copy(partial.at[rows], partial_hbm.at[rows], partial_sems.at[c]) for c, rows in enumerate(chunks)
+    ]
+    for copy in grad_copies:
+        copy.start()
+    for copy, rows in zip(partial_copies, chunks):
+        term = dot(grad[0, rows, :], w_ref[0], NT) + dot(grad[1, rows, :], w_ref[1], NT)
+        partial[rows, :] = term.astype(jnp.bfloat16)
+        copy.start()
+    for cols in head_cols:
         att_ref[:, cols] = pltpu.roll(att[:, cols], LEAD, 0).astype(jnp.bfloat16)
         dq_ref[:, cols] = pltpu.roll(dq[:, cols], LEAD, 0).astype(jnp.bfloat16)
-    for c in range(all_rows // chunk):
-        rows = pl.ds(c * chunk, chunk)
-        term = dot(grad[0, rows, :], w_ref[0], NT) + dot(grad[1, rows, :], w_ref[1], NT)
-        partial_ref[rows, :] = term.astype(jnp.bfloat16)
+    tail_ref[:, :width] = att_ref[:SPAN, :]
+    tail_ref[:, width:] = dq_ref[:SPAN, :]
+    for copy in grad_copies + partial_copies:
+        copy.wait()
 
 
 def low(*shape):
@@ -102,11 +117,20 @@
 def block(units_of, q, g, ahead, w, x):
     tokens, width = q.shape
     all_rows, enc_width = x.shape
-    out_shape = [low(tokens, width), low(tokens, width), low(2, all_rows, width), low(all_rows, enc_width)]
-    scratch = [pltpu.VMEM((all_rows, width), jnp.bfloat16)] * 2
-    scratch += [pltpu.VMEM((tokens, width), jnp.bfloat16)] * 2
-    scratch += [pltpu.VMEM((tokens, width), jnp.float32)] * 2
-    return call(block_body, "block", out_shape, scratch, units_of, q, g, ahead, w, x)
+    return pl.pallas_call(
+        block_body,
+        out_shape=[low(tokens, width), low(tokens, width), low(SPAN, 2 * width), low(2, all_rows, width), low(all_rows, enc_width)],
+        in_specs=[SMEM] + [VMEM] * 4 + [HBM],
+        out_specs=[VMEM] * 3 + [HBM] * 2,
+        scratch_shapes=[pltpu.VMEM((all_rows, enc_width), jnp.bfloat16)]
+        + [pltpu.VMEM((all_rows, width), jnp.bfloat16)] * 2
+        + [pltpu.VMEM((2, all_rows, width), jnp.bfloat16), pltpu.VMEM((all_rows, enc_width), jnp.bfloat16)]
+        + [pltpu.VMEM((tokens, width), jnp.bfloat16)] * 2
+        + [pltpu.VMEM((tokens, width), jnp.float32)] * 2
+        + [pltpu.SemaphoreType.DMA((4,)), pltpu.SemaphoreType.DMA((2,)), pltpu.SemaphoreType.DMA((4,))],
+        compiler_params=PARAMS,
+        name="block",
+    )(units_of, q, g, ahead, w, x)
 
 
 def products(place, x, grad):
@@ -140,12 +164,32 @@
     return call(body, "cut", [wide(2, rows, width)] + [low(2, rows, width)] * 3, [], place, kept, away)
 
 
-def y_pair(place, held, came, terms, att, dq, behind):
+def spread(x, groups):
+    units, piece, enc_width = x.shape
+
+    def body(x_ref, out_hbm, sems):
+        copies = [pltpu.make_async_copy(x_ref, out_hbm.at[:, n], sems.at[n]) for n in range(groups)]
+        for copy in copies:
+            copy.start()
+        for copy in copies:
+            copy.wait()
+
+    return pl.pallas_call(
+        body,
+        out_shape=low(units, groups, piece, enc_width),
+        in_specs=[VMEM],
+        out_specs=HBM,
+        scratch_shapes=[pltpu.SemaphoreType.DMA((groups,))],
+        compiler_params=PARAMS,
+        name="spread",
+    )(x)
+
+
+def gather_up(place, terms, att, dq, behind):
     units, groups, piece, enc_width = terms.shape
     width = att.shape[1]
 
-    def body(_, held_ref, came_ref, terms_ref, att_ref, dq_ref, behind_ref, both_ref, total_ref, *full_refs):
-        both_ref[...] = add(held_ref[...], came_ref[...]).astype(jnp.bfloat16)
+    def body(_, terms_ref, att_ref, dq_ref, behind_ref, total_ref, *full_refs):
         for u in range(units):
             total = add(terms_ref[u, 0], terms_ref[u, 1])
             for n in range(2, groups):
@@ -157,16 +201,37 @@
             full[:SPAN, :] = jnp.where(lead, came, ref[:SPAN, :].astype(jnp.float32)).astype(jnp.bfloat16)
             full[SPAN:, :] = ref[SPAN:, :]
 
-    out_shape = [low(*held.shape), low(units, piece, enc_width), low(*att.shape), low(*dq.shape)]
-    return call(body, "y_pair", out_shape, [], place, held, came, terms, att, dq, behind)
-
-
-def join(place, mine, theirs):
-    def body(place_ref, mine_ref, theirs_ref, out_ref):
+    out_shape = [low(units, piece, enc_width), low(*att.shape), low(*dq.shape)]
+    return call(body, "gather_up", out_shape, [], place, terms, att, dq, behind)
+
+
+def join(place, mine, theirs, after):
+    def body(place_ref, mine_ref, theirs_ref, _, out_ref):
         out_ref[place_ref[0]] = mine_ref[...]
         out_ref[1 - place_ref[0]] = theirs_ref[...]
 
-    return call(body, "join", wide(2, *mine.shape), [], place, mine, theirs)
+    return pl.pallas_call(
+        body,
+        out_shape=wide(2, *mine.shape),
+        in_specs=[SMEM, VMEM, VMEM, HBM],
+        out_specs=VMEM,
+        compiler_params=PARAMS,
+        name="join",
+    )(place, mine, theirs, after)
+
+
+def z_add(place, rows, came, after):
+    def body(_, rows_ref, came_ref, __, out_ref):
+        out_ref[...] = add(rows_ref[...], came_ref[...]).astype(jnp.bfloat16)
+
+    return pl.pallas_call(
+        body,
+        out_shape=low(*rows.shape),
+        in_specs=[SMEM, VMEM, VMEM, HBM],
+        out_specs=VMEM,
+        compiler_params=PARAMS,
+        name="z_add",
+    )(place, rows, came, after)
 
 
 def permute(x, axis, to):
@@ -188,17 +253,15 @@
     dp = lax.axis_index("dp")
     place = jnp.stack((ctx % 2, dp % 4, dp // 4)).astype(jnp.int32)
 
-    copies = jnp.broadcast_to(enc[:, None], (units, groups, piece, enc_width))
-    x = exchange(copies).reshape(units * PART, enc_width)
+    x = exchange(spread(enc, groups)).reshape(units * PART, enc_width)
 
     head = jnp.concatenate((q[:SPAN], g[:SPAN]), axis=1)
     ahead = permute(head, "ctx", lambda i: i - 1)
 
     unit_of = (neighbour_ids[0] // units).reshape(-1)
-    att, dq, grad, partial = block(unit_of, q, g, ahead, kv_weight, x)
+    att, dq, tail, grad, partial = block(unit_of, q, g, ahead, kv_weight, x)
 
     terms = exchange(partial.reshape(units, groups, piece, enc_width))
-    tail = jnp.concatenate((att[:SPAN], dq[:SPAN]), axis=1)
     behind = permute(tail, "ctx", lambda i: i + 1)
 
     sent, kept = products(place, x, grad)
@@ -208,12 +271,13 @@
     high = dp // 4
     other = lax.dynamic_index_in_dim(held, 1 - high, 0, keepdims=False).astype(jnp.bfloat16)
     mine = lax.dynamic_index_in_dim(held, high, 0, keepdims=False)
-    rows = add(mine, permute(other, "dp", lambda i: (i + 4) % 8)).astype(jnp.bfloat16)
-    came = permute(rows, "ctx", lambda i: i ^ 2)
-    rows, encoded_grad, attended, query_grad = y_pair(place, rows, came, terms, att, dq, behind)
-    by = [permute(rows, "ctx", lambda i, b=b: i ^ b) for b in (4, 8, 12)]
-    mine = add(rows, by[0]) + add(by[1], by[2])
-    weight_grad = join(place, mine, permute(mine, "ctx", lambda i: i ^ 1))
+    rows = z_add(place, mine, permute(other, "dp", lambda i: (i + 4) % 8), behind)
+    for bit in (2, 4, 8):
+        mine = add(rows, permute(rows, "ctx", lambda i, b=bit: i ^ b))
+        rows = mine.astype(jnp.bfloat16)
+    theirs = permute(mine, "ctx", lambda i: i ^ 1)
+    encoded_grad, attended, query_grad = gather_up(place, terms, att, dq, behind)
+    weight_grad = join(place, mine, theirs, encoded_grad)
     return (attended[None], query_grad[None], encoded_grad[None], weight_grad)
 
 

time: 172 us -> 173 us (level)
  starting transfers between devices: 77.7 us -> 73.1 us
  waiting for transfers between devices: 63.9 us -> 68.3 us
    pallas_call x0 -> x4, Pallas kernels: none -> 16 us  [the longest x1 12.8 us: block(): pl.pallas_call(block_body, out_shape=[low(tokens, width), low(tokens, wid...]
    pallas_call x5 -> x3, Pallas kernels: 22.3 us -> 7.29 us  [call(): pl.pallas_call(body, out_shape=out_shape, in_specs=[SMEM] + [VMEM] * len(...]
    ppermute x12 -> x11, starting transfers between devices: 56.2 us -> 51.6 us  [permute(): lax.ppermute(x, axis, [(i, to(i)) for i in range(n) if 0 <= to(i) < n])]
    ppermute x12 -> x11, waiting for transfers between devices: 61.7 us -> 66 us  [permute(): lax.ppermute(x, axis, [(i, to(i)) for i in range(n) if 0 <= to(i) < n])]
    broadcast_in_dim x1 -> x0, local copies, waits for them, and re-layouts: 2.41 us -> none  [shards(): copies = jnp.broadcast_to(enc[:, None], (units, groups, piece, enc_width))]
    unnamed x10 -> x14, local copies, waits for them, and re-layouts: 2.49 us -> 4.55 us
  transfers between devices with their start and end apart: 14 -> 13, of which waited for: 9 -> 10; matrix products, arithmetic and copies ran while one was open for 1% -> 1% of each run, Pallas kernels for 3% -> 5%
where the time goes in v7:
time: 173 us; the launch traced here: 172 us
  starting transfers between devices  73.1 us (42%)
  waiting for transfers between devices  68.3 us (39%)
  Pallas kernels  23.3 us (13%)
  local copies, waits for them, and re-layouts  4.7 us (3%)
    ppermute x11, waiting for transfers between devices, permute(): lax.ppermute(x, axis, [(i, to(i)) for i in range(n) if 0 <= to(i) < n])  66 us
    ppermute x11, starting transfers between devices, permute(): lax.ppermute(x, axis, [(i, to(i)) for i in range(n) if 0 <= to(i) < n])  51.6 us
    all_to_all x2, starting transfers between devices, exchange(): lax.all_to_all(x.reshape(outer * inner, *rest), ('ctx', 'nbr'), split_axi...  21.5 us
    pallas_call x1, Pallas kernels, block(): pl.pallas_call(block_body, out_shape=[low(tokens, width), low(tokens, wid...  12.8 us
    pallas_call x3, Pallas kernels, call(): pl.pallas_call(body, out_shape=out_shape, in_specs=[SMEM] + [VMEM] * len(...  7.29 us
    unnamed x14, local copies, waits for them, and re-layouts  4.55 us
  transfers between devices with their start and end apart: 13, of which 10 were waited for; matrix products, arithmetic and copies ran while one was open for 1% of the time, Pallas kernels for 5%

profile of v7, /device:TPU:1, one launch (start us, length us, event | category | flops | bytes accessed | tf_op | source)
XLA Modules:
  0.0 171.8 jit_solution(14104159415881838792)
XLA Ops:
  1.6 1.3 spread.1
  3.0 14.7 %all-to-all-start = ((bf16[64,16,896]{2,1,0:T(8,128)(2,1)}), bf16[64,16,896]{2,1,0:T(8,128)(2,1)S(1)}, u32[]{:S(2)}, u32[]{:S(2)}) async-start(bf16[64,16,896]{2,1,0:T(8,128)(2,1)} %bitcast.8), calls=%async_computation | async-start | bytes 3670016 | tf_op jit(solution)/shard_map/all_to_all | solution.py:244
  17.8 2.4 %collective-permute-start = (bf16[64,1024]{1,0:T(8,128)(2,1)S(1)}, bf16[64,1024]{1,0:T(8,128)(2,1)S(1)}, u32[]{:S(2)}, u32[]{:S(2)}) collective-permute-start(bf16[64,1024]{1,0:T(8,128)(2,1)S(1)} %pad_maximum_fusion), channel_id=1, source_target_pairs={{4,0},{8,4},{12,8},{16,12},{20,16},{24,20},{28,24},{32,28},{36,32}... | collective-permute-start | bytes 393224 | tf_op jit(solution)/shard_map/ppermute | solution.py:239
  20.2 40.7 %collective-permute-done.ahead_ref = bf16[64,1024]{1,0:T(8,128)(2,1)S(1)} collective-permute-done((bf16[64,1024]{1,0:T(8,128)(2,1)S(1)}, bf16[64,1024]{1,0:T(8,128)(2,1)S(1)}, u32[]{:S(2)}, u32[]{:S(2)}) %collective-permute-start) | collective-permute-done | bytes 131104 | tf_op jit(solution)/shard_map/ppermute | solution.py:239
  60.9 2.2 %all-to-all-done = bf16[64,16,896]{2,1,0:T(8,128)(2,1)S(1)} async-done(((bf16[64,16,896]{2,1,0:T(8,128)(2,1)}), bf16[64,16,896]{2,1,0:T(8,128)(2,1)S(1)}, u32[]{:S(2)}, u32[]{:S(2)}) %all-to-all-start) | async-done | bytes 1835040 | tf_op jit(solution)/shard_map/all_to_all | solution.py:244
  63.1 1.3 copy-done.5
  64.4 12.8 %block.1 = (bf16[256,512]{1,0:T(8,128)(2,1)S(1)}, bf16[256,512]{1,0:T(8,128)(2,1)S(1)}, bf16[64,1024]{1,0:T(8,128)(2,1)S(1)}, bf16[2,1024,512]{2,1,0:T(8,128)(2,1)}, bf16[1024,896]{1,0:T(8,128)(2,1)S(1)}) custom-call(s32[16]{0:T(128)S(1)} %and_select_fusion.units_ref, bf16[256,512]{1,0:T(8,128)(2,1)S(1)} %bitcast.25, bf16[256,512]{1,0:T(8,128)(2,1)S(1)} %bitcast.26, ...), custom_call_target="tpu_custom_call" | custom-call | tf_op jit(solution)/shard_map/block/pallas_call | solution.py:120
  77.2 1.2 copy-done
  78.5 6.8 %all-to-all-start.1 = ((bf16[64,16,896]{2,1,0:T(8,128)(2,1)}), bf16[64,16,896]{2,1,0:T(8,128)(2,1)S(1)}, u32[]{:S(2)}, u32[]{:S(2)}) async-start(bf16[64,16,896]{2,1,0:T(8,128)(2,1)} %bitcast.22), calls=%async_computation.1 | async-start | bytes 3670016 | tf_op jit(solution)/shard_map/all_to_all | solution.py:244
  85.4 4.2 %products.1 = (bf16[896,512]{1,0:T(8,128)(2,1)S(1)}, f32[896,512]{1,0:T(8,128)S(1)}) custom-call(s32[3]{0:T(128)S(1)} %pad_add_fusion._.place_ref, bf16[1024,896]{1,0:T(8,128)(2,1)} %bitcast.28, bf16[2,1024,512]{2,1,0:T(8,128)(2,1)} %get-tuple-element.25.grad_ref), custom_call_target="tpu_custom_call" | custom-call | tf_op jit(solution)/shard_map/products/pallas_call | solution.py:106
  89.6 2.4 %collective-permute-start.2 = (bf16[896,512]{1,0:T(8,128)(2,1)S(1)}, bf16[896,512]{1,0:T(8,128)(2,1)S(1)}, u32[]{:S(2)}, u32[]{:S(2)}) collective-permute-start(bf16[896,512]{1,0:T(8,128)(2,1)S(1)} %get-tuple-element.27), channel_id=1, source_target_pairs={{0,4},{4,0},{8,12},{12,8},{16,20},{20,16},{24,28},{28,24},{32,36},... | collective-permute-start | bytes 2752520 | tf_op jit(solution)/shard_map/ppermute | solution.py:239
  92.0 2.1 %collective-permute-done.2.away_ref = bf16[896,512]{1,0:T(8,128)(2,1)S(1)} collective-permute-done((bf16[896,512]{1,0:T(8,128)(2,1)S(1)}, bf16[896,512]{1,0:T(8,128)(2,1)S(1)}, u32[]{:S(2)}, u32[]{:S(2)}) %collective-permute-start.2) | collective-permute-done | bytes 917536 | tf_op jit(solution)/shard_map/ppermute | solution.py:239
  94.1 1.4 cut.1
  95.5 4.6 %collective-permute-start.5 = (bf16[2,112,512]{2,1,0:T(8,128)(2,1)}, bf16[2,112,512]{2,1,0:T(8,128)(2,1)}, u32[]{:S(2)}, u32[]{:S(2)}) collective-permute-start(bf16[2,112,512]{2,1,0:T(8,128)(2,1)} %get-tuple-element.31), channel_id=1, source_target_pairs={{0,128},{64,192},{128,0},{192,64},{256,384},{320,448},{384,256},{4... | collective-permute-start | bytes 688136 | tf_op jit(solution)/shard_map/ppermute | solution.py:239
  100.1 2.8 %collective-permute-start.4 = (bf16[2,112,512]{2,1,0:T(8,128)(2,1)S(1)}, bf16[2,112,512]{2,1,0:T(8,128)(2,1)}, u32[]{:S(2)}, u32[]{:S(2)}) collective-permute-start(bf16[2,112,512]{2,1,0:T(8,128)(2,1)S(1)} %get-tuple-element.30), channel_id=1, source_target_pairs={{0,192},{64,0},{128,64},{192,128},{256,448},{320,256},{384,320},{4... | collective-permute-start | bytes 688136 | tf_op jit(solution)/shard_map/ppermute | solution.py:239
  102.9 2.5 %collective-permute-start.3 = (bf16[2,112,512]{2,1,0:T(8,128)(2,1)S(1)}, bf16[2,112,512]{2,1,0:T(8,128)(2,1)}, u32[]{:S(2)}, u32[]{:S(2)}) collective-permute-start(bf16[2,112,512]{2,1,0:T(8,128)(2,1)S(1)} %get-tuple-element.29), channel_id=1, source_target_pairs={{0,64},{64,128},{128,192},{192,0},{256,320},{320,384},{384,448},{4... | collective-permute-start | bytes 688136 | tf_op jit(solution)/shard_map/ppermute | solution.py:239
  105.4 4.3 %collective-permute-start.1 = (bf16[64,1024]{1,0:T(8,128)(2,1)S(1)}, bf16[64,1024]{1,0:T(8,128)(2,1)S(1)}, u32[]{:S(2)}, u32[]{:S(2)}) collective-permute-start(bf16[64,1024]{1,0:T(8,128)(2,1)S(1)} %get-tuple-element.21), channel_id=1, source_target_pairs={{0,4},{4,8},{8,12},{12,16},{16,20},{20,24},{24,28},{28,32},{32,36}... | collective-permute-start | bytes 393224 | tf_op jit(solution)/shard_map/ppermute | solution.py:239
  109.7 1.3 collective-permute-done.4
  111.0 1.3 collective-permute-done.3
  112.3 1.3 convert_add_fusion
  113.6 7.9 %collective-permute-start.6 = (bf16[112,512]{1,0:T(8,128)(2,1)S(1)}, bf16[112,512]{1,0:T(8,128)(2,1)S(1)}, u32[]{:S(2)}, u32[]{:S(2)}) collective-permute-start(bf16[112,512]{1,0:T(8,128)(2,1)S(1)} %fusion), channel_id=1, source_target_pairs={{0,256},{64,320},{128,384},{192,448},{256,0},{320,64},{384,128},{4... | collective-permute-start | bytes 344072 | tf_op jit(solution)/shard_map/ppermute | solution.py:239
  121.6 4.1 %collective-permute-done.1.behind_ref.__ = bf16[64,1024]{1,0:T(8,128)(2,1)S(1)} collective-permute-done((bf16[64,1024]{1,0:T(8,128)(2,1)S(1)}, bf16[64,1024]{1,0:T(8,128)(2,1)S(1)}, u32[]{:S(2)}, u32[]{:S(2)}) %collective-permute-start.1) | collective-permute-done | bytes 131104 | tf_op jit(solution)/shard_map/ppermute | solution.py:239
  125.7 3.7 %collective-permute-done.6.came_ref = bf16[112,512]{1,0:T(8,128)(2,1)S(1)} collective-permute-done((bf16[112,512]{1,0:T(8,128)(2,1)S(1)}, bf16[112,512]{1,0:T(8,128)(2,1)S(1)}, u32[]{:S(2)}, u32[]{:S(2)}) %collective-permute-start.6) | collective-permute-done | bytes 114720 | tf_op jit(solution)/shard_map/ppermute | solution.py:239
  130.0 9.7 %collective-permute-start.7 = (bf16[112,512]{1,0:T(8,128)(2,1)S(1)}, bf16[112,512]{1,0:T(8,128)(2,1)S(1)}, u32[]{:S(2)}, u32[]{:S(2)}) collective-permute-start(bf16[112,512]{1,0:T(8,128)(2,1)S(1)} %z_add.1), channel_id=1, source_target_pairs={{0,8},{4,12},{8,0},{12,4},{16,24},{20,28},{24,16},{28,20},{32,40},... | collective-permute-start | bytes 344072 | tf_op jit(solution)/shard_map/ppermute | solution.py:239
  139.7 2.2 %collective-permute-done.7 = bf16[112,512]{1,0:T(8,128)(2,1)S(1)} collective-permute-done((bf16[112,512]{1,0:T(8,128)(2,1)S(1)}, bf16[112,512]{1,0:T(8,128)(2,1)S(1)}, u32[]{:S(2)}, u32[]{:S(2)}) %collective-permute-start.7) | collective-permute-done | bytes 114720 | tf_op jit(solution)/shard_map/ppermute | solution.py:239
  141.9 5.7 %collective-permute-start.8 = (bf16[112,512]{1,0:T(8,128)(2,1)S(1)}, bf16[112,512]{1,0:T(8,128)(2,1)S(1)}, u32[]{:S(2)}, u32[]{:S(2)}) collective-permute-start(bf16[112,512]{1,0:T(8,128)(2,1)S(1)} %add_convert_fusion.1), channel_id=1, source_target_pairs={{0,16},{4,20},{8,24},{12,28},{16,0},{20,4},{24,8},{28,12},{32,48},... | collective-permute-start | bytes 344072 | tf_op jit(solution)/shard_map/ppermute | solution.py:239
  147.6 4.0 %collective-permute-done.8 = bf16[112,512]{1,0:T(8,128)(2,1)S(1)} collective-permute-done((bf16[112,512]{1,0:T(8,128)(2,1)S(1)}, bf16[112,512]{1,0:T(8,128)(2,1)S(1)}, u32[]{:S(2)}, u32[]{:S(2)}) %collective-permute-start.8) | collective-permute-done | bytes 114720 | tf_op jit(solution)/shard_map/ppermute | solution.py:239
  151.6 3.0 %collective-permute-start.9 = (bf16[112,512]{1,0:T(8,128)(2,1)S(1)}, bf16[112,512]{1,0:T(8,128)(2,1)S(1)}, u32[]{:S(2)}, u32[]{:S(2)}) collective-permute-start(bf16[112,512]{1,0:T(8,128)(2,1)S(1)} %add_convert_fusion), channel_id=1, source_target_pairs={{0,32},{4,36},{8,40},{12,44},{16,48},{20,52},{24,56},{28,60},{32,0... | collective-permute-start | bytes 344072 | tf_op jit(solution)/shard_map/ppermute | solution.py:239
  154.6 6.7 %collective-permute-done.9 = bf16[112,512]{1,0:T(8,128)(2,1)S(1)} collective-permute-done((bf16[112,512]{1,0:T(8,128)(2,1)S(1)}, bf16[112,512]{1,0:T(8,128)(2,1)S(1)}, u32[]{:S(2)}, u32[]{:S(2)}) %collective-permute-start.9) | collective-permute-done | bytes 114720 | tf_op jit(solution)/shard_map/ppermute | solution.py:239
  161.4 6.4 %collective-permute-start.10 = (f32[112,512]{1,0:T(8,128)S(1)}, f32[112,512]{1,0:T(8,128)S(1)}, u32[]{:S(2)}, u32[]{:S(2)}) collective-permute-start(f32[112,512]{1,0:T(8,128)S(1)} %convert_add_fusion.1.mine_ref), channel_id=1, source_target_pairs={{0,4},{4,0},{8,12},{12,8},{16,20},{20,16},{24,28},{28,24},{32,36},... | collective-permute-start | bytes 688136 | tf_op jit(solution)/shard_map/ppermute | solution.py:239
  167.8 1.6 gather_up.1
  170.4 1.3 join.1
  (26 shorter events, 3.0 us)
Async XLA Ops:
  0.6 1.0 copy-start.2
  2.9 14.8 %copy-start.3 = (bf16[1,256,512]{2,1,0:T(8,128)(2,1)S(1)}, bf16[1,256,512]{2,1,0:T(8,128)(2,1)}, u32[]{:S(2)}) copy-start(bf16[1,256,512]{2,1,0:T(8,128)(2,1)} %param.5) | copy-start | bytes 786436
  3.0 14.8 %copy-start.4 = (bf16[1,256,512]{2,1,0:T(8,128)(2,1)S(1)}, bf16[1,256,512]{2,1,0:T(8,128)(2,1)}, u32[]{:S(2)}) copy-start(bf16[1,256,512]{2,1,0:T(8,128)(2,1)} %param.6) | copy-start | bytes 786436
  3.0 17.2 %copy-start.6 = (s32[1,4,4]{2,1,0:T(4,128)S(1)}, s32[1,4,4]{2,1,0:T(4,128)}, u32[]{:S(2)}) copy-start(s32[1,4,4]{2,1,0:T(4,128)} %param.9) | copy-start | bytes 196
  3.0 60.2 %all-to-all-start = ((bf16[64,16,896]{2,1,0:T(8,128)(2,1)}), bf16[64,16,896]{2,1,0:T(8,128)(2,1)S(1)}, u32[]{:S(2)}, u32[]{:S(2)}) async-start(bf16[64,16,896]{2,1,0:T(8,128)(2,1)} %bitcast.8), calls=%async_computation | async-start | bytes 3670016 | tf_op jit(solution)/shard_map/all_to_all | solution.py:244
  17.8 43.1 %collective-permute-start = (bf16[64,1024]{1,0:T(8,128)(2,1)S(1)}, bf16[64,1024]{1,0:T(8,128)(2,1)S(1)}, u32[]{:S(2)}, u32[]{:S(2)}) collective-permute-start(bf16[64,1024]{1,0:T(8,128)(2,1)S(1)} %pad_maximum_fusion), channel_id=1, source_target_pairs={{4,0},{8,4},{12,8},{16,12},{20,16},{24,20},{28,24},{32,28},{36,32}... | collective-permute-start | bytes 393224 | tf_op jit(solution)/shard_map/ppermute | solution.py:239
  63.1 1.3 copy-start.5
  77.2 1.2 copy-start
  78.5 89.3 %all-to-all-start.1 = ((bf16[64,16,896]{2,1,0:T(8,128)(2,1)}), bf16[64,16,896]{2,1,0:T(8,128)(2,1)S(1)}, u32[]{:S(2)}, u32[]{:S(2)}) async-start(bf16[64,16,896]{2,1,0:T(8,128)(2,1)} %bitcast.22), calls=%async_computation.1 | async-start | bytes 3670016 | tf_op jit(solution)/shard_map/all_to_all | solution.py:244
  89.6 4.5 %collective-permute-start.2 = (bf16[896,512]{1,0:T(8,128)(2,1)S(1)}, bf16[896,512]{1,0:T(8,128)(2,1)S(1)}, u32[]{:S(2)}, u32[]{:S(2)}) collective-permute-start(bf16[896,512]{1,0:T(8,128)(2,1)S(1)} %get-tuple-element.27), channel_id=1, source_target_pairs={{0,4},{4,0},{8,12},{12,8},{16,20},{20,16},{24,28},{28,24},{32,36},... | collective-permute-start | bytes 2752520 | tf_op jit(solution)/shard_map/ppermute | solution.py:239
  95.5 14.3 %collective-permute-start.5 = (bf16[2,112,512]{2,1,0:T(8,128)(2,1)}, bf16[2,112,512]{2,1,0:T(8,128)(2,1)}, u32[]{:S(2)}, u32[]{:S(2)}) collective-permute-start(bf16[2,112,512]{2,1,0:T(8,128)(2,1)} %get-tuple-element.31), channel_id=1, source_target_pairs={{0,128},{64,192},{128,0},{192,64},{256,384},{320,448},{384,256},{4... | collective-permute-start | bytes 688136 | tf_op jit(solution)/shard_map/ppermute | solution.py:239
  100.1 10.9 %collective-permute-start.4 = (bf16[2,112,512]{2,1,0:T(8,128)(2,1)S(1)}, bf16[2,112,512]{2,1,0:T(8,128)(2,1)}, u32[]{:S(2)}, u32[]{:S(2)}) collective-permute-start(bf16[2,112,512]{2,1,0:T(8,128)(2,1)S(1)} %get-tuple-element.30), channel_id=1, source_target_pairs={{0,192},{64,0},{128,64},{192,128},{256,448},{320,256},{384,320},{4... | collective-permute-start | bytes 688136 | tf_op jit(solution)/shard_map/ppermute | solution.py:239
  102.9 9.4 %collective-permute-start.3 = (bf16[2,112,512]{2,1,0:T(8,128)(2,1)S(1)}, bf16[2,112,512]{2,1,0:T(8,128)(2,1)}, u32[]{:S(2)}, u32[]{:S(2)}) collective-permute-start(bf16[2,112,512]{2,1,0:T(8,128)(2,1)S(1)} %get-tuple-element.29), channel_id=1, source_target_pairs={{0,64},{64,128},{128,192},{192,0},{256,320},{320,384},{384,448},{4... | collective-permute-start | bytes 688136 | tf_op jit(solution)/shard_map/ppermute | solution.py:239
  105.4 20.3 %collective-permute-start.1 = (bf16[64,1024]{1,0:T(8,128)(2,1)S(1)}, bf16[64,1024]{1,0:T(8,128)(2,1)S(1)}, u32[]{:S(2)}, u32[]{:S(2)}) collective-permute-start(bf16[64,1024]{1,0:T(8,128)(2,1)S(1)} %get-tuple-element.21), channel_id=1, source_target_pairs={{0,4},{4,8},{8,12},{12,16},{16,20},{20,24},{24,28},{28,32},{32,36}... | collective-permute-start | bytes 393224 | tf_op jit(solution)/shard_map/ppermute | solution.py:239
  113.6 15.9 %collective-permute-start.6 = (bf16[112,512]{1,0:T(8,128)(2,1)S(1)}, bf16[112,512]{1,0:T(8,128)(2,1)S(1)}, u32[]{:S(2)}, u32[]{:S(2)}) collective-permute-start(bf16[112,512]{1,0:T(8,128)(2,1)S(1)} %fusion), channel_id=1, source_target_pairs={{0,256},{64,320},{128,384},{192,448},{256,0},{320,64},{384,128},{4... | collective-permute-start | bytes 344072 | tf_op jit(solution)/shard_map/ppermute | solution.py:239
  130.0 11.8 %collective-permute-start.7 = (bf16[112,512]{1,0:T(8,128)(2,1)S(1)}, bf16[112,512]{1,0:T(8,128)(2,1)S(1)}, u32[]{:S(2)}, u32[]{:S(2)}) collective-permute-start(bf16[112,512]{1,0:T(8,128)(2,1)S(1)} %z_add.1), channel_id=1, source_target_pairs={{0,8},{4,12},{8,0},{12,4},{16,24},{20,28},{24,16},{28,20},{32,40},... | collective-permute-start | bytes 344072 | tf_op jit(solution)/shard_map/ppermute | solution.py:239
  141.9 9.7 %collective-permute-start.8 = (bf16[112,512]{1,0:T(8,128)(2,1)S(1)}, bf16[112,512]{1,0:T(8,128)(2,1)S(1)}, u32[]{:S(2)}, u32[]{:S(2)}) collective-permute-start(bf16[112,512]{1,0:T(8,128)(2,1)S(1)} %add_convert_fusion.1), channel_id=1, source_target_pairs={{0,16},{4,20},{8,24},{12,28},{16,0},{20,4},{24,8},{28,12},{32,48},... | collective-permute-start | bytes 344072 | tf_op jit(solution)/shard_map/ppermute | solution.py:239
  151.6 9.7 %collective-permute-start.9 = (bf16[112,512]{1,0:T(8,128)(2,1)S(1)}, bf16[112,512]{1,0:T(8,128)(2,1)S(1)}, u32[]{:S(2)}, u32[]{:S(2)}) collective-permute-start(bf16[112,512]{1,0:T(8,128)(2,1)S(1)} %add_convert_fusion), channel_id=1, source_target_pairs={{0,32},{4,36},{8,40},{12,44},{16,48},{20,52},{24,56},{28,60},{32,0... | collective-permute-start | bytes 344072 | tf_op jit(solution)/shard_map/ppermute | solution.py:239
  161.4 8.0 %collective-permute-start.10 = (f32[112,512]{1,0:T(8,128)S(1)}, f32[112,512]{1,0:T(8,128)S(1)}, u32[]{:S(2)}, u32[]{:S(2)}) collective-permute-start(f32[112,512]{1,0:T(8,128)S(1)} %convert_add_fusion.1.mine_ref), channel_id=1, source_target_pairs={{0,4},{4,0},{8,12},{12,8},{16,20},{20,16},{24,28},{28,24},{32,36},... | collective-permute-start | bytes 688136 | tf_op jit(solution)/shard_map/ppermute | solution.py:239
  169.4 1.0 copy-start.1

commit v8 on v7

--- a/solution.py
+++ b/solution.py
@@ -17,7 +17,7 @@
 NN = (((1,), (0,)), ((), ()))
 VMEM = pl.BlockSpec(memory_space=pltpu.VMEM)
 SMEM = pl.BlockSpec(memory_space=pltpu.SMEM)
-HBM = pl.BlockSpec(memory_space=pl.ANY)
+HBM = pl.BlockSpec(memory_space=pltpu.HBM)
 PARAMS = pltpu.CompilerParams(vmem_limit_bytes=50 * 1024 * 1024)
 
 
@@ -76,15 +76,17 @@
                 grad[0, pl.ds(s, PART), cols] = dk[r * PART : (r + 1) * PART]
                 grad[1, pl.ds(s, PART), cols] = dv[r * PART : (r + 1) * PART]
     grad_copies = [pltpu.make_async_copy(grad.at[n], grad_hbm.at[n], grad_sems.at[n]) for n in range(2)]
-    partial_copies = [
-        pltpu.make_async_copy(partial.at[rows], partial_hbm.at[rows], partial_sems.at[c]) for c, rows in enumerate(chunks)
-    ]
     for copy in grad_copies:
         copy.start()
-    for copy, rows in zip(partial_copies, chunks):
+    partial_copies = []
+    for c, rows in enumerate(chunks):
         term = dot(grad[0, rows, :], w_ref[0], NT) + dot(grad[1, rows, :], w_ref[1], NT)
-        partial[rows, :] = term.astype(jnp.bfloat16)
-        copy.start()
+        units = pl.ds(c * 4, 4)
+        partial[units] = term.astype(jnp.bfloat16).reshape(4, *partial.shape[1:])
+        for n in range(partial.shape[1]):
+            copy = pltpu.make_async_copy(partial.at[units, n], partial_hbm.at[n, units], partial_sems.at[c, n])
+            copy.start()
+            partial_copies.append(copy)
     for cols in head_cols:
         att_ref[:, cols] = pltpu.roll(att[:, cols], LEAD, 0).astype(jnp.bfloat16)
         dq_ref[:, cols] = pltpu.roll(dq[:, cols], LEAD, 0).astype(jnp.bfloat16)
@@ -114,20 +116,21 @@
     )(place, *args)
 
 
-def block(units_of, q, g, ahead, w, x):
+def block(units_of, q, g, ahead, w, x, slices):
     tokens, width = q.shape
     all_rows, enc_width = x.shape
+    units, piece = all_rows // PART, PART // slices
     return pl.pallas_call(
         block_body,
-        out_shape=[low(tokens, width), low(tokens, width), low(SPAN, 2 * width), low(2, all_rows, width), low(all_rows, enc_width)],
+        out_shape=[low(tokens, width), low(tokens, width), low(SPAN, 2 * width), low(2, all_rows, width), low(slices, units, piece, enc_width)],
         in_specs=[SMEM] + [VMEM] * 4 + [HBM],
         out_specs=[VMEM] * 3 + [HBM] * 2,
         scratch_shapes=[pltpu.VMEM((all_rows, enc_width), jnp.bfloat16)]
         + [pltpu.VMEM((all_rows, width), jnp.bfloat16)] * 2
-        + [pltpu.VMEM((2, all_rows, width), jnp.bfloat16), pltpu.VMEM((all_rows, enc_width), jnp.bfloat16)]
+        + [pltpu.VMEM((2, all_rows, width), jnp.bfloat16), pltpu.VMEM((units, slices, piece, enc_width), jnp.bfloat16)]
         + [pltpu.VMEM((tokens, width), jnp.bfloat16)] * 2
         + [pltpu.VMEM((tokens, width), jnp.float32)] * 2
-        + [pltpu.SemaphoreType.DMA((4,)), pltpu.SemaphoreType.DMA((2,)), pltpu.SemaphoreType.DMA((4,))],
+        + [pltpu.SemaphoreType.DMA((4,)), pltpu.SemaphoreType.DMA((2,)), pltpu.SemaphoreType.DMA((units // 4, slices))],
         compiler_params=PARAMS,
         name="block",
     )(units_of, q, g, ahead, w, x)
@@ -136,21 +139,43 @@
 def products(place, x, grad):
     enc_width, width = x.shape[1], grad.shape[2]
 
-    def body(place_ref, x_ref, grad_ref, sent_ref, kept_ref):
+    def body(place_ref, x_hbm, grad_hbm, sent_ref, kept_ref, x_ref, grad_ref, sems):
         core = place_ref[0]
+        copies = [
+            pltpu.make_async_copy(x_hbm, x_ref, sems.at[0]),
+            pltpu.make_async_copy(grad_hbm.at[1 - core], grad_ref.at[0], sems.at[1]),
+            pltpu.make_async_copy(grad_hbm.at[core], grad_ref.at[1], sems.at[2]),
+        ]
+        for copy in copies:
+            copy.start()
+        for copy in copies:
+            copy.wait()
         for e in range(0, enc_width, 128):
             part = x_ref[:, e : e + 128].T
-            sent_ref[e : e + 128, :] = dot(part, grad_ref[1 - core], NN).astype(jnp.bfloat16)
-            kept_ref[e : e + 128, :] = dot(part, grad_ref[core], NN)
-
-    return call(body, "products", [low(enc_width, width), wide(enc_width, width)], [], place, x, grad)
-
-
-def cut(place, kept, away):
+            sent_ref[e : e + 128, :] = dot(part, grad_ref[0], NN).astype(jnp.bfloat16)
+            kept_ref[e : e + 128, :] = dot(part, grad_ref[1], NN)
+
+    return pl.pallas_call(
+        body,
+        out_shape=[low(enc_width, width), wide(enc_width, width)],
+        in_specs=[SMEM, HBM, HBM],
+        out_specs=[VMEM, VMEM],
+        scratch_shapes=[
+            pltpu.VMEM(x.shape, jnp.bfloat16),
+            pltpu.VMEM(grad.shape, jnp.bfloat16),
+            pltpu.SemaphoreType.DMA((3,)),
+        ],
+        compiler_params=PARAMS,
+        name="products",
+    )(place, x, grad)
+
+
+def cut(place, kept, away, att, dq, behind):
     enc_width, width = kept.shape
     rows = enc_width // 8
 
-    def body(place_ref, kept_ref, away_ref, own_ref, *send_refs):
+    def body(place_ref, kept_ref, away_ref, att_ref, dq_ref, behind_ref, own_ref, *refs):
+        send_refs, full_refs = refs[:3], refs[3:]
         x = place_ref[1]
         for high in range(2):
             for k in range(4):
@@ -160,78 +185,55 @@
                     send_refs[k - 1][high] = term.astype(jnp.bfloat16)
                 else:
                     own_ref[high] = term
-
-    return call(body, "cut", [wide(2, rows, width)] + [low(2, rows, width)] * 3, [], place, kept, away)
-
-
-def spread(x, groups):
-    units, piece, enc_width = x.shape
-
-    def body(x_ref, out_hbm, sems):
-        copies = [pltpu.make_async_copy(x_ref, out_hbm.at[:, n], sems.at[n]) for n in range(groups)]
-        for copy in copies:
-            copy.start()
-        for copy in copies:
-            copy.wait()
-
-    return pl.pallas_call(
-        body,
-        out_shape=low(units, groups, piece, enc_width),
-        in_specs=[VMEM],
-        out_specs=HBM,
-        scratch_shapes=[pltpu.SemaphoreType.DMA((groups,))],
-        compiler_params=PARAMS,
-        name="spread",
-    )(x)
-
-
-def gather_up(place, terms, att, dq, behind):
-    units, groups, piece, enc_width = terms.shape
-    width = att.shape[1]
-
-    def body(_, terms_ref, att_ref, dq_ref, behind_ref, total_ref, *full_refs):
-        for u in range(units):
-            total = add(terms_ref[u, 0], terms_ref[u, 1])
-            for n in range(2, groups):
-                total = add(total, terms_ref[u, n])
-            total_ref[u] = total.astype(jnp.bfloat16)
         lead = lax.broadcasted_iota(jnp.int32, (SPAN, width), 0) < LEAD
         for n, (ref, full) in enumerate(zip((att_ref, dq_ref), full_refs)):
             came = behind_ref[:, n * width : (n + 1) * width].astype(jnp.float32)
             full[:SPAN, :] = jnp.where(lead, came, ref[:SPAN, :].astype(jnp.float32)).astype(jnp.bfloat16)
             full[SPAN:, :] = ref[SPAN:, :]
 
-    out_shape = [low(units, piece, enc_width), low(*att.shape), low(*dq.shape)]
-    return call(body, "gather_up", out_shape, [], place, terms, att, dq, behind)
-
-
-def join(place, mine, theirs, after):
-    def body(place_ref, mine_ref, theirs_ref, _, out_ref):
+    out_shape = [wide(2, rows, width)] + [low(2, rows, width)] * 3 + [low(*att.shape)] * 2
+    return call(body, "cut", out_shape, [], place, kept, away, att, dq, behind)
+
+
+def spread(x, groups):
+    units, piece, enc_width = x.shape
+    parts = [pl.ds(c, units // 4) for c in range(0, units, units // 4)]
+
+    def body(x_hbm, out_hbm, held, in_sems, out_sems):
+        ins = [pltpu.make_async_copy(x_hbm.at[part], held.at[part], in_sems.at[c]) for c, part in enumerate(parts)]
+        for copy in ins:
+            copy.start()
+        outs = []
+        for c, part in enumerate(parts):
+            ins[c].wait()
+            for n in range(groups):
+                copy = pltpu.make_async_copy(held.at[part], out_hbm.at[part, n], out_sems.at[c, n])
+                copy.start()
+                outs.append(copy)
+        for copy in outs:
+            copy.wait()
+
+    return pl.pallas_call(
+        body,
+        out_shape=low(units, groups, piece, enc_width),
+        in_specs=[HBM],
+        out_specs=HBM,
+        scratch_shapes=[
+            pltpu.VMEM(x.shape, jnp.bfloat16),
+            pltpu.SemaphoreType.DMA((4,)),
+            pltpu.SemaphoreType.DMA((4, groups)),
+        ],
+        compiler_params=PARAMS,
+        name="spread",
+    )(x)
+
+
+def join(place, mine, theirs):
+    def body(place_ref, mine_ref, theirs_ref, out_ref):
         out_ref[place_ref[0]] = mine_ref[...]
         out_ref[1 - place_ref[0]] = theirs_ref[...]
 
-    return pl.pallas_call(
-        body,
-        out_shape=wide(2, *mine.shape),
-        in_specs=[SMEM, VMEM, VMEM, HBM],
-        out_specs=VMEM,
-        compiler_params=PARAMS,
-        name="join",
-    )(place, mine, theirs, after)
-
-
-def z_add(place, rows, came, after):
-    def body(_, rows_ref, came_ref, __, out_ref):
-        out_ref[...] = add(rows_ref[...], came_ref[...]).astype(jnp.bfloat16)
-
-    return pl.pallas_call(
-        body,
-        out_shape=low(*rows.shape),
-        in_specs=[SMEM, VMEM, VMEM, HBM],
-        out_specs=VMEM,
-        compiler_params=PARAMS,
-        name="z_add",
-    )(place, rows, came, after)
+    return call(body, "join", wide(2, *mine.shape), [], place, mine, theirs)
 
 
 def permute(x, axis, to):
@@ -259,25 +261,25 @@
     ahead = permute(head, "ctx", lambda i: i - 1)
 
     unit_of = (neighbour_ids[0] // units).reshape(-1)
-    att, dq, tail, grad, partial = block(unit_of, q, g, ahead, kv_weight, x)
-
-    terms = exchange(partial.reshape(units, groups, piece, enc_width))
+    att, dq, tail, grad, partial = block(unit_of, q, g, ahead, kv_weight, x, groups)
     behind = permute(tail, "ctx", lambda i: i + 1)
 
+    total = lax.psum_scatter(partial, "nbr", scatter_dimension=0, tiled=False)
+    encoded_grad = lax.all_to_all(total, "ctx", split_axis=0, concat_axis=0, tiled=True)
+
     sent, kept = products(place, x, grad)
-    held, *sends = cut(place, kept, permute(sent, "ctx", lambda i: i ^ 1))
+    away = permute(sent, "ctx", lambda i: i ^ 1)
+    held, *sends, attended, query_grad = cut(place, kept, away, att, dq, behind)
     for k in (1, 3, 2):
         held = add(held, permute(sends[k - 1], "dp", lambda i, k=k: i // 4 * 4 + (i + k) % 4))
     high = dp // 4
     other = lax.dynamic_index_in_dim(held, 1 - high, 0, keepdims=False).astype(jnp.bfloat16)
     mine = lax.dynamic_index_in_dim(held, high, 0, keepdims=False)
-    rows = z_add(place, mine, permute(other, "dp", lambda i: (i + 4) % 8), behind)
+    mine = add(mine, permute(other, "dp", lambda i: (i + 4) % 8))
     for bit in (2, 4, 8):
+        rows = mine.astype(jnp.bfloat16)
         mine = add(rows, permute(rows, "ctx", lambda i, b=bit: i ^ b))
-        rows = mine.astype(jnp.bfloat16)
-    theirs = permute(mine, "ctx", lambda i: i ^ 1)
-    encoded_grad, attended, query_grad = gather_up(place, terms, att, dq, behind)
-    weight_grad = join(place, mine, theirs, encoded_grad)
+    weight_grad = join(place, mine, permute(mine, "ctx", lambda i: i ^ 1))
     return (attended[None], query_grad[None], encoded_grad[None], weight_grad)
 
 

time: 173 us -> 183 us (1.058)
  the two profiles are of different devices: /device:TPU:1 before, /device:TPU:67 now
where the time goes in v8:
time: 183 us
  waiting for transfers between devices  80.1 us (44%)
  starting transfers between devices  61 us (33%)
  Pallas kernels  22.4 us (12%)
  between operations  14.3 us (8%)
  local copies, waits for them, and re-layouts  4.42 us (2%)
    ppermute x11, waiting for transfers between devices, permute(): lax.ppermute(x, axis, [(i, to(i)) for i in range(n) if 0 <= to(i) < n])  78.3 us
    ppermute x11, starting transfers between devices, permute(): lax.ppermute(x, axis, [(i, to(i)) for i in range(n) if 0 <= to(i) < n])  40.8 us
    all_to_all x1, starting transfers between devices, exchange(): lax.all_to_all(x.reshape(outer * inner, *rest), ('ctx', 'nbr'), split_axi...  13.2 us
    pallas_call x1, Pallas kernels, block(): pl.pallas_call(block_body, out_shape=[low(tokens, width), low(tokens, wid...  11.7 us
    all_to_all x1, starting transfers between devices, shards(): lax.all_to_all(total, 'ctx', split_axis=0, concat_axis=0, tiled=True)  6.97 us
    pallas_call x1, Pallas kernels, products(): pl.pallas_call(body, out_shape=[low(enc_width, width), wide(enc_width, wi...  4.77 us
    unnamed x13, local copies, waits for them, and re-layouts  4.3 us
    pallas_call x2, Pallas kernels, call(): pl.pallas_call(body, out_shape=out_shape, in_specs=[SMEM] + [VMEM] * len(...  3.99 us
  transfers between devices with their start and end apart: 14, of which 10 were waited for; matrix products, arithmetic and copies ran while one was open for 0% of the time, Pallas kernels for 5%

profile of v8, /device:TPU:67, one launch (start us, length us, event | category | flops | bytes accessed | tf_op | source)
XLA Modules:
  0.0 182.6 jit_solution(13232281148938104424)
XLA Ops:
  7.2 1.0 copy-done.1
  8.2 2.0 %spread.1 = bf16[16,4,16,896]{3,2,1,0:T(8,128)(2,1)} custom-call(bf16[16,16,896]{2,1,0:T(8,128)(2,1)S(1)} %bitcast.22), custom_call_target="tpu_custom_call" | custom-call | tf_op jit(solution)/shard_map/spread/pallas_call | solution.py:216
  10.2 13.2 %all-to-all-start = ((bf16[64,16,896]{2,1,0:T(8,128)(2,1)}), bf16[64,16,896]{2,1,0:T(8,128)(2,1)S(1)}, u32[]{:S(2)}, u32[]{:S(2)}) async-start(bf16[64,16,896]{2,1,0:T(8,128)(2,1)} %bitcast.4), calls=%async_computation | async-start | bytes 3670016 | tf_op jit(solution)/shard_map/all_to_all | solution.py:246
  23.5 2.3 %collective-permute-start = (bf16[64,1024]{1,0:T(8,128)(2,1)S(1)}, bf16[64,1024]{1,0:T(8,128)(2,1)S(1)}, u32[]{:S(2)}, u32[]{:S(2)}) collective-permute-start(bf16[64,1024]{1,0:T(8,128)(2,1)S(1)} %pad_maximum_fusion), channel_id=1, source_target_pairs={{4,0},{8,4},{12,8},{16,12},{20,16},{24,20},{28,24},{32,28},{36,32}... | collective-permute-start | bytes 393224 | tf_op jit(solution)/shard_map/ppermute | solution.py:241
  25.9 40.2 %collective-permute-done.ahead_ref = bf16[64,1024]{1,0:T(8,128)(2,1)S(1)} collective-permute-done((bf16[64,1024]{1,0:T(8,128)(2,1)S(1)}, bf16[64,1024]{1,0:T(8,128)(2,1)S(1)}, u32[]{:S(2)}, u32[]{:S(2)}) %collective-permute-start) | collective-permute-done | bytes 131104 | tf_op jit(solution)/shard_map/ppermute | solution.py:241
  66.1 1.7 all-to-all-done
  67.8 1.3 copy-done.4
  69.1 11.7 %block.1 = (bf16[256,512]{1,0:T(8,128)(2,1)S(1)}, bf16[256,512]{1,0:T(8,128)(2,1)S(1)}, bf16[64,1024]{1,0:T(8,128)(2,1)S(1)}, bf16[2,1024,512]{2,1,0:T(8,128)(2,1)}, bf16[4,16,16,896]{3,2,1,0:T(8,128)(2,1)}) custom-call(s32[16]{0:T(128)S(1)} %and_select_fusion.units_ref, bf16[256,512]{1,0:T(8,128)(2,1)S(1)} %bitcast.23, bf16[256,512]{1,0:T(8,128)(2,1)S(1)} %bitcast.24, ...), custom_call_target="tpu_custom_call" | custom-call | tf_op jit(solution)/shard_map/block/pallas_call | solution.py:123
  80.9 4.8 %products.1 = (bf16[896,512]{1,0:T(8,128)(2,1)S(1)}, f32[896,512]{1,0:T(8,128)S(1)}) custom-call(s32[3]{0:T(128)S(1)} %pad_add_fusion.place_ref, bf16[1024,896]{1,0:T(8,128)(2,1)} %bitcast.26, bf16[2,1024,512]{2,1,0:T(8,128)(2,1)} %get-tuple-element.17.grad_hbm), custom_call_target="tpu_custom_call" | custom-call | tf_op jit(solution)/shard_map/products/pallas_call | solution.py:158
  85.7 1.3 copy-done
  87.0 3.5 %collective-permute-start.1 = (bf16[896,512]{1,0:T(8,128)(2,1)S(1)}, bf16[896,512]{1,0:T(8,128)(2,1)S(1)}, u32[]{:S(2)}, u32[]{:S(2)}) collective-permute-start(bf16[896,512]{1,0:T(8,128)(2,1)S(1)} %get-tuple-element.19), channel_id=1, source_target_pairs={{0,4},{4,0},{8,12},{12,8},{16,20},{20,16},{24,28},{28,24},{32,36},... | collective-permute-start | bytes 2752520 | tf_op jit(solution)/shard_map/ppermute | solution.py:241
  90.5 2.2 %collective-permute-start.2 = (bf16[64,1024]{1,0:T(8,128)(2,1)S(1)}, bf16[64,1024]{1,0:T(8,128)(2,1)S(1)}, u32[]{:S(2)}, u32[]{:S(2)}) collective-permute-start(bf16[64,1024]{1,0:T(8,128)(2,1)S(1)} %get-tuple-element.22), channel_id=1, source_target_pairs={{0,4},{4,8},{8,12},{12,16},{16,20},{20,24},{24,28},{28,32},{32,36}... | collective-permute-start | bytes 393224 | tf_op jit(solution)/shard_map/ppermute | solution.py:241
  92.6 1.9 %collective-permute-done.2.behind_ref = bf16[64,1024]{1,0:T(8,128)(2,1)S(1)} collective-permute-done((bf16[64,1024]{1,0:T(8,128)(2,1)S(1)}, bf16[64,1024]{1,0:T(8,128)(2,1)S(1)}, u32[]{:S(2)}, u32[]{:S(2)}) %collective-permute-start.2) | collective-permute-done | bytes 131104 | tf_op jit(solution)/shard_map/ppermute | solution.py:241
  94.6 2.6 %cut.1 = (f32[2,112,512]{2,1,0:T(8,128)S(1)}, bf16[2,112,512]{2,1,0:T(8,128)(2,1)S(1)}, bf16[2,112,512]{2,1,0:T(8,128)(2,1)S(1)}, bf16[2,112,512]{2,1,0:T(8,128)...) custom-call(s32[3]{0:T(128)S(1)} %pad_add_fusion.place_ref, f32[896,512]{1,0:T(8,128)} %copy-done, ...), custom_call_target="tpu_custom_call" | custom-call | tf_op jit(solution)/shard_map/cut/pallas_call | solution.py:108
  97.2 3.1 %collective-permute-start.3 = (bf16[2,112,512]{2,1,0:T(8,128)(2,1)S(1)}, bf16[2,112,512]{2,1,0:T(8,128)(2,1)S(1)}, u32[]{:S(2)}, u32[]{:S(2)}) collective-permute-start(bf16[2,112,512]{2,1,0:T(8,128)(2,1)S(1)} %get-tuple-element.27), channel_id=1, source_target_pairs={{0,64},{64,128},{128,192},{192,0},{256,320},{320,384},{384,448},{4... | collective-permute-start | bytes 688136 | tf_op jit(solution)/shard_map/ppermute | solution.py:241
  100.3 2.2 %collective-permute-start.4 = (bf16[2,112,512]{2,1,0:T(8,128)(2,1)S(1)}, bf16[2,112,512]{2,1,0:T(8,128)(2,1)S(1)}, u32[]{:S(2)}, u32[]{:S(2)}) collective-permute-start(bf16[2,112,512]{2,1,0:T(8,128)(2,1)S(1)} %get-tuple-element.28), channel_id=1, source_target_pairs={{0,192},{64,0},{128,64},{192,128},{256,448},{320,256},{384,320},{4... | collective-permute-start | bytes 688136 | tf_op jit(solution)/shard_map/ppermute | solution.py:241
  102.5 3.7 %collective-permute-start.5 = (bf16[2,112,512]{2,1,0:T(8,128)(2,1)S(1)}, bf16[2,112,512]{2,1,0:T(8,128)(2,1)S(1)}, u32[]{:S(2)}, u32[]{:S(2)}) collective-permute-start(bf16[2,112,512]{2,1,0:T(8,128)(2,1)S(1)} %get-tuple-element.29), channel_id=1, source_target_pairs={{0,128},{64,192},{128,0},{192,64},{256,384},{320,448},{384,256},{4... | collective-permute-start | bytes 688136 | tf_op jit(solution)/shard_map/ppermute | solution.py:241
  106.3 0.1 collective-permute-done.3
  106.4 3.4 %collective-permute-done.4 = bf16[2,112,512]{2,1,0:T(8,128)(2,1)S(1)} collective-permute-done((bf16[2,112,512]{2,1,0:T(8,128)(2,1)S(1)}, bf16[2,112,512]{2,1,0:T(8,128)(2,1)S(1)}, u32[]{:S(2)}, u32[]{:S(2)}) %collective-permute-start.4) | collective-permute-done | bytes 229408 | tf_op jit(solution)/shard_map/ppermute | solution.py:241
  109.8 5.3 %collective-permute-done.5 = bf16[2,112,512]{2,1,0:T(8,128)(2,1)S(1)} collective-permute-done((bf16[2,112,512]{2,1,0:T(8,128)(2,1)S(1)}, bf16[2,112,512]{2,1,0:T(8,128)(2,1)S(1)}, u32[]{:S(2)}, u32[]{:S(2)}) %collective-permute-start.5) | collective-permute-done | bytes 229408 | tf_op jit(solution)/shard_map/ppermute | solution.py:241
  115.2 7.9 %collective-permute-start.6 = (bf16[112,512]{1,0:T(8,128)(2,1)S(1)}, bf16[112,512]{1,0:T(8,128)(2,1)S(1)}, u32[]{:S(2)}, u32[]{:S(2)}) collective-permute-start(bf16[112,512]{1,0:T(8,128)(2,1)S(1)} %fusion.1), channel_id=1, source_target_pairs={{0,256},{64,320},{128,384},{192,448},{256,0},{320,64},{384,128},{4... | collective-permute-start | bytes 344072 | tf_op jit(solution)/shard_map/ppermute | solution.py:241
  123.2 11.0 %collective-permute-done.6 = bf16[112,512]{1,0:T(8,128)(2,1)S(1)} collective-permute-done((bf16[112,512]{1,0:T(8,128)(2,1)S(1)}, bf16[112,512]{1,0:T(8,128)(2,1)S(1)}, u32[]{:S(2)}, u32[]{:S(2)}) %collective-permute-start.6) | collective-permute-done | bytes 114720 | tf_op jit(solution)/shard_map/ppermute | solution.py:241
  134.2 1.9 %collective-permute-start.7 = (bf16[112,512]{1,0:T(8,128)(2,1)S(1)}, bf16[112,512]{1,0:T(8,128)(2,1)S(1)}, u32[]{:S(2)}, u32[]{:S(2)}) collective-permute-start(bf16[112,512]{1,0:T(8,128)(2,1)S(1)} %fusion), channel_id=1, source_target_pairs={{0,8},{4,12},{8,0},{12,4},{16,24},{20,28},{24,16},{28,20},{32,40},... | collective-permute-start | bytes 344072 | tf_op jit(solution)/shard_map/ppermute | solution.py:241
  136.1 3.6 %collective-permute-done.7 = bf16[112,512]{1,0:T(8,128)(2,1)S(1)} collective-permute-done((bf16[112,512]{1,0:T(8,128)(2,1)S(1)}, bf16[112,512]{1,0:T(8,128)(2,1)S(1)}, u32[]{:S(2)}, u32[]{:S(2)}) %collective-permute-start.7) | collective-permute-done | bytes 114720 | tf_op jit(solution)/shard_map/ppermute | solution.py:241
  139.8 1.9 %collective-permute-start.8 = (bf16[112,512]{1,0:T(8,128)(2,1)S(1)}, bf16[112,512]{1,0:T(8,128)(2,1)S(1)}, u32[]{:S(2)}, u32[]{:S(2)}) collective-permute-start(bf16[112,512]{1,0:T(8,128)(2,1)S(1)} %add_convert_fusion.1), channel_id=1, source_target_pairs={{0,16},{4,20},{8,24},{12,28},{16,0},{20,4},{24,8},{28,12},{32,48},... | collective-permute-start | bytes 344072 | tf_op jit(solution)/shard_map/ppermute | solution.py:241
  141.7 7.0 %all-to-all-start.1 = ((bf16[16,16,896]{2,1,0:T(8,128)(2,1)}), bf16[16,16,896]{2,1,0:T(8,128)(2,1)S(1)}, u32[]{:S(2)}, u32[]{:S(2)}) async-start(bf16[16,16,896]{2,1,0:T(8,128)(2,1)} %bitcast.28), calls=%async_computation.2 | async-start | bytes 917504 | tf_op jit(solution)/shard_map/all_to_all | solution.py:268
  148.7 7.2 %collective-permute-start.9 = (bf16[112,512]{1,0:T(8,128)(2,1)S(1)}, bf16[112,512]{1,0:T(8,128)(2,1)S(1)}, u32[]{:S(2)}, u32[]{:S(2)}) collective-permute-start(bf16[112,512]{1,0:T(8,128)(2,1)S(1)} %add_convert_fusion), channel_id=1, source_target_pairs={{0,32},{4,36},{8,40},{12,44},{16,48},{20,52},{24,56},{28,60},{32,0... | collective-permute-start | bytes 344072 | tf_op jit(solution)/shard_map/ppermute | solution.py:241
  156.0 11.6 %collective-permute-done.9 = bf16[112,512]{1,0:T(8,128)(2,1)S(1)} collective-permute-done((bf16[112,512]{1,0:T(8,128)(2,1)S(1)}, bf16[112,512]{1,0:T(8,128)(2,1)S(1)}, u32[]{:S(2)}, u32[]{:S(2)}) %collective-permute-start.9) | collective-permute-done | bytes 114720 | tf_op jit(solution)/shard_map/ppermute | solution.py:241
  167.7 4.9 %collective-permute-start.10 = (f32[112,512]{1,0:T(8,128)S(1)}, f32[112,512]{1,0:T(8,128)S(1)}, u32[]{:S(2)}, u32[]{:S(2)}) collective-permute-start(f32[112,512]{1,0:T(8,128)S(1)} %convert_add_fusion.1.mine_ref), channel_id=1, source_target_pairs={{0,4},{4,0},{8,12},{12,8},{16,20},{20,16},{24,28},{28,24},{32,36},... | collective-permute-start | bytes 688136 | tf_op jit(solution)/shard_map/ppermute | solution.py:241
  172.6 1.1 collective-permute-done.10.theirs_ref
  173.7 1.3 join.1
  175.0 0.8 copy.10
  (26 shorter events, 0.6 us)
Async XLA Ops:
  7.2 1.0 copy-start.1
  10.2 13.3 %copy-start.2 = (bf16[1,256,512]{2,1,0:T(8,128)(2,1)S(1)}, bf16[1,256,512]{2,1,0:T(8,128)(2,1)}, u32[]{:S(2)}) copy-start(bf16[1,256,512]{2,1,0:T(8,128)(2,1)} %param.5) | copy-start | bytes 786436
  10.2 13.3 %copy-start.3 = (bf16[1,256,512]{2,1,0:T(8,128)(2,1)S(1)}, bf16[1,256,512]{2,1,0:T(8,128)(2,1)}, u32[]{:S(2)}) copy-start(bf16[1,256,512]{2,1,0:T(8,128)(2,1)} %param.6) | copy-start | bytes 786436
  10.2 15.6 %copy-start.5 = (s32[1,4,4]{2,1,0:T(4,128)S(1)}, s32[1,4,4]{2,1,0:T(4,128)}, u32[]{:S(2)}) copy-start(s32[1,4,4]{2,1,0:T(4,128)} %param.9) | copy-start | bytes 196
  10.2 57.6 %all-to-all-start = ((bf16[64,16,896]{2,1,0:T(8,128)(2,1)}), bf16[64,16,896]{2,1,0:T(8,128)(2,1)S(1)}, u32[]{:S(2)}, u32[]{:S(2)}) async-start(bf16[64,16,896]{2,1,0:T(8,128)(2,1)} %bitcast.4), calls=%async_computation | async-start | bytes 3670016 | tf_op jit(solution)/shard_map/all_to_all | solution.py:246
  23.4 118.3 %reduce-scatter.2.cloned.1.call-start = ((), (), s32[]{:S(2)}) async-start(), calls=%async_computation.3 | async-start | bytes 2293760 | tf_op jit(solution)/shard_map/reduce_scatter | solution.py:267
  23.5 42.6 %collective-permute-start = (bf16[64,1024]{1,0:T(8,128)(2,1)S(1)}, bf16[64,1024]{1,0:T(8,128)(2,1)S(1)}, u32[]{:S(2)}, u32[]{:S(2)}) collective-permute-start(bf16[64,1024]{1,0:T(8,128)(2,1)S(1)} %pad_maximum_fusion), channel_id=1, source_target_pairs={{4,0},{8,4},{12,8},{16,12},{20,16},{24,20},{28,24},{32,28},{36,32}... | collective-permute-start | bytes 393224 | tf_op jit(solution)/shard_map/ppermute | solution.py:241
  67.8 1.3 copy-start.4
  85.7 1.3 copy-start
  87.0 7.6 %collective-permute-start.1 = (bf16[896,512]{1,0:T(8,128)(2,1)S(1)}, bf16[896,512]{1,0:T(8,128)(2,1)S(1)}, u32[]{:S(2)}, u32[]{:S(2)}) collective-permute-start(bf16[896,512]{1,0:T(8,128)(2,1)S(1)} %get-tuple-element.19), channel_id=1, source_target_pairs={{0,4},{4,0},{8,12},{12,8},{16,20},{20,16},{24,28},{28,24},{32,36},... | collective-permute-start | bytes 2752520 | tf_op jit(solution)/shard_map/ppermute | solution.py:241
  90.5 4.1 %collective-permute-start.2 = (bf16[64,1024]{1,0:T(8,128)(2,1)S(1)}, bf16[64,1024]{1,0:T(8,128)(2,1)S(1)}, u32[]{:S(2)}, u32[]{:S(2)}) collective-permute-start(bf16[64,1024]{1,0:T(8,128)(2,1)S(1)} %get-tuple-element.22), channel_id=1, source_target_pairs={{0,4},{4,8},{8,12},{12,16},{16,20},{20,24},{24,28},{28,32},{32,36}... | collective-permute-start | bytes 393224 | tf_op jit(solution)/shard_map/ppermute | solution.py:241
  97.2 9.2 %collective-permute-start.3 = (bf16[2,112,512]{2,1,0:T(8,128)(2,1)S(1)}, bf16[2,112,512]{2,1,0:T(8,128)(2,1)S(1)}, u32[]{:S(2)}, u32[]{:S(2)}) collective-permute-start(bf16[2,112,512]{2,1,0:T(8,128)(2,1)S(1)} %get-tuple-element.27), channel_id=1, source_target_pairs={{0,64},{64,128},{128,192},{192,0},{256,320},{320,384},{384,448},{4... | collective-permute-start | bytes 688136 | tf_op jit(solution)/shard_map/ppermute | solution.py:241
  100.3 9.5 %collective-permute-start.4 = (bf16[2,112,512]{2,1,0:T(8,128)(2,1)S(1)}, bf16[2,112,512]{2,1,0:T(8,128)(2,1)S(1)}, u32[]{:S(2)}, u32[]{:S(2)}) collective-permute-start(bf16[2,112,512]{2,1,0:T(8,128)(2,1)S(1)} %get-tuple-element.28), channel_id=1, source_target_pairs={{0,192},{64,0},{128,64},{192,128},{256,448},{320,256},{384,320},{4... | collective-permute-start | bytes 688136 | tf_op jit(solution)/shard_map/ppermute | solution.py:241
  102.5 12.6 %collective-permute-start.5 = (bf16[2,112,512]{2,1,0:T(8,128)(2,1)S(1)}, bf16[2,112,512]{2,1,0:T(8,128)(2,1)S(1)}, u32[]{:S(2)}, u32[]{:S(2)}) collective-permute-start(bf16[2,112,512]{2,1,0:T(8,128)(2,1)S(1)} %get-tuple-element.29), channel_id=1, source_target_pairs={{0,128},{64,192},{128,0},{192,64},{256,384},{320,448},{384,256},{4... | collective-permute-start | bytes 688136 | tf_op jit(solution)/shard_map/ppermute | solution.py:241
  115.2 18.9 %collective-permute-start.6 = (bf16[112,512]{1,0:T(8,128)(2,1)S(1)}, bf16[112,512]{1,0:T(8,128)(2,1)S(1)}, u32[]{:S(2)}, u32[]{:S(2)}) collective-permute-start(bf16[112,512]{1,0:T(8,128)(2,1)S(1)} %fusion.1), channel_id=1, source_target_pairs={{0,256},{64,320},{128,384},{192,448},{256,0},{320,64},{384,128},{4... | collective-permute-start | bytes 344072 | tf_op jit(solution)/shard_map/ppermute | solution.py:241
  134.2 5.5 %collective-permute-start.7 = (bf16[112,512]{1,0:T(8,128)(2,1)S(1)}, bf16[112,512]{1,0:T(8,128)(2,1)S(1)}, u32[]{:S(2)}, u32[]{:S(2)}) collective-permute-start(bf16[112,512]{1,0:T(8,128)(2,1)S(1)} %fusion), channel_id=1, source_target_pairs={{0,8},{4,12},{8,0},{12,4},{16,24},{20,28},{24,16},{28,20},{32,40},... | collective-permute-start | bytes 344072 | tf_op jit(solution)/shard_map/ppermute | solution.py:241
  139.8 8.9 %collective-permute-start.8 = (bf16[112,512]{1,0:T(8,128)(2,1)S(1)}, bf16[112,512]{1,0:T(8,128)(2,1)S(1)}, u32[]{:S(2)}, u32[]{:S(2)}) collective-permute-start(bf16[112,512]{1,0:T(8,128)(2,1)S(1)} %add_convert_fusion.1), channel_id=1, source_target_pairs={{0,16},{4,20},{8,24},{12,28},{16,0},{20,4},{24,8},{28,12},{32,48},... | collective-permute-start | bytes 344072 | tf_op jit(solution)/shard_map/ppermute | solution.py:241
  141.7 33.3 %all-to-all-start.1 = ((bf16[16,16,896]{2,1,0:T(8,128)(2,1)}), bf16[16,16,896]{2,1,0:T(8,128)(2,1)S(1)}, u32[]{:S(2)}, u32[]{:S(2)}) async-start(bf16[16,16,896]{2,1,0:T(8,128)(2,1)} %bitcast.28), calls=%async_computation.2 | async-start | bytes 917504 | tf_op jit(solution)/shard_map/all_to_all | solution.py:268
  148.7 18.9 %collective-permute-start.9 = (bf16[112,512]{1,0:T(8,128)(2,1)S(1)}, bf16[112,512]{1,0:T(8,128)(2,1)S(1)}, u32[]{:S(2)}, u32[]{:S(2)}) collective-permute-start(bf16[112,512]{1,0:T(8,128)(2,1)S(1)} %add_convert_fusion), channel_id=1, source_target_pairs={{0,32},{4,36},{8,40},{12,44},{16,48},{20,52},{24,56},{28,60},{32,0... | collective-permute-start | bytes 344072 | tf_op jit(solution)/shard_map/ppermute | solution.py:241
  167.7 6.0 %collective-permute-start.10 = (f32[112,512]{1,0:T(8,128)S(1)}, f32[112,512]{1,0:T(8,128)S(1)}, u32[]{:S(2)}, u32[]{:S(2)}) collective-permute-start(f32[112,512]{1,0:T(8,128)S(1)} %convert_add_fusion.1.mine_ref), channel_id=1, source_target_pairs={{0,4},{4,0},{8,12},{12,8},{16,20},{20,16},{24,28},{28,24},{32,36},... | collective-permute-start | bytes 688136 | tf_op jit(solution)/shard_map/ppermute | solution.py:241
Sparse Core Ops, SparseCore 0:
  80.9 45.1 reduce-scatter.1

commit v9 on v8

--- a/solution.py
+++ b/solution.py
@@ -18,7 +18,7 @@
 VMEM = pl.BlockSpec(memory_space=pltpu.VMEM)
 SMEM = pl.BlockSpec(memory_space=pltpu.SMEM)
 HBM = pl.BlockSpec(memory_space=pltpu.HBM)
-PARAMS = pltpu.CompilerParams(vmem_limit_bytes=50 * 1024 * 1024)
+PARAMS = pltpu.CompilerParams(vmem_limit_bytes=28 * 1024 * 1024)
 
 
 def dot(a, b, dims):
@@ -33,22 +33,20 @@
 
 
 def block_body(
-    units_ref, q_ref, g_ref, ahead_ref, w_ref, x_hbm, att_ref, dq_ref, tail_ref, grad_hbm, partial_hbm,
-    x, key, value, grad, partial, q_rows, g_rows, att, dq, x_sems, grad_sems, partial_sems,
+    units_ref, q_ref, g_ref, ahead_ref, w_ref, x, att_ref, dq_ref, tail_ref, sent_ref, kept_ref, *refs
 ):
+    partial_hbms = refs[:-9]
+    key, value, grad, partial, q_rows, g_rows, att, dq, partial_sems = refs[-9:]
     tokens, width = q_ref.shape
     heads = width // HEAD_DIM
     chunk = 4 * PART
+    nbr, core = units_ref[units_ref.shape[0] - 2], units_ref[units_ref.shape[0] - 1]
     chunks = [pl.ds(c * chunk, chunk) for c in range(x.shape[0] // chunk)]
     head_cols = [pl.ds(h * HEAD_DIM, HEAD_DIM) for h in range(heads)]
-    x_copies = [pltpu.make_async_copy(x_hbm.at[rows], x.at[rows], x_sems.at[c]) for c, rows in enumerate(chunks)]
-    for copy in x_copies:
-        copy.start()
     for h, cols in enumerate(head_cols):
         q_rows[:, cols] = span_rows(q_ref[:, cols], ahead_ref[:, cols])
         g_rows[:, cols] = span_rows(g_ref[:, cols], ahead_ref[:, pl.ds(width + h * HEAD_DIM, HEAD_DIM)])
-    for copy, rows in zip(x_copies, chunks):
-        copy.wait()
+    for rows in chunks:
         for kind, out in enumerate((key, value)):
             out[rows, :] = dot(x[rows, :], w_ref[kind], NN).astype(jnp.bfloat16)
     for j in range(tokens // SPAN):
@@ -75,24 +73,26 @@
             for r, s in enumerate(starts):
                 grad[0, pl.ds(s, PART), cols] = dk[r * PART : (r + 1) * PART]
                 grad[1, pl.ds(s, PART), cols] = dv[r * PART : (r + 1) * PART]
-    grad_copies = [pltpu.make_async_copy(grad.at[n], grad_hbm.at[n], grad_sems.at[n]) for n in range(2)]
-    for copy in grad_copies:
-        copy.start()
     partial_copies = []
     for c, rows in enumerate(chunks):
         term = dot(grad[0, rows, :], w_ref[0], NT) + dot(grad[1, rows, :], w_ref[1], NT)
         units = pl.ds(c * 4, 4)
         partial[units] = term.astype(jnp.bfloat16).reshape(4, *partial.shape[1:])
-        for n in range(partial.shape[1]):
-            copy = pltpu.make_async_copy(partial.at[units, n], partial_hbm.at[n, units], partial_sems.at[c, n])
+        for k, out in enumerate(partial_hbms):
+            slice_of = lax.rem(nbr + k, len(partial_hbms))
+            copy = pltpu.make_async_copy(partial.at[units, slice_of], out.at[units], partial_sems.at[c, k])
             copy.start()
             partial_copies.append(copy)
+    for e in range(0, x.shape[1], 128):
+        part = x[:, e : e + 128].T
+        sent_ref[e : e + 128, :] = dot(part, grad[1 - core], NN).astype(jnp.bfloat16)
+        kept_ref[e : e + 128, :] = dot(part, grad[core], NN)
     for cols in head_cols:
         att_ref[:, cols] = pltpu.roll(att[:, cols], LEAD, 0).astype(jnp.bfloat16)
         dq_ref[:, cols] = pltpu.roll(dq[:, cols], LEAD, 0).astype(jnp.bfloat16)
     tail_ref[:, :width] = att_ref[:SPAN, :]
     tail_ref[:, width:] = dq_ref[:SPAN, :]
-    for copy in grad_copies + partial_copies:
+    for copy in partial_copies:
         copy.wait()
 
 
@@ -116,58 +116,25 @@
     )(place, *args)
 
 
-def block(units_of, q, g, ahead, w, x, slices):
+def block(scalars, q, g, ahead, w, x, slices):
     tokens, width = q.shape
     all_rows, enc_width = x.shape
     units, piece = all_rows // PART, PART // slices
     return pl.pallas_call(
         block_body,
-        out_shape=[low(tokens, width), low(tokens, width), low(SPAN, 2 * width), low(2, all_rows, width), low(slices, units, piece, enc_width)],
-        in_specs=[SMEM] + [VMEM] * 4 + [HBM],
-        out_specs=[VMEM] * 3 + [HBM] * 2,
-        scratch_shapes=[pltpu.VMEM((all_rows, enc_width), jnp.bfloat16)]
-        + [pltpu.VMEM((all_rows, width), jnp.bfloat16)] * 2
+        out_shape=[low(tokens, width), low(tokens, width), low(SPAN, 2 * width)]
+        + [low(enc_width, width), wide(enc_width, width)]
+        + [low(units, piece, enc_width)] * slices,
+        in_specs=[SMEM] + [VMEM] * 5,
+        out_specs=[VMEM] * 5 + [HBM] * slices,
+        scratch_shapes=[pltpu.VMEM((all_rows, width), jnp.bfloat16)] * 2
         + [pltpu.VMEM((2, all_rows, width), jnp.bfloat16), pltpu.VMEM((units, slices, piece, enc_width), jnp.bfloat16)]
         + [pltpu.VMEM((tokens, width), jnp.bfloat16)] * 2
         + [pltpu.VMEM((tokens, width), jnp.float32)] * 2
-        + [pltpu.SemaphoreType.DMA((4,)), pltpu.SemaphoreType.DMA((2,)), pltpu.SemaphoreType.DMA((units // 4, slices))],
+        + [pltpu.SemaphoreType.DMA((units // 4, slices))],
         compiler_params=PARAMS,
         name="block",
-    )(units_of, q, g, ahead, w, x)
-
-
-def products(place, x, grad):
-    enc_width, width = x.shape[1], grad.shape[2]
-
-    def body(place_ref, x_hbm, grad_hbm, sent_ref, kept_ref, x_ref, grad_ref, sems):
-        core = place_ref[0]
-        copies = [
-            pltpu.make_async_copy(x_hbm, x_ref, sems.at[0]),
-            pltpu.make_async_copy(grad_hbm.at[1 - core], grad_ref.at[0], sems.at[1]),
-            pltpu.make_async_copy(grad_hbm.at[core], grad_ref.at[1], sems.at[2]),
-        ]
-        for copy in copies:
-            copy.start()
-        for copy in copies:
-            copy.wait()
-        for e in range(0, enc_width, 128):
-            part = x_ref[:, e : e + 128].T
-            sent_ref[e : e + 128, :] = dot(part, grad_ref[0], NN).astype(jnp.bfloat16)
-            kept_ref[e : e + 128, :] = dot(part, grad_ref[1], NN)
-
-    return pl.pallas_call(
-        body,
-        out_shape=[low(enc_width, width), wide(enc_width, width)],
-        in_specs=[SMEM, HBM, HBM],
-        out_specs=[VMEM, VMEM],
-        scratch_shapes=[
-            pltpu.VMEM(x.shape, jnp.bfloat16),
-            pltpu.VMEM(grad.shape, jnp.bfloat16),
-            pltpu.SemaphoreType.DMA((3,)),
-        ],
-        compiler_params=PARAMS,
-        name="products",
-    )(place, x, grad)
+    )(scalars, q, g, ahead, w, x)
 
 
 def cut(place, kept, away, att, dq, behind):
@@ -223,9 +190,51 @@
             pltpu.SemaphoreType.DMA((4,)),
             pltpu.SemaphoreType.DMA((4, groups)),
         ],
-        compiler_params=PARAMS,
+        compiler_params=pltpu.CompilerParams(vmem_limit_bytes=56 * 1024 * 1024),
         name="spread",
     )(x)
+
+
+def x_sum(place, own, parts, partial, term):
+    _, rows, width = own.shape
+
+    def body(place_ref, own_ref, *refs):
+        part_refs, partial_ref, term_ref, mine_ref, other_ref, acc_ref = refs[:3], *refs[3:]
+        high = place_ref[2]
+        for ref, at in ((mine_ref, high), (other_ref, 1 - high)):
+            total = own_ref[at]
+            for part in part_refs:
+                total = add(total, part[at])
+            ref[...] = total.astype(ref.dtype)
+        acc_ref[...] = add(partial_ref[...], term_ref[...])
+
+    out_shape = [wide(rows, width), low(rows, width), wide(*partial.shape)]
+    return call(body, "x_sum", out_shape, [], place, own, *parts, partial, term)
+
+
+def z_sum(place, mine, came, *held):
+    def body(_, mine_ref, came_ref, *refs):
+        refs[len(held)][...] = add(mine_ref[...], came_ref[...]).astype(jnp.bfloat16)
+
+    return pl.pallas_call(
+        body,
+        out_shape=[low(*mine.shape)] + [low(*h.shape) for h in held],
+        in_specs=[SMEM, VMEM, VMEM] + [HBM] * len(held),
+        out_specs=[VMEM] + [HBM] * len(held),
+        input_output_aliases={3 + n: 1 + n for n in range(len(held))},
+        compiler_params=PARAMS,
+        name="z_sum",
+    )(place, mine, came, *held)
+
+
+def y_sum(place, rows, came, acc, term, last):
+    def body(_, rows_ref, came_ref, acc_ref, term_ref, sum_ref, out_ref):
+        sum_ref[...] = add(rows_ref[...], came_ref[...]).astype(sum_ref.dtype)
+        out_ref[...] = add(acc_ref[...], term_ref[...]).astype(out_ref.dtype)
+
+    kind = low if last else wide
+    out_shape = [(wide if last else low)(*rows.shape), kind(*acc.shape)]
+    return call(body, "y_last" if last else "y_sum", out_shape, [], place, rows, came, acc, term)
 
 
 def join(place, mine, theirs):
@@ -253,6 +262,7 @@
     groups = lax.axis_size("nbr")
     ctx = lax.axis_index("ctx")
     dp = lax.axis_index("dp")
+    nbr = lax.axis_index("nbr")
     place = jnp.stack((ctx % 2, dp % 4, dp // 4)).astype(jnp.int32)
 
     x = exchange(spread(enc, groups)).reshape(units * PART, enc_width)
@@ -261,24 +271,24 @@
     ahead = permute(head, "ctx", lambda i: i - 1)
 
     unit_of = (neighbour_ids[0] // units).reshape(-1)
-    att, dq, tail, grad, partial = block(unit_of, q, g, ahead, kv_weight, x, groups)
+    scalars = jnp.concatenate((unit_of, nbr[None], (ctx % 2)[None])).astype(jnp.int32)
+    att, dq, tail, sent, kept, *partials = block(scalars, q, g, ahead, kv_weight, x, groups)
+
+    def returned(x, k):
+        return permute(x, "nbr", lambda i: (i + k) % groups)
+
+    term = returned(partials[2], 2)
     behind = permute(tail, "ctx", lambda i: i + 1)
-
-    total = lax.psum_scatter(partial, "nbr", scatter_dimension=0, tiled=False)
+    away = permute(sent, "ctx", lambda i: i ^ 1)
+    own, *sends, attended, query_grad = cut(place, kept, away, att, dq, behind)
+    parts = [permute(sends[k - 1], "dp", lambda i, k=k: i // 4 * 4 + (i + k) % 4) for k in (1, 2, 3)]
+    mine, other, acc = x_sum(place, own, parts, partials[0], term)
+    rows, first, third = z_sum(place, mine, permute(other, "dp", lambda i: (i + 4) % 8), partials[1], partials[3])
+
+    rows = add(rows, permute(rows, "ctx", lambda i: i ^ 2)).astype(jnp.bfloat16)
+    rows, acc = y_sum(place, rows, permute(rows, "ctx", lambda i: i ^ 4), acc, returned(first, 1), False)
+    mine, total = y_sum(place, rows, permute(rows, "ctx", lambda i: i ^ 8), acc, returned(third, 3), True)
     encoded_grad = lax.all_to_all(total, "ctx", split_axis=0, concat_axis=0, tiled=True)
-
-    sent, kept = products(place, x, grad)
-    away = permute(sent, "ctx", lambda i: i ^ 1)
-    held, *sends, attended, query_grad = cut(place, kept, away, att, dq, behind)
-    for k in (1, 3, 2):
-        held = add(held, permute(sends[k - 1], "dp", lambda i, k=k: i // 4 * 4 + (i + k) % 4))
-    high = dp // 4
-    other = lax.dynamic_index_in_dim(held, 1 - high, 0, keepdims=False).astype(jnp.bfloat16)
-    mine = lax.dynamic_index_in_dim(held, high, 0, keepdims=False)
-    mine = add(mine, permute(other, "dp", lambda i: (i + 4) % 8))
-    for bit in (2, 4, 8):
-        rows = mine.astype(jnp.bfloat16)
-        mine = add(rows, permute(rows, "ctx", lambda i, b=bit: i ^ b))
     weight_grad = join(place, mine, permute(mine, "ctx", lambda i: i ^ 1))
     return (attended[None], query_grad[None], encoded_grad[None], weight_grad)
 

time: 183 us -> 186 us (1.016)
  the two profiles are of different devices: /device:TPU:67 before, /device:TPU:1 now
where the time goes in v9:
time: 186 us; the launch traced here: 185 us
  waiting for transfers between devices  76.5 us (41%)
  starting transfers between devices  73.9 us (40%)
  Pallas kernels  21.4 us (12%)
  local copies, waits for them, and re-layouts  11.8 us (6%)
    ppermute x14, waiting for transfers between devices, permute(): lax.ppermute(x, axis, [(i, to(i)) for i in range(n) if 0 <= to(i) < n])  63.7 us
    ppermute x14, starting transfers between devices, permute(): lax.ppermute(x, axis, [(i, to(i)) for i in range(n) if 0 <= to(i) < n])  49 us
    all_to_all x1, starting transfers between devices, exchange(): lax.all_to_all(x.reshape(outer * inner, *rest), ('ctx', 'nbr'), split_axi...  14.7 us
    pallas_call x1, Pallas kernels, block(): pl.pallas_call(block_body, out_shape=[low(tokens, width), low(tokens, wid...  12.8 us
    all_to_all x1, waiting for transfers between devices, shards(): lax.all_to_all(total, 'ctx', split_axis=0, concat_axis=0, tiled=True)  11.3 us
    unnamed x25, local copies, waits for them, and re-layouts  10.8 us
    all_to_all x1, starting transfers between devices, shards(): lax.all_to_all(total, 'ctx', split_axis=0, concat_axis=0, tiled=True)  10.1 us
    pallas_call x5, Pallas kernels, call(): pl.pallas_call(body, out_shape=out_shape, in_specs=[SMEM] + [VMEM] * len(...  5.63 us
  transfers between devices with their start and end apart: 16, of which 13 were waited for; matrix products, arithmetic and copies ran while one was open for 1% of the time, Pallas kernels for 2%

profile of v9, /device:TPU:1, one launch (start us, length us, event | category | flops | bytes accessed | tf_op | source)
XLA Modules:
  0.0 184.7 jit_solution(14001372875296058339)
XLA Ops:
  0.6 2.3 %spread.1 = bf16[16,4,16,896]{3,2,1,0:T(8,128)(2,1)} custom-call(bf16[16,16,896]{2,1,0:T(8,128)(2,1)} %bitcast.21), custom_call_target="tpu_custom_call" | custom-call | tf_op jit(solution)/shard_map/spread/pallas_call | solution.py:183
  3.0 14.7 %all-to-all-start = ((bf16[64,16,896]{2,1,0:T(8,128)(2,1)}), bf16[64,16,896]{2,1,0:T(8,128)(2,1)S(1)}, u32[]{:S(2)}, u32[]{:S(2)}) async-start(bf16[64,16,896]{2,1,0:T(8,128)(2,1)} %bitcast.19), calls=%async_computation | async-start | bytes 3670016 | tf_op jit(solution)/shard_map/all_to_all | solution.py:255
  18.6 2.4 %collective-permute-start = (bf16[64,1024]{1,0:T(8,128)(2,1)S(1)}, bf16[64,1024]{1,0:T(8,128)(2,1)S(1)}, u32[]{:S(2)}, u32[]{:S(2)}) collective-permute-start(bf16[64,1024]{1,0:T(8,128)(2,1)S(1)} %pad_maximum_fusion), channel_id=1, source_target_pairs={{4,0},{8,4},{12,8},{16,12},{20,16},{24,20},{28,24},{32,28},{36,32}... | collective-permute-start | bytes 393224 | tf_op jit(solution)/shard_map/ppermute | solution.py:250
  21.2 39.8 %collective-permute-done.ahead_ref = bf16[64,1024]{1,0:T(8,128)(2,1)S(1)} collective-permute-done((bf16[64,1024]{1,0:T(8,128)(2,1)S(1)}, bf16[64,1024]{1,0:T(8,128)(2,1)S(1)}, u32[]{:S(2)}, u32[]{:S(2)}) %collective-permute-start) | collective-permute-done | bytes 131104 | tf_op jit(solution)/shard_map/ppermute | solution.py:250
  61.6 1.6 all-to-all-done
  63.2 1.5 copy-done
  66.5 12.8 %block.1 = (bf16[256,512]{1,0:T(8,128)(2,1)S(1)}, bf16[256,512]{1,0:T(8,128)(2,1)S(1)}, bf16[64,1024]{1,0:T(8,128)(2,1)}, bf16[896,512]{1,0:T(8,128)(2,1)}, f32[...) custom-call(s32[18]{0:T(128)S(1)} %pad_add_fusion.1.units_ref, ...), custom_call_target="tpu_custom_call" | custom-call | tf_op jit(solution)/shard_map/block/pallas_call | solution.py:123
  82.0 2.7 %collective-permute-start.1 = (bf16[896,512]{1,0:T(8,128)(2,1)}, bf16[896,512]{1,0:T(8,128)(2,1)S(1)}, u32[]{:S(2)}, u32[]{:S(2)}) collective-permute-start(bf16[896,512]{1,0:T(8,128)(2,1)} %get-tuple-element.30), channel_id=1, source_target_pairs={{0,4},{4,0},{8,12},{12,8},{16,20},{20,16},{24,28},{28,24},{32,36},... | collective-permute-start | bytes 2752520 | tf_op jit(solution)/shard_map/ppermute | solution.py:250
  84.7 3.3 %collective-permute-start.6 = (bf16[16,16,896]{2,1,0:T(8,128)(2,1)}, bf16[16,16,896]{2,1,0:T(8,128)(2,1)S(1)}, u32[]{:S(2)}, u32[]{:S(2)}) collective-permute-start(bf16[16,16,896]{2,1,0:T(8,128)(2,1)} %get-tuple-element.41), channel_id=1, source_target_pairs={{0,2},{1,3},{2,0},{3,1},{4,6},{5,7},{6,4},{7,5},{8,10},{9,11},{10,... | collective-permute-start | bytes 1376264 | tf_op jit(solution)/shard_map/ppermute | solution.py:250
  88.0 3.2 %collective-permute-start.2 = (bf16[64,1024]{1,0:T(8,128)(2,1)}, bf16[64,1024]{1,0:T(8,128)(2,1)S(1)}, u32[]{:S(2)}, u32[]{:S(2)}) collective-permute-start(bf16[64,1024]{1,0:T(8,128)(2,1)} %get-tuple-element.33), channel_id=1, source_target_pairs={{0,4},{4,8},{8,12},{12,16},{16,20},{20,24},{24,28},{28,32},{32,36}... | collective-permute-start | bytes 393224 | tf_op jit(solution)/shard_map/ppermute | solution.py:250
  91.3 2.1 %collective-permute-done.2.behind_ref = bf16[64,1024]{1,0:T(8,128)(2,1)S(1)} collective-permute-done((bf16[64,1024]{1,0:T(8,128)(2,1)}, bf16[64,1024]{1,0:T(8,128)(2,1)S(1)}, u32[]{:S(2)}, u32[]{:S(2)}) %collective-permute-start.2) | collective-permute-done | bytes 131104 | tf_op jit(solution)/shard_map/ppermute | solution.py:250
  93.4 1.5 copy-done.2
  96.8 1.5 cut.1
  98.4 3.1 %collective-permute-start.3 = (bf16[2,112,512]{2,1,0:T(8,128)(2,1)S(1)}, bf16[2,112,512]{2,1,0:T(8,128)(2,1)S(1)}, u32[]{:S(2)}, u32[]{:S(2)}) collective-permute-start(bf16[2,112,512]{2,1,0:T(8,128)(2,1)S(1)} %get-tuple-element.37), channel_id=1, source_target_pairs={{0,64},{64,128},{128,192},{192,0},{256,320},{320,384},{384,448},{4... | collective-permute-start | bytes 688136 | tf_op jit(solution)/shard_map/ppermute | solution.py:250
  101.5 4.4 %collective-permute-start.4 = (bf16[2,112,512]{2,1,0:T(8,128)(2,1)S(1)}, bf16[2,112,512]{2,1,0:T(8,128)(2,1)S(1)}, u32[]{:S(2)}, u32[]{:S(2)}) collective-permute-start(bf16[2,112,512]{2,1,0:T(8,128)(2,1)S(1)} %get-tuple-element.38), channel_id=1, source_target_pairs={{0,128},{64,192},{128,0},{192,64},{256,384},{320,448},{384,256},{4... | collective-permute-start | bytes 688136 | tf_op jit(solution)/shard_map/ppermute | solution.py:250
  105.9 3.1 %collective-permute-start.5 = (bf16[2,112,512]{2,1,0:T(8,128)(2,1)S(1)}, bf16[2,112,512]{2,1,0:T(8,128)(2,1)S(1)}, u32[]{:S(2)}, u32[]{:S(2)}) collective-permute-start(bf16[2,112,512]{2,1,0:T(8,128)(2,1)S(1)} %get-tuple-element.39), channel_id=1, source_target_pairs={{0,192},{64,0},{128,64},{192,128},{256,448},{320,256},{384,320},{4... | collective-permute-start | bytes 688136 | tf_op jit(solution)/shard_map/ppermute | solution.py:250
  109.7 3.6 %collective-permute-done.4.refs_1_ = bf16[2,112,512]{2,1,0:T(8,128)(2,1)S(1)} collective-permute-done((bf16[2,112,512]{2,1,0:T(8,128)(2,1)S(1)}, bf16[2,112,512]{2,1,0:T(8,128)(2,1)S(1)}, u32[]{:S(2)}, u32[]{:S(2)}) %collective-permute-start.4) | collective-permute-done | bytes 229408 | tf_op jit(solution)/shard_map/ppermute | solution.py:250
  113.3 1.8 collective-permute-done.5.refs_2_
  115.8 7.9 %collective-permute-start.7 = (bf16[112,512]{1,0:T(8,128)(2,1)S(1)}, bf16[112,512]{1,0:T(8,128)(2,1)S(1)}, u32[]{:S(2)}, u32[]{:S(2)}) collective-permute-start(bf16[112,512]{1,0:T(8,128)(2,1)S(1)} %get-tuple-element.43), channel_id=1, source_target_pairs={{0,256},{64,320},{128,384},{192,448},{256,0},{320,64},{384,128},{4... | collective-permute-start | bytes 344072 | tf_op jit(solution)/shard_map/ppermute | solution.py:250
  123.8 3.6 %collective-permute-done.7.came_ref = bf16[112,512]{1,0:T(8,128)(2,1)S(1)} collective-permute-done((bf16[112,512]{1,0:T(8,128)(2,1)S(1)}, bf16[112,512]{1,0:T(8,128)(2,1)S(1)}, u32[]{:S(2)}, u32[]{:S(2)}) %collective-permute-start.7) | collective-permute-done | bytes 114720 | tf_op jit(solution)/shard_map/ppermute | solution.py:250
  128.0 1.9 %collective-permute-start.8 = (bf16[112,512]{1,0:T(8,128)(2,1)S(1)}, bf16[112,512]{1,0:T(8,128)(2,1)S(1)}, u32[]{:S(2)}, u32[]{:S(2)}) collective-permute-start(bf16[112,512]{1,0:T(8,128)(2,1)S(1)} %get-tuple-element.46), channel_id=1, source_target_pairs={{0,8},{4,12},{8,0},{12,4},{16,24},{20,28},{24,16},{28,20},{32,40},... | collective-permute-start | bytes 344072 | tf_op jit(solution)/shard_map/ppermute | solution.py:250
  129.9 6.2 %collective-permute-start.10 = (bf16[16,16,896]{2,1,0:T(8,128)(2,1)S(1)}, bf16[16,16,896]{2,1,0:T(8,128)(2,1)S(1)}, u32[]{:S(2)}, u32[]{:S(2)}) collective-permute-start(bf16[16,16,896]{2,1,0:T(8,128)(2,1)S(1)} %get-tuple-element.48), channel_id=1, source_target_pairs={{0,1},{1,2},{2,3},{3,0},{4,5},{5,6},{6,7},{7,4},{8,9},{9,10},{10,1... | collective-permute-start | bytes 1376264 | tf_op jit(solution)/shard_map/ppermute | solution.py:250
  136.1 1.9 %collective-permute-start.12 = (bf16[16,16,896]{2,1,0:T(8,128)(2,1)S(1)}, bf16[16,16,896]{2,1,0:T(8,128)(2,1)S(1)}, u32[]{:S(2)}, u32[]{:S(2)}) collective-permute-start(bf16[16,16,896]{2,1,0:T(8,128)(2,1)S(1)} %get-tuple-element.51), channel_id=1, source_target_pairs={{0,3},{1,0},{2,1},{3,2},{4,7},{5,4},{6,5},{7,6},{8,11},{9,8},{10,9... | collective-permute-start | bytes 1376264 | tf_op jit(solution)/shard_map/ppermute | solution.py:250
  138.1 4.0 %collective-permute-start.9 = (bf16[112,512]{1,0:T(8,128)(2,1)S(1)}, bf16[112,512]{1,0:T(8,128)(2,1)S(1)}, u32[]{:S(2)}, u32[]{:S(2)}) collective-permute-start(bf16[112,512]{1,0:T(8,128)(2,1)S(1)} %add_convert_fusion.rows_ref), channel_id=1, source_target_pairs={{0,16},{4,20},{8,24},{12,28},{16,0},{20,4},{24,8},{28,12},{32,48},... | collective-permute-start | bytes 344072 | tf_op jit(solution)/shard_map/ppermute | solution.py:250
  142.1 2.7 %collective-permute-done.9.came_ref = bf16[112,512]{1,0:T(8,128)(2,1)S(1)} collective-permute-done((bf16[112,512]{1,0:T(8,128)(2,1)S(1)}, bf16[112,512]{1,0:T(8,128)(2,1)S(1)}, u32[]{:S(2)}, u32[]{:S(2)}) %collective-permute-start.9) | collective-permute-done | bytes 114720 | tf_op jit(solution)/shard_map/ppermute | solution.py:250
  146.0 3.0 %collective-permute-start.11 = (bf16[112,512]{1,0:T(8,128)(2,1)S(1)}, bf16[112,512]{1,0:T(8,128)(2,1)S(1)}, u32[]{:S(2)}, u32[]{:S(2)}) collective-permute-start(bf16[112,512]{1,0:T(8,128)(2,1)S(1)} %get-tuple-element.49.rows_ref), channel_id=1, source_target_pairs={{0,32},{4,36},{8,40},{12,44},{16,48},{20,52},{24,56},{28,60},{32,0... | collective-permute-start | bytes 344072 | tf_op jit(solution)/shard_map/ppermute | solution.py:250
  149.0 6.9 %collective-permute-done.12.term_ref = bf16[16,16,896]{2,1,0:T(8,128)(2,1)S(1)} collective-permute-done((bf16[16,16,896]{2,1,0:T(8,128)(2,1)S(1)}, bf16[16,16,896]{2,1,0:T(8,128)(2,1)S(1)}, u32[]{:S(2)}, u32[]{:S(2)}) %collective-permute-start.12) | collective-permute-done | bytes 458784 | tf_op jit(solution)/shard_map/ppermute | solution.py:250
  156.4 1.4 y_last.1
  157.8 10.1 %all-to-all-start.1 = ((bf16[16,16,896]{2,1,0:T(8,128)(2,1)}), bf16[16,16,896]{2,1,0:T(8,128)(2,1)S(1)}, u32[]{:S(2)}, u32[]{:S(2)}) async-start(bf16[16,16,896]{2,1,0:T(8,128)(2,1)} %get-tuple-element.52), calls=%async_computation.1 | async-start | bytes 917504 | tf_op jit(solution)/shard_map/all_to_all | solution.py:291
  167.9 2.0 %collective-permute-start.13 = (f32[112,512]{1,0:T(8,128)S(1)}, f32[112,512]{1,0:T(8,128)S(1)}, u32[]{:S(2)}, u32[]{:S(2)}) collective-permute-start(f32[112,512]{1,0:T(8,128)S(1)} %get-tuple-element.53.mine_ref), channel_id=1, source_target_pairs={{0,4},{4,0},{8,12},{12,8},{16,20},{20,16},{24,28},{28,24},{32,36},... | collective-permute-start | bytes 688136 | tf_op jit(solution)/shard_map/ppermute | solution.py:250
  170.0 1.4 collective-permute-done.13.theirs_ref
  172.6 11.3 %all-to-all-done.1 = bf16[16,16,896]{2,1,0:T(8,128)(2,1)S(1)} async-done(((bf16[16,16,896]{2,1,0:T(8,128)(2,1)}), bf16[16,16,896]{2,1,0:T(8,128)(2,1)S(1)}, u32[]{:S(2)}, u32[]{:S(2)}) %all-to-all-start.1) | async-done | bytes 458784 | tf_op jit(solution)/shard_map/all_to_all | solution.py:291
  (40 shorter events, 14.1 us)
Async XLA Ops:
  3.0 14.8 %copy-start.3 = (bf16[1,256,512]{2,1,0:T(8,128)(2,1)S(1)}, bf16[1,256,512]{2,1,0:T(8,128)(2,1)}, u32[]{:S(2)}) copy-start(bf16[1,256,512]{2,1,0:T(8,128)(2,1)} %param.5) | copy-start | bytes 786436
  3.0 18.0 %copy-start.11 = (s32[1,4,4]{2,1,0:T(4,128)S(1)}, s32[1,4,4]{2,1,0:T(4,128)}, u32[]{:S(2)}) copy-start(s32[1,4,4]{2,1,0:T(4,128)} %param.9) | copy-start | bytes 196
  3.0 60.2 %all-to-all-start = ((bf16[64,16,896]{2,1,0:T(8,128)(2,1)}), bf16[64,16,896]{2,1,0:T(8,128)(2,1)S(1)}, u32[]{:S(2)}, u32[]{:S(2)}) async-start(bf16[64,16,896]{2,1,0:T(8,128)(2,1)} %bitcast.19), calls=%async_computation | async-start | bytes 3670016 | tf_op jit(solution)/shard_map/all_to_all | solution.py:255
  18.6 42.3 %collective-permute-start = (bf16[64,1024]{1,0:T(8,128)(2,1)S(1)}, bf16[64,1024]{1,0:T(8,128)(2,1)S(1)}, u32[]{:S(2)}, u32[]{:S(2)}) collective-permute-start(bf16[64,1024]{1,0:T(8,128)(2,1)S(1)} %pad_maximum_fusion), channel_id=1, source_target_pairs={{4,0},{8,4},{12,8},{16,12},{20,16},{24,20},{28,24},{32,28},{36,32}... | collective-permute-start | bytes 393224 | tf_op jit(solution)/shard_map/ppermute | solution.py:250
  60.9 0.7 copy-start.9
  63.1 1.5 copy-start
  64.7 0.9 copy-start.4
  65.6 0.9 copy-start.10
  79.3 1.3 copy-start.1
  80.6 0.7 copy-start.5
  81.3 0.7 copy-start.7
  82.0 11.4 %collective-permute-start.1 = (bf16[896,512]{1,0:T(8,128)(2,1)}, bf16[896,512]{1,0:T(8,128)(2,1)S(1)}, u32[]{:S(2)}, u32[]{:S(2)}) collective-permute-start(bf16[896,512]{1,0:T(8,128)(2,1)} %get-tuple-element.30), channel_id=1, source_target_pairs={{0,4},{4,0},{8,12},{12,8},{16,20},{20,16},{24,28},{28,24},{32,36},... | collective-permute-start | bytes 2752520 | tf_op jit(solution)/shard_map/ppermute | solution.py:250
  84.7 25.0 %collective-permute-start.6 = (bf16[16,16,896]{2,1,0:T(8,128)(2,1)}, bf16[16,16,896]{2,1,0:T(8,128)(2,1)S(1)}, u32[]{:S(2)}, u32[]{:S(2)}) collective-permute-start(bf16[16,16,896]{2,1,0:T(8,128)(2,1)} %get-tuple-element.41), channel_id=1, source_target_pairs={{0,2},{1,3},{2,0},{3,1},{4,6},{5,7},{6,4},{7,5},{8,10},{9,11},{10,... | collective-permute-start | bytes 1376264 | tf_op jit(solution)/shard_map/ppermute | solution.py:250
  88.0 5.4 %collective-permute-start.2 = (bf16[64,1024]{1,0:T(8,128)(2,1)}, bf16[64,1024]{1,0:T(8,128)(2,1)S(1)}, u32[]{:S(2)}, u32[]{:S(2)}) collective-permute-start(bf16[64,1024]{1,0:T(8,128)(2,1)} %get-tuple-element.33), channel_id=1, source_target_pairs={{0,4},{4,8},{8,12},{12,16},{16,20},{20,24},{24,28},{28,32},{32,36}... | collective-permute-start | bytes 393224 | tf_op jit(solution)/shard_map/ppermute | solution.py:250
  93.4 1.5 copy-start.2
  94.9 0.9 copy-start.6
  95.9 0.9 copy-start.8
  98.4 11.3 %collective-permute-start.3 = (bf16[2,112,512]{2,1,0:T(8,128)(2,1)S(1)}, bf16[2,112,512]{2,1,0:T(8,128)(2,1)S(1)}, u32[]{:S(2)}, u32[]{:S(2)}) collective-permute-start(bf16[2,112,512]{2,1,0:T(8,128)(2,1)S(1)} %get-tuple-element.37), channel_id=1, source_target_pairs={{0,64},{64,128},{128,192},{192,0},{256,320},{320,384},{384,448},{4... | collective-permute-start | bytes 688136 | tf_op jit(solution)/shard_map/ppermute | solution.py:250
  101.5 11.8 %collective-permute-start.4 = (bf16[2,112,512]{2,1,0:T(8,128)(2,1)S(1)}, bf16[2,112,512]{2,1,0:T(8,128)(2,1)S(1)}, u32[]{:S(2)}, u32[]{:S(2)}) collective-permute-start(bf16[2,112,512]{2,1,0:T(8,128)(2,1)S(1)} %get-tuple-element.38), channel_id=1, source_target_pairs={{0,128},{64,192},{128,0},{192,64},{256,384},{320,448},{384,256},{4... | collective-permute-start | bytes 688136 | tf_op jit(solution)/shard_map/ppermute | solution.py:250
  105.9 9.2 %collective-permute-start.5 = (bf16[2,112,512]{2,1,0:T(8,128)(2,1)S(1)}, bf16[2,112,512]{2,1,0:T(8,128)(2,1)S(1)}, u32[]{:S(2)}, u32[]{:S(2)}) collective-permute-start(bf16[2,112,512]{2,1,0:T(8,128)(2,1)S(1)} %get-tuple-element.39), channel_id=1, source_target_pairs={{0,192},{64,0},{128,64},{192,128},{256,448},{320,256},{384,320},{4... | collective-permute-start | bytes 688136 | tf_op jit(solution)/shard_map/ppermute | solution.py:250
  115.8 11.5 %collective-permute-start.7 = (bf16[112,512]{1,0:T(8,128)(2,1)S(1)}, bf16[112,512]{1,0:T(8,128)(2,1)S(1)}, u32[]{:S(2)}, u32[]{:S(2)}) collective-permute-start(bf16[112,512]{1,0:T(8,128)(2,1)S(1)} %get-tuple-element.43), channel_id=1, source_target_pairs={{0,256},{64,320},{128,384},{192,448},{256,0},{320,64},{384,128},{4... | collective-permute-start | bytes 344072 | tf_op jit(solution)/shard_map/ppermute | solution.py:250
  128.0 10.1 %collective-permute-start.8 = (bf16[112,512]{1,0:T(8,128)(2,1)S(1)}, bf16[112,512]{1,0:T(8,128)(2,1)S(1)}, u32[]{:S(2)}, u32[]{:S(2)}) collective-permute-start(bf16[112,512]{1,0:T(8,128)(2,1)S(1)} %get-tuple-element.46), channel_id=1, source_target_pairs={{0,8},{4,12},{8,0},{12,4},{16,24},{20,28},{24,16},{28,20},{32,40},... | collective-permute-start | bytes 344072 | tf_op jit(solution)/shard_map/ppermute | solution.py:250
  129.9 15.4 %collective-permute-start.10 = (bf16[16,16,896]{2,1,0:T(8,128)(2,1)S(1)}, bf16[16,16,896]{2,1,0:T(8,128)(2,1)S(1)}, u32[]{:S(2)}, u32[]{:S(2)}) collective-permute-start(bf16[16,16,896]{2,1,0:T(8,128)(2,1)S(1)} %get-tuple-element.48), channel_id=1, source_target_pairs={{0,1},{1,2},{2,3},{3,0},{4,5},{5,6},{6,7},{7,4},{8,9},{9,10},{10,1... | collective-permute-start | bytes 1376264 | tf_op jit(solution)/shard_map/ppermute | solution.py:250
  136.1 19.7 %collective-permute-start.12 = (bf16[16,16,896]{2,1,0:T(8,128)(2,1)S(1)}, bf16[16,16,896]{2,1,0:T(8,128)(2,1)S(1)}, u32[]{:S(2)}, u32[]{:S(2)}) collective-permute-start(bf16[16,16,896]{2,1,0:T(8,128)(2,1)S(1)} %get-tuple-element.51), channel_id=1, source_target_pairs={{0,3},{1,0},{2,1},{3,2},{4,7},{5,4},{6,5},{7,6},{8,11},{9,8},{10,9... | collective-permute-start | bytes 1376264 | tf_op jit(solution)/shard_map/ppermute | solution.py:250
  138.1 6.7 %collective-permute-start.9 = (bf16[112,512]{1,0:T(8,128)(2,1)S(1)}, bf16[112,512]{1,0:T(8,128)(2,1)S(1)}, u32[]{:S(2)}, u32[]{:S(2)}) collective-permute-start(bf16[112,512]{1,0:T(8,128)(2,1)S(1)} %add_convert_fusion.rows_ref), channel_id=1, source_target_pairs={{0,16},{4,20},{8,24},{12,28},{16,0},{20,4},{24,8},{28,12},{32,48},... | collective-permute-start | bytes 344072 | tf_op jit(solution)/shard_map/ppermute | solution.py:250
  146.0 10.4 %collective-permute-start.11 = (bf16[112,512]{1,0:T(8,128)(2,1)S(1)}, bf16[112,512]{1,0:T(8,128)(2,1)S(1)}, u32[]{:S(2)}, u32[]{:S(2)}) collective-permute-start(bf16[112,512]{1,0:T(8,128)(2,1)S(1)} %get-tuple-element.49.rows_ref), channel_id=1, source_target_pairs={{0,32},{4,36},{8,40},{12,44},{16,48},{20,52},{24,56},{28,60},{32,0... | collective-permute-start | bytes 344072 | tf_op jit(solution)/shard_map/ppermute | solution.py:250
  157.8 26.1 %all-to-all-start.1 = ((bf16[16,16,896]{2,1,0:T(8,128)(2,1)}), bf16[16,16,896]{2,1,0:T(8,128)(2,1)S(1)}, u32[]{:S(2)}, u32[]{:S(2)}) async-start(bf16[16,16,896]{2,1,0:T(8,128)(2,1)} %get-tuple-element.52), calls=%async_computation.1 | async-start | bytes 917504 | tf_op jit(solution)/shard_map/all_to_all | solution.py:291
  167.9 3.4 %collective-permute-start.13 = (f32[112,512]{1,0:T(8,128)S(1)}, f32[112,512]{1,0:T(8,128)S(1)}, u32[]{:S(2)}, u32[]{:S(2)}) collective-permute-start(f32[112,512]{1,0:T(8,128)S(1)} %get-tuple-element.53.mine_ref), channel_id=1, source_target_pairs={{0,4},{4,0},{8,12},{12,8},{16,20},{20,16},{24,28},{28,24},{32,36},... | collective-permute-start | bytes 688136 | tf_op jit(solution)/shard_map/ppermute | solution.py:250

commit v10 on v9

--- a/solution.py
+++ b/solution.py
@@ -18,7 +18,7 @@
 VMEM = pl.BlockSpec(memory_space=pltpu.VMEM)
 SMEM = pl.BlockSpec(memory_space=pltpu.SMEM)
 HBM = pl.BlockSpec(memory_space=pltpu.HBM)
-PARAMS = pltpu.CompilerParams(vmem_limit_bytes=28 * 1024 * 1024)
+PARAMS = pltpu.CompilerParams(vmem_limit_bytes=50 * 1024 * 1024)
 
 
 def dot(a, b, dims):
@@ -33,22 +33,28 @@
 
 
 def block_body(
-    units_ref, q_ref, g_ref, ahead_ref, w_ref, x, att_ref, dq_ref, tail_ref, sent_ref, kept_ref, *refs
+    units_ref, q_hbm, g_hbm, ahead_hbm, w_hbm, x, att_ref, dq_ref, tail_ref, sent_ref, kept_ref, partial_hbm,
+    key, value, grad, partial, q_ref, g_ref, ahead_ref, w_ref, q_rows, g_rows, att, dq, in_sems, out_sems,
 ):
-    partial_hbms = refs[:-9]
-    key, value, grad, partial, q_rows, g_rows, att, dq, partial_sems = refs[-9:]
+    pairs = ((w_hbm, w_ref), (q_hbm, q_ref), (g_hbm, g_ref), (ahead_hbm, ahead_ref))
+    copies_in = [pltpu.make_async_copy(source, held, in_sems.at[n]) for n, (source, held) in enumerate(pairs)]
+    for copy in copies_in:
+        copy.start()
     tokens, width = q_ref.shape
     heads = width // HEAD_DIM
     chunk = 4 * PART
-    nbr, core = units_ref[units_ref.shape[0] - 2], units_ref[units_ref.shape[0] - 1]
+    core = units_ref[units_ref.shape[0] - 1]
     chunks = [pl.ds(c * chunk, chunk) for c in range(x.shape[0] // chunk)]
     head_cols = [pl.ds(h * HEAD_DIM, HEAD_DIM) for h in range(heads)]
+    copies_in[0].wait()
+    for rows in chunks:
+        for kind, out in enumerate((key, value)):
+            out[rows, :] = dot(x[rows, :], w_ref[kind], NN).astype(jnp.bfloat16)
+    for copy in copies_in[1:]:
+        copy.wait()
     for h, cols in enumerate(head_cols):
         q_rows[:, cols] = span_rows(q_ref[:, cols], ahead_ref[:, cols])
         g_rows[:, cols] = span_rows(g_ref[:, cols], ahead_ref[:, pl.ds(width + h * HEAD_DIM, HEAD_DIM)])
-    for rows in chunks:
-        for kind, out in enumerate((key, value)):
-            out[rows, :] = dot(x[rows, :], w_ref[kind], NN).astype(jnp.bfloat16)
     for j in range(tokens // SPAN):
         starts = [pl.multiple_of(units_ref[j * 4 + r] * PART, PART) for r in range(4)]
         rows = pl.ds(j * SPAN, SPAN)
@@ -76,13 +82,10 @@
     partial_copies = []
     for c, rows in enumerate(chunks):
         term = dot(grad[0, rows, :], w_ref[0], NT) + dot(grad[1, rows, :], w_ref[1], NT)
-        units = pl.ds(c * 4, 4)
-        partial[units] = term.astype(jnp.bfloat16).reshape(4, *partial.shape[1:])
-        for k, out in enumerate(partial_hbms):
-            slice_of = lax.rem(nbr + k, len(partial_hbms))
-            copy = pltpu.make_async_copy(partial.at[units, slice_of], out.at[units], partial_sems.at[c, k])
-            copy.start()
-            partial_copies.append(copy)
+        partial[rows, :] = term.astype(jnp.bfloat16)
+        copy = pltpu.make_async_copy(partial.at[rows], partial_hbm.at[rows], out_sems.at[c])
+        copy.start()
+        partial_copies.append(copy)
     for e in range(0, x.shape[1], 128):
         part = x[:, e : e + 128].T
         sent_ref[e : e + 128, :] = dot(part, grad[1 - core], NN).astype(jnp.bfloat16)
@@ -116,33 +119,32 @@
     )(place, *args)
 
 
-def block(scalars, q, g, ahead, w, x, slices):
+def block(scalars, q, g, ahead, w, x):
     tokens, width = q.shape
     all_rows, enc_width = x.shape
-    units, piece = all_rows // PART, PART // slices
+    rows = pltpu.VMEM((all_rows, width), jnp.bfloat16)
+    half = pltpu.VMEM((tokens, width), jnp.bfloat16)
     return pl.pallas_call(
         block_body,
         out_shape=[low(tokens, width), low(tokens, width), low(SPAN, 2 * width)]
-        + [low(enc_width, width), wide(enc_width, width)]
-        + [low(units, piece, enc_width)] * slices,
-        in_specs=[SMEM] + [VMEM] * 5,
-        out_specs=[VMEM] * 5 + [HBM] * slices,
-        scratch_shapes=[pltpu.VMEM((all_rows, width), jnp.bfloat16)] * 2
-        + [pltpu.VMEM((2, all_rows, width), jnp.bfloat16), pltpu.VMEM((units, slices, piece, enc_width), jnp.bfloat16)]
-        + [pltpu.VMEM((tokens, width), jnp.bfloat16)] * 2
+        + [low(enc_width, width), wide(enc_width, width), low(all_rows, enc_width)],
+        in_specs=[SMEM] + [HBM] * 4 + [VMEM],
+        out_specs=[VMEM] * 5 + [HBM],
+        scratch_shapes=[rows, rows, pltpu.VMEM((2, all_rows, width), jnp.bfloat16)]
+        + [pltpu.VMEM((all_rows, enc_width), jnp.bfloat16), half, half]
+        + [pltpu.VMEM(ahead.shape, jnp.bfloat16), pltpu.VMEM(w.shape, jnp.bfloat16), half, half]
         + [pltpu.VMEM((tokens, width), jnp.float32)] * 2
-        + [pltpu.SemaphoreType.DMA((units // 4, slices))],
-        compiler_params=PARAMS,
+        + [pltpu.SemaphoreType.DMA((4,))] * 2,
+        compiler_params=pltpu.CompilerParams(vmem_limit_bytes=52 * 1024 * 1024),
         name="block",
     )(scalars, q, g, ahead, w, x)
 
 
-def cut(place, kept, away, att, dq, behind):
+def cut(place, kept, away):
     enc_width, width = kept.shape
     rows = enc_width // 8
 
-    def body(place_ref, kept_ref, away_ref, att_ref, dq_ref, behind_ref, own_ref, *refs):
-        send_refs, full_refs = refs[:3], refs[3:]
+    def body(place_ref, kept_ref, away_ref, own_ref, *send_refs):
         x = place_ref[1]
         for high in range(2):
             for k in range(4):
@@ -152,14 +154,8 @@
                     send_refs[k - 1][high] = term.astype(jnp.bfloat16)
                 else:
                     own_ref[high] = term
-        lead = lax.broadcasted_iota(jnp.int32, (SPAN, width), 0) < LEAD
-        for n, (ref, full) in enumerate(zip((att_ref, dq_ref), full_refs)):
-            came = behind_ref[:, n * width : (n + 1) * width].astype(jnp.float32)
-            full[:SPAN, :] = jnp.where(lead, came, ref[:SPAN, :].astype(jnp.float32)).astype(jnp.bfloat16)
-            full[SPAN:, :] = ref[SPAN:, :]
-
-    out_shape = [wide(2, rows, width)] + [low(2, rows, width)] * 3 + [low(*att.shape)] * 2
-    return call(body, "cut", out_shape, [], place, kept, away, att, dq, behind)
+
+    return call(body, "cut", [wide(2, rows, width)] + [low(2, rows, width)] * 3, [], place, kept, away)
 
 
 def spread(x, groups):
@@ -195,46 +191,41 @@
     )(x)
 
 
-def x_sum(place, own, parts, partial, term):
-    _, rows, width = own.shape
-
-    def body(place_ref, own_ref, *refs):
-        part_refs, partial_ref, term_ref, mine_ref, other_ref, acc_ref = refs[:3], *refs[3:]
-        high = place_ref[2]
-        for ref, at in ((mine_ref, high), (other_ref, 1 - high)):
-            total = own_ref[at]
-            for part in part_refs:
-                total = add(total, part[at])
-            ref[...] = total.astype(ref.dtype)
-        acc_ref[...] = add(partial_ref[...], term_ref[...])
-
-    out_shape = [wide(rows, width), low(rows, width), wide(*partial.shape)]
-    return call(body, "x_sum", out_shape, [], place, own, *parts, partial, term)
-
-
-def z_sum(place, mine, came, *held):
-    def body(_, mine_ref, came_ref, *refs):
-        refs[len(held)][...] = add(mine_ref[...], came_ref[...]).astype(jnp.bfloat16)
+def gather_up(place, terms, att, dq, behind):
+    units, groups, piece, enc_width = terms.shape
+    width = att.shape[1]
+
+    def body(_, terms_ref, att_ref, dq_ref, behind_ref, total_ref, *full_refs):
+        for u in range(units):
+            total = add(terms_ref[u, 0], terms_ref[u, 1])
+            for n in range(2, groups):
+                total = add(total, terms_ref[u, n])
+            total_ref[u] = total.astype(jnp.bfloat16)
+        lead = lax.broadcasted_iota(jnp.int32, (SPAN, width), 0) < LEAD
+        for n, (ref, full) in enumerate(zip((att_ref, dq_ref), full_refs)):
+            came = behind_ref[:, n * width : (n + 1) * width].astype(jnp.float32)
+            full[:SPAN, :] = jnp.where(lead, came, ref[:SPAN, :].astype(jnp.float32)).astype(jnp.bfloat16)
+            full[SPAN:, :] = ref[SPAN:, :]
+
+    out_shape = [low(units, piece, enc_width), low(*att.shape), low(*dq.shape)]
+    return call(body, "gather_up", out_shape, [], place, terms, att, dq, behind)
+
+
+def sum_rows(place, name, rows, *after):
+    def body(_, *refs):
+        terms = [ref[...] for ref in refs[: len(rows)]]
+        while len(terms) > 1:
+            terms = [add(a, b) for a, b in zip(terms[::2], terms[1::2])]
+        refs[-1][...] = terms[0].astype(jnp.bfloat16)
 
     return pl.pallas_call(
         body,
-        out_shape=[low(*mine.shape)] + [low(*h.shape) for h in held],
-        in_specs=[SMEM, VMEM, VMEM] + [HBM] * len(held),
-        out_specs=[VMEM] + [HBM] * len(held),
-        input_output_aliases={3 + n: 1 + n for n in range(len(held))},
+        out_shape=low(*rows[0].shape),
+        in_specs=[SMEM] + [VMEM] * len(rows) + [HBM] * len(after),
+        out_specs=VMEM,
         compiler_params=PARAMS,
-        name="z_sum",
-    )(place, mine, came, *held)
-
-
-def y_sum(place, rows, came, acc, term, last):
-    def body(_, rows_ref, came_ref, acc_ref, term_ref, sum_ref, out_ref):
-        sum_ref[...] = add(rows_ref[...], came_ref[...]).astype(sum_ref.dtype)
-        out_ref[...] = add(acc_ref[...], term_ref[...]).astype(out_ref.dtype)
-
-    kind = low if last else wide
-    out_shape = [(wide if last else low)(*rows.shape), kind(*acc.shape)]
-    return call(body, "y_last" if last else "y_sum", out_shape, [], place, rows, came, acc, term)
+        name=name,
+    )(place, *rows, *after)
 
 
 def join(place, mine, theirs):
@@ -262,7 +253,6 @@
     groups = lax.axis_size("nbr")
     ctx = lax.axis_index("ctx")
     dp = lax.axis_index("dp")
-    nbr = lax.axis_index("nbr")
     place = jnp.stack((ctx % 2, dp % 4, dp // 4)).astype(jnp.int32)
 
     x = exchange(spread(enc, groups)).reshape(units * PART, enc_width)
@@ -271,24 +261,30 @@
     ahead = permute(head, "ctx", lambda i: i - 1)
 
     unit_of = (neighbour_ids[0] // units).reshape(-1)
-    scalars = jnp.concatenate((unit_of, nbr[None], (ctx % 2)[None])).astype(jnp.int32)
-    att, dq, tail, sent, kept, *partials = block(scalars, q, g, ahead, kv_weight, x, groups)
-
-    def returned(x, k):
-        return permute(x, "nbr", lambda i: (i + k) % groups)
-
-    term = returned(partials[2], 2)
+    scalars = jnp.concatenate((unit_of, (ctx % 2)[None])).astype(jnp.int32)
+    att, dq, tail, sent, kept, partial = block(scalars, q, g, ahead, kv_weight, x)
+
+    terms = exchange(partial.reshape(units, groups, piece, enc_width))
     behind = permute(tail, "ctx", lambda i: i + 1)
-    away = permute(sent, "ctx", lambda i: i ^ 1)
-    own, *sends, attended, query_grad = cut(place, kept, away, att, dq, behind)
-    parts = [permute(sends[k - 1], "dp", lambda i, k=k: i // 4 * 4 + (i + k) % 4) for k in (1, 2, 3)]
-    mine, other, acc = x_sum(place, own, parts, partials[0], term)
-    rows, first, third = z_sum(place, mine, permute(other, "dp", lambda i: (i + 4) % 8), partials[1], partials[3])
-
-    rows = add(rows, permute(rows, "ctx", lambda i: i ^ 2)).astype(jnp.bfloat16)
-    rows, acc = y_sum(place, rows, permute(rows, "ctx", lambda i: i ^ 4), acc, returned(first, 1), False)
-    mine, total = y_sum(place, rows, permute(rows, "ctx", lambda i: i ^ 8), acc, returned(third, 3), True)
-    encoded_grad = lax.all_to_all(total, "ctx", split_axis=0, concat_axis=0, tiled=True)
+
+    held, *sends = cut(place, kept, permute(sent, "ctx", lambda i: i ^ 1))
+    for k in (1, 3, 2):
+        held = add(held, permute(sends[k - 1], "dp", lambda i, k=k: i // 4 * 4 + (i + k) % 4))
+    high = dp // 4
+    held = held.astype(jnp.bfloat16)
+    other = lax.dynamic_index_in_dim(held, 1 - high, 0, keepdims=False)
+    mine = lax.dynamic_index_in_dim(held, high, 0, keepdims=False)
+    owners = lax.axis_size("ctx")
+    quad = (
+        mine,
+        permute(other, "dp", lambda i: i ^ 4),
+        permute(mine, "ctx", lambda i: i ^ 2),
+        permute(other, ("dp", "ctx"), lambda i: i ^ (4 * owners + 2)),
+    )
+    rows = sum_rows(place, "z_and_y", quad, behind)
+    encoded_grad, attended, query_grad = gather_up(place, terms, att, dq, behind)
+    rows = sum_rows(place, "y", (rows, permute(rows, "ctx", lambda i: i ^ 4)), encoded_grad)
+    mine = add(rows, permute(rows, "ctx", lambda i: i ^ 8))
     weight_grad = join(place, mine, permute(mine, "ctx", lambda i: i ^ 1))
     return (attended[None], query_grad[None], encoded_grad[None], weight_grad)
 

time: 186 us -> 171 us (0.919)
  local copies, waits for them, and re-layouts: 11.8 us -> 4.01 us
  waiting for transfers between devices: 76.5 us -> 69.8 us
  starting transfers between devices: 73.9 us -> 71.4 us
    all_to_all x1 -> x0, waiting for transfers between devices: 11.3 us -> none  [shards(): lax.all_to_all(total, 'ctx', split_axis=0, concat_axis=0, tiled=True)]
    all_to_all x1 -> x0, starting transfers between devices: 10.1 us -> none  [shards(): lax.all_to_all(total, 'ctx', split_axis=0, concat_axis=0, tiled=True)]
    unnamed x25 -> x18, local copies, waits for them, and re-layouts: 10.8 us -> 3.9 us
    all_to_all x1 -> x2, starting transfers between devices: 14.7 us -> 21.6 us  [exchange(): lax.all_to_all(x.reshape(outer * inner, *rest), ('ctx', 'nbr'), split_axi...]
    ppermute x14 -> x12, waiting for transfers between devices: 63.7 us -> 67.6 us  [permute(): lax.ppermute(x, axis, [(i, to(i)) for i in range(n) if 0 <= to(i) < n])]
    pallas_call x5 -> x3, Pallas kernels: 5.63 us -> 4.52 us  [call(): pl.pallas_call(body, out_shape=out_shape, in_specs=[SMEM] + [VMEM] * len(...]
    ppermute x14 -> x12, starting transfers between devices: 49 us -> 49.8 us  [permute(): lax.ppermute(x, axis, [(i, to(i)) for i in range(n) if 0 <= to(i) < n])]
  transfers between devices with their start and end apart: 16 -> 14, of which waited for: 13 -> 9; matrix products, arithmetic and copies ran while one was open for 1% -> 1% of each run, Pallas kernels for 2% -> 2%
where the time goes in v10:
time: 171 us; the launch traced here: 170 us
  starting transfers between devices  71.4 us (42%)
  waiting for transfers between devices  69.8 us (41%)
  Pallas kernels  22.4 us (13%)
  local copies, waits for them, and re-layouts  4.01 us (2%)
    ppermute x12, waiting for transfers between devices, permute(): lax.ppermute(x, axis, [(i, to(i)) for i in range(n) if 0 <= to(i) < n])  67.6 us
    ppermute x12, starting transfers between devices, permute(): lax.ppermute(x, axis, [(i, to(i)) for i in range(n) if 0 <= to(i) < n])  49.8 us
    all_to_all x2, starting transfers between devices, exchange(): lax.all_to_all(x.reshape(outer * inner, *rest), ('ctx', 'nbr'), split_axi...  21.6 us
    pallas_call x1, Pallas kernels, block(): pl.pallas_call(block_body, out_shape=[low(tokens, width), low(tokens, wid...  14.4 us
    pallas_call x3, Pallas kernels, call(): pl.pallas_call(body, out_shape=out_shape, in_specs=[SMEM] + [VMEM] * len(...  4.52 us
    unnamed x18, local copies, waits for them, and re-layouts  3.9 us
  transfers between devices with their start and end apart: 14, of which 9 were waited for; matrix products, arithmetic and copies ran while one was open for 1% of the time, Pallas kernels for 2%

profile of v10, /device:TPU:1, one launch (start us, length us, event | category | flops | bytes accessed | tf_op | source)
XLA Modules:
  0.0 170.0 jit_solution(18296399119972151456)
XLA Ops:
  0.6 2.3 %spread.1 = bf16[16,4,16,896]{3,2,1,0:T(8,128)(2,1)} custom-call(bf16[16,16,896]{2,1,0:T(8,128)(2,1)} %bitcast.27), custom_call_target="tpu_custom_call" | custom-call | tf_op jit(solution)/shard_map/spread/pallas_call | solution.py:179
  3.0 14.9 %all-to-all-start = ((bf16[64,16,896]{2,1,0:T(8,128)(2,1)}), bf16[64,16,896]{2,1,0:T(8,128)(2,1)}, u32[]{:S(2)}, u32[]{:S(2)}) async-start(bf16[64,16,896]{2,1,0:T(8,128)(2,1)} %bitcast.25), calls=%async_computation | async-start | bytes 3670016 | tf_op jit(solution)/shard_map/all_to_all | solution.py:246
  18.0 2.4 %collective-permute-start = (bf16[64,1024]{1,0:T(8,128)(2,1)S(1)}, bf16[64,1024]{1,0:T(8,128)(2,1)S(1)}, u32[]{:S(2)}, u32[]{:S(2)}) collective-permute-start(bf16[64,1024]{1,0:T(8,128)(2,1)S(1)} %pad_maximum_fusion), channel_id=1, source_target_pairs={{4,0},{8,4},{12,8},{16,12},{20,16},{24,20},{28,24},{32,28},{36,32}... | collective-permute-start | bytes 393224 | tf_op jit(solution)/shard_map/ppermute | solution.py:241
  20.6 40.5 %collective-permute-done.ahead_hbm = bf16[64,1024]{1,0:T(8,128)(2,1)S(1)} collective-permute-done((bf16[64,1024]{1,0:T(8,128)(2,1)S(1)}, bf16[64,1024]{1,0:T(8,128)(2,1)S(1)}, u32[]{:S(2)}, u32[]{:S(2)}) %collective-permute-start) | collective-permute-done | bytes 131104 | tf_op jit(solution)/shard_map/ppermute | solution.py:241
  61.1 2.2 %all-to-all-done = bf16[64,16,896]{2,1,0:T(8,128)(2,1)} async-done(((bf16[64,16,896]{2,1,0:T(8,128)(2,1)}), bf16[64,16,896]{2,1,0:T(8,128)(2,1)}, u32[]{:S(2)}, u32[]{:S(2)}) %all-to-all-start) | async-done | bytes 1835040 | tf_op jit(solution)/shard_map/all_to_all | solution.py:246
  63.3 14.4 %block.1 = (bf16[256,512]{1,0:T(8,128)(2,1)S(1)}, bf16[256,512]{1,0:T(8,128)(2,1)S(1)}, bf16[64,1024]{1,0:T(8,128)(2,1)S(1)}, bf16[896,512]{1,0:T(8,128)(2,1)}, ...) custom-call(s32[17]{0:T(128)S(1)} %pad_add_fusion.1.units_ref, bf16[256,512]{1,0:T(8,128)(2,1)S(1)} %bitcast.23, ...), custom_call_target="tpu_custom_call" | custom-call | tf_op jit(solution)/shard_map/block/pallas_call | solution.py:127
  77.7 0.7 copy-done.4
  79.0 6.7 %all-to-all-start.1 = ((bf16[64,16,896]{2,1,0:T(8,128)(2,1)}), bf16[64,16,896]{2,1,0:T(8,128)(2,1)S(1)}, u32[]{:S(2)}, u32[]{:S(2)}) async-start(bf16[64,16,896]{2,1,0:T(8,128)(2,1)} %bitcast.26), calls=%async_computation.1 | async-start | bytes 3670016 | tf_op jit(solution)/shard_map/all_to_all | solution.py:246
  85.7 2.4 %collective-permute-start.2 = (bf16[896,512]{1,0:T(8,128)(2,1)}, bf16[896,512]{1,0:T(8,128)(2,1)S(1)}, u32[]{:S(2)}, u32[]{:S(2)}) collective-permute-start(bf16[896,512]{1,0:T(8,128)(2,1)} %get-tuple-element.25), channel_id=1, source_target_pairs={{0,4},{4,0},{8,12},{12,8},{16,20},{20,16},{24,28},{28,24},{32,36},... | collective-permute-start | bytes 2752520 | tf_op jit(solution)/shard_map/ppermute | solution.py:241
  88.2 2.2 %collective-permute-done.2.away_ref = bf16[896,512]{1,0:T(8,128)(2,1)S(1)} collective-permute-done((bf16[896,512]{1,0:T(8,128)(2,1)}, bf16[896,512]{1,0:T(8,128)(2,1)S(1)}, u32[]{:S(2)}, u32[]{:S(2)}) %collective-permute-start.2) | collective-permute-done | bytes 917536 | tf_op jit(solution)/shard_map/ppermute | solution.py:241
  90.4 1.5 copy-done
  91.9 1.5 cut.1
  93.4 3.3 %collective-permute-start.3 = (bf16[2,112,512]{2,1,0:T(8,128)(2,1)}, bf16[2,112,512]{2,1,0:T(8,128)(2,1)S(1)}, u32[]{:S(2)}, u32[]{:S(2)}) collective-permute-start(bf16[2,112,512]{2,1,0:T(8,128)(2,1)} %get-tuple-element.27), channel_id=1, source_target_pairs={{0,64},{64,128},{128,192},{192,0},{256,320},{320,384},{384,448},{4... | collective-permute-start | bytes 688136 | tf_op jit(solution)/shard_map/ppermute | solution.py:241
  96.7 3.4 %collective-permute-start.4 = (bf16[2,112,512]{2,1,0:T(8,128)(2,1)}, bf16[2,112,512]{2,1,0:T(8,128)(2,1)S(1)}, u32[]{:S(2)}, u32[]{:S(2)}) collective-permute-start(bf16[2,112,512]{2,1,0:T(8,128)(2,1)} %get-tuple-element.28), channel_id=1, source_target_pairs={{0,192},{64,0},{128,64},{192,128},{256,448},{320,256},{384,320},{4... | collective-permute-start | bytes 688136 | tf_op jit(solution)/shard_map/ppermute | solution.py:241
  100.0 3.4 %collective-permute-start.5 = (bf16[2,112,512]{2,1,0:T(8,128)(2,1)}, bf16[2,112,512]{2,1,0:T(8,128)(2,1)}, u32[]{:S(2)}, u32[]{:S(2)}) collective-permute-start(bf16[2,112,512]{2,1,0:T(8,128)(2,1)} %get-tuple-element.29), channel_id=1, source_target_pairs={{0,128},{64,192},{128,0},{192,64},{256,384},{320,448},{384,256},{4... | collective-permute-start | bytes 688136 | tf_op jit(solution)/shard_map/ppermute | solution.py:241
  103.5 4.3 %collective-permute-start.1 = (bf16[64,1024]{1,0:T(8,128)(2,1)}, bf16[64,1024]{1,0:T(8,128)(2,1)S(1)}, u32[]{:S(2)}, u32[]{:S(2)}) collective-permute-start(bf16[64,1024]{1,0:T(8,128)(2,1)} %copy-done.6), channel_id=1, source_target_pairs={{0,4},{4,8},{8,12},{12,16},{16,20},{20,24},{24,28},{28,32},{32,36}... | collective-permute-start | bytes 393224 | tf_op jit(solution)/shard_map/ppermute | solution.py:241
  107.8 2.1 %collective-permute-done.5 = bf16[2,112,512]{2,1,0:T(8,128)(2,1)} collective-permute-done((bf16[2,112,512]{2,1,0:T(8,128)(2,1)}, bf16[2,112,512]{2,1,0:T(8,128)(2,1)}, u32[]{:S(2)}, u32[]{:S(2)}) %collective-permute-start.5) | collective-permute-done | bytes 229408 | tf_op jit(solution)/shard_map/ppermute | solution.py:241
  109.9 1.2 add_convert_fusion
  111.2 7.9 %collective-permute-start.6 = (bf16[112,512]{1,0:T(8,128)(2,1)S(1)}, bf16[112,512]{1,0:T(8,128)(2,1)S(1)}, u32[]{:S(2)}, u32[]{:S(2)}) collective-permute-start(bf16[112,512]{1,0:T(8,128)(2,1)S(1)} %get-tuple-element.30), channel_id=1, source_target_pairs={{0,256},{64,320},{128,384},{192,448},{256,0},{320,64},{384,128},{4... | collective-permute-start | bytes 344072 | tf_op jit(solution)/shard_map/ppermute | solution.py:241
  119.1 3.2 %collective-permute-start.7 = (bf16[112,512]{1,0:T(8,128)(2,1)S(1)}, bf16[112,512]{1,0:T(8,128)(2,1)S(1)}, u32[]{:S(2)}, u32[]{:S(2)}) collective-permute-start(bf16[112,512]{1,0:T(8,128)(2,1)S(1)} %get-tuple-element.31.refs_0_), channel_id=1, source_target_pairs={{0,8},{4,12},{8,0},{12,4},{16,24},{20,28},{24,16},{28,20},{32,40},... | collective-permute-start | bytes 344072 | tf_op jit(solution)/shard_map/ppermute | solution.py:241
  122.3 1.9 %collective-permute-start.8 = (bf16[112,512]{1,0:T(8,128)(2,1)S(1)}, bf16[112,512]{1,0:T(8,128)(2,1)S(1)}, u32[]{:S(2)}, u32[]{:S(2)}) collective-permute-start(bf16[112,512]{1,0:T(8,128)(2,1)S(1)} %get-tuple-element.30), channel_id=1, source_target_pairs={{0,264},{4,268},{8,256},{12,260},{16,280},{20,284},{24,272},{28,27... | collective-permute-start | bytes 344072 | tf_op jit(solution)/shard_map/ppermute | solution.py:241
  124.3 2.5 %collective-permute-done.1.behind_ref.refs_4_ = bf16[64,1024]{1,0:T(8,128)(2,1)S(1)} collective-permute-done((bf16[64,1024]{1,0:T(8,128)(2,1)}, bf16[64,1024]{1,0:T(8,128)(2,1)S(1)}, u32[]{:S(2)}, u32[]{:S(2)}) %collective-permute-start.1) | collective-permute-done | bytes 131104 | tf_op jit(solution)/shard_map/ppermute | solution.py:241
  126.8 13.9 %collective-permute-done.6.refs_1_ = bf16[112,512]{1,0:T(8,128)(2,1)S(1)} collective-permute-done((bf16[112,512]{1,0:T(8,128)(2,1)S(1)}, bf16[112,512]{1,0:T(8,128)(2,1)S(1)}, u32[]{:S(2)}, u32[]{:S(2)}) %collective-permute-start.6) | collective-permute-done | bytes 114720 | tf_op jit(solution)/shard_map/ppermute | solution.py:241
  141.3 3.4 %collective-permute-start.9 = (bf16[112,512]{1,0:T(8,128)(2,1)S(1)}, bf16[112,512]{1,0:T(8,128)(2,1)S(1)}, u32[]{:S(2)}, u32[]{:S(2)}) collective-permute-start(bf16[112,512]{1,0:T(8,128)(2,1)S(1)} %z_and_y.1.refs_0_), channel_id=1, source_target_pairs={{0,16},{4,20},{8,24},{12,28},{16,0},{20,4},{24,8},{28,12},{32,48},... | collective-permute-start | bytes 344072 | tf_op jit(solution)/shard_map/ppermute | solution.py:241
  144.7 1.6 gather_up.1
  146.3 1.4 collective-permute-done.9.refs_1_
  147.8 1.0 copy-done.1
  149.3 5.6 %collective-permute-start.10 = (bf16[112,512]{1,0:T(8,128)(2,1)S(1)}, bf16[112,512]{1,0:T(8,128)(2,1)S(1)}, u32[]{:S(2)}, u32[]{:S(2)}) collective-permute-start(bf16[112,512]{1,0:T(8,128)(2,1)S(1)} %y.1), channel_id=1, source_target_pairs={{0,32},{4,36},{8,40},{12,44},{16,48},{20,52},{24,56},{28,60},{32,0... | collective-permute-start | bytes 344072 | tf_op jit(solution)/shard_map/ppermute | solution.py:241
  155.0 3.9 %collective-permute-done.10 = bf16[112,512]{1,0:T(8,128)(2,1)S(1)} collective-permute-done((bf16[112,512]{1,0:T(8,128)(2,1)S(1)}, bf16[112,512]{1,0:T(8,128)(2,1)S(1)}, u32[]{:S(2)}, u32[]{:S(2)}) %collective-permute-start.10) | collective-permute-done | bytes 114720 | tf_op jit(solution)/shard_map/ppermute | solution.py:241
  158.9 8.6 %collective-permute-start.11 = (f32[112,512]{1,0:T(8,128)S(1)}, f32[112,512]{1,0:T(8,128)S(1)}, u32[]{:S(2)}, u32[]{:S(2)}) collective-permute-start(f32[112,512]{1,0:T(8,128)S(1)} %convert_add_fusion.mine_ref), channel_id=1, source_target_pairs={{0,4},{4,0},{8,12},{12,8},{16,20},{20,16},{24,28},{28,24},{32,36},... | collective-permute-start | bytes 688136 | tf_op jit(solution)/shard_map/ppermute | solution.py:241
  167.5 1.1 collective-permute-done.11.theirs_ref
  168.6 1.3 join.1
  (30 shorter events, 2.2 us)
Async XLA Ops:
  3.0 14.9 %copy-start.2 = (bf16[1,256,512]{2,1,0:T(8,128)(2,1)S(1)}, bf16[1,256,512]{2,1,0:T(8,128)(2,1)}, u32[]{:S(2)}) copy-start(bf16[1,256,512]{2,1,0:T(8,128)(2,1)} %param.5) | copy-start | bytes 786436
  3.0 14.9 %copy-start.3 = (bf16[1,256,512]{2,1,0:T(8,128)(2,1)S(1)}, bf16[1,256,512]{2,1,0:T(8,128)(2,1)}, u32[]{:S(2)}) copy-start(bf16[1,256,512]{2,1,0:T(8,128)(2,1)} %param.6) | copy-start | bytes 786436
  3.0 17.4 %copy-start.8 = (s32[1,4,4]{2,1,0:T(4,128)S(1)}, s32[1,4,4]{2,1,0:T(4,128)}, u32[]{:S(2)}) copy-start(s32[1,4,4]{2,1,0:T(4,128)} %param.9) | copy-start | bytes 196
  3.0 60.3 %all-to-all-start = ((bf16[64,16,896]{2,1,0:T(8,128)(2,1)}), bf16[64,16,896]{2,1,0:T(8,128)(2,1)}, u32[]{:S(2)}, u32[]{:S(2)}) async-start(bf16[64,16,896]{2,1,0:T(8,128)(2,1)} %bitcast.25), calls=%async_computation | async-start | bytes 3670016 | tf_op jit(solution)/shard_map/all_to_all | solution.py:246
  18.0 43.1 %collective-permute-start = (bf16[64,1024]{1,0:T(8,128)(2,1)S(1)}, bf16[64,1024]{1,0:T(8,128)(2,1)S(1)}, u32[]{:S(2)}, u32[]{:S(2)}) collective-permute-start(bf16[64,1024]{1,0:T(8,128)(2,1)S(1)} %pad_maximum_fusion), channel_id=1, source_target_pairs={{4,0},{8,4},{12,8},{16,12},{20,16},{24,20},{28,24},{32,28},{36,32}... | collective-permute-start | bytes 393224 | tf_op jit(solution)/shard_map/ppermute | solution.py:241
  77.7 0.7 copy-start.4
  78.4 0.7 copy-start.6
  79.0 65.6 %all-to-all-start.1 = ((bf16[64,16,896]{2,1,0:T(8,128)(2,1)}), bf16[64,16,896]{2,1,0:T(8,128)(2,1)S(1)}, u32[]{:S(2)}, u32[]{:S(2)}) async-start(bf16[64,16,896]{2,1,0:T(8,128)(2,1)} %bitcast.26), calls=%async_computation.1 | async-start | bytes 3670016 | tf_op jit(solution)/shard_map/all_to_all | solution.py:246
  85.7 4.7 %collective-permute-start.2 = (bf16[896,512]{1,0:T(8,128)(2,1)}, bf16[896,512]{1,0:T(8,128)(2,1)S(1)}, u32[]{:S(2)}, u32[]{:S(2)}) collective-permute-start(bf16[896,512]{1,0:T(8,128)(2,1)} %get-tuple-element.25), channel_id=1, source_target_pairs={{0,4},{4,0},{8,12},{12,8},{16,20},{20,16},{24,28},{28,24},{32,36},... | collective-permute-start | bytes 2752520 | tf_op jit(solution)/shard_map/ppermute | solution.py:241
  90.4 1.5 copy-start
  93.4 51.3 %copy-start.5 = (bf16[256,512]{1,0:T(8,128)(2,1)S(1)}, bf16[256,512]{1,0:T(8,128)(2,1)}, u32[]{:S(2)}) copy-start(bf16[256,512]{1,0:T(8,128)(2,1)} %copy-done.4) | copy-start | bytes 786436
  93.4 14.4 %collective-permute-start.3 = (bf16[2,112,512]{2,1,0:T(8,128)(2,1)}, bf16[2,112,512]{2,1,0:T(8,128)(2,1)S(1)}, u32[]{:S(2)}, u32[]{:S(2)}) collective-permute-start(bf16[2,112,512]{2,1,0:T(8,128)(2,1)} %get-tuple-element.27), channel_id=1, source_target_pairs={{0,64},{64,128},{128,192},{192,0},{256,320},{320,384},{384,448},{4... | collective-permute-start | bytes 688136 | tf_op jit(solution)/shard_map/ppermute | solution.py:241
  96.7 11.2 %collective-permute-start.4 = (bf16[2,112,512]{2,1,0:T(8,128)(2,1)}, bf16[2,112,512]{2,1,0:T(8,128)(2,1)S(1)}, u32[]{:S(2)}, u32[]{:S(2)}) collective-permute-start(bf16[2,112,512]{2,1,0:T(8,128)(2,1)} %get-tuple-element.28), channel_id=1, source_target_pairs={{0,192},{64,0},{128,64},{192,128},{256,448},{320,256},{384,320},{4... | collective-permute-start | bytes 688136 | tf_op jit(solution)/shard_map/ppermute | solution.py:241
  100.0 9.9 %collective-permute-start.5 = (bf16[2,112,512]{2,1,0:T(8,128)(2,1)}, bf16[2,112,512]{2,1,0:T(8,128)(2,1)}, u32[]{:S(2)}, u32[]{:S(2)}) collective-permute-start(bf16[2,112,512]{2,1,0:T(8,128)(2,1)} %get-tuple-element.29), channel_id=1, source_target_pairs={{0,128},{64,192},{128,0},{192,64},{256,384},{320,448},{384,256},{4... | collective-permute-start | bytes 688136 | tf_op jit(solution)/shard_map/ppermute | solution.py:241
  103.5 23.3 %collective-permute-start.1 = (bf16[64,1024]{1,0:T(8,128)(2,1)}, bf16[64,1024]{1,0:T(8,128)(2,1)S(1)}, u32[]{:S(2)}, u32[]{:S(2)}) collective-permute-start(bf16[64,1024]{1,0:T(8,128)(2,1)} %copy-done.6), channel_id=1, source_target_pairs={{0,4},{4,8},{8,12},{12,16},{16,20},{20,24},{24,28},{28,32},{32,36}... | collective-permute-start | bytes 393224 | tf_op jit(solution)/shard_map/ppermute | solution.py:241
  107.8 2.1 %copy-start.7 = (bf16[2,112,512]{2,1,0:T(8,128)(2,1)}, bf16[2,112,512]{2,1,0:T(8,128)(2,1)S(1)}, u32[]{:S(2)}) copy-start(bf16[2,112,512]{2,1,0:T(8,128)(2,1)S(1)} %collective-permute-done.4) | copy-start | bytes 688132
  111.2 29.5 %collective-permute-start.6 = (bf16[112,512]{1,0:T(8,128)(2,1)S(1)}, bf16[112,512]{1,0:T(8,128)(2,1)S(1)}, u32[]{:S(2)}, u32[]{:S(2)}) collective-permute-start(bf16[112,512]{1,0:T(8,128)(2,1)S(1)} %get-tuple-element.30), channel_id=1, source_target_pairs={{0,256},{64,320},{128,384},{192,448},{256,0},{320,64},{384,128},{4... | collective-permute-start | bytes 344072 | tf_op jit(solution)/shard_map/ppermute | solution.py:241
  119.1 21.6 %collective-permute-start.7 = (bf16[112,512]{1,0:T(8,128)(2,1)S(1)}, bf16[112,512]{1,0:T(8,128)(2,1)S(1)}, u32[]{:S(2)}, u32[]{:S(2)}) collective-permute-start(bf16[112,512]{1,0:T(8,128)(2,1)S(1)} %get-tuple-element.31.refs_0_), channel_id=1, source_target_pairs={{0,8},{4,12},{8,0},{12,4},{16,24},{20,28},{24,16},{28,20},{32,40},... | collective-permute-start | bytes 344072 | tf_op jit(solution)/shard_map/ppermute | solution.py:241
  122.3 18.4 %collective-permute-start.8 = (bf16[112,512]{1,0:T(8,128)(2,1)S(1)}, bf16[112,512]{1,0:T(8,128)(2,1)S(1)}, u32[]{:S(2)}, u32[]{:S(2)}) collective-permute-start(bf16[112,512]{1,0:T(8,128)(2,1)S(1)} %get-tuple-element.30), channel_id=1, source_target_pairs={{0,264},{4,268},{8,256},{12,260},{16,280},{20,284},{24,272},{28,27... | collective-permute-start | bytes 344072 | tf_op jit(solution)/shard_map/ppermute | solution.py:241
  141.3 6.4 %collective-permute-start.9 = (bf16[112,512]{1,0:T(8,128)(2,1)S(1)}, bf16[112,512]{1,0:T(8,128)(2,1)S(1)}, u32[]{:S(2)}, u32[]{:S(2)}) collective-permute-start(bf16[112,512]{1,0:T(8,128)(2,1)S(1)} %z_and_y.1.refs_0_), channel_id=1, source_target_pairs={{0,16},{4,20},{8,24},{12,28},{16,0},{20,4},{24,8},{28,12},{32,48},... | collective-permute-start | bytes 344072 | tf_op jit(solution)/shard_map/ppermute | solution.py:241
  147.8 1.0 copy-start.1
  149.3 9.5 %collective-permute-start.10 = (bf16[112,512]{1,0:T(8,128)(2,1)S(1)}, bf16[112,512]{1,0:T(8,128)(2,1)S(1)}, u32[]{:S(2)}, u32[]{:S(2)}) collective-permute-start(bf16[112,512]{1,0:T(8,128)(2,1)S(1)} %y.1), channel_id=1, source_target_pairs={{0,32},{4,36},{8,40},{12,44},{16,48},{20,52},{24,56},{28,60},{32,0... | collective-permute-start | bytes 344072 | tf_op jit(solution)/shard_map/ppermute | solution.py:241
  158.9 9.7 %collective-permute-start.11 = (f32[112,512]{1,0:T(8,128)S(1)}, f32[112,512]{1,0:T(8,128)S(1)}, u32[]{:S(2)}, u32[]{:S(2)}) collective-permute-start(f32[112,512]{1,0:T(8,128)S(1)} %convert_add_fusion.mine_ref), channel_id=1, source_target_pairs={{0,4},{4,0},{8,12},{12,8},{16,20},{20,16},{24,28},{28,24},{32,36},... | collective-permute-start | bytes 688136 | tf_op jit(solution)/shard_map/ppermute | solution.py:241

commit v11 on v10

--- a/solution.py
+++ b/solution.py
@@ -33,10 +33,10 @@
 
 
 def block_body(
-    units_ref, q_hbm, g_hbm, ahead_hbm, w_hbm, x, att_ref, dq_ref, tail_ref, sent_ref, kept_ref, partial_hbm,
-    key, value, grad, partial, q_ref, g_ref, ahead_ref, w_ref, q_rows, g_rows, att, dq, in_sems, out_sems,
+    units_ref, q_hbm, g_hbm, ahead_hbm, w_hbm, x, rows_ref, sent_hbm, kept_hbm, partial_hbm,
+    key, value, grad, partial, sent, kept, q_ref, g_ref, ahead_ref, w_ref, q_rows, g_rows, att, dq, in_sems, out_sems, product_sems,
 ):
-    pairs = ((w_hbm, w_ref), (q_hbm, q_ref), (g_hbm, g_ref), (ahead_hbm, ahead_ref))
+    pairs = ((q_hbm, q_ref), (g_hbm, g_ref), (ahead_hbm, ahead_ref), (w_hbm, w_ref))
     copies_in = [pltpu.make_async_copy(source, held, in_sems.at[n]) for n, (source, held) in enumerate(pairs)]
     for copy in copies_in:
         copy.start()
@@ -46,15 +46,15 @@
     core = units_ref[units_ref.shape[0] - 1]
     chunks = [pl.ds(c * chunk, chunk) for c in range(x.shape[0] // chunk)]
     head_cols = [pl.ds(h * HEAD_DIM, HEAD_DIM) for h in range(heads)]
-    copies_in[0].wait()
-    for rows in chunks:
-        for kind, out in enumerate((key, value)):
-            out[rows, :] = dot(x[rows, :], w_ref[kind], NN).astype(jnp.bfloat16)
-    for copy in copies_in[1:]:
+    for copy in copies_in[:3]:
         copy.wait()
     for h, cols in enumerate(head_cols):
         q_rows[:, cols] = span_rows(q_ref[:, cols], ahead_ref[:, cols])
         g_rows[:, cols] = span_rows(g_ref[:, cols], ahead_ref[:, pl.ds(width + h * HEAD_DIM, HEAD_DIM)])
+    copies_in[3].wait()
+    for rows in chunks:
+        for kind, out in enumerate((key, value)):
+            out[rows, :] = dot(x[rows, :], w_ref[kind], NN).astype(jnp.bfloat16)
     for j in range(tokens // SPAN):
         starts = [pl.multiple_of(units_ref[j * 4 + r] * PART, PART) for r in range(4)]
         rows = pl.ds(j * SPAN, SPAN)
@@ -86,16 +86,20 @@
         copy = pltpu.make_async_copy(partial.at[rows], partial_hbm.at[rows], out_sems.at[c])
         copy.start()
         partial_copies.append(copy)
-    for e in range(0, x.shape[1], 128):
-        part = x[:, e : e + 128].T
-        sent_ref[e : e + 128, :] = dot(part, grad[1 - core], NN).astype(jnp.bfloat16)
-        kept_ref[e : e + 128, :] = dot(part, grad[core], NN)
+    product_copies = []
+    for n in range(x.shape[1] // 128):
+        e = pl.ds(n * 128, 128)
+        part = x[:, n * 128 : (n + 1) * 128].T
+        sent[e, :] = dot(part, grad[1 - core], NN).astype(jnp.bfloat16)
+        kept[e, :] = dot(part, grad[core], NN)
+        for m, (held, out) in enumerate(((sent, sent_hbm), (kept, kept_hbm))):
+            copy = pltpu.make_async_copy(held.at[e], out.at[e], product_sems.at[n, m])
+            copy.start()
+            product_copies.append(copy)
     for cols in head_cols:
-        att_ref[:, cols] = pltpu.roll(att[:, cols], LEAD, 0).astype(jnp.bfloat16)
-        dq_ref[:, cols] = pltpu.roll(dq[:, cols], LEAD, 0).astype(jnp.bfloat16)
-    tail_ref[:, :width] = att_ref[:SPAN, :]
-    tail_ref[:, width:] = dq_ref[:SPAN, :]
-    for copy in partial_copies:
+        rows_ref[0, :, cols] = pltpu.roll(att[:, cols], LEAD, 0).astype(jnp.bfloat16)
+        rows_ref[1, :, cols] = pltpu.roll(dq[:, cols], LEAD, 0).astype(jnp.bfloat16)
+    for copy in partial_copies + product_copies:
         copy.wait()
 
 
@@ -126,16 +130,18 @@
     half = pltpu.VMEM((tokens, width), jnp.bfloat16)
     return pl.pallas_call(
         block_body,
-        out_shape=[low(tokens, width), low(tokens, width), low(SPAN, 2 * width)]
+        out_shape=[low(2, tokens, width)]
         + [low(enc_width, width), wide(enc_width, width), low(all_rows, enc_width)],
         in_specs=[SMEM] + [HBM] * 4 + [VMEM],
-        out_specs=[VMEM] * 5 + [HBM],
+        out_specs=[VMEM] + [HBM] * 3,
         scratch_shapes=[rows, rows, pltpu.VMEM((2, all_rows, width), jnp.bfloat16)]
-        + [pltpu.VMEM((all_rows, enc_width), jnp.bfloat16), half, half]
+        + [pltpu.VMEM((all_rows, enc_width), jnp.bfloat16), pltpu.VMEM((enc_width, width), jnp.bfloat16)]
+        + [pltpu.VMEM((enc_width, width), jnp.float32), half, half]
         + [pltpu.VMEM(ahead.shape, jnp.bfloat16), pltpu.VMEM(w.shape, jnp.bfloat16), half, half]
         + [pltpu.VMEM((tokens, width), jnp.float32)] * 2
-        + [pltpu.SemaphoreType.DMA((4,))] * 2,
-        compiler_params=pltpu.CompilerParams(vmem_limit_bytes=52 * 1024 * 1024),
+        + [pltpu.SemaphoreType.DMA((4,))] * 2
+        + [pltpu.SemaphoreType.DMA((enc_width // 128, 2))],
+        compiler_params=pltpu.CompilerParams(vmem_limit_bytes=51 * 1024 * 1024),
         name="block",
     )(scalars, q, g, ahead, w, x)
 
@@ -191,24 +197,25 @@
     )(x)
 
 
-def gather_up(place, terms, att, dq, behind):
+def gather_up(place, terms, done, behind):
     units, groups, piece, enc_width = terms.shape
-    width = att.shape[1]
-
-    def body(_, terms_ref, att_ref, dq_ref, behind_ref, total_ref, *full_refs):
+    _, tokens, width = done.shape
+
+    def body(_, terms_ref, done_ref, behind_ref, total_ref, att_ref, dq_ref, token_ref):
+        token_ref[...] = jnp.zeros(token_ref.shape, jnp.float32)
         for u in range(units):
             total = add(terms_ref[u, 0], terms_ref[u, 1])
             for n in range(2, groups):
                 total = add(total, terms_ref[u, n])
             total_ref[u] = total.astype(jnp.bfloat16)
         lead = lax.broadcasted_iota(jnp.int32, (SPAN, width), 0) < LEAD
-        for n, (ref, full) in enumerate(zip((att_ref, dq_ref), full_refs)):
-            came = behind_ref[:, n * width : (n + 1) * width].astype(jnp.float32)
-            full[:SPAN, :] = jnp.where(lead, came, ref[:SPAN, :].astype(jnp.float32)).astype(jnp.bfloat16)
-            full[SPAN:, :] = ref[SPAN:, :]
-
-    out_shape = [low(units, piece, enc_width), low(*att.shape), low(*dq.shape)]
-    return call(body, "gather_up", out_shape, [], place, terms, att, dq, behind)
+        for n, full in enumerate((att_ref, dq_ref)):
+            came, own = behind_ref[n].astype(jnp.float32), done_ref[n, :SPAN, :].astype(jnp.float32)
+            full[:SPAN, :] = jnp.where(lead, came, own).astype(jnp.bfloat16)
+            full[SPAN:, :] = done_ref[n, SPAN:, :]
+
+    out_shape = [low(units, piece, enc_width), low(tokens, width), low(tokens, width), wide(8, 128)]
+    return call(body, "gather_up", out_shape, [], place, terms, done, behind)
 
 
 def sum_rows(place, name, rows, *after):
@@ -221,19 +228,11 @@
     return pl.pallas_call(
         body,
         out_shape=low(*rows[0].shape),
-        in_specs=[SMEM] + [VMEM] * len(rows) + [HBM] * len(after),
+        in_specs=[SMEM] + [VMEM] * (len(rows) + len(after)),
         out_specs=VMEM,
         compiler_params=PARAMS,
         name=name,
     )(place, *rows, *after)
-
-
-def join(place, mine, theirs):
-    def body(place_ref, mine_ref, theirs_ref, out_ref):
-        out_ref[place_ref[0]] = mine_ref[...]
-        out_ref[1 - place_ref[0]] = theirs_ref[...]
-
-    return call(body, "join", wide(2, *mine.shape), [], place, mine, theirs)
 
 
 def permute(x, axis, to):
@@ -262,10 +261,10 @@
 
     unit_of = (neighbour_ids[0] // units).reshape(-1)
     scalars = jnp.concatenate((unit_of, (ctx % 2)[None])).astype(jnp.int32)
-    att, dq, tail, sent, kept, partial = block(scalars, q, g, ahead, kv_weight, x)
+    done, sent, kept, partial = block(scalars, q, g, ahead, kv_weight, x)
 
     terms = exchange(partial.reshape(units, groups, piece, enc_width))
-    behind = permute(tail, "ctx", lambda i: i + 1)
+    behind = permute(done[:, :SPAN], "ctx", lambda i: i + 1)
 
     held, *sends = cut(place, kept, permute(sent, "ctx", lambda i: i ^ 1))
     for k in (1, 3, 2):
@@ -282,10 +281,12 @@
         permute(other, ("dp", "ctx"), lambda i: i ^ (4 * owners + 2)),
     )
     rows = sum_rows(place, "z_and_y", quad, behind)
-    encoded_grad, attended, query_grad = gather_up(place, terms, att, dq, behind)
-    rows = sum_rows(place, "y", (rows, permute(rows, "ctx", lambda i: i ^ 4)), encoded_grad)
+    encoded_grad, attended, query_grad, token = gather_up(place, terms, done, behind)
+    rows = sum_rows(place, "y", (rows, permute(rows, "ctx", lambda i: i ^ 4)), token)
     mine = add(rows, permute(rows, "ctx", lambda i: i ^ 8))
-    weight_grad = join(place, mine, permute(mine, "ctx", lambda i: i ^ 1))
+    theirs = permute(mine, "ctx", lambda i: i ^ 1)
+    keys_here = ctx % 2 == 0
+    weight_grad = jnp.stack((jnp.where(keys_here, mine, theirs), jnp.where(keys_here, theirs, mine)), axis=0)
     return (attended[None], query_grad[None], encoded_grad[None], weight_grad)
 
 

time: 171 us -> 170 us (level)
  waiting for transfers between devices: 69.8 us -> 67.9 us
    ppermute x12, waiting for transfers between devices: 67.6 us -> 65.6 us  [permute(): lax.ppermute(x, axis, [(i, to(i)) for i in range(n) if 0 <= to(i) < n])]
    pallas_call x1, Pallas kernels: 14.4 us -> 16.2 us  [block(): pl.pallas_call(block_body, out_shape=[low(2, tokens, width)] + [low(enc_w...]
    pallas_call x3 -> x2, Pallas kernels: 4.52 us -> 3.14 us  [call(): pl.pallas_call(body, out_shape=out_shape, in_specs=[SMEM] + [VMEM] * len(...]
    unnamed x18 -> x12, local copies, waits for them, and re-layouts: 3.9 us -> 3.22 us
  transfers between devices with their start and end apart: 14 -> 14, of which waited for: 9 -> 10; matrix products, arithmetic and copies ran while one was open for 1% -> 1% of each run, Pallas kernels for 2% -> 2%
where the time goes in v11:
time: 170 us; the launch traced here: 169 us
  starting transfers between devices  71.4 us (42%)
  waiting for transfers between devices  67.9 us (40%)
  Pallas kernels  22.8 us (13%)
  local copies, waits for them, and re-layouts  3.35 us (2%)
  other arithmetic  2.22 us (1%)
    ppermute x12, waiting for transfers between devices, permute(): lax.ppermute(x, axis, [(i, to(i)) for i in range(n) if 0 <= to(i) < n])  65.6 us
    ppermute x12, starting transfers between devices, permute(): lax.ppermute(x, axis, [(i, to(i)) for i in range(n) if 0 <= to(i) < n])  49.8 us
    all_to_all x2, starting transfers between devices, exchange(): lax.all_to_all(x.reshape(outer * inner, *rest), ('ctx', 'nbr'), split_axi...  21.6 us
    pallas_call x1, Pallas kernels, block(): pl.pallas_call(block_body, out_shape=[low(2, tokens, width)] + [low(enc_w...  16.2 us
  transfers between devices with their start and end apart: 14, of which 10 were waited for; matrix products, arithmetic and copies ran while one was open for 1% of the time, Pallas kernels for 2%

profile of v11, /device:TPU:1, one launch (start us, length us, event | category | flops | bytes accessed | tf_op | source)
XLA Modules:
  0.0 168.6 jit_solution(8189792432974899016)
XLA Ops:
  0.6 2.3 %spread.1 = bf16[16,4,16,896]{3,2,1,0:T(8,128)(2,1)} custom-call(bf16[16,16,896]{2,1,0:T(8,128)(2,1)} %bitcast.30), custom_call_target="tpu_custom_call" | custom-call | tf_op jit(solution)/shard_map/spread/pallas_call | solution.py:185
  3.0 14.9 %all-to-all-start = ((bf16[64,16,896]{2,1,0:T(8,128)(2,1)}), bf16[64,16,896]{2,1,0:T(8,128)(2,1)}, u32[]{:S(2)}, u32[]{:S(2)}) async-start(bf16[64,16,896]{2,1,0:T(8,128)(2,1)} %bitcast.28), calls=%async_computation | async-start | bytes 3670016 | tf_op jit(solution)/shard_map/all_to_all | solution.py:245
  17.9 2.4 %collective-permute-start = (bf16[64,1024]{1,0:T(8,128)(2,1)S(1)}, bf16[64,1024]{1,0:T(8,128)(2,1)S(1)}, u32[]{:S(2)}, u32[]{:S(2)}) collective-permute-start(bf16[64,1024]{1,0:T(8,128)(2,1)S(1)} %pad_maximum_fusion.1), channel_id=1, source_target_pairs={{4,0},{8,4},{12,8},{16,12},{20,16},{24,20},{28,24},{32,28},{36,32}... | collective-permute-start | bytes 393224 | tf_op jit(solution)/shard_map/ppermute | solution.py:240
  20.6 40.5 %collective-permute-done.ahead_hbm = bf16[64,1024]{1,0:T(8,128)(2,1)S(1)} collective-permute-done((bf16[64,1024]{1,0:T(8,128)(2,1)S(1)}, bf16[64,1024]{1,0:T(8,128)(2,1)S(1)}, u32[]{:S(2)}, u32[]{:S(2)}) %collective-permute-start) | collective-permute-done | bytes 131104 | tf_op jit(solution)/shard_map/ppermute | solution.py:240
  61.0 2.2 %all-to-all-done = bf16[64,16,896]{2,1,0:T(8,128)(2,1)} async-done(((bf16[64,16,896]{2,1,0:T(8,128)(2,1)}), bf16[64,16,896]{2,1,0:T(8,128)(2,1)}, u32[]{:S(2)}, u32[]{:S(2)}) %all-to-all-start) | async-done | bytes 1835040 | tf_op jit(solution)/shard_map/all_to_all | solution.py:245
  63.2 16.2 %block.1 = (bf16[2,256,512]{2,1,0:T(8,128)(2,1)S(1)}, bf16[896,512]{1,0:T(8,128)(2,1)S(1)}, f32[896,512]{1,0:T(8,128)}, bf16[1024,896]{1,0:T(8,128)(2,1)}) custom-call(s32[17]{0:T(128)S(1)} %pad_add_fusion.1.units_ref, bf16[256,512]{1,0:T(8,128)(2,1)S(1)} %bitcast.26, bf16[256,512]{1,0:T(8,128)(2,1)S(1)} %bitcast.27, ...), custom_call_target="tpu_custom_call" | custom-call | tf_op jit(solution)/shard_map/block/pallas_call | solution.py:131
  79.5 0.9 copy-done.4
  80.4 6.7 %all-to-all-start.1 = ((bf16[64,16,896]{2,1,0:T(8,128)(2,1)}), bf16[64,16,896]{2,1,0:T(8,128)(2,1)S(1)}, u32[]{:S(2)}, u32[]{:S(2)}) async-start(bf16[64,16,896]{2,1,0:T(8,128)(2,1)} %bitcast.29), calls=%async_computation.1 | async-start | bytes 3670016 | tf_op jit(solution)/shard_map/all_to_all | solution.py:245
  87.1 2.4 %collective-permute-start.2 = (bf16[896,512]{1,0:T(8,128)(2,1)}, bf16[896,512]{1,0:T(8,128)(2,1)S(1)}, u32[]{:S(2)}, u32[]{:S(2)}) collective-permute-start(bf16[896,512]{1,0:T(8,128)(2,1)} %copy-done.4), channel_id=1, source_target_pairs={{0,4},{4,0},{8,12},{12,8},{16,20},{20,16},{24,28},{28,24},{32,36},... | collective-permute-start | bytes 2752520 | tf_op jit(solution)/shard_map/ppermute | solution.py:240
  89.5 2.2 %collective-permute-done.2.away_ref = bf16[896,512]{1,0:T(8,128)(2,1)S(1)} collective-permute-done((bf16[896,512]{1,0:T(8,128)(2,1)}, bf16[896,512]{1,0:T(8,128)(2,1)S(1)}, u32[]{:S(2)}, u32[]{:S(2)}) %collective-permute-start.2) | collective-permute-done | bytes 917536 | tf_op jit(solution)/shard_map/ppermute | solution.py:240
  91.7 1.5 copy-done
  93.2 1.5 cut.1
  95.5 3.1 %collective-permute-start.3 = (bf16[2,112,512]{2,1,0:T(8,128)(2,1)}, bf16[2,112,512]{2,1,0:T(8,128)(2,1)S(1)}, u32[]{:S(2)}, u32[]{:S(2)}) collective-permute-start(bf16[2,112,512]{2,1,0:T(8,128)(2,1)} %get-tuple-element.24), channel_id=1, source_target_pairs={{0,64},{64,128},{128,192},{192,0},{256,320},{320,384},{384,448},{4... | collective-permute-start | bytes 688136 | tf_op jit(solution)/shard_map/ppermute | solution.py:240
  98.6 3.4 %collective-permute-start.4 = (bf16[2,112,512]{2,1,0:T(8,128)(2,1)}, bf16[2,112,512]{2,1,0:T(8,128)(2,1)S(1)}, u32[]{:S(2)}, u32[]{:S(2)}) collective-permute-start(bf16[2,112,512]{2,1,0:T(8,128)(2,1)} %get-tuple-element.25), channel_id=1, source_target_pairs={{0,192},{64,0},{128,64},{192,128},{256,448},{320,256},{384,320},{4... | collective-permute-start | bytes 688136 | tf_op jit(solution)/shard_map/ppermute | solution.py:240
  102.0 3.4 %collective-permute-start.5 = (bf16[2,112,512]{2,1,0:T(8,128)(2,1)S(1)}, bf16[2,112,512]{2,1,0:T(8,128)(2,1)S(1)}, u32[]{:S(2)}, u32[]{:S(2)}) collective-permute-start(bf16[2,112,512]{2,1,0:T(8,128)(2,1)S(1)} %get-tuple-element.26), channel_id=1, source_target_pairs={{0,128},{64,192},{128,0},{192,64},{256,384},{320,448},{384,256},{4... | collective-permute-start | bytes 688136 | tf_op jit(solution)/shard_map/ppermute | solution.py:240
  105.5 4.3 %collective-permute-start.1 = (bf16[2,64,512]{2,1,0:T(8,128)(2,1)S(1)}, bf16[2,64,512]{2,1,0:T(8,128)(2,1)S(1)}, u32[]{:S(2)}, u32[]{:S(2)}) collective-permute-start(bf16[2,64,512]{2,1,0:T(8,128)(2,1)S(1)} %slice.19), channel_id=1, source_target_pairs={{0,4},{4,8},{8,12},{12,16},{16,20},{20,24},{24,28},{28,32},{32,36}... | collective-permute-start | bytes 393224 | tf_op jit(solution)/shard_map/ppermute | solution.py:240
  109.8 1.8 %collective-permute-done.5 = bf16[2,112,512]{2,1,0:T(8,128)(2,1)S(1)} collective-permute-done((bf16[2,112,512]{2,1,0:T(8,128)(2,1)S(1)}, bf16[2,112,512]{2,1,0:T(8,128)(2,1)S(1)}, u32[]{:S(2)}, u32[]{:S(2)}) %collective-permute-start.5) | collective-permute-done | bytes 229408 | tf_op jit(solution)/shard_map/ppermute | solution.py:240
  111.6 1.2 add_convert_fusion
  112.8 7.9 %collective-permute-start.6 = (bf16[112,512]{1,0:T(8,128)(2,1)S(1)}, bf16[112,512]{1,0:T(8,128)(2,1)S(1)}, u32[]{:S(2)}, u32[]{:S(2)}) collective-permute-start(bf16[112,512]{1,0:T(8,128)(2,1)S(1)} %get-tuple-element.30), channel_id=1, source_target_pairs={{0,256},{64,320},{128,384},{192,448},{256,0},{320,64},{384,128},{4... | collective-permute-start | bytes 344072 | tf_op jit(solution)/shard_map/ppermute | solution.py:240
  120.7 3.2 %collective-permute-start.7 = (bf16[112,512]{1,0:T(8,128)(2,1)S(1)}, bf16[112,512]{1,0:T(8,128)(2,1)S(1)}, u32[]{:S(2)}, u32[]{:S(2)}) collective-permute-start(bf16[112,512]{1,0:T(8,128)(2,1)S(1)} %get-tuple-element.31.refs_0_), channel_id=1, source_target_pairs={{0,8},{4,12},{8,0},{12,4},{16,24},{20,28},{24,16},{28,20},{32,40},... | collective-permute-start | bytes 344072 | tf_op jit(solution)/shard_map/ppermute | solution.py:240
  124.0 1.9 %collective-permute-start.8 = (bf16[112,512]{1,0:T(8,128)(2,1)S(1)}, bf16[112,512]{1,0:T(8,128)(2,1)S(1)}, u32[]{:S(2)}, u32[]{:S(2)}) collective-permute-start(bf16[112,512]{1,0:T(8,128)(2,1)S(1)} %get-tuple-element.30), channel_id=1, source_target_pairs={{0,264},{4,268},{8,256},{12,260},{16,280},{20,284},{24,272},{28,27... | collective-permute-start | bytes 344072 | tf_op jit(solution)/shard_map/ppermute | solution.py:240
  125.9 2.0 %collective-permute-done.1.behind_ref.refs_4_ = bf16[2,64,512]{2,1,0:T(8,128)(2,1)S(1)} collective-permute-done((bf16[2,64,512]{2,1,0:T(8,128)(2,1)S(1)}, bf16[2,64,512]{2,1,0:T(8,128)(2,1)S(1)}, u32[]{:S(2)}, u32[]{:S(2)}) %collective-permute-start.1) | collective-permute-done | bytes 131104 | tf_op jit(solution)/shard_map/ppermute | solution.py:240
  127.9 7.2 %collective-permute-done.6.refs_1_ = bf16[112,512]{1,0:T(8,128)(2,1)S(1)} collective-permute-done((bf16[112,512]{1,0:T(8,128)(2,1)S(1)}, bf16[112,512]{1,0:T(8,128)(2,1)S(1)}, u32[]{:S(2)}, u32[]{:S(2)}) %collective-permute-start.6) | collective-permute-done | bytes 114720 | tf_op jit(solution)/shard_map/ppermute | solution.py:240
  135.1 6.5 %collective-permute-done.8.refs_3_ = bf16[112,512]{1,0:T(8,128)(2,1)S(1)} collective-permute-done((bf16[112,512]{1,0:T(8,128)(2,1)S(1)}, bf16[112,512]{1,0:T(8,128)(2,1)S(1)}, u32[]{:S(2)}, u32[]{:S(2)}) %collective-permute-start.8) | collective-permute-done | bytes 114720 | tf_op jit(solution)/shard_map/ppermute | solution.py:240
  142.2 3.8 %collective-permute-start.9 = (bf16[112,512]{1,0:T(8,128)(2,1)S(1)}, bf16[112,512]{1,0:T(8,128)(2,1)S(1)}, u32[]{:S(2)}, u32[]{:S(2)}) collective-permute-start(bf16[112,512]{1,0:T(8,128)(2,1)S(1)} %z_and_y.1.refs_0_), channel_id=1, source_target_pairs={{0,16},{4,20},{8,24},{12,28},{16,0},{20,4},{24,8},{28,12},{32,48},... | collective-permute-start | bytes 344072 | tf_op jit(solution)/shard_map/ppermute | solution.py:240
  146.1 1.6 gather_up.1
  147.7 1.0 collective-permute-done.9.refs_1_
  149.3 6.1 %collective-permute-start.10 = (bf16[112,512]{1,0:T(8,128)(2,1)S(1)}, bf16[112,512]{1,0:T(8,128)(2,1)S(1)}, u32[]{:S(2)}, u32[]{:S(2)}) collective-permute-start(bf16[112,512]{1,0:T(8,128)(2,1)S(1)} %y.1), channel_id=1, source_target_pairs={{0,32},{4,36},{8,40},{12,44},{16,48},{20,52},{24,56},{28,60},{32,0... | collective-permute-start | bytes 344072 | tf_op jit(solution)/shard_map/ppermute | solution.py:240
  155.4 3.4 %collective-permute-done.10 = bf16[112,512]{1,0:T(8,128)(2,1)S(1)} collective-permute-done((bf16[112,512]{1,0:T(8,128)(2,1)S(1)}, bf16[112,512]{1,0:T(8,128)(2,1)S(1)}, u32[]{:S(2)}, u32[]{:S(2)}) %collective-permute-start.10) | collective-permute-done | bytes 114720 | tf_op jit(solution)/shard_map/ppermute | solution.py:240
  158.8 7.8 %collective-permute-start.11 = (f32[112,512]{1,0:T(8,128)S(1)}, f32[112,512]{1,0:T(8,128)S(1)}, u32[]{:S(2)}, u32[]{:S(2)}) collective-permute-start(f32[112,512]{1,0:T(8,128)S(1)} %convert_add_fusion), channel_id=1, source_target_pairs={{0,4},{4,0},{8,12},{12,8},{16,20},{20,16},{24,28},{28,24},{32,36},... | collective-permute-start | bytes 688136 | tf_op jit(solution)/shard_map/ppermute | solution.py:240
  166.6 1.1 collective-permute-done.11
  167.8 0.8 pad_maximum_fusion
  (26 shorter events, 2.3 us)
Async XLA Ops:
  2.9 14.9 %copy-start.2 = (bf16[1,256,512]{2,1,0:T(8,128)(2,1)S(1)}, bf16[1,256,512]{2,1,0:T(8,128)(2,1)}, u32[]{:S(2)}) copy-start(bf16[1,256,512]{2,1,0:T(8,128)(2,1)} %param.5) | copy-start | bytes 786436
  2.9 14.9 %copy-start.3 = (bf16[1,256,512]{2,1,0:T(8,128)(2,1)S(1)}, bf16[1,256,512]{2,1,0:T(8,128)(2,1)}, u32[]{:S(2)}) copy-start(bf16[1,256,512]{2,1,0:T(8,128)(2,1)} %param.6) | copy-start | bytes 786436
  3.0 17.4 %copy-start.5 = (s32[1,4,4]{2,1,0:T(4,128)S(1)}, s32[1,4,4]{2,1,0:T(4,128)}, u32[]{:S(2)}) copy-start(s32[1,4,4]{2,1,0:T(4,128)} %param.9) | copy-start | bytes 196
  3.0 60.3 %all-to-all-start = ((bf16[64,16,896]{2,1,0:T(8,128)(2,1)}), bf16[64,16,896]{2,1,0:T(8,128)(2,1)}, u32[]{:S(2)}, u32[]{:S(2)}) async-start(bf16[64,16,896]{2,1,0:T(8,128)(2,1)} %bitcast.28), calls=%async_computation | async-start | bytes 3670016 | tf_op jit(solution)/shard_map/all_to_all | solution.py:245
  17.9 43.1 %collective-permute-start = (bf16[64,1024]{1,0:T(8,128)(2,1)S(1)}, bf16[64,1024]{1,0:T(8,128)(2,1)S(1)}, u32[]{:S(2)}, u32[]{:S(2)}) collective-permute-start(bf16[64,1024]{1,0:T(8,128)(2,1)S(1)} %pad_maximum_fusion.1), channel_id=1, source_target_pairs={{4,0},{8,4},{12,8},{16,12},{20,16},{24,20},{28,24},{32,28},{36,32}... | collective-permute-start | bytes 393224 | tf_op jit(solution)/shard_map/ppermute | solution.py:240
  79.4 0.9 copy-start.4
  80.4 65.7 %all-to-all-start.1 = ((bf16[64,16,896]{2,1,0:T(8,128)(2,1)}), bf16[64,16,896]{2,1,0:T(8,128)(2,1)S(1)}, u32[]{:S(2)}, u32[]{:S(2)}) async-start(bf16[64,16,896]{2,1,0:T(8,128)(2,1)} %bitcast.29), calls=%async_computation.1 | async-start | bytes 3670016 | tf_op jit(solution)/shard_map/all_to_all | solution.py:245
  87.1 4.7 %collective-permute-start.2 = (bf16[896,512]{1,0:T(8,128)(2,1)}, bf16[896,512]{1,0:T(8,128)(2,1)S(1)}, u32[]{:S(2)}, u32[]{:S(2)}) collective-permute-start(bf16[896,512]{1,0:T(8,128)(2,1)} %copy-done.4), channel_id=1, source_target_pairs={{0,4},{4,0},{8,12},{12,8},{16,20},{20,16},{24,28},{28,24},{32,36},... | collective-permute-start | bytes 2752520 | tf_op jit(solution)/shard_map/ppermute | solution.py:240
  91.7 1.5 copy-start
  94.7 0.8 copy-start.1
  95.5 14.3 %collective-permute-start.3 = (bf16[2,112,512]{2,1,0:T(8,128)(2,1)}, bf16[2,112,512]{2,1,0:T(8,128)(2,1)S(1)}, u32[]{:S(2)}, u32[]{:S(2)}) collective-permute-start(bf16[2,112,512]{2,1,0:T(8,128)(2,1)} %get-tuple-element.24), channel_id=1, source_target_pairs={{0,64},{64,128},{128,192},{192,0},{256,320},{320,384},{384,448},{4... | collective-permute-start | bytes 688136 | tf_op jit(solution)/shard_map/ppermute | solution.py:240
  98.6 11.2 %collective-permute-start.4 = (bf16[2,112,512]{2,1,0:T(8,128)(2,1)}, bf16[2,112,512]{2,1,0:T(8,128)(2,1)S(1)}, u32[]{:S(2)}, u32[]{:S(2)}) collective-permute-start(bf16[2,112,512]{2,1,0:T(8,128)(2,1)} %get-tuple-element.25), channel_id=1, source_target_pairs={{0,192},{64,0},{128,64},{192,128},{256,448},{320,256},{384,320},{4... | collective-permute-start | bytes 688136 | tf_op jit(solution)/shard_map/ppermute | solution.py:240
  102.0 9.6 %collective-permute-start.5 = (bf16[2,112,512]{2,1,0:T(8,128)(2,1)S(1)}, bf16[2,112,512]{2,1,0:T(8,128)(2,1)S(1)}, u32[]{:S(2)}, u32[]{:S(2)}) collective-permute-start(bf16[2,112,512]{2,1,0:T(8,128)(2,1)S(1)} %get-tuple-element.26), channel_id=1, source_target_pairs={{0,128},{64,192},{128,0},{192,64},{256,384},{320,448},{384,256},{4... | collective-permute-start | bytes 688136 | tf_op jit(solution)/shard_map/ppermute | solution.py:240
  105.5 22.4 %collective-permute-start.1 = (bf16[2,64,512]{2,1,0:T(8,128)(2,1)S(1)}, bf16[2,64,512]{2,1,0:T(8,128)(2,1)S(1)}, u32[]{:S(2)}, u32[]{:S(2)}) collective-permute-start(bf16[2,64,512]{2,1,0:T(8,128)(2,1)S(1)} %slice.19), channel_id=1, source_target_pairs={{0,4},{4,8},{8,12},{12,16},{16,20},{20,24},{24,28},{28,32},{32,36}... | collective-permute-start | bytes 393224 | tf_op jit(solution)/shard_map/ppermute | solution.py:240
  112.8 22.3 %collective-permute-start.6 = (bf16[112,512]{1,0:T(8,128)(2,1)S(1)}, bf16[112,512]{1,0:T(8,128)(2,1)S(1)}, u32[]{:S(2)}, u32[]{:S(2)}) collective-permute-start(bf16[112,512]{1,0:T(8,128)(2,1)S(1)} %get-tuple-element.30), channel_id=1, source_target_pairs={{0,256},{64,320},{128,384},{192,448},{256,0},{320,64},{384,128},{4... | collective-permute-start | bytes 344072 | tf_op jit(solution)/shard_map/ppermute | solution.py:240
  120.7 14.4 %collective-permute-start.7 = (bf16[112,512]{1,0:T(8,128)(2,1)S(1)}, bf16[112,512]{1,0:T(8,128)(2,1)S(1)}, u32[]{:S(2)}, u32[]{:S(2)}) collective-permute-start(bf16[112,512]{1,0:T(8,128)(2,1)S(1)} %get-tuple-element.31.refs_0_), channel_id=1, source_target_pairs={{0,8},{4,12},{8,0},{12,4},{16,24},{20,28},{24,16},{28,20},{32,40},... | collective-permute-start | bytes 344072 | tf_op jit(solution)/shard_map/ppermute | solution.py:240
  124.0 17.7 %collective-permute-start.8 = (bf16[112,512]{1,0:T(8,128)(2,1)S(1)}, bf16[112,512]{1,0:T(8,128)(2,1)S(1)}, u32[]{:S(2)}, u32[]{:S(2)}) collective-permute-start(bf16[112,512]{1,0:T(8,128)(2,1)S(1)} %get-tuple-element.30), channel_id=1, source_target_pairs={{0,264},{4,268},{8,256},{12,260},{16,280},{20,284},{24,272},{28,27... | collective-permute-start | bytes 344072 | tf_op jit(solution)/shard_map/ppermute | solution.py:240
  142.2 6.4 %collective-permute-start.9 = (bf16[112,512]{1,0:T(8,128)(2,1)S(1)}, bf16[112,512]{1,0:T(8,128)(2,1)S(1)}, u32[]{:S(2)}, u32[]{:S(2)}) collective-permute-start(bf16[112,512]{1,0:T(8,128)(2,1)S(1)} %z_and_y.1.refs_0_), channel_id=1, source_target_pairs={{0,16},{4,20},{8,24},{12,28},{16,0},{20,4},{24,8},{28,12},{32,48},... | collective-permute-start | bytes 344072 | tf_op jit(solution)/shard_map/ppermute | solution.py:240
  149.3 9.5 %collective-permute-start.10 = (bf16[112,512]{1,0:T(8,128)(2,1)S(1)}, bf16[112,512]{1,0:T(8,128)(2,1)S(1)}, u32[]{:S(2)}, u32[]{:S(2)}) collective-permute-start(bf16[112,512]{1,0:T(8,128)(2,1)S(1)} %y.1), channel_id=1, source_target_pairs={{0,32},{4,36},{8,40},{12,44},{16,48},{20,52},{24,56},{28,60},{32,0... | collective-permute-start | bytes 344072 | tf_op jit(solution)/shard_map/ppermute | solution.py:240
  158.8 8.9 %collective-permute-start.11 = (f32[112,512]{1,0:T(8,128)S(1)}, f32[112,512]{1,0:T(8,128)S(1)}, u32[]{:S(2)}, u32[]{:S(2)}) collective-permute-start(f32[112,512]{1,0:T(8,128)S(1)} %convert_add_fusion), channel_id=1, source_target_pairs={{0,4},{4,0},{8,12},{12,8},{16,20},{20,16},{24,28},{28,24},{32,36},... | collective-permute-start | bytes 688136 | tf_op jit(solution)/shard_map/ppermute | solution.py:240

commit v12 on v11

--- a/solution.py
+++ b/solution.py
@@ -36,7 +36,7 @@
     units_ref, q_hbm, g_hbm, ahead_hbm, w_hbm, x, rows_ref, sent_hbm, kept_hbm, partial_hbm,
     key, value, grad, partial, sent, kept, q_ref, g_ref, ahead_ref, w_ref, q_rows, g_rows, att, dq, in_sems, out_sems, product_sems,
 ):
-    pairs = ((q_hbm, q_ref), (g_hbm, g_ref), (ahead_hbm, ahead_ref), (w_hbm, w_ref))
+    pairs = ((w_hbm.at[0], w_ref.at[0]), (w_hbm.at[1], w_ref.at[1]), (q_hbm, q_ref), (g_hbm, g_ref), (ahead_hbm, ahead_ref))
     copies_in = [pltpu.make_async_copy(source, held, in_sems.at[n]) for n, (source, held) in enumerate(pairs)]
     for copy in copies_in:
         copy.start()
@@ -46,15 +46,15 @@
     core = units_ref[units_ref.shape[0] - 1]
     chunks = [pl.ds(c * chunk, chunk) for c in range(x.shape[0] // chunk)]
     head_cols = [pl.ds(h * HEAD_DIM, HEAD_DIM) for h in range(heads)]
-    for copy in copies_in[:3]:
+    for kind, out in enumerate((key, value)):
+        copies_in[kind].wait()
+        for rows in chunks:
+            out[rows, :] = dot(x[rows, :], w_ref[kind], NN).astype(jnp.bfloat16)
+    for copy in copies_in[2:]:
         copy.wait()
     for h, cols in enumerate(head_cols):
         q_rows[:, cols] = span_rows(q_ref[:, cols], ahead_ref[:, cols])
         g_rows[:, cols] = span_rows(g_ref[:, cols], ahead_ref[:, pl.ds(width + h * HEAD_DIM, HEAD_DIM)])
-    copies_in[3].wait()
-    for rows in chunks:
-        for kind, out in enumerate((key, value)):
-            out[rows, :] = dot(x[rows, :], w_ref[kind], NN).astype(jnp.bfloat16)
     for j in range(tokens // SPAN):
         starts = [pl.multiple_of(units_ref[j * 4 + r] * PART, PART) for r in range(4)]
         rows = pl.ds(j * SPAN, SPAN)
@@ -139,7 +139,7 @@
         + [pltpu.VMEM((enc_width, width), jnp.float32), half, half]
         + [pltpu.VMEM(ahead.shape, jnp.bfloat16), pltpu.VMEM(w.shape, jnp.bfloat16), half, half]
         + [pltpu.VMEM((tokens, width), jnp.float32)] * 2
-        + [pltpu.SemaphoreType.DMA((4,))] * 2
+        + [pltpu.SemaphoreType.DMA((5,)), pltpu.SemaphoreType.DMA((4,))]
         + [pltpu.SemaphoreType.DMA((enc_width // 128, 2))],
         compiler_params=pltpu.CompilerParams(vmem_limit_bytes=51 * 1024 * 1024),
         name="block",

time: 170 us -> 170 us (level)
  no operation moved by 1% of the time
where the time goes in v12:
time: 170 us; the launch traced here: 168 us
  starting transfers between devices  71.4 us (42%)
  waiting for transfers between devices  67.9 us (40%)
  Pallas kernels  22.4 us (13%)
  local copies, waits for them, and re-layouts  3.35 us (2%)
  other arithmetic  2.22 us (1%)
    ppermute x12, waiting for transfers between devices, permute(): lax.ppermute(x, axis, [(i, to(i)) for i in range(n) if 0 <= to(i) < n])  65.6 us
    ppermute x12, starting transfers between devices, permute(): lax.ppermute(x, axis, [(i, to(i)) for i in range(n) if 0 <= to(i) < n])  49.8 us
    all_to_all x2, starting transfers between devices, exchange(): lax.all_to_all(x.reshape(outer * inner, *rest), ('ctx', 'nbr'), split_axi...  21.6 us
    pallas_call x1, Pallas kernels, block(): pl.pallas_call(block_body, out_shape=[low(2, tokens, width)] + [low(enc_w...  15.8 us
  transfers between devices with their start and end apart: 14, of which 10 were waited for; matrix products, arithmetic and copies ran while one was open for 1% of the time, Pallas kernels for 2%

profile of v12, /device:TPU:1, one launch (start us, length us, event | category | flops | bytes accessed | tf_op | source)
XLA Modules:
  0.0 168.2 jit_solution(156552873057660807)
XLA Ops:
  0.6 2.3 %spread.1 = bf16[16,4,16,896]{3,2,1,0:T(8,128)(2,1)} custom-call(bf16[16,16,896]{2,1,0:T(8,128)(2,1)} %bitcast.30), custom_call_target="tpu_custom_call" | custom-call | tf_op jit(solution)/shard_map/spread/pallas_call | solution.py:185
  3.0 14.9 %all-to-all-start = ((bf16[64,16,896]{2,1,0:T(8,128)(2,1)}), bf16[64,16,896]{2,1,0:T(8,128)(2,1)}, u32[]{:S(2)}, u32[]{:S(2)}) async-start(bf16[64,16,896]{2,1,0:T(8,128)(2,1)} %bitcast.28), calls=%async_computation | async-start | bytes 3670016 | tf_op jit(solution)/shard_map/all_to_all | solution.py:245
  17.9 2.4 %collective-permute-start = (bf16[64,1024]{1,0:T(8,128)(2,1)S(1)}, bf16[64,1024]{1,0:T(8,128)(2,1)S(1)}, u32[]{:S(2)}, u32[]{:S(2)}) collective-permute-start(bf16[64,1024]{1,0:T(8,128)(2,1)S(1)} %pad_maximum_fusion.1), channel_id=1, source_target_pairs={{4,0},{8,4},{12,8},{16,12},{20,16},{24,20},{28,24},{32,28},{36,32}... | collective-permute-start | bytes 393224 | tf_op jit(solution)/shard_map/ppermute | solution.py:240
  20.6 40.5 %collective-permute-done.ahead_hbm = bf16[64,1024]{1,0:T(8,128)(2,1)S(1)} collective-permute-done((bf16[64,1024]{1,0:T(8,128)(2,1)S(1)}, bf16[64,1024]{1,0:T(8,128)(2,1)S(1)}, u32[]{:S(2)}, u32[]{:S(2)}) %collective-permute-start) | collective-permute-done | bytes 131104 | tf_op jit(solution)/shard_map/ppermute | solution.py:240
  61.0 2.2 %all-to-all-done = bf16[64,16,896]{2,1,0:T(8,128)(2,1)} async-done(((bf16[64,16,896]{2,1,0:T(8,128)(2,1)}), bf16[64,16,896]{2,1,0:T(8,128)(2,1)}, u32[]{:S(2)}, u32[]{:S(2)}) %all-to-all-start) | async-done | bytes 1835040 | tf_op jit(solution)/shard_map/all_to_all | solution.py:245
  63.2 15.8 %block.1 = (bf16[2,256,512]{2,1,0:T(8,128)(2,1)S(1)}, bf16[896,512]{1,0:T(8,128)(2,1)S(1)}, f32[896,512]{1,0:T(8,128)}, bf16[1024,896]{1,0:T(8,128)(2,1)}) custom-call(s32[17]{0:T(128)S(1)} %pad_add_fusion.1.units_ref, bf16[256,512]{1,0:T(8,128)(2,1)S(1)} %bitcast.26, bf16[256,512]{1,0:T(8,128)(2,1)S(1)} %bitcast.27, ...), custom_call_target="tpu_custom_call" | custom-call | tf_op jit(solution)/shard_map/block/pallas_call | solution.py:131
  79.1 0.9 copy-done.4
  80.0 6.7 %all-to-all-start.1 = ((bf16[64,16,896]{2,1,0:T(8,128)(2,1)}), bf16[64,16,896]{2,1,0:T(8,128)(2,1)S(1)}, u32[]{:S(2)}, u32[]{:S(2)}) async-start(bf16[64,16,896]{2,1,0:T(8,128)(2,1)} %bitcast.29), calls=%async_computation.1 | async-start | bytes 3670016 | tf_op jit(solution)/shard_map/all_to_all | solution.py:245
  86.7 2.4 %collective-permute-start.2 = (bf16[896,512]{1,0:T(8,128)(2,1)}, bf16[896,512]{1,0:T(8,128)(2,1)S(1)}, u32[]{:S(2)}, u32[]{:S(2)}) collective-permute-start(bf16[896,512]{1,0:T(8,128)(2,1)} %copy-done.4), channel_id=1, source_target_pairs={{0,4},{4,0},{8,12},{12,8},{16,20},{20,16},{24,28},{28,24},{32,36},... | collective-permute-start | bytes 2752520 | tf_op jit(solution)/shard_map/ppermute | solution.py:240
  89.1 2.2 %collective-permute-done.2.away_ref = bf16[896,512]{1,0:T(8,128)(2,1)S(1)} collective-permute-done((bf16[896,512]{1,0:T(8,128)(2,1)}, bf16[896,512]{1,0:T(8,128)(2,1)S(1)}, u32[]{:S(2)}, u32[]{:S(2)}) %collective-permute-start.2) | collective-permute-done | bytes 917536 | tf_op jit(solution)/shard_map/ppermute | solution.py:240
  91.3 1.5 copy-done
  92.8 1.5 cut.1
  95.1 3.1 %collective-permute-start.3 = (bf16[2,112,512]{2,1,0:T(8,128)(2,1)}, bf16[2,112,512]{2,1,0:T(8,128)(2,1)S(1)}, u32[]{:S(2)}, u32[]{:S(2)}) collective-permute-start(bf16[2,112,512]{2,1,0:T(8,128)(2,1)} %get-tuple-element.24), channel_id=1, source_target_pairs={{0,64},{64,128},{128,192},{192,0},{256,320},{320,384},{384,448},{4... | collective-permute-start | bytes 688136 | tf_op jit(solution)/shard_map/ppermute | solution.py:240
  98.2 3.4 %collective-permute-start.4 = (bf16[2,112,512]{2,1,0:T(8,128)(2,1)}, bf16[2,112,512]{2,1,0:T(8,128)(2,1)S(1)}, u32[]{:S(2)}, u32[]{:S(2)}) collective-permute-start(bf16[2,112,512]{2,1,0:T(8,128)(2,1)} %get-tuple-element.25), channel_id=1, source_target_pairs={{0,192},{64,0},{128,64},{192,128},{256,448},{320,256},{384,320},{4... | collective-permute-start | bytes 688136 | tf_op jit(solution)/shard_map/ppermute | solution.py:240
  101.6 3.4 %collective-permute-start.5 = (bf16[2,112,512]{2,1,0:T(8,128)(2,1)S(1)}, bf16[2,112,512]{2,1,0:T(8,128)(2,1)S(1)}, u32[]{:S(2)}, u32[]{:S(2)}) collective-permute-start(bf16[2,112,512]{2,1,0:T(8,128)(2,1)S(1)} %get-tuple-element.26), channel_id=1, source_target_pairs={{0,128},{64,192},{128,0},{192,64},{256,384},{320,448},{384,256},{4... | collective-permute-start | bytes 688136 | tf_op jit(solution)/shard_map/ppermute | solution.py:240
  105.1 4.3 %collective-permute-start.1 = (bf16[2,64,512]{2,1,0:T(8,128)(2,1)S(1)}, bf16[2,64,512]{2,1,0:T(8,128)(2,1)S(1)}, u32[]{:S(2)}, u32[]{:S(2)}) collective-permute-start(bf16[2,64,512]{2,1,0:T(8,128)(2,1)S(1)} %slice.19), channel_id=1, source_target_pairs={{0,4},{4,8},{8,12},{12,16},{16,20},{20,24},{24,28},{28,32},{32,36}... | collective-permute-start | bytes 393224 | tf_op jit(solution)/shard_map/ppermute | solution.py:240
  109.4 1.8 %collective-permute-done.5 = bf16[2,112,512]{2,1,0:T(8,128)(2,1)S(1)} collective-permute-done((bf16[2,112,512]{2,1,0:T(8,128)(2,1)S(1)}, bf16[2,112,512]{2,1,0:T(8,128)(2,1)S(1)}, u32[]{:S(2)}, u32[]{:S(2)}) %collective-permute-start.5) | collective-permute-done | bytes 229408 | tf_op jit(solution)/shard_map/ppermute | solution.py:240
  111.2 1.2 add_convert_fusion
  112.4 7.9 %collective-permute-start.6 = (bf16[112,512]{1,0:T(8,128)(2,1)S(1)}, bf16[112,512]{1,0:T(8,128)(2,1)S(1)}, u32[]{:S(2)}, u32[]{:S(2)}) collective-permute-start(bf16[112,512]{1,0:T(8,128)(2,1)S(1)} %get-tuple-element.30), channel_id=1, source_target_pairs={{0,256},{64,320},{128,384},{192,448},{256,0},{320,64},{384,128},{4... | collective-permute-start | bytes 344072 | tf_op jit(solution)/shard_map/ppermute | solution.py:240
  120.3 3.2 %collective-permute-start.7 = (bf16[112,512]{1,0:T(8,128)(2,1)S(1)}, bf16[112,512]{1,0:T(8,128)(2,1)S(1)}, u32[]{:S(2)}, u32[]{:S(2)}) collective-permute-start(bf16[112,512]{1,0:T(8,128)(2,1)S(1)} %get-tuple-element.31.refs_0_), channel_id=1, source_target_pairs={{0,8},{4,12},{8,0},{12,4},{16,24},{20,28},{24,16},{28,20},{32,40},... | collective-permute-start | bytes 344072 | tf_op jit(solution)/shard_map/ppermute | solution.py:240
  123.6 1.9 %collective-permute-start.8 = (bf16[112,512]{1,0:T(8,128)(2,1)S(1)}, bf16[112,512]{1,0:T(8,128)(2,1)S(1)}, u32[]{:S(2)}, u32[]{:S(2)}) collective-permute-start(bf16[112,512]{1,0:T(8,128)(2,1)S(1)} %get-tuple-element.30), channel_id=1, source_target_pairs={{0,264},{4,268},{8,256},{12,260},{16,280},{20,284},{24,272},{28,27... | collective-permute-start | bytes 344072 | tf_op jit(solution)/shard_map/ppermute | solution.py:240
  125.5 2.0 %collective-permute-done.1.behind_ref.refs_4_ = bf16[2,64,512]{2,1,0:T(8,128)(2,1)S(1)} collective-permute-done((bf16[2,64,512]{2,1,0:T(8,128)(2,1)S(1)}, bf16[2,64,512]{2,1,0:T(8,128)(2,1)S(1)}, u32[]{:S(2)}, u32[]{:S(2)}) %collective-permute-start.1) | collective-permute-done | bytes 131104 | tf_op jit(solution)/shard_map/ppermute | solution.py:240
  127.5 7.2 %collective-permute-done.6.refs_1_ = bf16[112,512]{1,0:T(8,128)(2,1)S(1)} collective-permute-done((bf16[112,512]{1,0:T(8,128)(2,1)S(1)}, bf16[112,512]{1,0:T(8,128)(2,1)S(1)}, u32[]{:S(2)}, u32[]{:S(2)}) %collective-permute-start.6) | collective-permute-done | bytes 114720 | tf_op jit(solution)/shard_map/ppermute | solution.py:240
  134.7 6.5 %collective-permute-done.8.refs_3_ = bf16[112,512]{1,0:T(8,128)(2,1)S(1)} collective-permute-done((bf16[112,512]{1,0:T(8,128)(2,1)S(1)}, bf16[112,512]{1,0:T(8,128)(2,1)S(1)}, u32[]{:S(2)}, u32[]{:S(2)}) %collective-permute-start.8) | collective-permute-done | bytes 114720 | tf_op jit(solution)/shard_map/ppermute | solution.py:240
  141.8 3.8 %collective-permute-start.9 = (bf16[112,512]{1,0:T(8,128)(2,1)S(1)}, bf16[112,512]{1,0:T(8,128)(2,1)S(1)}, u32[]{:S(2)}, u32[]{:S(2)}) collective-permute-start(bf16[112,512]{1,0:T(8,128)(2,1)S(1)} %z_and_y.1.refs_0_), channel_id=1, source_target_pairs={{0,16},{4,20},{8,24},{12,28},{16,0},{20,4},{24,8},{28,12},{32,48},... | collective-permute-start | bytes 344072 | tf_op jit(solution)/shard_map/ppermute | solution.py:240
  145.7 1.6 gather_up.1
  147.3 1.0 collective-permute-done.9.refs_1_
  148.9 6.1 %collective-permute-start.10 = (bf16[112,512]{1,0:T(8,128)(2,1)S(1)}, bf16[112,512]{1,0:T(8,128)(2,1)S(1)}, u32[]{:S(2)}, u32[]{:S(2)}) collective-permute-start(bf16[112,512]{1,0:T(8,128)(2,1)S(1)} %y.1), channel_id=1, source_target_pairs={{0,32},{4,36},{8,40},{12,44},{16,48},{20,52},{24,56},{28,60},{32,0... | collective-permute-start | bytes 344072 | tf_op jit(solution)/shard_map/ppermute | solution.py:240
  155.0 3.4 %collective-permute-done.10 = bf16[112,512]{1,0:T(8,128)(2,1)S(1)} collective-permute-done((bf16[112,512]{1,0:T(8,128)(2,1)S(1)}, bf16[112,512]{1,0:T(8,128)(2,1)S(1)}, u32[]{:S(2)}, u32[]{:S(2)}) %collective-permute-start.10) | collective-permute-done | bytes 114720 | tf_op jit(solution)/shard_map/ppermute | solution.py:240
  158.4 7.8 %collective-permute-start.11 = (f32[112,512]{1,0:T(8,128)S(1)}, f32[112,512]{1,0:T(8,128)S(1)}, u32[]{:S(2)}, u32[]{:S(2)}) collective-permute-start(f32[112,512]{1,0:T(8,128)S(1)} %convert_add_fusion), channel_id=1, source_target_pairs={{0,4},{4,0},{8,12},{12,8},{16,20},{20,16},{24,28},{28,24},{32,36},... | collective-permute-start | bytes 688136 | tf_op jit(solution)/shard_map/ppermute | solution.py:240
  166.2 1.1 collective-permute-done.11
  167.4 0.8 pad_maximum_fusion
  (26 shorter events, 2.3 us)
Async XLA Ops:
  2.9 14.9 %copy-start.2 = (bf16[1,256,512]{2,1,0:T(8,128)(2,1)S(1)}, bf16[1,256,512]{2,1,0:T(8,128)(2,1)}, u32[]{:S(2)}) copy-start(bf16[1,256,512]{2,1,0:T(8,128)(2,1)} %param.5) | copy-start | bytes 786436
  2.9 14.9 %copy-start.3 = (bf16[1,256,512]{2,1,0:T(8,128)(2,1)S(1)}, bf16[1,256,512]{2,1,0:T(8,128)(2,1)}, u32[]{:S(2)}) copy-start(bf16[1,256,512]{2,1,0:T(8,128)(2,1)} %param.6) | copy-start | bytes 786436
  3.0 17.4 %copy-start.5 = (s32[1,4,4]{2,1,0:T(4,128)S(1)}, s32[1,4,4]{2,1,0:T(4,128)}, u32[]{:S(2)}) copy-start(s32[1,4,4]{2,1,0:T(4,128)} %param.9) | copy-start | bytes 196
  3.0 60.3 %all-to-all-start = ((bf16[64,16,896]{2,1,0:T(8,128)(2,1)}), bf16[64,16,896]{2,1,0:T(8,128)(2,1)}, u32[]{:S(2)}, u32[]{:S(2)}) async-start(bf16[64,16,896]{2,1,0:T(8,128)(2,1)} %bitcast.28), calls=%async_computation | async-start | bytes 3670016 | tf_op jit(solution)/shard_map/all_to_all | solution.py:245
  17.9 43.1 %collective-permute-start = (bf16[64,1024]{1,0:T(8,128)(2,1)S(1)}, bf16[64,1024]{1,0:T(8,128)(2,1)S(1)}, u32[]{:S(2)}, u32[]{:S(2)}) collective-permute-start(bf16[64,1024]{1,0:T(8,128)(2,1)S(1)} %pad_maximum_fusion.1), channel_id=1, source_target_pairs={{4,0},{8,4},{12,8},{16,12},{20,16},{24,20},{28,24},{32,28},{36,32}... | collective-permute-start | bytes 393224 | tf_op jit(solution)/shard_map/ppermute | solution.py:240
  79.1 0.9 copy-start.4
  80.0 65.7 %all-to-all-start.1 = ((bf16[64,16,896]{2,1,0:T(8,128)(2,1)}), bf16[64,16,896]{2,1,0:T(8,128)(2,1)S(1)}, u32[]{:S(2)}, u32[]{:S(2)}) async-start(bf16[64,16,896]{2,1,0:T(8,128)(2,1)} %bitcast.29), calls=%async_computation.1 | async-start | bytes 3670016 | tf_op jit(solution)/shard_map/all_to_all | solution.py:245
  86.7 4.7 %collective-permute-start.2 = (bf16[896,512]{1,0:T(8,128)(2,1)}, bf16[896,512]{1,0:T(8,128)(2,1)S(1)}, u32[]{:S(2)}, u32[]{:S(2)}) collective-permute-start(bf16[896,512]{1,0:T(8,128)(2,1)} %copy-done.4), channel_id=1, source_target_pairs={{0,4},{4,0},{8,12},{12,8},{16,20},{20,16},{24,28},{28,24},{32,36},... | collective-permute-start | bytes 2752520 | tf_op jit(solution)/shard_map/ppermute | solution.py:240
  91.3 1.5 copy-start
  94.3 0.8 copy-start.1
  95.1 14.3 %collective-permute-start.3 = (bf16[2,112,512]{2,1,0:T(8,128)(2,1)}, bf16[2,112,512]{2,1,0:T(8,128)(2,1)S(1)}, u32[]{:S(2)}, u32[]{:S(2)}) collective-permute-start(bf16[2,112,512]{2,1,0:T(8,128)(2,1)} %get-tuple-element.24), channel_id=1, source_target_pairs={{0,64},{64,128},{128,192},{192,0},{256,320},{320,384},{384,448},{4... | collective-permute-start | bytes 688136 | tf_op jit(solution)/shard_map/ppermute | solution.py:240
  98.2 11.2 %collective-permute-start.4 = (bf16[2,112,512]{2,1,0:T(8,128)(2,1)}, bf16[2,112,512]{2,1,0:T(8,128)(2,1)S(1)}, u32[]{:S(2)}, u32[]{:S(2)}) collective-permute-start(bf16[2,112,512]{2,1,0:T(8,128)(2,1)} %get-tuple-element.25), channel_id=1, source_target_pairs={{0,192},{64,0},{128,64},{192,128},{256,448},{320,256},{384,320},{4... | collective-permute-start | bytes 688136 | tf_op jit(solution)/shard_map/ppermute | solution.py:240
  101.6 9.6 %collective-permute-start.5 = (bf16[2,112,512]{2,1,0:T(8,128)(2,1)S(1)}, bf16[2,112,512]{2,1,0:T(8,128)(2,1)S(1)}, u32[]{:S(2)}, u32[]{:S(2)}) collective-permute-start(bf16[2,112,512]{2,1,0:T(8,128)(2,1)S(1)} %get-tuple-element.26), channel_id=1, source_target_pairs={{0,128},{64,192},{128,0},{192,64},{256,384},{320,448},{384,256},{4... | collective-permute-start | bytes 688136 | tf_op jit(solution)/shard_map/ppermute | solution.py:240
  105.1 22.4 %collective-permute-start.1 = (bf16[2,64,512]{2,1,0:T(8,128)(2,1)S(1)}, bf16[2,64,512]{2,1,0:T(8,128)(2,1)S(1)}, u32[]{:S(2)}, u32[]{:S(2)}) collective-permute-start(bf16[2,64,512]{2,1,0:T(8,128)(2,1)S(1)} %slice.19), channel_id=1, source_target_pairs={{0,4},{4,8},{8,12},{12,16},{16,20},{20,24},{24,28},{28,32},{32,36}... | collective-permute-start | bytes 393224 | tf_op jit(solution)/shard_map/ppermute | solution.py:240
  112.4 22.3 %collective-permute-start.6 = (bf16[112,512]{1,0:T(8,128)(2,1)S(1)}, bf16[112,512]{1,0:T(8,128)(2,1)S(1)}, u32[]{:S(2)}, u32[]{:S(2)}) collective-permute-start(bf16[112,512]{1,0:T(8,128)(2,1)S(1)} %get-tuple-element.30), channel_id=1, source_target_pairs={{0,256},{64,320},{128,384},{192,448},{256,0},{320,64},{384,128},{4... | collective-permute-start | bytes 344072 | tf_op jit(solution)/shard_map/ppermute | solution.py:240
  120.3 14.4 %collective-permute-start.7 = (bf16[112,512]{1,0:T(8,128)(2,1)S(1)}, bf16[112,512]{1,0:T(8,128)(2,1)S(1)}, u32[]{:S(2)}, u32[]{:S(2)}) collective-permute-start(bf16[112,512]{1,0:T(8,128)(2,1)S(1)} %get-tuple-element.31.refs_0_), channel_id=1, source_target_pairs={{0,8},{4,12},{8,0},{12,4},{16,24},{20,28},{24,16},{28,20},{32,40},... | collective-permute-start | bytes 344072 | tf_op jit(solution)/shard_map/ppermute | solution.py:240
  123.6 17.7 %collective-permute-start.8 = (bf16[112,512]{1,0:T(8,128)(2,1)S(1)}, bf16[112,512]{1,0:T(8,128)(2,1)S(1)}, u32[]{:S(2)}, u32[]{:S(2)}) collective-permute-start(bf16[112,512]{1,0:T(8,128)(2,1)S(1)} %get-tuple-element.30), channel_id=1, source_target_pairs={{0,264},{4,268},{8,256},{12,260},{16,280},{20,284},{24,272},{28,27... | collective-permute-start | bytes 344072 | tf_op jit(solution)/shard_map/ppermute | solution.py:240
  141.8 6.4 %collective-permute-start.9 = (bf16[112,512]{1,0:T(8,128)(2,1)S(1)}, bf16[112,512]{1,0:T(8,128)(2,1)S(1)}, u32[]{:S(2)}, u32[]{:S(2)}) collective-permute-start(bf16[112,512]{1,0:T(8,128)(2,1)S(1)} %z_and_y.1.refs_0_), channel_id=1, source_target_pairs={{0,16},{4,20},{8,24},{12,28},{16,0},{20,4},{24,8},{28,12},{32,48},... | collective-permute-start | bytes 344072 | tf_op jit(solution)/shard_map/ppermute | solution.py:240
  148.9 9.5 %collective-permute-start.10 = (bf16[112,512]{1,0:T(8,128)(2,1)S(1)}, bf16[112,512]{1,0:T(8,128)(2,1)S(1)}, u32[]{:S(2)}, u32[]{:S(2)}) collective-permute-start(bf16[112,512]{1,0:T(8,128)(2,1)S(1)} %y.1), channel_id=1, source_target_pairs={{0,32},{4,36},{8,40},{12,44},{16,48},{20,52},{24,56},{28,60},{32,0... | collective-permute-start | bytes 344072 | tf_op jit(solution)/shard_map/ppermute | solution.py:240
  158.4 8.9 %collective-permute-start.11 = (f32[112,512]{1,0:T(8,128)S(1)}, f32[112,512]{1,0:T(8,128)S(1)}, u32[]{:S(2)}, u32[]{:S(2)}) collective-permute-start(f32[112,512]{1,0:T(8,128)S(1)} %convert_add_fusion), channel_id=1, source_target_pairs={{0,4},{4,0},{8,12},{12,8},{16,20},{20,16},{24,28},{28,24},{32,36},... | collective-permute-start | bytes 688136 | tf_op jit(solution)/shard_map/ppermute | solution.py:240

commit v13 on v10

--- a/solution.py
+++ b/solution.py
@@ -195,7 +195,9 @@
     units, groups, piece, enc_width = terms.shape
     width = att.shape[1]
 
-    def body(_, terms_ref, att_ref, dq_ref, behind_ref, total_ref, *full_refs):
+    def body(_, terms_ref, att_ref, dq_ref, behind_ref, total_ref, *refs):
+        full_refs, token_ref = refs[:2], refs[2]
+        token_ref[...] = jnp.zeros(token_ref.shape, jnp.float32)
         for u in range(units):
             total = add(terms_ref[u, 0], terms_ref[u, 1])
             for n in range(2, groups):
@@ -207,7 +209,7 @@
             full[:SPAN, :] = jnp.where(lead, came, ref[:SPAN, :].astype(jnp.float32)).astype(jnp.bfloat16)
             full[SPAN:, :] = ref[SPAN:, :]
 
-    out_shape = [low(units, piece, enc_width), low(*att.shape), low(*dq.shape)]
+    out_shape = [low(units, piece, enc_width), low(*att.shape), low(*dq.shape), wide(8, 128)]
     return call(body, "gather_up", out_shape, [], place, terms, att, dq, behind)
 
 
@@ -221,19 +223,11 @@
     return pl.pallas_call(
         body,
         out_shape=low(*rows[0].shape),
-        in_specs=[SMEM] + [VMEM] * len(rows) + [HBM] * len(after),
+        in_specs=[SMEM] + [VMEM] * (len(rows) + len(after)),
         out_specs=VMEM,
         compiler_params=PARAMS,
         name=name,
     )(place, *rows, *after)
-
-
-def join(place, mine, theirs):
-    def body(place_ref, mine_ref, theirs_ref, out_ref):
-        out_ref[place_ref[0]] = mine_ref[...]
-        out_ref[1 - place_ref[0]] = theirs_ref[...]
-
-    return call(body, "join", wide(2, *mine.shape), [], place, mine, theirs)
 
 
 def permute(x, axis, to):
@@ -282,10 +276,12 @@
         permute(other, ("dp", "ctx"), lambda i: i ^ (4 * owners + 2)),
     )
     rows = sum_rows(place, "z_and_y", quad, behind)
-    encoded_grad, attended, query_grad = gather_up(place, terms, att, dq, behind)
-    rows = sum_rows(place, "y", (rows, permute(rows, "ctx", lambda i: i ^ 4)), encoded_grad)
+    encoded_grad, attended, query_grad, token = gather_up(place, terms, att, dq, behind)
+    rows = sum_rows(place, "y", (rows, permute(rows, "ctx", lambda i: i ^ 4)), token)
     mine = add(rows, permute(rows, "ctx", lambda i: i ^ 8))
-    weight_grad = join(place, mine, permute(mine, "ctx", lambda i: i ^ 1))
+    theirs = permute(mine, "ctx", lambda i: i ^ 1)
+    keys_here = ctx % 2 == 0
+    weight_grad = jnp.stack((jnp.where(keys_here, mine, theirs), jnp.where(keys_here, theirs, mine)), axis=0)
     return (attended[None], query_grad[None], encoded_grad[None], weight_grad)
 
 

time: 171 us -> 169 us (0.988)
    pallas_call x3 -> x2, Pallas kernels: 4.52 us -> 3.18 us  [call(): pl.pallas_call(body, out_shape=out_shape, in_specs=[SMEM] + [VMEM] * len(...]
    unnamed x18 -> x16, local copies, waits for them, and re-layouts: 3.9 us -> 2.86 us
where the time goes in v13:
time: 169 us; the launch traced here: 168 us
  starting transfers between devices  71.4 us (42%)
  waiting for transfers between devices  69.8 us (41%)
  Pallas kernels  21.1 us (12%)
  local copies, waits for them, and re-layouts  2.98 us (2%)
  other arithmetic  2.24 us (1%)
    ppermute x12, waiting for transfers between devices, permute(): lax.ppermute(x, axis, [(i, to(i)) for i in range(n) if 0 <= to(i) < n])  67.6 us
    ppermute x12, starting transfers between devices, permute(): lax.ppermute(x, axis, [(i, to(i)) for i in range(n) if 0 <= to(i) < n])  49.8 us
    all_to_all x2, starting transfers between devices, exchange(): lax.all_to_all(x.reshape(outer * inner, *rest), ('ctx', 'nbr'), split_axi...  21.6 us
    pallas_call x1, Pallas kernels, block(): pl.pallas_call(block_body, out_shape=[low(tokens, width), low(tokens, wid...  14.4 us
  transfers between devices with their start and end apart: 14, of which 9 were waited for; matrix products, arithmetic and copies ran while one was open for 1% of the time, Pallas kernels for 2%

profile of v13, /device:TPU:1, one launch (start us, length us, event | category | flops | bytes accessed | tf_op | source)
XLA Modules:
  0.0 168.5 jit_solution(5569847158743543992)
XLA Ops:
  0.6 2.3 %spread.1 = bf16[16,4,16,896]{3,2,1,0:T(8,128)(2,1)} custom-call(bf16[16,16,896]{2,1,0:T(8,128)(2,1)} %bitcast.30), custom_call_target="tpu_custom_call" | custom-call | tf_op jit(solution)/shard_map/spread/pallas_call | solution.py:179
  3.0 14.9 %all-to-all-start = ((bf16[64,16,896]{2,1,0:T(8,128)(2,1)}), bf16[64,16,896]{2,1,0:T(8,128)(2,1)}, u32[]{:S(2)}, u32[]{:S(2)}) async-start(bf16[64,16,896]{2,1,0:T(8,128)(2,1)} %bitcast.28), calls=%async_computation | async-start | bytes 3670016 | tf_op jit(solution)/shard_map/all_to_all | solution.py:240
  18.0 2.4 %collective-permute-start = (bf16[64,1024]{1,0:T(8,128)(2,1)S(1)}, bf16[64,1024]{1,0:T(8,128)(2,1)S(1)}, u32[]{:S(2)}, u32[]{:S(2)}) collective-permute-start(bf16[64,1024]{1,0:T(8,128)(2,1)S(1)} %pad_maximum_fusion.1), channel_id=1, source_target_pairs={{4,0},{8,4},{12,8},{16,12},{20,16},{24,20},{28,24},{32,28},{36,32}... | collective-permute-start | bytes 393224 | tf_op jit(solution)/shard_map/ppermute | solution.py:235
  20.6 40.5 %collective-permute-done.ahead_hbm = bf16[64,1024]{1,0:T(8,128)(2,1)S(1)} collective-permute-done((bf16[64,1024]{1,0:T(8,128)(2,1)S(1)}, bf16[64,1024]{1,0:T(8,128)(2,1)S(1)}, u32[]{:S(2)}, u32[]{:S(2)}) %collective-permute-start) | collective-permute-done | bytes 131104 | tf_op jit(solution)/shard_map/ppermute | solution.py:235
  61.1 2.2 %all-to-all-done = bf16[64,16,896]{2,1,0:T(8,128)(2,1)} async-done(((bf16[64,16,896]{2,1,0:T(8,128)(2,1)}), bf16[64,16,896]{2,1,0:T(8,128)(2,1)}, u32[]{:S(2)}, u32[]{:S(2)}) %all-to-all-start) | async-done | bytes 1835040 | tf_op jit(solution)/shard_map/all_to_all | solution.py:240
  63.3 14.4 %block.1 = (bf16[256,512]{1,0:T(8,128)(2,1)S(1)}, bf16[256,512]{1,0:T(8,128)(2,1)S(1)}, bf16[64,1024]{1,0:T(8,128)(2,1)S(1)}, bf16[896,512]{1,0:T(8,128)(2,1)}, ...) custom-call(s32[17]{0:T(128)S(1)} %pad_add_fusion.1.units_ref, bf16[256,512]{1,0:T(8,128)(2,1)S(1)} %bitcast.26, ...), custom_call_target="tpu_custom_call" | custom-call | tf_op jit(solution)/shard_map/block/pallas_call | solution.py:127
  77.7 0.7 copy-done.3
  78.4 0.6 copy-done.5
  79.1 6.7 %all-to-all-start.1 = ((bf16[64,16,896]{2,1,0:T(8,128)(2,1)}), bf16[64,16,896]{2,1,0:T(8,128)(2,1)S(1)}, u32[]{:S(2)}, u32[]{:S(2)}) async-start(bf16[64,16,896]{2,1,0:T(8,128)(2,1)} %bitcast.29), calls=%async_computation.1 | async-start | bytes 3670016 | tf_op jit(solution)/shard_map/all_to_all | solution.py:240
  85.7 2.4 %collective-permute-start.2 = (bf16[896,512]{1,0:T(8,128)(2,1)}, bf16[896,512]{1,0:T(8,128)(2,1)S(1)}, u32[]{:S(2)}, u32[]{:S(2)}) collective-permute-start(bf16[896,512]{1,0:T(8,128)(2,1)} %get-tuple-element.26), channel_id=1, source_target_pairs={{0,4},{4,0},{8,12},{12,8},{16,20},{20,16},{24,28},{28,24},{32,36},... | collective-permute-start | bytes 2752520 | tf_op jit(solution)/shard_map/ppermute | solution.py:235
  88.2 2.2 %collective-permute-done.2.away_ref = bf16[896,512]{1,0:T(8,128)(2,1)S(1)} collective-permute-done((bf16[896,512]{1,0:T(8,128)(2,1)}, bf16[896,512]{1,0:T(8,128)(2,1)S(1)}, u32[]{:S(2)}, u32[]{:S(2)}) %collective-permute-start.2) | collective-permute-done | bytes 917536 | tf_op jit(solution)/shard_map/ppermute | solution.py:235
  90.4 1.5 copy-done
  91.9 1.5 cut.1
  93.4 3.3 %collective-permute-start.3 = (bf16[2,112,512]{2,1,0:T(8,128)(2,1)}, bf16[2,112,512]{2,1,0:T(8,128)(2,1)S(1)}, u32[]{:S(2)}, u32[]{:S(2)}) collective-permute-start(bf16[2,112,512]{2,1,0:T(8,128)(2,1)} %get-tuple-element.28), channel_id=1, source_target_pairs={{0,64},{64,128},{128,192},{192,0},{256,320},{320,384},{384,448},{4... | collective-permute-start | bytes 688136 | tf_op jit(solution)/shard_map/ppermute | solution.py:235
  96.7 3.4 %collective-permute-start.4 = (bf16[2,112,512]{2,1,0:T(8,128)(2,1)}, bf16[2,112,512]{2,1,0:T(8,128)(2,1)S(1)}, u32[]{:S(2)}, u32[]{:S(2)}) collective-permute-start(bf16[2,112,512]{2,1,0:T(8,128)(2,1)} %get-tuple-element.29), channel_id=1, source_target_pairs={{0,192},{64,0},{128,64},{192,128},{256,448},{320,256},{384,320},{4... | collective-permute-start | bytes 688136 | tf_op jit(solution)/shard_map/ppermute | solution.py:235
  100.1 3.4 %collective-permute-start.5 = (bf16[2,112,512]{2,1,0:T(8,128)(2,1)}, bf16[2,112,512]{2,1,0:T(8,128)(2,1)}, u32[]{:S(2)}, u32[]{:S(2)}) collective-permute-start(bf16[2,112,512]{2,1,0:T(8,128)(2,1)} %get-tuple-element.30), channel_id=1, source_target_pairs={{0,128},{64,192},{128,0},{192,64},{256,384},{320,448},{384,256},{4... | collective-permute-start | bytes 688136 | tf_op jit(solution)/shard_map/ppermute | solution.py:235
  103.5 4.3 %collective-permute-start.1 = (bf16[64,1024]{1,0:T(8,128)(2,1)}, bf16[64,1024]{1,0:T(8,128)(2,1)S(1)}, u32[]{:S(2)}, u32[]{:S(2)}) collective-permute-start(bf16[64,1024]{1,0:T(8,128)(2,1)} %copy-done.5), channel_id=1, source_target_pairs={{0,4},{4,8},{8,12},{12,16},{16,20},{20,24},{24,28},{28,32},{32,36}... | collective-permute-start | bytes 393224 | tf_op jit(solution)/shard_map/ppermute | solution.py:235
  107.9 2.1 %collective-permute-done.5 = bf16[2,112,512]{2,1,0:T(8,128)(2,1)} collective-permute-done((bf16[2,112,512]{2,1,0:T(8,128)(2,1)}, bf16[2,112,512]{2,1,0:T(8,128)(2,1)}, u32[]{:S(2)}, u32[]{:S(2)}) %collective-permute-start.5) | collective-permute-done | bytes 229408 | tf_op jit(solution)/shard_map/ppermute | solution.py:235
  109.9 1.2 add_convert_fusion
  111.2 7.9 %collective-permute-start.6 = (bf16[112,512]{1,0:T(8,128)(2,1)S(1)}, bf16[112,512]{1,0:T(8,128)(2,1)S(1)}, u32[]{:S(2)}, u32[]{:S(2)}) collective-permute-start(bf16[112,512]{1,0:T(8,128)(2,1)S(1)} %get-tuple-element.34), channel_id=1, source_target_pairs={{0,256},{64,320},{128,384},{192,448},{256,0},{320,64},{384,128},{4... | collective-permute-start | bytes 344072 | tf_op jit(solution)/shard_map/ppermute | solution.py:235
  119.1 3.2 %collective-permute-start.7 = (bf16[112,512]{1,0:T(8,128)(2,1)S(1)}, bf16[112,512]{1,0:T(8,128)(2,1)S(1)}, u32[]{:S(2)}, u32[]{:S(2)}) collective-permute-start(bf16[112,512]{1,0:T(8,128)(2,1)S(1)} %get-tuple-element.35.refs_0_), channel_id=1, source_target_pairs={{0,8},{4,12},{8,0},{12,4},{16,24},{20,28},{24,16},{28,20},{32,40},... | collective-permute-start | bytes 344072 | tf_op jit(solution)/shard_map/ppermute | solution.py:235
  122.4 1.9 %collective-permute-start.8 = (bf16[112,512]{1,0:T(8,128)(2,1)S(1)}, bf16[112,512]{1,0:T(8,128)(2,1)S(1)}, u32[]{:S(2)}, u32[]{:S(2)}) collective-permute-start(bf16[112,512]{1,0:T(8,128)(2,1)S(1)} %get-tuple-element.34), channel_id=1, source_target_pairs={{0,264},{4,268},{8,256},{12,260},{16,280},{20,284},{24,272},{28,27... | collective-permute-start | bytes 344072 | tf_op jit(solution)/shard_map/ppermute | solution.py:235
  124.3 2.5 %collective-permute-done.1.behind_ref.refs_4_ = bf16[64,1024]{1,0:T(8,128)(2,1)S(1)} collective-permute-done((bf16[64,1024]{1,0:T(8,128)(2,1)}, bf16[64,1024]{1,0:T(8,128)(2,1)S(1)}, u32[]{:S(2)}, u32[]{:S(2)}) %collective-permute-start.1) | collective-permute-done | bytes 131104 | tf_op jit(solution)/shard_map/ppermute | solution.py:235
  126.8 13.9 %collective-permute-done.6.refs_1_ = bf16[112,512]{1,0:T(8,128)(2,1)S(1)} collective-permute-done((bf16[112,512]{1,0:T(8,128)(2,1)S(1)}, bf16[112,512]{1,0:T(8,128)(2,1)S(1)}, u32[]{:S(2)}, u32[]{:S(2)}) %collective-permute-start.6) | collective-permute-done | bytes 114720 | tf_op jit(solution)/shard_map/ppermute | solution.py:235
  141.3 3.4 %collective-permute-start.9 = (bf16[112,512]{1,0:T(8,128)(2,1)S(1)}, bf16[112,512]{1,0:T(8,128)(2,1)S(1)}, u32[]{:S(2)}, u32[]{:S(2)}) collective-permute-start(bf16[112,512]{1,0:T(8,128)(2,1)S(1)} %z_and_y.1.refs_0_), channel_id=1, source_target_pairs={{0,16},{4,20},{8,24},{12,28},{16,0},{20,4},{24,8},{28,12},{32,48},... | collective-permute-start | bytes 344072 | tf_op jit(solution)/shard_map/ppermute | solution.py:235
  144.7 1.6 gather_up.1
  146.4 1.4 collective-permute-done.9.refs_1_
  148.3 5.6 %collective-permute-start.10 = (bf16[112,512]{1,0:T(8,128)(2,1)S(1)}, bf16[112,512]{1,0:T(8,128)(2,1)S(1)}, u32[]{:S(2)}, u32[]{:S(2)}) collective-permute-start(bf16[112,512]{1,0:T(8,128)(2,1)S(1)} %y.1), channel_id=1, source_target_pairs={{0,32},{4,36},{8,40},{12,44},{16,48},{20,52},{24,56},{28,60},{32,0... | collective-permute-start | bytes 344072 | tf_op jit(solution)/shard_map/ppermute | solution.py:235
  154.0 3.9 %collective-permute-done.10 = bf16[112,512]{1,0:T(8,128)(2,1)S(1)} collective-permute-done((bf16[112,512]{1,0:T(8,128)(2,1)S(1)}, bf16[112,512]{1,0:T(8,128)(2,1)S(1)}, u32[]{:S(2)}, u32[]{:S(2)}) %collective-permute-start.10) | collective-permute-done | bytes 114720 | tf_op jit(solution)/shard_map/ppermute | solution.py:235
  157.9 8.6 %collective-permute-start.11 = (f32[112,512]{1,0:T(8,128)S(1)}, f32[112,512]{1,0:T(8,128)S(1)}, u32[]{:S(2)}, u32[]{:S(2)}) collective-permute-start(f32[112,512]{1,0:T(8,128)S(1)} %convert_add_fusion), channel_id=1, source_target_pairs={{0,4},{4,0},{8,12},{12,8},{16,20},{20,16},{24,28},{28,24},{32,36},... | collective-permute-start | bytes 688136 | tf_op jit(solution)/shard_map/ppermute | solution.py:235
  166.5 1.1 collective-permute-done.11
  167.7 0.8 pad_maximum_fusion
  (29 shorter events, 1.6 us)
Async XLA Ops:
  3.0 14.9 %copy-start.1 = (bf16[1,256,512]{2,1,0:T(8,128)(2,1)S(1)}, bf16[1,256,512]{2,1,0:T(8,128)(2,1)}, u32[]{:S(2)}) copy-start(bf16[1,256,512]{2,1,0:T(8,128)(2,1)} %param.5) | copy-start | bytes 786436
  3.0 14.9 %copy-start.2 = (bf16[1,256,512]{2,1,0:T(8,128)(2,1)S(1)}, bf16[1,256,512]{2,1,0:T(8,128)(2,1)}, u32[]{:S(2)}) copy-start(bf16[1,256,512]{2,1,0:T(8,128)(2,1)} %param.6) | copy-start | bytes 786436
  3.0 17.4 %copy-start.7 = (s32[1,4,4]{2,1,0:T(4,128)S(1)}, s32[1,4,4]{2,1,0:T(4,128)}, u32[]{:S(2)}) copy-start(s32[1,4,4]{2,1,0:T(4,128)} %param.9) | copy-start | bytes 196
  3.0 60.3 %all-to-all-start = ((bf16[64,16,896]{2,1,0:T(8,128)(2,1)}), bf16[64,16,896]{2,1,0:T(8,128)(2,1)}, u32[]{:S(2)}, u32[]{:S(2)}) async-start(bf16[64,16,896]{2,1,0:T(8,128)(2,1)} %bitcast.28), calls=%async_computation | async-start | bytes 3670016 | tf_op jit(solution)/shard_map/all_to_all | solution.py:240
  18.0 43.1 %collective-permute-start = (bf16[64,1024]{1,0:T(8,128)(2,1)S(1)}, bf16[64,1024]{1,0:T(8,128)(2,1)S(1)}, u32[]{:S(2)}, u32[]{:S(2)}) collective-permute-start(bf16[64,1024]{1,0:T(8,128)(2,1)S(1)} %pad_maximum_fusion.1), channel_id=1, source_target_pairs={{4,0},{8,4},{12,8},{16,12},{20,16},{24,20},{28,24},{32,28},{36,32}... | collective-permute-start | bytes 393224 | tf_op jit(solution)/shard_map/ppermute | solution.py:235
  77.7 0.7 copy-start.3
  78.4 0.6 copy-start.5
  79.1 65.6 %all-to-all-start.1 = ((bf16[64,16,896]{2,1,0:T(8,128)(2,1)}), bf16[64,16,896]{2,1,0:T(8,128)(2,1)S(1)}, u32[]{:S(2)}, u32[]{:S(2)}) async-start(bf16[64,16,896]{2,1,0:T(8,128)(2,1)} %bitcast.29), calls=%async_computation.1 | async-start | bytes 3670016 | tf_op jit(solution)/shard_map/all_to_all | solution.py:240
  85.7 4.7 %collective-permute-start.2 = (bf16[896,512]{1,0:T(8,128)(2,1)}, bf16[896,512]{1,0:T(8,128)(2,1)S(1)}, u32[]{:S(2)}, u32[]{:S(2)}) collective-permute-start(bf16[896,512]{1,0:T(8,128)(2,1)} %get-tuple-element.26), channel_id=1, source_target_pairs={{0,4},{4,0},{8,12},{12,8},{16,20},{20,16},{24,28},{28,24},{32,36},... | collective-permute-start | bytes 2752520 | tf_op jit(solution)/shard_map/ppermute | solution.py:235
  90.4 1.5 copy-start
  93.4 51.3 %copy-start.4 = (bf16[256,512]{1,0:T(8,128)(2,1)S(1)}, bf16[256,512]{1,0:T(8,128)(2,1)}, u32[]{:S(2)}) copy-start(bf16[256,512]{1,0:T(8,128)(2,1)} %copy-done.3) | copy-start | bytes 786436
  93.4 14.4 %collective-permute-start.3 = (bf16[2,112,512]{2,1,0:T(8,128)(2,1)}, bf16[2,112,512]{2,1,0:T(8,128)(2,1)S(1)}, u32[]{:S(2)}, u32[]{:S(2)}) collective-permute-start(bf16[2,112,512]{2,1,0:T(8,128)(2,1)} %get-tuple-element.28), channel_id=1, source_target_pairs={{0,64},{64,128},{128,192},{192,0},{256,320},{320,384},{384,448},{4... | collective-permute-start | bytes 688136 | tf_op jit(solution)/shard_map/ppermute | solution.py:235
  96.7 11.2 %collective-permute-start.4 = (bf16[2,112,512]{2,1,0:T(8,128)(2,1)}, bf16[2,112,512]{2,1,0:T(8,128)(2,1)S(1)}, u32[]{:S(2)}, u32[]{:S(2)}) collective-permute-start(bf16[2,112,512]{2,1,0:T(8,128)(2,1)} %get-tuple-element.29), channel_id=1, source_target_pairs={{0,192},{64,0},{128,64},{192,128},{256,448},{320,256},{384,320},{4... | collective-permute-start | bytes 688136 | tf_op jit(solution)/shard_map/ppermute | solution.py:235
  100.1 9.9 %collective-permute-start.5 = (bf16[2,112,512]{2,1,0:T(8,128)(2,1)}, bf16[2,112,512]{2,1,0:T(8,128)(2,1)}, u32[]{:S(2)}, u32[]{:S(2)}) collective-permute-start(bf16[2,112,512]{2,1,0:T(8,128)(2,1)} %get-tuple-element.30), channel_id=1, source_target_pairs={{0,128},{64,192},{128,0},{192,64},{256,384},{320,448},{384,256},{4... | collective-permute-start | bytes 688136 | tf_op jit(solution)/shard_map/ppermute | solution.py:235
  103.5 23.3 %collective-permute-start.1 = (bf16[64,1024]{1,0:T(8,128)(2,1)}, bf16[64,1024]{1,0:T(8,128)(2,1)S(1)}, u32[]{:S(2)}, u32[]{:S(2)}) collective-permute-start(bf16[64,1024]{1,0:T(8,128)(2,1)} %copy-done.5), channel_id=1, source_target_pairs={{0,4},{4,8},{8,12},{12,16},{16,20},{20,24},{24,28},{28,32},{32,36}... | collective-permute-start | bytes 393224 | tf_op jit(solution)/shard_map/ppermute | solution.py:235
  107.9 2.1 %copy-start.6 = (bf16[2,112,512]{2,1,0:T(8,128)(2,1)}, bf16[2,112,512]{2,1,0:T(8,128)(2,1)S(1)}, u32[]{:S(2)}) copy-start(bf16[2,112,512]{2,1,0:T(8,128)(2,1)S(1)} %collective-permute-done.4) | copy-start | bytes 688132
  111.2 29.5 %collective-permute-start.6 = (bf16[112,512]{1,0:T(8,128)(2,1)S(1)}, bf16[112,512]{1,0:T(8,128)(2,1)S(1)}, u32[]{:S(2)}, u32[]{:S(2)}) collective-permute-start(bf16[112,512]{1,0:T(8,128)(2,1)S(1)} %get-tuple-element.34), channel_id=1, source_target_pairs={{0,256},{64,320},{128,384},{192,448},{256,0},{320,64},{384,128},{4... | collective-permute-start | bytes 344072 | tf_op jit(solution)/shard_map/ppermute | solution.py:235
  119.1 21.6 %collective-permute-start.7 = (bf16[112,512]{1,0:T(8,128)(2,1)S(1)}, bf16[112,512]{1,0:T(8,128)(2,1)S(1)}, u32[]{:S(2)}, u32[]{:S(2)}) collective-permute-start(bf16[112,512]{1,0:T(8,128)(2,1)S(1)} %get-tuple-element.35.refs_0_), channel_id=1, source_target_pairs={{0,8},{4,12},{8,0},{12,4},{16,24},{20,28},{24,16},{28,20},{32,40},... | collective-permute-start | bytes 344072 | tf_op jit(solution)/shard_map/ppermute | solution.py:235
  122.4 18.4 %collective-permute-start.8 = (bf16[112,512]{1,0:T(8,128)(2,1)S(1)}, bf16[112,512]{1,0:T(8,128)(2,1)S(1)}, u32[]{:S(2)}, u32[]{:S(2)}) collective-permute-start(bf16[112,512]{1,0:T(8,128)(2,1)S(1)} %get-tuple-element.34), channel_id=1, source_target_pairs={{0,264},{4,268},{8,256},{12,260},{16,280},{20,284},{24,272},{28,27... | collective-permute-start | bytes 344072 | tf_op jit(solution)/shard_map/ppermute | solution.py:235
  141.3 6.4 %collective-permute-start.9 = (bf16[112,512]{1,0:T(8,128)(2,1)S(1)}, bf16[112,512]{1,0:T(8,128)(2,1)S(1)}, u32[]{:S(2)}, u32[]{:S(2)}) collective-permute-start(bf16[112,512]{1,0:T(8,128)(2,1)S(1)} %z_and_y.1.refs_0_), channel_id=1, source_target_pairs={{0,16},{4,20},{8,24},{12,28},{16,0},{20,4},{24,8},{28,12},{32,48},... | collective-permute-start | bytes 344072 | tf_op jit(solution)/shard_map/ppermute | solution.py:235
  148.3 9.5 %collective-permute-start.10 = (bf16[112,512]{1,0:T(8,128)(2,1)S(1)}, bf16[112,512]{1,0:T(8,128)(2,1)S(1)}, u32[]{:S(2)}, u32[]{:S(2)}) collective-permute-start(bf16[112,512]{1,0:T(8,128)(2,1)S(1)} %y.1), channel_id=1, source_target_pairs={{0,32},{4,36},{8,40},{12,44},{16,48},{20,52},{24,56},{28,60},{32,0... | collective-permute-start | bytes 344072 | tf_op jit(solution)/shard_map/ppermute | solution.py:235
  157.9 9.7 %collective-permute-start.11 = (f32[112,512]{1,0:T(8,128)S(1)}, f32[112,512]{1,0:T(8,128)S(1)}, u32[]{:S(2)}, u32[]{:S(2)}) collective-permute-start(f32[112,512]{1,0:T(8,128)S(1)} %convert_add_fusion), channel_id=1, source_target_pairs={{0,4},{4,0},{8,12},{12,8},{16,20},{20,16},{24,28},{28,24},{32,36},... | collective-permute-start | bytes 688136 | tf_op jit(solution)/shard_map/ppermute | solution.py:235
